TPU v7x, 32 devices: a whole 2x2x4 slice. The times are simulated.
32 devices in a mesh: segment: 2 (over x), dp: 4 (over z), tensor: 4 (over y, core).
Axes of the slice: x: 2, y: 2, z: 4, core: 2. Of those that a mesh axis runs over, the one named last changes fastest.
Arguments:
- hidden_in: bfloat16 [2, 2, 1024, 8192], P('segment', None, ('dp', 'tensor')), may hold values from -600 to 600
- norm_gain: float32 [2, 8192], P('segment'), may hold values from 0.5 to 1.5
- kv_cot: bfloat16 [2, 2, 1024, 1024], P('segment', None, 'dp', 'tensor'), may hold values from -6 to 6
- master_kv: float32 [2, 8192, 1024], P('segment', 'dp', 'tensor'), may hold values from -0.0625 to 0.0625
- moment_m: float32 [2, 8192, 1024], P('segment', 'dp', 'tensor'), may hold values from -128 to 128
- moment_v: float32 [2, 8192, 1024], P('segment', 'dp', 'tensor'), may hold values from 102.4 to 2048
Outputs:
- kv_own: bfloat16 [2, 2, 1024, 1024], P('segment', None, 'dp', 'tensor')
- grad_in: bfloat16 [2, 2, 1024, 8192], P('segment', None, ('dp', 'tensor'))
- master_new: float32 [2, 8192, 1024], P('segment', 'dp', 'tensor')
- kv_next: bfloat16 [2, 2, 1024, 1024], P('segment', None, 'dp', 'tensor')
All inputs are finite; a program needn't handle non-finite values.
Results may differ from a plain program's by a relative error of at most 0.012.
Values may be sent and summed in bfloat16 or wider, within the bound.
No kernel may reach another device: no remote copies, remote signals or barrier semaphores. Data moves between devices by JAX's collectives and lax.ppermute only.
A program may use at most 128 MiB of HBM per device.

v0:
```python
import jax
import jax.numpy as jnp
from jax import lax
from jax.sharding import PartitionSpec as P

beta_first = 0.9
beta_second = 0.95
learn_rate = 0.03
weight_decay = 0.1
adam_eps = 1e-08
norm_eps = 1e-05
step_count = 20.0


def from_behind(x, axis, by):
    peers = lax.axis_size(axis)
    return lax.ppermute(x, axis, [(i, (i + by) % peers) for i in range(peers)])


def shards(hidden_in, norm_gain, kv_cot, master_kv, moment_m, moment_v):
    gain_row = norm_gain[0]
    widened = hidden_in[0].astype(jnp.float32)
    tokens_local = widened.shape[1]
    scaling = lax.rsqrt(jnp.mean(widened * widened, axis=-1, keepdims=True) + norm_eps)
    normed = (widened * scaling * gain_row).astype(jnp.bfloat16)
    gathered = lax.all_gather(normed, "tensor", axis=1, tiled=True)
    weights = master_kv[0].astype(jnp.bfloat16)
    full_weights = lax.all_gather(weights, "dp", axis=0, tiled=True)
    cotangent = kv_cot[0]
    kv_own = jnp.einsum(
        "mrd,dc->mrc", gathered, full_weights, preferred_element_type=jnp.float32
    ).astype(jnp.bfloat16)
    grad_w = lax.psum_scatter(
        jnp.einsum("mrd,mrc->dc", gathered, cotangent, preferred_element_type=jnp.float32).astype(
            jnp.bfloat16
        ),
        "dp",
        scatter_dimension=0,
        tiled=True,
    ).astype(jnp.float32)
    partial_value = jnp.einsum(
        "mrc,dc->mrd", cotangent, full_weights, preferred_element_type=jnp.float32
    )
    summed = lax.psum(partial_value.astype(jnp.bfloat16), "tensor").astype(jnp.float32)
    d_normed = lax.dynamic_slice_in_dim(
        summed, lax.axis_index("tensor") * tokens_local, tokens_local, 1
    )
    upper = d_normed * gain_row
    grad_in = (
        scaling * upper - widened * scaling**3 * jnp.mean(upper * widened, axis=-1, keepdims=True)
    ).astype(jnp.bfloat16)
    master = master_kv[0]
    m_new = beta_first * moment_m[0] + (1.0 - beta_first) * grad_w
    v_new = beta_second * moment_v[0] + (1.0 - beta_second) * grad_w * grad_w
    m_hat = m_new / (1.0 - beta_first**step_count)
    v_hat = v_new / (1.0 - beta_second**step_count)
    master_new = master - learn_rate * (
        m_hat / (jnp.sqrt(v_hat) + adam_eps) + weight_decay * master
    )
    updated = master_new.astype(jnp.bfloat16)
    updated_whole = lax.all_gather(updated, "dp", axis=0, tiled=True)
    mine = jnp.einsum(
        "mrd,dc->mrc", gathered, updated_whole, preferred_element_type=jnp.float32
    ).astype(jnp.bfloat16)
    kv_next = from_behind(mine, "segment", -1)
    return (kv_own[None], grad_in[None], master_new[None], kv_next[None])


def solution(mesh):
    in_specs = (
        P("segment", None, ("dp", "tensor"), None),
        P("segment", None),
        P("segment", None, "dp", "tensor"),
        P("segment", "dp", "tensor"),
        P("segment", "dp", "tensor"),
        P("segment", "dp", "tensor"),
    )
    out_specs = (
        P("segment", None, "dp", "tensor"),
        P("segment", None, ("dp", "tensor"), None),
        P("segment", "dp", "tensor"),
        P("segment", None, "dp", "tensor"),
    )
    return jax.shard_map(shards, mesh=mesh, in_specs=in_specs, out_specs=out_specs, check_vma=False)
```

profile of v0, /device:TPU:0, one launch (start us, length us, event | category | flops | bytes accessed | tf_op | source)
XLA Modules:
  0.0 514.4 jit_solution(5955743388856928706)
XLA Ops:
  7.2 0.0 copy-start
  7.2 0.0 all-gather.6.cloned.1.call-start
  7.2 2.7 bitcast_convert_fusion
  9.9 0.0 all-gather.6.cloned.1.call-update
  9.9 0.0 all-reduce.2.cloned.1.call-start
  10.0 83.7 %all-gather.6.cloned.1.call-done = bf16[8192,256]{1,0:T(8,128)(2,1)} async-done(((bf16[2048,256]{1,0:T(8,128)(2,1)}), bf16[8192,256]{1,0:T(8,128)(2,1)}) %all-gather.6.cloned.1.call-update) | async-done | bytes 4194320 | tf_op jit(solution)/shard_map/all_gather | solution.py:28
  93.7 0.0 copy-done
  93.7 7.8 %convolution_convert_fusion = bf16[2,256,8192]{2,1,0:T(8,128)(2,1)} fusion(bf16[8192,256]{1,0:T(8,128)(2,1)} %all-gather.6.cloned.1.call-done, bf16[1,2,256,256]{3,2,1,0:T(8,128)(2,1)S(1)} %copy-done), kind=kOutput, calls=%fused_computation | convolution fusion | flops 2151677952 | bytes 12845056 | tf_op jit(solution)/shard_map/mrc,dc->mrd/dot_general | solution.py:41
  101.5 0.0 all-reduce.2.cloned.1.call-update
  101.5 0.0 all-gather.4.cloned.1.call-start
  101.5 151.5 %all-reduce.2.cloned.1.call-done = bf16[2,256,8192]{2,1,0:T(8,128)(2,1)} async-done(((bf16[2,256,8192]{2,1,0:T(8,128)(2,1)}), bf16[2,256,8192]{2,1,0:T(8,128)(2,1)}) %all-reduce.2.cloned.1.call-update) | async-done | bytes 8388624 | tf_op jit(solution)/shard_map/psum | solution.py:44
  253.0 0.0 copy-done.1
  253.0 0.0 copy-done.4
  253.0 2.7 fusion.7
  255.7 5.6 %fusion.23 = (bf16[1,2,64,8192]{3,2,1,0:T(8,128)(2,1)}, bf16[2,64,8192]{2,1,0:T(8,128)(2,1)}) fusion(bf16[1,2,64,8192]{3,2,1,0:T(8,128)(2,1)S(1)} %copy-done.1, f32[2,64]{1,0:T(2,128)S(1)} %get-tuple-element.12, f32[2,64]{1,0:T(2,128)S(1)} %get-tuple-element.10, f32[8192]{0:T(1024)S(1)} %bitcast.55, f32[2,64]{1,0:T(2,128)S(1)} %get-tuple-element.11, ...), kind=kLoop, calls=%fused_computation.32 | loop fusion | flops 11534336 | bytes 8422916 | tf_op jit(solution)/shard_map/broadcast_in_dim | solution.py:66
  261.3 0.0 all-gather.4.cloned.1.call-update
  261.3 0.0 reduce-scatter.2.cloned.1.call-start
  261.4 58.5 %all-gather.4.cloned.1.call-done = bf16[2,256,8192]{2,1,0:T(8,128)(2,1)} async-done(((bf16[2,64,8192]{2,1,0:T(8,128)(2,1)}), bf16[2,256,8192]{2,1,0:T(8,128)(2,1)}) %all-gather.4.cloned.1.call-update) | async-done | bytes 8388624 | tf_op jit(solution)/shard_map/all_gather | solution.py:26
  319.9 7.8 %fusion = bf16[8192,256]{1,0:T(8,128)(2,1)} fusion(bf16[2,256,8192]{2,1,0:T(8,128)(2,1)} %all-gather.4.cloned.1.call-done, bf16[1,2,256,256]{3,2,1,0:T(8,128)(2,1)S(1)} %copy-done), kind=kOutput, calls=%fused_computation.2 | convolution fusion | flops 2149580800 | bytes 12845056 | tf_op jit(solution)/shard_map/mrd,mrc->dc/dot_general | solution.py:34
  327.7 0.0 reduce-scatter.2.cloned.1.call-update
  327.7 0.2 all-gather.8.cloned.1.call-start
  327.9 76.7 %reduce-scatter.2.cloned.1.call-done = bf16[2048,256]{1,0:T(8,128)(2,1)} async-done(((bf16[8192,256]{1,0:T(8,128)(2,1)}), bf16[2048,256]{1,0:T(8,128)(2,1)}) %reduce-scatter.2.cloned.1.call-update) | async-done | bytes 1048592 | tf_op jit(solution)/shard_map/reduce_scatter | solution.py:33
  404.6 0.0 copy-done.2
  404.6 5.9 %fusion.35 = (bf16[2048,256]{1,0:T(8,128)(2,1)}, f32[2048,256]{1,0:T(8,128)}) fusion(f32[1,2048,256]{2,1,0:T(8,128)} %param.11, bf16[2048,256]{1,0:T(8,128)(2,1)} %reduce-scatter.2.cloned.1.call-done, f32[1,2048,256]{2,1,0:T(8,128)} %param.10, f32[1,2048,256]{2,1,0:T(8,128)S(1)} %copy-done.2), kind=kLoop, calls=%fused_computation.43 | loop fusion | flops 8912896 | bytes 10485760 | tf_op jit(solution)/shard_map/convert_element_type | solution.py:60
  410.5 0.0 all-gather.8.cloned.1.call-update
  410.5 81.4 %all-gather.8.cloned.1.call-done = bf16[8192,256]{1,0:T(8,128)(2,1)} async-done(((bf16[2048,256]{1,0:T(8,128)(2,1)}), bf16[8192,256]{1,0:T(8,128)(2,1)}) %all-gather.8.cloned.1.call-update) | async-done | bytes 4194320 | tf_op jit(solution)/shard_map/all_gather | solution.py:61
  491.9 7.0 %fusion.27 = bf16[2,256,256]{2,1,0:T(8,128)(2,1)S(1)} fusion(bf16[2,256,8192]{2,1,0:T(8,128)(2,1)} %all-gather.4.cloned.1.call-done, bf16[8192,256]{1,0:T(8,128)(2,1)} %all-gather.8.cloned.1.call-done), kind=kOutput, calls=%fused_computation.36 | convolution fusion | flops 2147614720 | bytes 12845056 | tf_op jit(solution)/shard_map/mrd,dc->mrc/dot_general | solution.py:62
  499.0 1.6 collective-permute-start
  500.6 0.0 copy-done.3
  500.6 6.4 %fusion.30 = bf16[1,2,256,256]{3,2,1,0:T(8,128)(2,1)} fusion(bf16[2,256,8192]{2,1,0:T(8,128)(2,1)} %all-gather.4.cloned.1.call-done, bf16[8192,256]{1,0:T(8,128)(2,1)S(1)} %copy-done.3), kind=kOutput, calls=%fused_computation.37 | convolution fusion | flops 2147614720 | bytes 12845056 | tf_op jit(solution)/shard_map/mrd,dc->mrc/dot_general | solution.py:30
  507.0 0.1 collective-permute-done
  507.1 0.7 copy.12
  (5 shorter events, 0.0 us)
Async XLA Ops:
  7.2 86.5 %copy-start = (bf16[1,2,256,256]{3,2,1,0:T(8,128)(2,1)S(1)}, bf16[1,2,256,256]{3,2,1,0:T(8,128)(2,1)}, u32[]{:S(2)}) copy-start(bf16[1,2,256,256]{3,2,1,0:T(8,128)(2,1)} %param.8) | copy-start | bytes 786436
  7.2 86.5 %all-gather.6.cloned.1.call-start = ((), (), s32[]{:S(2)}) async-start(), calls=%async_computation.2 | async-start | bytes 5242880 | tf_op jit(solution)/shard_map/all_gather | solution.py:28
  9.9 243.1 %all-reduce.2.cloned.1.call-start = ((), (), s32[]{:S(2)}) async-start(), calls=%async_computation.3 | async-start | bytes 16777216 | tf_op jit(solution)/shard_map/psum | solution.py:44
  101.5 151.6 %copy-start.1 = (bf16[1,2,64,8192]{3,2,1,0:T(8,128)(2,1)S(1)}, bf16[1,2,64,8192]{3,2,1,0:T(8,128)(2,1)}, u32[]{:S(2)}) copy-start(bf16[1,2,64,8192]{3,2,1,0:T(8,128)(2,1)} %param.6) | copy-start | bytes 6291460
  101.5 151.6 %copy-start.4 = (f32[1,8192]{1,0:T(1,128)S(1)}, f32[1,8192]{1,0:T(1,128)}, u32[]{:S(2)}) copy-start(f32[1,8192]{1,0:T(1,128)} %param.7) | copy-start | bytes 98308
  101.5 218.4 %all-gather.4.cloned.1.call-start = ((), (), s32[]{:S(2)}) async-start(), calls=%async_computation.1 | async-start | bytes 10485760 | tf_op jit(solution)/shard_map/all_gather | solution.py:26
  261.3 143.3 %reduce-scatter.2.cloned.1.call-start = ((), (), s32[]{:S(2)}) async-start(), calls=%async_computation.4 | async-start | bytes 5242880 | tf_op jit(solution)/shard_map/reduce_scatter | solution.py:33
  327.7 77.0 %copy-start.2 = (f32[1,2048,256]{2,1,0:T(8,128)S(1)}, f32[1,2048,256]{2,1,0:T(8,128)}, u32[]{:S(2)}) copy-start(f32[1,2048,256]{2,1,0:T(8,128)} %param.9) | copy-start | bytes 6291460
  327.7 164.3 %all-gather.8.cloned.1.call-start = ((), (), s32[]{:S(2)}) async-start(), calls=%async_computation.5 | async-start | bytes 5242880 | tf_op jit(solution)/shard_map/all_gather | solution.py:61
  491.9 8.6 %copy-start.3 = (bf16[8192,256]{1,0:T(8,128)(2,1)S(1)}, bf16[8192,256]{1,0:T(8,128)(2,1)}, u32[]{:S(2)}) copy-start(bf16[8192,256]{1,0:T(8,128)(2,1)} %all-gather.6.cloned.1.call-done) | copy-start | bytes 12582916
  499.0 8.1 %collective-permute-start = (bf16[2,256,256]{2,1,0:T(8,128)(2,1)S(1)}, bf16[2,256,256]{2,1,0:T(8,128)(2,1)S(1)}, u32[]{:S(2)}, u32[]{:S(2)}) collective-permute-start(bf16[2,256,256]{2,1,0:T(8,128)(2,1)S(1)} %fusion.27), channel_id=1, source_target_pairs={{0,16},{16,0},{1,17},{17,1},{2,18},{18,2},{3,19},{19,3},{4,20},{20... | collective-permute-start | bytes 786440 | tf_op jit(solution)/shard_map/ppermute | solution.py:17
Sparse Core Ops, SparseCore 0:
  10.2 83.4 all-gather.5
  101.6 151.3 all-reduce.1
  261.4 58.4 all-gather.3
  327.8 76.7 reduce-scatter.1
  410.6 81.2 all-gather.7
where the time goes:
time: 515 us; the launch traced here: 514 us
  waiting for transfers between devices  452 us (88%)
  matrix products  29 us (6%)
  other arithmetic  16.8 us (3%)
  between operations  13.8 us (3%)
    psum x1, waiting for transfers between devices, shards(): lax.psum(partial_value.astype(jnp.bfloat16), 'tensor').astype(jnp.float32)  151 us
    all_gather x1, waiting for transfers between devices, shards(): full_weights = lax.all_gather(weights, 'dp', axis=0, tiled=True)  83.7 us
    all_gather x1, waiting for transfers between devices, shards(): updated_whole = lax.all_gather(updated, 'dp', axis=0, tiled=True)  81.4 us
    reduce_scatter x1, waiting for transfers between devices, shards(): lax.psum_scatter(jnp.einsum('mrd,mrc->dc', gathered, cotangent, preferred...  76.7 us
    all_gather x1, waiting for transfers between devices, shards(): gathered = lax.all_gather(normed, 'tensor', axis=1, tiled=True)  58.5 us
  transfers between devices with their start and end apart: 6, of which 6 were waited for; matrix products, arithmetic and copies ran while one was open for 1% of the time, Pallas kernels for 0%

commit v1 on v0

v1 whole, which is shorter than its diff:
```python
import jax
import jax.numpy as jnp
from jax import lax
from jax.sharding import PartitionSpec as P

beta_first = 0.9
beta_second = 0.95
learn_rate = 0.03
weight_decay = 0.1
adam_eps = 1e-08
norm_eps = 1e-05
step_count = 20.0

f32 = jnp.float32
bf16 = jnp.bfloat16


def swap(x, axis, bits):
    peers = lax.axis_size(axis)
    return lax.ppermute(x, axis, [(i, i ^ bits) for i in range(peers)])


def from_behind(x, axis, by):
    peers = lax.axis_size(axis)
    return lax.ppermute(x, axis, [(i, (i + by) % peers) for i in range(peers)])


def dot(a, b, contract):
    return lax.dot_general(a, b, (contract, ((), ())), preferred_element_type=f32)


def reorder(blocks, me):
    bit = 1
    while bit < len(blocks):
        flip = (me & bit) != 0
        blocks = [jnp.where(flip, blocks[i ^ bit], blocks[i]) for i in range(len(blocks))]
        bit *= 2
    return blocks


def scatter_sum(parts):
    r1 = swap(parts[1], "dp", 1)
    r3 = swap(parts[3], "dp", 1)
    mine = parts[0].astype(f32) + r1.astype(f32)
    other = (parts[2].astype(f32) + r3.astype(f32)).astype(bf16)
    return mine + swap(other, "dp", 2).astype(f32)


def shards(hidden_in, norm_gain, kv_cot, master_kv, moment_m, moment_v):
    dp, tensor = lax.axis_size("dp"), lax.axis_size("tensor")
    z, t = lax.axis_index("dp"), lax.axis_index("tensor")
    gain_row = norm_gain[0]
    widened = hidden_in[0].astype(f32)
    micro, rows, width = widened.shape
    depth = width // dp
    cols = kv_cot.shape[-1]
    scaling = lax.rsqrt(jnp.mean(widened * widened, axis=-1, keepdims=True) + norm_eps)
    normed = (widened * scaling * gain_row).astype(bf16)

    def feature_block(x, k):
        return lax.dynamic_slice_in_dim(x, (z ^ k) * depth, depth, x.ndim - 1)

    own = [feature_block(normed, k).reshape(micro * rows, depth) for k in range(dp)]
    pieces = [own[0]] + [swap(own[k], "dp", k) for k in range(1, dp)]
    cot = kv_cot[0].reshape(micro, tensor, rows, cols)
    cot = jnp.stack(
        [
            lax.dynamic_slice_in_dim(cot, t ^ j, 1, 1).reshape(micro * rows, cols)
            for j in range(tensor)
        ]
    )
    cot2 = swap(cot, "dp", 2)
    cots = [cot, swap(cot, "dp", 1), cot2, swap(cot2, "dp", 1)]
    weights = master_kv[0].astype(bf16)
    w2 = swap(weights, "tensor", 2)
    whole_w = jnp.concatenate([weights, swap(weights, "tensor", 1), w2, swap(w2, "tensor", 1)], 1)
    gathered = []
    for piece in pieces:
        across = swap(piece, "tensor", 2)
        gathered += [piece, swap(piece, "tensor", 1), across, swap(across, "tensor", 1)]
    tokens = jnp.concatenate(gathered)
    cot_all = jnp.concatenate(cots).reshape(-1, cols)
    block = tensor * micro * rows

    def by_replica(x):
        return [x[k * block : (k + 1) * block] for k in range(dp)]

    def place(x):
        x = x.reshape(tensor, micro, rows, cols)
        return jnp.stack(reorder([x[j] for j in range(tensor)], t), 1).reshape(
            1, micro, tensor * rows, cols
        )

    kv_part = dot(tokens, weights, ((1,), (0,))).astype(bf16)
    kv_own = place(scatter_sum(by_replica(kv_part)).astype(bf16))

    mine_cot = []
    for j in range(tensor):
        rows_j = jnp.concatenate([c[j] for c in cots])
        mine_cot.append(rows_j if j == 0 else swap(rows_j, "tensor", j))
    d_part = dot(jnp.concatenate(mine_cot, 1), whole_w, ((1,), (1,))).astype(bf16)
    d_part = d_part.reshape(dp, micro, rows, depth)
    d_blocks = [d_part[0]] + [swap(d_part[k], "dp", k) for k in range(1, dp)]
    d_normed = jnp.concatenate(reorder(d_blocks, z), -1).astype(f32)
    upper = d_normed * gain_row
    grad_in = (
        scaling * upper - widened * scaling**3 * jnp.mean(upper * widened, axis=-1, keepdims=True)
    ).astype(bf16)

    grad_w = dot(tokens, cot_all, ((0,), (0,)))
    master = master_kv[0]
    m_new = beta_first * moment_m[0] + (1.0 - beta_first) * grad_w
    v_new = beta_second * moment_v[0] + (1.0 - beta_second) * grad_w * grad_w
    m_hat = m_new / (1.0 - beta_first**step_count)
    v_hat = v_new / (1.0 - beta_second**step_count)
    master_new = master - learn_rate * (
        m_hat / (jnp.sqrt(v_hat) + adam_eps) + weight_decay * master
    )
    updated = master_new.astype(bf16)
    next_part = dot(tokens, updated, ((1,), (0,))).astype(bf16)
    mine = place(scatter_sum(by_replica(next_part)).astype(bf16))
    kv_next = from_behind(mine, "segment", -1)
    return (kv_own, grad_in[None], master_new[None], kv_next)


def solution(mesh):
    in_specs = (
        P("segment", None, ("dp", "tensor"), None),
        P("segment", None),
        P("segment", None, "dp", "tensor"),
        P("segment", "dp", "tensor"),
        P("segment", "dp", "tensor"),
        P("segment", "dp", "tensor"),
    )
    out_specs = (
        P("segment", None, "dp", "tensor"),
        P("segment", None, ("dp", "tensor"), None),
        P("segment", "dp", "tensor"),
        P("segment", None, "dp", "tensor"),
    )
    return jax.shard_map(shards, mesh=mesh, in_specs=in_specs, out_specs=out_specs, check_vma=False)
```

time: 515 us -> 225 us (0.44)
  waiting for transfers between devices: 452 us -> 150 us
  starting transfers between devices: 1.96 us -> 41.1 us
  matrix products: 29 us -> 13.2 us
  between operations: 13.8 us -> 1.11 us
  local copies, waits for them, and re-layouts: 0.73 us -> 9.34 us
  other arithmetic: 16.8 us -> 10.6 us
    all_gather x3 -> x0, waiting for transfers between devices: 224 us -> none  [the longest x1 83.7 us: shards(): full_weights = lax.all_gather(weights, 'dp', axis=0, tiled=True)]
    psum x1 -> x0, waiting for transfers between devices: 151 us -> none  [shards(): lax.psum(partial_value.astype(jnp.bfloat16), 'tensor').astype(jnp.float32)]
    ppermute x0 -> x33, waiting for transfers between devices: none -> 150 us  [swap(): return lax.ppermute(x, axis, [(i, i ^ bits) for i in range(peers)])]
    reduce_scatter x1 -> x0, waiting for transfers between devices: 76.7 us -> none  [shards(): lax.psum_scatter(jnp.einsum('mrd,mrc->dc', gathered, cotangent, preferred...]
    ppermute x0 -> x33, starting transfers between devices: none -> 39.5 us  [swap(): return lax.ppermute(x, axis, [(i, i ^ bits) for i in range(peers)])]
    dot_general x4, matrix products: 29 us -> 13.2 us  [dot(): lax.dot_general(a, b, (contract, ((), ())), preferred_element_type=f32)]
  transfers between devices with their start and end apart: 6 -> 34, of which waited for: 6 -> 16; matrix products, arithmetic and copies ran while one was open for 1% -> 7% of each run, Pallas kernels for 0% -> 0%
where the time goes in v1:
time: 225 us
  waiting for transfers between devices  150 us (67%)
  starting transfers between devices  41.1 us (18%)
  matrix products  13.2 us (6%)
  other arithmetic  10.6 us (5%)
  local copies, waits for them, and re-layouts  9.34 us (4%)
    ppermute x33, waiting for transfers between devices, swap(): return lax.ppermute(x, axis, [(i, i ^ bits) for i in range(peers)])  150 us
    ppermute x33, starting transfers between devices, swap(): return lax.ppermute(x, axis, [(i, i ^ bits) for i in range(peers)])  39.5 us
    dot_general x4, matrix products, dot(): lax.dot_general(a, b, (contract, ((), ())), preferred_element_type=f32)  13.2 us
    unnamed x36, local copies, waits for them, and re-layouts  5.32 us
  transfers between devices with their start and end apart: 34, of which 16 were waited for; matrix products, arithmetic and copies ran while one was open for 7% of the time, Pallas kernels for 0%

profile of v1, /device:TPU:0, one launch (start us, length us, event | category | flops | bytes accessed | tf_op | source)
XLA Modules:
  0.0 225.0 jit_solution(11359589726092071323)
XLA Ops:
  0.6 1.7 bitcast_convert_fusion
  2.3 3.0 %collective-permute-start.25 = (bf16[2048,256]{1,0:T(8,128)(2,1)S(1)}, bf16[2048,256]{1,0:T(8,128)(2,1)}, u32[]{:S(2)}, u32[]{:S(2)}) collective-permute-start(bf16[2048,256]{1,0:T(8,128)(2,1)S(1)} %bitcast_convert_fusion), channel_id=1, source_target_pairs={{0,2},{1,3},{2,0},{3,1},{4,6},{5,7},{6,4},{7,5},{8,10},{9,11},{10,... | collective-permute-start | bytes 3145736 | tf_op jit(solution)/shard_map/ppermute | solution.py:20
  6.4 2.7 %collective-permute-start.19 = (bf16[4,128,256]{2,1,0:T(8,128)(2,1)S(1)}, bf16[4,128,256]{2,1,0:T(8,128)(2,1)S(1)}, u32[]{:S(2)}, u32[]{:S(2)}) collective-permute-start(bf16[4,128,256]{2,1,0:T(8,128)(2,1)S(1)} %pad_maximum_fusion.1), channel_id=1, source_target_pairs={{0,8},{4,12},{8,0},{12,4},{1,9},{5,13},{9,1},{13,5},{2,10},{6,14},... | collective-permute-start | bytes 786440 | tf_op jit(solution)/shard_map/ppermute | solution.py:20
  9.0 1.6 collective-permute-start.18
  10.6 10.2 %collective-permute-done.19 = bf16[4,128,256]{2,1,0:T(8,128)(2,1)S(1)} collective-permute-done((bf16[4,128,256]{2,1,0:T(8,128)(2,1)S(1)}, bf16[4,128,256]{2,1,0:T(8,128)(2,1)S(1)}, u32[]{:S(2)}, u32[]{:S(2)}) %collective-permute-start.19) | collective-permute-done | bytes 262176 | tf_op jit(solution)/shard_map/ppermute | solution.py:20
  21.4 7.2 %collective-permute-done.25 = bf16[2048,256]{1,0:T(8,128)(2,1)} collective-permute-done((bf16[2048,256]{1,0:T(8,128)(2,1)S(1)}, bf16[2048,256]{1,0:T(8,128)(2,1)}, u32[]{:S(2)}, u32[]{:S(2)}) %collective-permute-start.25) | collective-permute-done | bytes 1048608 | tf_op jit(solution)/shard_map/ppermute | solution.py:20
  29.3 1.8 collective-permute-start.22
  32.5 6.1 %collective-permute-done.22 = bf16[512,256]{1,0:T(8,128)(2,1)S(1)} collective-permute-done((bf16[512,256]{1,0:T(8,128)(2,1)S(1)}, bf16[512,256]{1,0:T(8,128)(2,1)S(1)}, u32[]{:S(2)}, u32[]{:S(2)}) %collective-permute-start.22) | collective-permute-done | bytes 262176 | tf_op jit(solution)/shard_map/ppermute | solution.py:20
  38.6 3.9 %collective-permute-done.23 = bf16[512,256]{1,0:T(8,128)(2,1)S(1)} collective-permute-done((bf16[512,256]{1,0:T(8,128)(2,1)S(1)}, bf16[512,256]{1,0:T(8,128)(2,1)S(1)}, u32[]{:S(2)}, u32[]{:S(2)}) %collective-permute-start.23) | collective-permute-done | bytes 262176 | tf_op jit(solution)/shard_map/ppermute | solution.py:20
  42.5 3.6 %fusion.18 = bf16[512,2048]{1,0:T(8,128)(2,1)S(1)} fusion(bf16[2048,256]{1,0:T(8,128)(2,1)S(1)} %collective-permute-done.26, bf16[2048,256]{1,0:T(8,128)(2,1)} %collective-permute-done.25, bf16[2048,256]{1,0:T(8,128)(2,1)S(1)} %collective-permute-done.24, bf16[2048,256]{1,0:T(8,128)(2,1)S(1)} %bitcast_convert_fusion, ...), kind=kOutput, calls=%fused_computation.21 | convolution fusion | flops 2172649472 | bytes 7340032 | tf_op jit(solution)/shard_map/dot_general | solution.py:29
  47.4 3.6 %collective-permute-start.27 = (bf16[2,64,2048]{2,1,0:T(8,128)(2,1)}, bf16[2,64,2048]{2,1,0:T(8,128)(2,1)}, u32[]{:S(2)}, u32[]{:S(2)}) collective-permute-start(bf16[2,64,2048]{2,1,0:T(8,128)(2,1)} %bitcast.33), channel_id=1, source_target_pairs={{0,12},{4,8},{8,4},{12,0},{1,13},{5,9},{9,5},{13,1},{2,14},{6,10},... | collective-permute-start | bytes 1572872 | tf_op jit(solution)/shard_map/ppermute | solution.py:20
  55.2 9.2 %collective-permute-done.27 = bf16[2,64,2048]{2,1,0:T(8,128)(2,1)} collective-permute-done((bf16[2,64,2048]{2,1,0:T(8,128)(2,1)}, bf16[2,64,2048]{2,1,0:T(8,128)(2,1)}, u32[]{:S(2)}, u32[]{:S(2)}) %collective-permute-start.27) | collective-permute-done | bytes 524320 | tf_op jit(solution)/shard_map/ppermute | solution.py:20
  64.4 32.6 %collective-permute-done.28 = bf16[2,64,2048]{2,1,0:T(8,128)(2,1)} collective-permute-done((bf16[2,64,2048]{2,1,0:T(8,128)(2,1)}, bf16[2,64,2048]{2,1,0:T(8,128)(2,1)}, u32[]{:S(2)}, u32[]{:S(2)}) %collective-permute-start.28) | collective-permute-done | bytes 524320 | tf_op jit(solution)/shard_map/ppermute | solution.py:20
  100.7 1.6 collective-permute-start.1
  102.3 3.0 %collective-permute-start.7 = (bf16[128,2048]{1,0:T(8,128)(2,1)S(1)}, bf16[128,2048]{1,0:T(8,128)(2,1)S(1)}, u32[]{:S(2)}, u32[]{:S(2)}) collective-permute-start(bf16[128,2048]{1,0:T(8,128)(2,1)S(1)} %bitcast.136), channel_id=1, source_target_pairs={{0,8},{4,12},{8,0},{12,4},{1,9},{5,13},{9,1},{13,5},{2,10},{6,14},... | collective-permute-start | bytes 1572872 | tf_op jit(solution)/shard_map/ppermute | solution.py:20
  106.7 2.1 fusion.9
  108.8 6.3 %collective-permute-done.1 = bf16[128,2048]{1,0:T(8,128)(2,1)S(1)} collective-permute-done((bf16[128,2048]{1,0:T(8,128)(2,1)S(1)}, bf16[128,2048]{1,0:T(8,128)(2,1)S(1)}, u32[]{:S(2)}, u32[]{:S(2)}) %collective-permute-start.1) | collective-permute-done | bytes 524320 | tf_op jit(solution)/shard_map/ppermute | solution.py:20
  115.1 12.0 %collective-permute-done.3 = bf16[128,2048]{1,0:T(8,128)(2,1)S(1)} collective-permute-done((bf16[128,2048]{1,0:T(8,128)(2,1)S(1)}, bf16[128,2048]{1,0:T(8,128)(2,1)S(1)}, u32[]{:S(2)}, u32[]{:S(2)}) %collective-permute-start.3) | collective-permute-done | bytes 524320 | tf_op jit(solution)/shard_map/ppermute | solution.py:20
  127.8 12.8 %collective-permute-done.7 = bf16[128,2048]{1,0:T(8,128)(2,1)S(1)} collective-permute-done((bf16[128,2048]{1,0:T(8,128)(2,1)S(1)}, bf16[128,2048]{1,0:T(8,128)(2,1)S(1)}, u32[]{:S(2)}, u32[]{:S(2)}) %collective-permute-start.7) | collective-permute-done | bytes 524320 | tf_op jit(solution)/shard_map/ppermute | solution.py:20
  143.4 11.9 %collective-permute-done.9 = bf16[128,2048]{1,0:T(8,128)(2,1)S(1)} collective-permute-done((bf16[128,2048]{1,0:T(8,128)(2,1)S(1)}, bf16[128,2048]{1,0:T(8,128)(2,1)S(1)}, u32[]{:S(2)}, u32[]{:S(2)}) %collective-permute-start.9) | collective-permute-done | bytes 524320 | tf_op jit(solution)/shard_map/ppermute | solution.py:20
  155.4 10.8 %collective-permute-done.13 = bf16[128,2048]{1,0:T(8,128)(2,1)S(1)} collective-permute-done((bf16[128,2048]{1,0:T(8,128)(2,1)S(1)}, bf16[128,2048]{1,0:T(8,128)(2,1)S(1)}, u32[]{:S(2)}, u32[]{:S(2)}) %collective-permute-start.13) | collective-permute-done | bytes 524320 | tf_op jit(solution)/shard_map/ppermute | solution.py:20
  168.2 4.0 %fusion.55 = f32[2048,256]{1,0:T(8,128)S(1)} fusion(bf16[2048,2048]{1,0:T(8,128)(2,1)S(1)} %constant_dynamic-update-slice_fusion, bf16[2048,256]{1,0:T(8,128)(2,1)} %bitcast.42), kind=kOutput, calls=%fused_computation.142 | convolution fusion | flops 2147483648 | bytes 11534336 | tf_op jit(solution)/shard_map/dot_general | solution.py:29
  172.2 3.2 %convolution_convert_fusion = bf16[2048,256]{1,0:T(8,128)(2,1)S(1)} fusion(bf16[2048,2048]{1,0:T(8,128)(2,1)S(1)} %constant_dynamic-update-slice_fusion, f32[1,2048,256]{2,1,0:T(8,128)S(1)} %copy-done.1, f32[2048,256]{1,0:T(8,128)S(1)} %fusion.55, f32[1,2048,256]{2,1,0:T(8,128)S(1)} %copy-done.2, f32[1,2048,256]{2,1,0:T(8,128)S(1)} %copy-done.3), kind=kOutput, calls=%fused_computation.22 | convolution fusion | flops 2156396544 | bytes 17825792 | tf_op jit(solution)/shard_map/dot_general | solution.py:29
  175.4 9.9 %collective-permute-start.31 = (bf16[512,256]{1,0:T(8,128)(2,1)S(1)}, bf16[512,256]{1,0:T(8,128)(2,1)S(1)}, u32[]{:S(2)}, u32[]{:S(2)}) collective-permute-start(bf16[512,256]{1,0:T(8,128)(2,1)S(1)} %get-tuple-element.19), channel_id=1, source_target_pairs={{0,4},{4,0},{8,12},{12,8},{1,5},{5,1},{9,13},{13,9},{2,6},{6,2},{1... | collective-permute-start | bytes 786440 | tf_op jit(solution)/shard_map/ppermute | solution.py:20
  185.4 2.4 %convolution_convert_fusion.1 = bf16[2048,256]{1,0:T(8,128)(2,1)S(1)} fusion(bf16[2048,2048]{1,0:T(8,128)(2,1)S(1)} %constant_dynamic-update-slice_fusion, bf16[2048,256]{1,0:T(8,128)(2,1)S(1)} %copy-done.5), kind=kOutput, calls=%fused_computation.23 | convolution fusion | flops 2148007936 | bytes 10485760 | tf_op jit(solution)/shard_map/dot_general | solution.py:29
  187.9 2.1 collective-permute-start.16
  190.0 2.4 %collective-permute-done.31 = bf16[512,256]{1,0:T(8,128)(2,1)S(1)} collective-permute-done((bf16[512,256]{1,0:T(8,128)(2,1)S(1)}, bf16[512,256]{1,0:T(8,128)(2,1)S(1)}, u32[]{:S(2)}, u32[]{:S(2)}) %collective-permute-start.31) | collective-permute-done | bytes 262176 | tf_op jit(solution)/shard_map/ppermute | solution.py:20
  192.5 3.0 %collective-permute-start.32 = (bf16[512,256]{1,0:T(8,128)(2,1)S(1)}, bf16[512,256]{1,0:T(8,128)(2,1)S(1)}, u32[]{:S(2)}, u32[]{:S(2)}) collective-permute-start(bf16[512,256]{1,0:T(8,128)(2,1)S(1)} %add_convert_fusion.1), channel_id=1, source_target_pairs={{0,8},{4,12},{8,0},{12,4},{1,9},{5,13},{9,1},{13,5},{2,10},{6,14},... | collective-permute-start | bytes 786440 | tf_op jit(solution)/shard_map/ppermute | solution.py:20
  195.6 2.9 %fusion.42 = f32[1,2048,256]{2,1,0:T(8,128)} fusion(f32[2048,256]{1,0:T(8,128)S(1)} %fusion.55, f32[1,2048,256]{2,1,0:T(8,128)S(1)} %copy-done.2, f32[1,2048,256]{2,1,0:T(8,128)S(1)} %copy-done.3, f32[1,2048,256]{2,1,0:T(8,128)S(1)} %copy-done.1), kind=kLoop, calls=%fused_computation.118 | loop fusion | flops 7864320 | bytes 10485760 | tf_op jit(solution)/shard_map/broadcast_in_dim | solution.py:123
  198.4 10.9 %collective-permute-done.16 = bf16[512,256]{1,0:T(8,128)(2,1)S(1)} collective-permute-done((bf16[512,256]{1,0:T(8,128)(2,1)S(1)}, bf16[512,256]{1,0:T(8,128)(2,1)S(1)}, u32[]{:S(2)}, u32[]{:S(2)}) %collective-permute-start.16) | collective-permute-done | bytes 262176 | tf_op jit(solution)/shard_map/ppermute | solution.py:20
  211.7 7.2 %collective-permute-done.15 = bf16[512,256]{1,0:T(8,128)(2,1)S(1)} collective-permute-done((bf16[512,256]{1,0:T(8,128)(2,1)S(1)}, bf16[512,256]{1,0:T(8,128)(2,1)S(1)}, u32[]{:S(2)}, u32[]{:S(2)}) %collective-permute-start.15) | collective-permute-done | bytes 262176 | tf_op jit(solution)/shard_map/ppermute | solution.py:20
  218.9 4.5 %collective-permute-done.17 = bf16[512,256]{1,0:T(8,128)(2,1)S(1)} collective-permute-done((bf16[512,256]{1,0:T(8,128)(2,1)S(1)}, bf16[512,256]{1,0:T(8,128)(2,1)S(1)}, u32[]{:S(2)}, u32[]{:S(2)}) %collective-permute-start.17) | collective-permute-done | bytes 262176 | tf_op jit(solution)/shard_map/ppermute | solution.py:20
  (108 shorter events, 23.6 us)
Async XLA Ops:
  2.3 26.3 %collective-permute-start.25 = (bf16[2048,256]{1,0:T(8,128)(2,1)S(1)}, bf16[2048,256]{1,0:T(8,128)(2,1)}, u32[]{:S(2)}, u32[]{:S(2)}) collective-permute-start(bf16[2048,256]{1,0:T(8,128)(2,1)S(1)} %bitcast_convert_fusion), channel_id=1, source_target_pairs={{0,2},{1,3},{2,0},{3,1},{4,6},{5,7},{6,4},{7,5},{8,10},{9,11},{10,... | collective-permute-start | bytes 3145736 | tf_op jit(solution)/shard_map/ppermute | solution.py:20
  6.4 14.5 %collective-permute-start.19 = (bf16[4,128,256]{2,1,0:T(8,128)(2,1)S(1)}, bf16[4,128,256]{2,1,0:T(8,128)(2,1)S(1)}, u32[]{:S(2)}, u32[]{:S(2)}) collective-permute-start(bf16[4,128,256]{2,1,0:T(8,128)(2,1)S(1)} %pad_maximum_fusion.1), channel_id=1, source_target_pairs={{0,8},{4,12},{8,0},{12,4},{1,9},{5,13},{9,1},{13,5},{2,10},{6,14},... | collective-permute-start | bytes 786440 | tf_op jit(solution)/shard_map/ppermute | solution.py:20
  9.0 19.6 %collective-permute-start.18 = (bf16[4,128,256]{2,1,0:T(8,128)(2,1)S(1)}, bf16[4,128,256]{2,1,0:T(8,128)(2,1)S(1)}, u32[]{:S(2)}, u32[]{:S(2)}) collective-permute-start(bf16[4,128,256]{2,1,0:T(8,128)(2,1)S(1)} %pad_maximum_fusion.1), channel_id=1, source_target_pairs={{0,4},{4,0},{8,12},{12,8},{1,5},{5,1},{9,13},{13,9},{2,6},{6,2},{1... | collective-permute-start | bytes 786440 | tf_op jit(solution)/shard_map/ppermute | solution.py:20
  10.6 31.9 %collective-permute-start.24 = (bf16[2048,256]{1,0:T(8,128)(2,1)S(1)}, bf16[2048,256]{1,0:T(8,128)(2,1)S(1)}, u32[]{:S(2)}, u32[]{:S(2)}) collective-permute-start(bf16[2048,256]{1,0:T(8,128)(2,1)S(1)} %bitcast_convert_fusion), channel_id=1, source_target_pairs={{0,1},{1,0},{2,3},{3,2},{4,5},{5,4},{6,7},{7,6},{8,9},{9,8},{10,11... | collective-permute-start | bytes 3145736 | tf_op jit(solution)/shard_map/ppermute | solution.py:20
  20.8 7.8 %collective-permute-start.20 = (bf16[4,128,256]{2,1,0:T(8,128)(2,1)S(1)}, bf16[4,128,256]{2,1,0:T(8,128)(2,1)S(1)}, u32[]{:S(2)}, u32[]{:S(2)}) collective-permute-start(bf16[4,128,256]{2,1,0:T(8,128)(2,1)S(1)} %collective-permute-done.19), channel_id=1, source_target_pairs={{0,4},{4,0},{8,12},{12,8},{1,5},{5,1},{9,13},{13,9},{2,6},{6,2},{1... | collective-permute-start | bytes 786440 | tf_op jit(solution)/shard_map/ppermute | solution.py:20
  28.6 13.9 %collective-permute-start.26 = (bf16[2048,256]{1,0:T(8,128)(2,1)}, bf16[2048,256]{1,0:T(8,128)(2,1)S(1)}, u32[]{:S(2)}, u32[]{:S(2)}) collective-permute-start(bf16[2048,256]{1,0:T(8,128)(2,1)} %collective-permute-done.25), channel_id=1, source_target_pairs={{0,1},{1,0},{2,3},{3,2},{4,5},{5,4},{6,7},{7,6},{8,9},{9,8},{10,11... | collective-permute-start | bytes 3145736 | tf_op jit(solution)/shard_map/ppermute | solution.py:20
  29.3 9.2 %collective-permute-start.22 = (bf16[512,256]{1,0:T(8,128)(2,1)S(1)}, bf16[512,256]{1,0:T(8,128)(2,1)S(1)}, u32[]{:S(2)}, u32[]{:S(2)}) collective-permute-start(bf16[512,256]{1,0:T(8,128)(2,1)S(1)} %pad_maximum_fusion.3), channel_id=1, source_target_pairs={{0,2},{1,3},{2,0},{3,1},{4,6},{5,7},{6,4},{7,5},{8,10},{9,11},{10,... | collective-permute-start | bytes 786440 | tf_op jit(solution)/shard_map/ppermute | solution.py:20
  31.2 11.3 %collective-permute-start.23 = (bf16[512,256]{1,0:T(8,128)(2,1)S(1)}, bf16[512,256]{1,0:T(8,128)(2,1)S(1)}, u32[]{:S(2)}, u32[]{:S(2)}) collective-permute-start(bf16[512,256]{1,0:T(8,128)(2,1)S(1)} %pad_maximum_fusion.4), channel_id=1, source_target_pairs={{0,3},{1,2},{2,1},{3,0},{4,7},{5,6},{6,5},{7,4},{8,11},{9,10},{10,... | collective-permute-start | bytes 786440 | tf_op jit(solution)/shard_map/ppermute | solution.py:20
  47.4 17.1 %collective-permute-start.27 = (bf16[2,64,2048]{2,1,0:T(8,128)(2,1)}, bf16[2,64,2048]{2,1,0:T(8,128)(2,1)}, u32[]{:S(2)}, u32[]{:S(2)}) collective-permute-start(bf16[2,64,2048]{2,1,0:T(8,128)(2,1)} %bitcast.33), channel_id=1, source_target_pairs={{0,12},{4,8},{8,4},{12,0},{1,13},{5,9},{9,5},{13,1},{2,14},{6,10},... | collective-permute-start | bytes 1572872 | tf_op jit(solution)/shard_map/ppermute | solution.py:20
  51.0 46.0 %collective-permute-start.28 = (bf16[2,64,2048]{2,1,0:T(8,128)(2,1)}, bf16[2,64,2048]{2,1,0:T(8,128)(2,1)}, u32[]{:S(2)}, u32[]{:S(2)}) collective-permute-start(bf16[2,64,2048]{2,1,0:T(8,128)(2,1)} %bitcast.34), channel_id=1, source_target_pairs={{0,8},{4,12},{8,0},{12,4},{1,9},{5,13},{9,1},{13,5},{2,10},{6,14},... | collective-permute-start | bytes 1572872 | tf_op jit(solution)/shard_map/ppermute | solution.py:20
  51.0 46.0 %collective-permute-start.29 = (bf16[2,64,2048]{2,1,0:T(8,128)(2,1)}, bf16[2,64,2048]{2,1,0:T(8,128)(2,1)}, u32[]{:S(2)}, u32[]{:S(2)}) collective-permute-start(bf16[2,64,2048]{2,1,0:T(8,128)(2,1)} %bitcast.35), channel_id=1, source_target_pairs={{0,4},{4,0},{8,12},{12,8},{1,5},{5,1},{9,13},{13,9},{2,6},{6,2},{1... | collective-permute-start | bytes 1572872 | tf_op jit(solution)/shard_map/ppermute | solution.py:20
  100.7 26.9 %collective-permute-start = (bf16[128,2048]{1,0:T(8,128)(2,1)S(1)}, bf16[128,2048]{1,0:T(8,128)(2,1)S(1)}, u32[]{:S(2)}, u32[]{:S(2)}) collective-permute-start(bf16[128,2048]{1,0:T(8,128)(2,1)S(1)} %bitcast.120), channel_id=1, source_target_pairs={{0,1},{1,0},{2,3},{3,2},{4,5},{5,4},{6,7},{7,6},{8,9},{9,8},{10,11... | collective-permute-start | bytes 1572872 | tf_op jit(solution)/shard_map/ppermute | solution.py:20
  100.7 14.3 %collective-permute-start.1 = (bf16[128,2048]{1,0:T(8,128)(2,1)S(1)}, bf16[128,2048]{1,0:T(8,128)(2,1)S(1)}, u32[]{:S(2)}, u32[]{:S(2)}) collective-permute-start(bf16[128,2048]{1,0:T(8,128)(2,1)S(1)} %bitcast.121), channel_id=1, source_target_pairs={{0,2},{1,3},{2,0},{3,1},{4,6},{5,7},{6,4},{7,5},{8,10},{9,11},{10,... | collective-permute-start | bytes 1572872 | tf_op jit(solution)/shard_map/ppermute | solution.py:20
  102.3 24.7 %collective-permute-start.3 = (bf16[128,2048]{1,0:T(8,128)(2,1)S(1)}, bf16[128,2048]{1,0:T(8,128)(2,1)S(1)}, u32[]{:S(2)}, u32[]{:S(2)}) collective-permute-start(bf16[128,2048]{1,0:T(8,128)(2,1)S(1)} %bitcast.137), channel_id=1, source_target_pairs={{0,4},{4,0},{8,12},{12,8},{1,5},{5,1},{9,13},{13,9},{2,6},{6,2},{1... | collective-permute-start | bytes 1572872 | tf_op jit(solution)/shard_map/ppermute | solution.py:20
  102.3 38.3 %collective-permute-start.7 = (bf16[128,2048]{1,0:T(8,128)(2,1)S(1)}, bf16[128,2048]{1,0:T(8,128)(2,1)S(1)}, u32[]{:S(2)}, u32[]{:S(2)}) collective-permute-start(bf16[128,2048]{1,0:T(8,128)(2,1)S(1)} %bitcast.136), channel_id=1, source_target_pairs={{0,8},{4,12},{8,0},{12,4},{1,9},{5,13},{9,1},{13,5},{2,10},{6,14},... | collective-permute-start | bytes 1572872 | tf_op jit(solution)/shard_map/ppermute | solution.py:20
  105.4 35.3 %collective-permute-start.11 = (bf16[128,2048]{1,0:T(8,128)(2,1)S(1)}, bf16[128,2048]{1,0:T(8,128)(2,1)S(1)}, u32[]{:S(2)}, u32[]{:S(2)}) collective-permute-start(bf16[128,2048]{1,0:T(8,128)(2,1)S(1)} %bitcast.135), channel_id=1, source_target_pairs={{0,12},{4,8},{8,4},{12,0},{1,13},{5,9},{9,5},{13,1},{2,14},{6,10},... | collective-permute-start | bytes 1572872 | tf_op jit(solution)/shard_map/ppermute | solution.py:20
  115.1 26.1 %collective-permute-start.2 = (bf16[128,2048]{1,0:T(8,128)(2,1)S(1)}, bf16[128,2048]{1,0:T(8,128)(2,1)S(1)}, u32[]{:S(2)}, u32[]{:S(2)}) collective-permute-start(bf16[128,2048]{1,0:T(8,128)(2,1)S(1)} %collective-permute-done.1), channel_id=1, source_target_pairs={{0,1},{1,0},{2,3},{3,2},{4,5},{5,4},{6,7},{7,6},{8,9},{9,8},{10,11... | collective-permute-start | bytes 1572872 | tf_op jit(solution)/shard_map/ppermute | solution.py:20
  127.1 15.6 %collective-permute-start.5 = (bf16[128,2048]{1,0:T(8,128)(2,1)S(1)}, bf16[128,2048]{1,0:T(8,128)(2,1)S(1)}, u32[]{:S(2)}, u32[]{:S(2)}) collective-permute-start(bf16[128,2048]{1,0:T(8,128)(2,1)S(1)} %collective-permute-done.3), channel_id=1, source_target_pairs={{0,2},{1,3},{2,0},{3,1},{4,6},{5,7},{6,4},{7,5},{8,10},{9,11},{10,... | collective-permute-start | bytes 1572872 | tf_op jit(solution)/shard_map/ppermute | solution.py:20
  127.6 15.1 %collective-permute-start.4 = (bf16[128,2048]{1,0:T(8,128)(2,1)S(1)}, bf16[128,2048]{1,0:T(8,128)(2,1)S(1)}, u32[]{:S(2)}, u32[]{:S(2)}) collective-permute-start(bf16[128,2048]{1,0:T(8,128)(2,1)S(1)} %collective-permute-done.3), channel_id=1, source_target_pairs={{0,1},{1,0},{2,3},{3,2},{4,5},{5,4},{6,7},{7,6},{8,9},{9,8},{10,11... | collective-permute-start | bytes 1572872 | tf_op jit(solution)/shard_map/ppermute | solution.py:20
  140.6 25.7 %collective-permute-start.8 = (bf16[128,2048]{1,0:T(8,128)(2,1)S(1)}, bf16[128,2048]{1,0:T(8,128)(2,1)S(1)}, u32[]{:S(2)}, u32[]{:S(2)}) collective-permute-start(bf16[128,2048]{1,0:T(8,128)(2,1)S(1)} %collective-permute-done.7), channel_id=1, source_target_pairs={{0,1},{1,0},{2,3},{3,2},{4,5},{5,4},{6,7},{7,6},{8,9},{9,8},{10,11... | collective-permute-start | bytes 1572872 | tf_op jit(solution)/shard_map/ppermute | solution.py:20
  140.6 14.7 %collective-permute-start.9 = (bf16[128,2048]{1,0:T(8,128)(2,1)S(1)}, bf16[128,2048]{1,0:T(8,128)(2,1)S(1)}, u32[]{:S(2)}, u32[]{:S(2)}) collective-permute-start(bf16[128,2048]{1,0:T(8,128)(2,1)S(1)} %collective-permute-done.7), channel_id=1, source_target_pairs={{0,2},{1,3},{2,0},{3,1},{4,6},{5,7},{6,4},{7,5},{8,10},{9,11},{10,... | collective-permute-start | bytes 1572872 | tf_op jit(solution)/shard_map/ppermute | solution.py:20
  141.1 25.1 %collective-permute-start.13 = (bf16[128,2048]{1,0:T(8,128)(2,1)S(1)}, bf16[128,2048]{1,0:T(8,128)(2,1)S(1)}, u32[]{:S(2)}, u32[]{:S(2)}) collective-permute-start(bf16[128,2048]{1,0:T(8,128)(2,1)S(1)} %collective-permute-done.11), channel_id=1, source_target_pairs={{0,2},{1,3},{2,0},{3,1},{4,6},{5,7},{6,4},{7,5},{8,10},{9,11},{10,... | collective-permute-start | bytes 1572872 | tf_op jit(solution)/shard_map/ppermute | solution.py:20
  142.7 23.5 %collective-permute-start.6 = (bf16[128,2048]{1,0:T(8,128)(2,1)S(1)}, bf16[128,2048]{1,0:T(8,128)(2,1)S(1)}, u32[]{:S(2)}, u32[]{:S(2)}) collective-permute-start(bf16[128,2048]{1,0:T(8,128)(2,1)S(1)} %collective-permute-done.5), channel_id=1, source_target_pairs={{0,1},{1,0},{2,3},{3,2},{4,5},{5,4},{6,7},{7,6},{8,9},{9,8},{10,11... | collective-permute-start | bytes 1572872 | tf_op jit(solution)/shard_map/ppermute | solution.py:20
  142.8 23.7 %collective-permute-start.12 = (bf16[128,2048]{1,0:T(8,128)(2,1)S(1)}, bf16[128,2048]{1,0:T(8,128)(2,1)S(1)}, u32[]{:S(2)}, u32[]{:S(2)}) collective-permute-start(bf16[128,2048]{1,0:T(8,128)(2,1)S(1)} %collective-permute-done.11), channel_id=1, source_target_pairs={{0,1},{1,0},{2,3},{3,2},{4,5},{5,4},{6,7},{7,6},{8,9},{9,8},{10,11... | collective-permute-start | bytes 1572872 | tf_op jit(solution)/shard_map/ppermute | solution.py:20
  155.4 11.1 %collective-permute-start.10 = (bf16[128,2048]{1,0:T(8,128)(2,1)S(1)}, bf16[128,2048]{1,0:T(8,128)(2,1)S(1)}, u32[]{:S(2)}, u32[]{:S(2)}) collective-permute-start(bf16[128,2048]{1,0:T(8,128)(2,1)S(1)} %collective-permute-done.9), channel_id=1, source_target_pairs={{0,1},{1,0},{2,3},{3,2},{4,5},{5,4},{6,7},{7,6},{8,9},{9,8},{10,11... | collective-permute-start | bytes 1572872 | tf_op jit(solution)/shard_map/ppermute | solution.py:20
  175.4 17.0 %collective-permute-start.31 = (bf16[512,256]{1,0:T(8,128)(2,1)S(1)}, bf16[512,256]{1,0:T(8,128)(2,1)S(1)}, u32[]{:S(2)}, u32[]{:S(2)}) collective-permute-start(bf16[512,256]{1,0:T(8,128)(2,1)S(1)} %get-tuple-element.19), channel_id=1, source_target_pairs={{0,4},{4,0},{8,12},{12,8},{1,5},{5,1},{9,13},{13,9},{2,6},{6,2},{1... | collective-permute-start | bytes 786440 | tf_op jit(solution)/shard_map/ppermute | solution.py:20
  187.8 22.1 %collective-permute-start.30 = (bf16[512,256]{1,0:T(8,128)(2,1)S(1)}, bf16[512,256]{1,0:T(8,128)(2,1)S(1)}, u32[]{:S(2)}, u32[]{:S(2)}) collective-permute-start(bf16[512,256]{1,0:T(8,128)(2,1)S(1)} %get-tuple-element.18), channel_id=1, source_target_pairs={{0,4},{4,0},{8,12},{12,8},{1,5},{5,1},{9,13},{13,9},{2,6},{6,2},{1... | collective-permute-start | bytes 786440 | tf_op jit(solution)/shard_map/ppermute | solution.py:20
  187.9 21.4 %collective-permute-start.16 = (bf16[512,256]{1,0:T(8,128)(2,1)S(1)}, bf16[512,256]{1,0:T(8,128)(2,1)S(1)}, u32[]{:S(2)}, u32[]{:S(2)}) collective-permute-start(bf16[512,256]{1,0:T(8,128)(2,1)S(1)} %get-tuple-element.21), channel_id=1, source_target_pairs={{0,4},{4,0},{8,12},{12,8},{1,5},{5,1},{9,13},{13,9},{2,6},{6,2},{1... | collective-permute-start | bytes 786440 | tf_op jit(solution)/shard_map/ppermute | solution.py:20
  192.5 17.4 %collective-permute-start.32 = (bf16[512,256]{1,0:T(8,128)(2,1)S(1)}, bf16[512,256]{1,0:T(8,128)(2,1)S(1)}, u32[]{:S(2)}, u32[]{:S(2)}) collective-permute-start(bf16[512,256]{1,0:T(8,128)(2,1)S(1)} %add_convert_fusion.1), channel_id=1, source_target_pairs={{0,8},{4,12},{8,0},{12,4},{1,9},{5,13},{9,1},{13,5},{2,10},{6,14},... | collective-permute-start | bytes 786440 | tf_op jit(solution)/shard_map/ppermute | solution.py:20
  198.4 20.5 %collective-permute-start.15 = (bf16[512,256]{1,0:T(8,128)(2,1)S(1)}, bf16[512,256]{1,0:T(8,128)(2,1)S(1)}, u32[]{:S(2)}, u32[]{:S(2)}) collective-permute-start(bf16[512,256]{1,0:T(8,128)(2,1)S(1)} %get-tuple-element.20), channel_id=1, source_target_pairs={{0,4},{4,0},{8,12},{12,8},{1,5},{5,1},{9,13},{13,9},{2,6},{6,2},{1... | collective-permute-start | bytes 786440 | tf_op jit(solution)/shard_map/ppermute | solution.py:20
  209.4 14.0 %collective-permute-start.17 = (bf16[512,256]{1,0:T(8,128)(2,1)S(1)}, bf16[512,256]{1,0:T(8,128)(2,1)S(1)}, u32[]{:S(2)}, u32[]{:S(2)}) collective-permute-start(bf16[512,256]{1,0:T(8,128)(2,1)S(1)} %add_convert_fusion.3), channel_id=1, source_target_pairs={{0,8},{4,12},{8,0},{12,4},{1,9},{5,13},{9,1},{13,5},{2,10},{6,14},... | collective-permute-start | bytes 786440 | tf_op jit(solution)/shard_map/ppermute | solution.py:20
  210.1 14.2 %collective-permute-start.33 = (bf16[1,2,256,256]{3,2,1,0:T(8,128)(2,1)S(1)}, bf16[1,2,256,256]{3,2,1,0:T(8,128)(2,1)S(1)}, u32[]{:S(2)}, u32[]{:S(2)}) collective-permute-start(bf16[1,2,256,256]{3,2,1,0:T(8,128)(2,1)S(1)} %bitcast.142), channel_id=1, source_target_pairs={{0,16},{16,0},{1,17},{17,1},{2,18},{18,2},{3,19},{19,3},{4,20},{20... | collective-permute-start | bytes 786440 | tf_op jit(solution)/shard_map/ppermute | solution.py:25
  (9 other events, 175.9 us)

commit v2 on v1

--- a/solution.py
+++ b/solution.py
@@ -1,6 +1,7 @@
 import jax
 import jax.numpy as jnp
 from jax import lax
+from jax.experimental import pallas as pl
 from jax.sharding import PartitionSpec as P
 
 beta_first = 0.9
@@ -18,6 +19,18 @@
 def swap(x, axis, bits):
     peers = lax.axis_size(axis)
     return lax.ppermute(x, axis, [(i, i ^ bits) for i in range(peers)])
+
+
+def after(x, *earlier):
+    hbm = pl.BlockSpec(memory_space=pl.ANY)
+    return pl.pallas_call(
+        lambda *refs: None,
+        out_shape=jax.ShapeDtypeStruct(x.shape, x.dtype),
+        in_specs=[hbm] * (1 + len(earlier)),
+        out_specs=hbm,
+        input_output_aliases={0: 0},
+        name="after",
+    )(x, *earlier)
 
 
 def from_behind(x, axis, by):
@@ -60,8 +73,7 @@
     def feature_block(x, k):
         return lax.dynamic_slice_in_dim(x, (z ^ k) * depth, depth, x.ndim - 1)
 
-    own = [feature_block(normed, k).reshape(micro * rows, depth) for k in range(dp)]
-    pieces = [own[0]] + [swap(own[k], "dp", k) for k in range(1, dp)]
+    weights = master_kv[0].astype(bf16)
     cot = kv_cot[0].reshape(micro, tensor, rows, cols)
     cot = jnp.stack(
         [
@@ -69,17 +81,21 @@
             for j in range(tensor)
         ]
     )
+    w2 = swap(weights, "tensor", 2)
     cot2 = swap(cot, "dp", 2)
-    cots = [cot, swap(cot, "dp", 1), cot2, swap(cot2, "dp", 1)]
-    weights = master_kv[0].astype(bf16)
-    w2 = swap(weights, "tensor", 2)
-    whole_w = jnp.concatenate([weights, swap(weights, "tensor", 1), w2, swap(w2, "tensor", 1)], 1)
+    own = [feature_block(normed, k).reshape(micro * rows, depth) for k in range(dp)]
+    pieces = [own[0]] + [swap(own[k], "dp", k) for k in range(1, dp)]
+    pair = swap(jnp.stack([cot, cot2]), "dp", 1)
+    cots = [cot, pair[0], cot2, pair[1]]
+    w13 = swap(jnp.concatenate([weights, w2], 1), "tensor", 1)
+    whole_w = jnp.concatenate([weights, w2, w13], 1)
+    cot_order = (0, 2, 1, 3)
     gathered = []
     for piece in pieces:
-        across = swap(piece, "tensor", 2)
-        gathered += [piece, swap(piece, "tensor", 1), across, swap(across, "tensor", 1)]
+        near = jnp.concatenate([piece, swap(piece, "tensor", 2)])
+        gathered += [near, swap(near, "tensor", 1)]
     tokens = jnp.concatenate(gathered)
-    cot_all = jnp.concatenate(cots).reshape(-1, cols)
+    cot_all = jnp.concatenate([c[j] for c in cots for j in cot_order])
     block = tensor * micro * rows
 
     def by_replica(x):
@@ -87,7 +103,7 @@
 
     def place(x):
         x = x.reshape(tensor, micro, rows, cols)
-        return jnp.stack(reorder([x[j] for j in range(tensor)], t), 1).reshape(
+        return jnp.stack(reorder([x[j] for j in (0, 2, 1, 3)], t), 1).reshape(
             1, micro, tensor * rows, cols
         )
 
@@ -95,10 +111,10 @@
     kv_own = place(scatter_sum(by_replica(kv_part)).astype(bf16))
 
     mine_cot = []
-    for j in range(tensor):
+    for j in cot_order:
         rows_j = jnp.concatenate([c[j] for c in cots])
         mine_cot.append(rows_j if j == 0 else swap(rows_j, "tensor", j))
-    d_part = dot(jnp.concatenate(mine_cot, 1), whole_w, ((1,), (1,))).astype(bf16)
+    d_part = dot(after(jnp.concatenate(mine_cot, 1), pieces[1], pieces[2], pieces[3]), whole_w, ((1,), (1,))).astype(bf16)
     d_part = d_part.reshape(dp, micro, rows, depth)
     d_blocks = [d_part[0]] + [swap(d_part[k], "dp", k) for k in range(1, dp)]
     d_normed = jnp.concatenate(reorder(d_blocks, z), -1).astype(f32)
@@ -107,7 +123,7 @@
         scaling * upper - widened * scaling**3 * jnp.mean(upper * widened, axis=-1, keepdims=True)
     ).astype(bf16)
 
-    grad_w = dot(tokens, cot_all, ((0,), (0,)))
+    grad_w = dot(tokens, after(cot_all, d_part), ((0,), (0,)))
     master = master_kv[0]
     m_new = beta_first * moment_m[0] + (1.0 - beta_first) * grad_w
     v_new = beta_second * moment_v[0] + (1.0 - beta_second) * grad_w * grad_w

time: 225 us -> 244 us (1.084)
  local copies, waits for them, and re-layouts: 9.34 us -> 25.4 us
  starting transfers between devices: 41.1 us -> 29.2 us
  other arithmetic: 10.6 us -> 21.3 us
  matrix products: 13.2 us -> 19.8 us
  waiting for transfers between devices: 150 us -> 147 us
    unnamed x36 -> x67, local copies, waits for them, and re-layouts: 5.32 us -> 17.8 us
    ppermute x33 -> x27, starting transfers between devices: 39.5 us -> 27.6 us  [swap(): return lax.ppermute(x, axis, [(i, i ^ bits) for i in range(peers)])]
    ppermute x33 -> x27, waiting for transfers between devices: 150 us -> 142 us  [swap(): return lax.ppermute(x, axis, [(i, i ^ bits) for i in range(peers)])]
    dot_general x4, matrix products: 13.2 us -> 19.8 us  [dot(): lax.dot_general(a, b, (contract, ((), ())), preferred_element_type=f32)]
    concatenate x0 -> x6, other arithmetic: none -> 5.32 us  [the longest x4 2.64 us: shards(): near = jnp.concatenate([piece, swap(piece, 'tensor', 2)])]
    ppermute x1, waiting for transfers between devices: 0.01 us -> 4.67 us  [from_behind(): return lax.ppermute(x, axis, [(i, (i + by) % peers) for i in range(peers)])]
    dynamic_slice x1, local copies, waits for them, and re-layouts: 0.22 us -> 2.91 us  [feature_block(): return lax.dynamic_slice_in_dim(x, (z ^ k) * depth, depth, x.ndim - 1)]
  transfers between devices with their start and end apart: 34 -> 28, of which waited for: 16 -> 13; matrix products, arithmetic and copies ran while one was open for 7% -> 21% of each run, Pallas kernels for 0% -> 0%
where the time goes in v2:
time: 244 us; the launch traced here: 243 us
  waiting for transfers between devices  147 us (60%)
  starting transfers between devices  29.2 us (12%)
  local copies, waits for them, and re-layouts  25.4 us (10%)
  other arithmetic  21.3 us (9%)
  matrix products  19.8 us (8%)
    ppermute x27, waiting for transfers between devices, swap(): return lax.ppermute(x, axis, [(i, i ^ bits) for i in range(peers)])  142 us
    ppermute x27, starting transfers between devices, swap(): return lax.ppermute(x, axis, [(i, i ^ bits) for i in range(peers)])  27.6 us
    dot_general x4, matrix products, dot(): lax.dot_general(a, b, (contract, ((), ())), preferred_element_type=f32)  19.8 us
    unnamed x67, local copies, waits for them, and re-layouts  17.8 us
  transfers between devices with their start and end apart: 28, of which 13 were waited for; matrix products, arithmetic and copies ran while one was open for 21% of the time, Pallas kernels for 0%

profile of v2, /device:TPU:0, one launch (start us, length us, event | category | flops | bytes accessed | tf_op | source)
XLA Modules:
  0.0 243.4 jit_solution(17816825251315732348)
XLA Ops:
  0.7 2.3 fusion.3
  2.9 1.9 fusion.5
  4.8 2.9 %constant_dynamic-slice_fusion.4 = (bf16[2,64,2048]{2,1,0:T(8,128)(2,1)}, bf16[2,64,2048]{2,1,0:T(8,128)(2,1)}, bf16[2,64,2048]{2,1,0:T(8,128)(2,1)}, bf16[2,64,2048]{2,1,0:T(8,128)(2,1)}) fusion(bf16[2,64,8192]{2,1,0:T(8,128)(2,1)} %fusion.5, s32[]{:T(128)S(6)} %select_n.313, s32[]{:T(128)S(6)} %select_n.312, s32[]{:T(128)S(6)} %select_n.311, s32[]{:T(128)S(6)} %select_n.310), kind=kLoop, calls=%fused_computation.120 | loop fusion | bytes 4194320 | tf_op jit(solution)/shard_map/dynamic_slice | solution.py:74
  7.8 3.0 %collective-permute-start = (bf16[128,2048]{1,0:T(8,128)(2,1)}, bf16[128,2048]{1,0:T(8,128)(2,1)}, u32[]{:S(2)}, u32[]{:S(2)}) collective-permute-start(bf16[128,2048]{1,0:T(8,128)(2,1)} %bitcast.2), channel_id=1, source_target_pairs={{0,2},{1,3},{2,0},{3,1},{4,6},{5,7},{6,4},{7,5},{8,10},{9,11},{10,... | collective-permute-start | bytes 1572872 | tf_op jit(solution)/shard_map/ppermute | solution.py:21
  12.3 2.6 %collective-permute-start.5 = (bf16[128,2048]{1,0:T(8,128)(2,1)}, bf16[128,2048]{1,0:T(8,128)(2,1)S(1)}, u32[]{:S(2)}, u32[]{:S(2)}) collective-permute-start(bf16[128,2048]{1,0:T(8,128)(2,1)} %bitcast.4), channel_id=1, source_target_pairs={{0,8},{4,12},{8,0},{12,4},{1,9},{5,13},{9,1},{13,5},{2,10},{6,14},... | collective-permute-start | bytes 1572872 | tf_op jit(solution)/shard_map/ppermute | solution.py:21
  17.1 1.7 collective-permute-start.14
  18.8 1.9 constant_dynamic-update-slice_fusion.11
  25.1 46.4 %collective-permute-done.14 = bf16[4,128,256]{2,1,0:T(8,128)(2,1)S(1)} collective-permute-done((bf16[4,128,256]{2,1,0:T(8,128)(2,1)}, bf16[4,128,256]{2,1,0:T(8,128)(2,1)S(1)}, u32[]{:S(2)}, u32[]{:S(2)}) %collective-permute-start.14) | collective-permute-done | bytes 262176 | tf_op jit(solution)/shard_map/ppermute | solution.py:21
  73.2 1.9 constant_dynamic-update-slice_fusion.10
  78.6 6.2 %collective-permute-done.15 = bf16[2,4,128,256]{3,2,1,0:T(8,128)(2,1)S(1)} collective-permute-done((bf16[2,4,128,256]{3,2,1,0:T(8,128)(2,1)S(1)}, bf16[2,4,128,256]{3,2,1,0:T(8,128)(2,1)S(1)}, u32[]{:S(2)}, u32[]{:S(2)}) %collective-permute-start.15) | collective-permute-done | bytes 524320 | tf_op jit(solution)/shard_map/ppermute | solution.py:21
  91.1 19.1 %collective-permute-done.3 = bf16[128,2048]{1,0:T(8,128)(2,1)S(1)} collective-permute-done((bf16[128,2048]{1,0:T(8,128)(2,1)S(1)}, bf16[128,2048]{1,0:T(8,128)(2,1)S(1)}, u32[]{:S(2)}, u32[]{:S(2)}) %collective-permute-start.3) | collective-permute-done | bytes 524320 | tf_op jit(solution)/shard_map/ppermute | solution.py:21
  110.3 11.1 %collective-permute-done.6 = bf16[128,2048]{1,0:T(8,128)(2,1)S(1)} collective-permute-done((bf16[128,2048]{1,0:T(8,128)(2,1)S(1)}, bf16[128,2048]{1,0:T(8,128)(2,1)S(1)}, u32[]{:S(2)}, u32[]{:S(2)}) %collective-permute-start.6) | collective-permute-done | bytes 524320 | tf_op jit(solution)/shard_map/ppermute | solution.py:21
  121.6 11.1 %collective-permute-done.9 = bf16[128,2048]{1,0:T(8,128)(2,1)S(1)} collective-permute-done((bf16[128,2048]{1,0:T(8,128)(2,1)}, bf16[128,2048]{1,0:T(8,128)(2,1)S(1)}, u32[]{:S(2)}, u32[]{:S(2)}) %collective-permute-start.9) | collective-permute-done | bytes 524320 | tf_op jit(solution)/shard_map/ppermute | solution.py:21
  140.2 2.5 %convolution_convert_fusion.1 = bf16[2048,256]{1,0:T(8,128)(2,1)S(1)} fusion(bf16[2048,2048]{1,0:T(8,128)(2,1)S(1)} %constant_dynamic-update-slice_fusion, bf16[2048,256]{1,0:T(8,128)(2,1)S(1)} %copy-done.7), kind=kOutput, calls=%fused_computation.21 | convolution fusion | flops 2148007936 | bytes 10485760 | tf_op jit(solution)/shard_map/dot_general | solution.py:42
  144.2 1.9 collective-permute-start.12
  147.4 5.5 %collective-permute-done.12 = bf16[512,256]{1,0:T(8,128)(2,1)S(1)} collective-permute-done((bf16[512,256]{1,0:T(8,128)(2,1)S(1)}, bf16[512,256]{1,0:T(8,128)(2,1)S(1)}, u32[]{:S(2)}, u32[]{:S(2)}) %collective-permute-start.12) | collective-permute-done | bytes 262176 | tf_op jit(solution)/shard_map/ppermute | solution.py:21
  152.9 1.7 collective-permute-start.11
  157.9 8.7 %collective-permute-done.11 = bf16[512,256]{1,0:T(8,128)(2,1)} collective-permute-done((bf16[512,256]{1,0:T(8,128)(2,1)}, bf16[512,256]{1,0:T(8,128)(2,1)}, u32[]{:S(2)}, u32[]{:S(2)}) %collective-permute-start.11) | collective-permute-done | bytes 262176 | tf_op jit(solution)/shard_map/ppermute | solution.py:21
  166.6 2.2 collective-permute-done.13
  170.8 4.2 %fusion.16 = bf16[512,2048]{1,0:T(8,128)(2,1)S(1)} fusion(bf16[512,1024]{1,0:T(8,128)(2,1)S(1)} %copy-done.6, bf16[2048,512]{1,0:T(8,128)(2,1)} %collective-permute-done.20, bf16[2048,256]{1,0:T(8,128)(2,1)} %copy-done.11, bf16[2048,256]{1,0:T(8,128)(2,1)S(1)} %copy-done.8), kind=kOutput, calls=%fused_computation.19 | convolution fusion | flops 2161115136 | bytes 7340032 | tf_op jit(solution)/shard_map/dot_general | solution.py:42
  176.9 2.5 %collective-permute-start.21 = (bf16[2,64,2048]{2,1,0:T(8,128)(2,1)}, bf16[2,64,2048]{2,1,0:T(8,128)(2,1)S(1)}, u32[]{:S(2)}, u32[]{:S(2)}) collective-permute-start(bf16[2,64,2048]{2,1,0:T(8,128)(2,1)} %bitcast.35), channel_id=1, source_target_pairs={{0,12},{4,8},{8,4},{12,0},{1,13},{5,9},{9,5},{13,1},{2,14},{6,10},... | collective-permute-start | bytes 1572872 | tf_op jit(solution)/shard_map/ppermute | solution.py:21
  179.3 1.9 collective-permute-start.23
  181.2 6.6 %fusion.41 = f32[2048,256]{1,0:T(8,128)S(1)} fusion(bf16[2048,2048]{1,0:T(8,128)(2,1)} %copy-done.19, bf16[2048,256]{1,0:T(8,128)(2,1)} %after.3), kind=kOutput, calls=%fused_computation.140 | convolution fusion | flops 2147483648 | bytes 11534336 | tf_op jit(solution)/shard_map/dot_general | solution.py:42
  187.8 6.5 %convolution_convert_fusion = bf16[2048,256]{1,0:T(8,128)(2,1)S(1)} fusion(bf16[2048,2048]{1,0:T(8,128)(2,1)} %copy-done.19, f32[1,2048,256]{2,1,0:T(8,128)S(1)} %copy-done.2, f32[2048,256]{1,0:T(8,128)S(1)} %fusion.41, f32[1,2048,256]{2,1,0:T(8,128)S(1)} %copy-done.9, f32[1,2048,256]{2,1,0:T(8,128)S(1)} %copy-done.10), kind=kOutput, calls=%fused_computation.20 | convolution fusion | flops 2156396544 | bytes 17825792 | tf_op jit(solution)/shard_map/dot_general | solution.py:42
  194.6 2.9 %fusion.27 = f32[1,2048,256]{2,1,0:T(8,128)} fusion(f32[2048,256]{1,0:T(8,128)S(1)} %fusion.41, f32[1,2048,256]{2,1,0:T(8,128)S(1)} %copy-done.9, f32[1,2048,256]{2,1,0:T(8,128)S(1)} %copy-done.10, f32[1,2048,256]{2,1,0:T(8,128)S(1)} %copy-done.2), kind=kLoop, calls=%fused_computation.115 | loop fusion | flops 7864320 | bytes 10485760 | tf_op jit(solution)/shard_map/broadcast_in_dim | solution.py:139
  197.5 1.9 collective-permute-start.24
  199.4 20.6 %collective-permute-done.25 = bf16[512,256]{1,0:T(8,128)(2,1)S(1)} collective-permute-done((bf16[512,256]{1,0:T(8,128)(2,1)S(1)}, bf16[512,256]{1,0:T(8,128)(2,1)S(1)}, u32[]{:S(2)}, u32[]{:S(2)}) %collective-permute-start.25) | collective-permute-done | bytes 262176 | tf_op jit(solution)/shard_map/ppermute | solution.py:21
  220.1 2.4 %collective-permute-start.26 = (bf16[512,256]{1,0:T(8,128)(2,1)S(1)}, bf16[512,256]{1,0:T(8,128)(2,1)S(1)}, u32[]{:S(2)}, u32[]{:S(2)}) collective-permute-start(bf16[512,256]{1,0:T(8,128)(2,1)S(1)} %add_convert_fusion.1), channel_id=1, source_target_pairs={{0,8},{4,12},{8,0},{12,4},{1,9},{5,13},{9,1},{13,5},{2,10},{6,14},... | collective-permute-start | bytes 786440 | tf_op jit(solution)/shard_map/ppermute | solution.py:21
  222.5 3.4 %collective-permute-done.22 = bf16[2,64,2048]{2,1,0:T(8,128)(2,1)} collective-permute-done((bf16[2,64,2048]{2,1,0:T(8,128)(2,1)}, bf16[2,64,2048]{2,1,0:T(8,128)(2,1)}, u32[]{:S(2)}, u32[]{:S(2)}) %collective-permute-start.22) | collective-permute-done | bytes 524320 | tf_op jit(solution)/shard_map/ppermute | solution.py:21
  228.3 5.9 %collective-permute-done.26 = bf16[512,256]{1,0:T(8,128)(2,1)S(1)} collective-permute-done((bf16[512,256]{1,0:T(8,128)(2,1)S(1)}, bf16[512,256]{1,0:T(8,128)(2,1)S(1)}, u32[]{:S(2)}, u32[]{:S(2)}) %collective-permute-start.26) | collective-permute-done | bytes 262176 | tf_op jit(solution)/shard_map/ppermute | solution.py:21
  236.0 2.1 fusion.9
  238.0 4.7 %collective-permute-done.27 = bf16[1,2,256,256]{3,2,1,0:T(8,128)(2,1)S(1)} collective-permute-done((bf16[1,2,256,256]{3,2,1,0:T(8,128)(2,1)S(1)}, bf16[1,2,256,256]{3,2,1,0:T(8,128)(2,1)S(1)}, u32[]{:S(2)}, u32[]{:S(2)}) %collective-permute-start.27) | collective-permute-done | bytes 262176 | tf_op jit(solution)/shard_map/ppermute | solution.py:38
  (136 shorter events, 42.2 us)
Async XLA Ops:
  7.8 64.9 %collective-permute-start = (bf16[128,2048]{1,0:T(8,128)(2,1)}, bf16[128,2048]{1,0:T(8,128)(2,1)}, u32[]{:S(2)}, u32[]{:S(2)}) collective-permute-start(bf16[128,2048]{1,0:T(8,128)(2,1)} %bitcast.2), channel_id=1, source_target_pairs={{0,2},{1,3},{2,0},{3,1},{4,6},{5,7},{6,4},{7,5},{8,10},{9,11},{10,... | collective-permute-start | bytes 1572872 | tf_op jit(solution)/shard_map/ppermute | solution.py:21
  10.7 65.7 %collective-permute-start.2 = (bf16[128,2048]{1,0:T(8,128)(2,1)}, bf16[128,2048]{1,0:T(8,128)(2,1)S(1)}, u32[]{:S(2)}, u32[]{:S(2)}) collective-permute-start(bf16[128,2048]{1,0:T(8,128)(2,1)} %bitcast.3), channel_id=1, source_target_pairs={{0,4},{4,0},{8,12},{12,8},{1,5},{5,1},{9,13},{13,9},{2,6},{6,2},{1... | collective-permute-start | bytes 1572872 | tf_op jit(solution)/shard_map/ppermute | solution.py:21
  12.3 64.2 %collective-permute-start.5 = (bf16[128,2048]{1,0:T(8,128)(2,1)}, bf16[128,2048]{1,0:T(8,128)(2,1)S(1)}, u32[]{:S(2)}, u32[]{:S(2)}) collective-permute-start(bf16[128,2048]{1,0:T(8,128)(2,1)} %bitcast.4), channel_id=1, source_target_pairs={{0,8},{4,12},{8,0},{12,4},{1,9},{5,13},{9,1},{13,5},{2,10},{6,14},... | collective-permute-start | bytes 1572872 | tf_op jit(solution)/shard_map/ppermute | solution.py:21
  14.9 63.2 %collective-permute-start.8 = (bf16[128,2048]{1,0:T(8,128)(2,1)}, bf16[128,2048]{1,0:T(8,128)(2,1)}, u32[]{:S(2)}, u32[]{:S(2)}) collective-permute-start(bf16[128,2048]{1,0:T(8,128)(2,1)} %bitcast.5), channel_id=1, source_target_pairs={{0,12},{4,8},{8,4},{12,0},{1,13},{5,9},{9,5},{13,1},{2,14},{6,10},... | collective-permute-start | bytes 1572872 | tf_op jit(solution)/shard_map/ppermute | solution.py:21
  17.1 54.4 %collective-permute-start.14 = (bf16[4,128,256]{2,1,0:T(8,128)(2,1)}, bf16[4,128,256]{2,1,0:T(8,128)(2,1)S(1)}, u32[]{:S(2)}, u32[]{:S(2)}) collective-permute-start(bf16[4,128,256]{2,1,0:T(8,128)(2,1)} %get-tuple-element.37), channel_id=1, source_target_pairs={{0,8},{4,12},{8,0},{12,4},{1,9},{5,13},{9,1},{13,5},{2,10},{6,14},... | collective-permute-start | bytes 786440 | tf_op jit(solution)/shard_map/ppermute | solution.py:21
  72.5 12.3 %collective-permute-start.15 = (bf16[2,4,128,256]{3,2,1,0:T(8,128)(2,1)S(1)}, bf16[2,4,128,256]{3,2,1,0:T(8,128)(2,1)S(1)}, u32[]{:S(2)}, u32[]{:S(2)}) collective-permute-start(bf16[2,4,128,256]{3,2,1,0:T(8,128)(2,1)S(1)} %pad_maximum_fusion.6), channel_id=1, source_target_pairs={{0,4},{4,0},{8,12},{12,8},{1,5},{5,1},{9,13},{13,9},{2,6},{6,2},{1... | collective-permute-start | bytes 1572872 | tf_op jit(solution)/shard_map/ppermute | solution.py:21
  72.6 61.2 %collective-permute-start.19 = (bf16[2048,256]{1,0:T(8,128)(2,1)}, bf16[2048,256]{1,0:T(8,128)(2,1)S(1)}, u32[]{:S(2)}, u32[]{:S(2)}) collective-permute-start(bf16[2048,256]{1,0:T(8,128)(2,1)} %bitcast_convert_fusion), channel_id=1, source_target_pairs={{0,2},{1,3},{2,0},{3,1},{4,6},{5,7},{6,4},{7,5},{8,10},{9,11},{10,... | collective-permute-start | bytes 3145736 | tf_op jit(solution)/shard_map/ppermute | solution.py:21
  76.4 59.8 %copy-start.4 = (bf16[128,2048]{1,0:T(8,128)(2,1)}, bf16[128,2048]{1,0:T(8,128)(2,1)S(1)}, u32[]{:S(2)}) copy-start(bf16[128,2048]{1,0:T(8,128)(2,1)S(1)} %collective-permute-done.2.refs_1_) | copy-start | bytes 1572868
  76.4 59.5 %collective-permute-start.1 = (bf16[256,2048]{1,0:T(8,128)(2,1)S(1)}, bf16[256,2048]{1,0:T(8,128)(2,1)S(1)}, u32[]{:S(2)}, u32[]{:S(2)}) collective-permute-start(bf16[256,2048]{1,0:T(8,128)(2,1)S(1)} %pad_maximum_fusion.1), channel_id=1, source_target_pairs={{0,1},{1,0},{2,3},{3,2},{4,5},{5,4},{6,7},{7,6},{8,9},{9,8},{10,11... | collective-permute-start | bytes 3145736 | tf_op jit(solution)/shard_map/ppermute | solution.py:21
  76.5 60.3 %copy-start.5 = (bf16[128,2048]{1,0:T(8,128)(2,1)}, bf16[128,2048]{1,0:T(8,128)(2,1)S(1)}, u32[]{:S(2)}) copy-start(bf16[128,2048]{1,0:T(8,128)(2,1)S(1)} %collective-permute-done.5.refs_2_) | copy-start | bytes 1572868
  76.5 33.7 %collective-permute-start.3 = (bf16[128,2048]{1,0:T(8,128)(2,1)S(1)}, bf16[128,2048]{1,0:T(8,128)(2,1)S(1)}, u32[]{:S(2)}, u32[]{:S(2)}) collective-permute-start(bf16[128,2048]{1,0:T(8,128)(2,1)S(1)} %collective-permute-done.2.refs_1_), channel_id=1, source_target_pairs={{0,2},{1,3},{2,0},{3,1},{4,6},{5,7},{6,4},{7,5},{8,10},{9,11},{10,... | collective-permute-start | bytes 1572872 | tf_op jit(solution)/shard_map/ppermute | solution.py:21
  78.1 43.3 %collective-permute-start.6 = (bf16[128,2048]{1,0:T(8,128)(2,1)S(1)}, bf16[128,2048]{1,0:T(8,128)(2,1)S(1)}, u32[]{:S(2)}, u32[]{:S(2)}) collective-permute-start(bf16[128,2048]{1,0:T(8,128)(2,1)S(1)} %collective-permute-done.5.refs_2_), channel_id=1, source_target_pairs={{0,2},{1,3},{2,0},{3,1},{4,6},{5,7},{6,4},{7,5},{8,10},{9,11},{10,... | collective-permute-start | bytes 1572872 | tf_op jit(solution)/shard_map/ppermute | solution.py:21
  84.8 47.9 %collective-permute-start.9 = (bf16[128,2048]{1,0:T(8,128)(2,1)}, bf16[128,2048]{1,0:T(8,128)(2,1)S(1)}, u32[]{:S(2)}, u32[]{:S(2)}) collective-permute-start(bf16[128,2048]{1,0:T(8,128)(2,1)} %collective-permute-done.8.refs_3_), channel_id=1, source_target_pairs={{0,2},{1,3},{2,0},{3,1},{4,6},{5,7},{6,4},{7,5},{8,10},{9,11},{10,... | collective-permute-start | bytes 1572872 | tf_op jit(solution)/shard_map/ppermute | solution.py:21
  85.3 50.9 %copy-start.18 = (bf16[2048,2048]{1,0:T(8,128)(2,1)S(1)}, bf16[2048,2048]{1,0:T(8,128)(2,1)}, u32[]{:S(2)}) copy-start(bf16[2048,2048]{1,0:T(8,128)(2,1)} %constant_dynamic-update-slice_fusion.10) | copy-start | bytes 25165828
  110.2 44.5 %collective-permute-start.18 = (bf16[512,256]{1,0:T(8,128)(2,1)S(1)}, bf16[512,256]{1,0:T(8,128)(2,1)S(1)}, u32[]{:S(2)}, u32[]{:S(2)}) collective-permute-start(bf16[512,256]{1,0:T(8,128)(2,1)S(1)} %pad_maximum_fusion.11), channel_id=1, source_target_pairs={{0,3},{1,2},{2,1},{3,0},{4,7},{5,6},{6,5},{7,4},{8,11},{9,10},{10,... | collective-permute-start | bytes 786440 | tf_op jit(solution)/shard_map/ppermute | solution.py:21
  110.3 24.1 %copy-start.7 = (bf16[2048,256]{1,0:T(8,128)(2,1)S(1)}, bf16[2048,256]{1,0:T(8,128)(2,1)}, u32[]{:S(2)}) copy-start(bf16[2048,256]{1,0:T(8,128)(2,1)} %bitcast_convert_fusion) | copy-start | bytes 3145732
  121.5 35.2 %collective-permute-start.17 = (bf16[512,256]{1,0:T(8,128)(2,1)S(1)}, bf16[512,256]{1,0:T(8,128)(2,1)S(1)}, u32[]{:S(2)}, u32[]{:S(2)}) collective-permute-start(bf16[512,256]{1,0:T(8,128)(2,1)S(1)} %pad_maximum_fusion.10), channel_id=1, source_target_pairs={{0,1},{1,0},{2,3},{3,2},{4,5},{5,4},{6,7},{7,6},{8,9},{9,8},{10,11... | collective-permute-start | bytes 786440 | tf_op jit(solution)/shard_map/ppermute | solution.py:21
  132.7 3.7 %collective-permute-start.4 = (bf16[256,2048]{1,0:T(8,128)(2,1)S(1)}, bf16[256,2048]{1,0:T(8,128)(2,1)S(1)}, u32[]{:S(2)}, u32[]{:S(2)}) collective-permute-start(bf16[256,2048]{1,0:T(8,128)(2,1)S(1)} %pad_maximum_fusion.2), channel_id=1, source_target_pairs={{0,1},{1,0},{2,3},{3,2},{4,5},{5,4},{6,7},{7,6},{8,9},{9,8},{10,11... | collective-permute-start | bytes 3145736 | tf_op jit(solution)/shard_map/ppermute | solution.py:21
  133.9 22.8 %collective-permute-start.16 = (bf16[512,256]{1,0:T(8,128)(2,1)S(1)}, bf16[512,256]{1,0:T(8,128)(2,1)S(1)}, u32[]{:S(2)}, u32[]{:S(2)}) collective-permute-start(bf16[512,256]{1,0:T(8,128)(2,1)S(1)} %pad_maximum_fusion.9), channel_id=1, source_target_pairs={{0,2},{1,3},{2,0},{3,1},{4,6},{5,7},{6,4},{7,5},{8,10},{9,11},{10,... | collective-permute-start | bytes 786440 | tf_op jit(solution)/shard_map/ppermute | solution.py:21
  135.9 2.7 %collective-permute-start.7 = (bf16[256,2048]{1,0:T(8,128)(2,1)S(1)}, bf16[256,2048]{1,0:T(8,128)(2,1)S(1)}, u32[]{:S(2)}, u32[]{:S(2)}) collective-permute-start(bf16[256,2048]{1,0:T(8,128)(2,1)S(1)} %pad_maximum_fusion.3), channel_id=1, source_target_pairs={{0,1},{1,0},{2,3},{3,2},{4,5},{5,4},{6,7},{7,6},{8,9},{9,8},{10,11... | collective-permute-start | bytes 3145736 | tf_op jit(solution)/shard_map/ppermute | solution.py:21
  136.4 3.7 %collective-permute-start.10 = (bf16[256,2048]{1,0:T(8,128)(2,1)S(1)}, bf16[256,2048]{1,0:T(8,128)(2,1)S(1)}, u32[]{:S(2)}, u32[]{:S(2)}) collective-permute-start(bf16[256,2048]{1,0:T(8,128)(2,1)S(1)} %pad_maximum_fusion.4), channel_id=1, source_target_pairs={{0,1},{1,0},{2,3},{3,2},{4,5},{5,4},{6,7},{7,6},{8,9},{9,8},{10,11... | collective-permute-start | bytes 3145736 | tf_op jit(solution)/shard_map/ppermute | solution.py:21
  138.6 32.2 %collective-permute-start.20 = (bf16[2048,512]{1,0:T(8,128)(2,1)}, bf16[2048,512]{1,0:T(8,128)(2,1)}, u32[]{:S(2)}, u32[]{:S(2)}) collective-permute-start(bf16[2048,512]{1,0:T(8,128)(2,1)} %pad_maximum_fusion), channel_id=1, source_target_pairs={{0,1},{1,0},{2,3},{3,2},{4,5},{5,4},{6,7},{7,6},{8,9},{9,8},{10,11... | collective-permute-start | bytes 6291464 | tf_op jit(solution)/shard_map/ppermute | solution.py:21
  144.2 8.6 %collective-permute-start.12 = (bf16[512,256]{1,0:T(8,128)(2,1)S(1)}, bf16[512,256]{1,0:T(8,128)(2,1)S(1)}, u32[]{:S(2)}, u32[]{:S(2)}) collective-permute-start(bf16[512,256]{1,0:T(8,128)(2,1)S(1)} %get-tuple-element.19), channel_id=1, source_target_pairs={{0,4},{4,0},{8,12},{12,8},{1,5},{5,1},{9,13},{13,9},{2,6},{6,2},{1... | collective-permute-start | bytes 786440 | tf_op jit(solution)/shard_map/ppermute | solution.py:21
  152.9 13.7 %collective-permute-start.11 = (bf16[512,256]{1,0:T(8,128)(2,1)}, bf16[512,256]{1,0:T(8,128)(2,1)}, u32[]{:S(2)}, u32[]{:S(2)}) collective-permute-start(bf16[512,256]{1,0:T(8,128)(2,1)} %get-tuple-element.18), channel_id=1, source_target_pairs={{0,4},{4,0},{8,12},{12,8},{1,5},{5,1},{9,13},{13,9},{2,6},{6,2},{1... | collective-permute-start | bytes 786440 | tf_op jit(solution)/shard_map/ppermute | solution.py:21
  154.7 14.1 %collective-permute-start.13 = (bf16[512,256]{1,0:T(8,128)(2,1)S(1)}, bf16[512,256]{1,0:T(8,128)(2,1)}, u32[]{:S(2)}, u32[]{:S(2)}) collective-permute-start(bf16[512,256]{1,0:T(8,128)(2,1)S(1)} %add_convert_fusion.3), channel_id=1, source_target_pairs={{0,8},{4,12},{8,0},{12,4},{1,9},{5,13},{9,1},{13,5},{2,10},{6,14},... | collective-permute-start | bytes 786440 | tf_op jit(solution)/shard_map/ppermute | solution.py:21
  176.9 45.7 %collective-permute-start.21 = (bf16[2,64,2048]{2,1,0:T(8,128)(2,1)}, bf16[2,64,2048]{2,1,0:T(8,128)(2,1)S(1)}, u32[]{:S(2)}, u32[]{:S(2)}) collective-permute-start(bf16[2,64,2048]{2,1,0:T(8,128)(2,1)} %bitcast.35), channel_id=1, source_target_pairs={{0,12},{4,8},{8,4},{12,0},{1,13},{5,9},{9,5},{13,1},{2,14},{6,10},... | collective-permute-start | bytes 1572872 | tf_op jit(solution)/shard_map/ppermute | solution.py:21
  179.3 46.6 %collective-permute-start.22 = (bf16[2,64,2048]{2,1,0:T(8,128)(2,1)}, bf16[2,64,2048]{2,1,0:T(8,128)(2,1)}, u32[]{:S(2)}, u32[]{:S(2)}) collective-permute-start(bf16[2,64,2048]{2,1,0:T(8,128)(2,1)} %bitcast.36), channel_id=1, source_target_pairs={{0,8},{4,12},{8,0},{12,4},{1,9},{5,13},{9,1},{13,5},{2,10},{6,14},... | collective-permute-start | bytes 1572872 | tf_op jit(solution)/shard_map/ppermute | solution.py:21
  179.3 46.6 %collective-permute-start.23 = (bf16[2,64,2048]{2,1,0:T(8,128)(2,1)}, bf16[2,64,2048]{2,1,0:T(8,128)(2,1)}, u32[]{:S(2)}, u32[]{:S(2)}) collective-permute-start(bf16[2,64,2048]{2,1,0:T(8,128)(2,1)} %bitcast.37), channel_id=1, source_target_pairs={{0,4},{4,0},{8,12},{12,8},{1,5},{5,1},{9,13},{13,9},{2,6},{6,2},{1... | collective-permute-start | bytes 1572872 | tf_op jit(solution)/shard_map/ppermute | solution.py:21
  194.4 25.6 %collective-permute-start.25 = (bf16[512,256]{1,0:T(8,128)(2,1)S(1)}, bf16[512,256]{1,0:T(8,128)(2,1)S(1)}, u32[]{:S(2)}, u32[]{:S(2)}) collective-permute-start(bf16[512,256]{1,0:T(8,128)(2,1)S(1)} %get-tuple-element.17), channel_id=1, source_target_pairs={{0,4},{4,0},{8,12},{12,8},{1,5},{5,1},{9,13},{13,9},{2,6},{6,2},{1... | collective-permute-start | bytes 786440 | tf_op jit(solution)/shard_map/ppermute | solution.py:21
  197.5 30.8 %collective-permute-start.24 = (bf16[512,256]{1,0:T(8,128)(2,1)S(1)}, bf16[512,256]{1,0:T(8,128)(2,1)S(1)}, u32[]{:S(2)}, u32[]{:S(2)}) collective-permute-start(bf16[512,256]{1,0:T(8,128)(2,1)S(1)} %get-tuple-element.16), channel_id=1, source_target_pairs={{0,4},{4,0},{8,12},{12,8},{1,5},{5,1},{9,13},{13,9},{2,6},{6,2},{1... | collective-permute-start | bytes 786440 | tf_op jit(solution)/shard_map/ppermute | solution.py:21
  220.1 14.1 %collective-permute-start.26 = (bf16[512,256]{1,0:T(8,128)(2,1)S(1)}, bf16[512,256]{1,0:T(8,128)(2,1)S(1)}, u32[]{:S(2)}, u32[]{:S(2)}) collective-permute-start(bf16[512,256]{1,0:T(8,128)(2,1)S(1)} %add_convert_fusion.1), channel_id=1, source_target_pairs={{0,8},{4,12},{8,0},{12,4},{1,9},{5,13},{9,1},{13,5},{2,10},{6,14},... | collective-permute-start | bytes 786440 | tf_op jit(solution)/shard_map/ppermute | solution.py:21
  234.4 8.3 %collective-permute-start.27 = (bf16[1,2,256,256]{3,2,1,0:T(8,128)(2,1)S(1)}, bf16[1,2,256,256]{3,2,1,0:T(8,128)(2,1)S(1)}, u32[]{:S(2)}, u32[]{:S(2)}) collective-permute-start(bf16[1,2,256,256]{3,2,1,0:T(8,128)(2,1)S(1)} %bitcast.179), channel_id=1, source_target_pairs={{0,16},{16,0},{1,17},{17,1},{2,18},{18,2},{3,19},{19,3},{4,20},{20... | collective-permute-start | bytes 786440 | tf_op jit(solution)/shard_map/ppermute | solution.py:38
  (16 other events, 103.9 us)

commit v3 on v2

v3 whole, which is shorter than its diff:
```python
import functools

import jax
import jax.numpy as jnp
from jax import lax
from jax.experimental import pallas as pl
from jax.experimental.pallas import tpu as pltpu
from jax.sharding import PartitionSpec as P

beta_first = 0.9
beta_second = 0.95
learn_rate = 0.03
weight_decay = 0.1
adam_eps = 1e-08
norm_eps = 1e-05
step_count = 20.0

f32 = jnp.float32
bf16 = jnp.bfloat16


def swap(x, axis, bits):
    peers = lax.axis_size(axis)
    return lax.ppermute(x, axis, [(i, i ^ bits) for i in range(peers)])


def mark(x):
    return x[tuple(slice(0, 1) for _ in x.shape[:-2])][..., :16, :128]


def after(values, *earlier):
    hbm = pl.BlockSpec(memory_space=pl.ANY)
    marks = [mark(e) for e in earlier]
    tied = pl.pallas_call(
        lambda *refs: None,
        out_shape=[jax.ShapeDtypeStruct(x.shape, x.dtype) for x in values],
        in_specs=[hbm] * (len(values) + len(marks)),
        out_specs=[hbm] * len(values),
        input_output_aliases={i: i for i in range(len(values))},
        name="after",
    )(*values, *marks)
    return list(tied)


def from_behind(x, axis, by):
    peers = lax.axis_size(axis)
    return lax.ppermute(x, axis, [(i, (i + by) % peers) for i in range(peers)])


def dot(a, b, contract):
    return lax.dot_general(a, b, (contract, ((), ())), preferred_element_type=f32)


def reorder(blocks, me):
    bit = 1
    while bit < len(blocks):
        flip = (me & bit) != 0
        blocks = [jnp.where(flip, blocks[i ^ bit], blocks[i]) for i in range(len(blocks))]
        bit *= 2
    return blocks


def scatter_sum(keep, send):
    got = swap(send, "dp", 1)
    mine = keep[0].astype(f32) + got[0].astype(f32)
    other = (keep[1].astype(f32) + got[1].astype(f32)).astype(bf16)
    return mine + swap(other, "dp", 2).astype(f32), other


def update_kernel(mark_ref, cot_ref, master_ref, m_ref, v_ref, *rest, layout, tile):
    count = len(layout)
    token_refs, (new_ref, keep_ref, send_ref, updated_ref) = rest[:count], rest[count:]
    starts = [sum(x.shape[0] for x in token_refs[:p]) for p in range(count)]

    @pl.loop(0, master_ref.shape[0] // tile)
    def _(i):
        at = pl.ds(pl.multiple_of(i * tile, tile), tile)
        grad = sum(
            dot(cot_ref[:, start : start + x.shape[0]], x[:, at], ((1,), (0,)))
            for start, x in zip(starts, token_refs)
        ).T
        m_new = beta_first * m_ref[at, :] + (1.0 - beta_first) * grad
        v_new = beta_second * v_ref[at, :] + (1.0 - beta_second) * grad * grad
        m_hat = m_new / (1.0 - beta_first**step_count)
        v_hat = v_new / (1.0 - beta_second**step_count)
        master = master_ref[at, :]
        master_new = master - learn_rate * (
            m_hat / (jnp.sqrt(v_hat) + adam_eps) + weight_decay * master
        )
        new_ref[at, :] = master_new
        updated_ref[at, :] = master_new.astype(bf16)

    project(layout, token_refs, updated_ref, keep_ref, send_ref)


def project(layout, token_refs, weights_ref, keep_ref, send_ref):
    for (first, side, replicas), token_ref in zip(layout, token_refs):
        height = token_ref.shape[0] // replicas
        for i in range(replicas):
            k = first + i
            part_ref = send_ref if k % 2 else keep_ref
            part_ref[k // 2, side * height : (side + 1) * height, :] = dot(
                token_ref[i * height : (i + 1) * height, :], weights_ref[...], ((1,), (0,))
            ).astype(bf16)


def project_kernel(mark_ref, weights_ref, *rest, layout):
    project(layout, rest[: len(layout)], weights_ref, *rest[len(layout) :])


vmem = pl.BlockSpec(memory_space=pltpu.VMEM)
anywhere = pl.BlockSpec(memory_space=pl.ANY)
params = pltpu.CompilerParams(vmem_limit_bytes=28 * 1024 * 1024)
light = pl.CostEstimate(flops=1000, bytes_accessed=1000, transcendentals=0)


def shards(hidden_in, norm_gain, kv_cot, master_kv, moment_m, moment_v):
    dp, tensor = lax.axis_size("dp"), lax.axis_size("tensor")
    z, t = lax.axis_index("dp"), lax.axis_index("tensor")
    gain_row = norm_gain[0]
    widened = hidden_in[0].astype(f32)
    micro, rows, width = widened.shape
    depth = width // dp
    cols = kv_cot.shape[-1]
    scaling = lax.rsqrt(jnp.mean(widened * widened, axis=-1, keepdims=True) + norm_eps)
    normed = (widened * scaling * gain_row).astype(bf16)

    def feature_block(x, k):
        return lax.dynamic_slice_in_dim(x, (z ^ k) * depth, depth, x.ndim - 1)

    weights = master_kv[0].astype(bf16)
    blocks = kv_cot[0].reshape(micro, tensor, rows, cols)
    blocks = [
        lax.dynamic_slice_in_dim(blocks, t ^ j, 1, 1).reshape(micro * rows, cols)
        for j in range(tensor)
    ]
    order = (0, 2, 1, 3)
    cot = jnp.concatenate([blocks[0]] + [swap(blocks[j], "tensor", j) for j in order[1:]], 1)
    w2 = swap(weights, "tensor", 2)
    cot2 = swap(cot, "dp", 2)
    own = [feature_block(normed, k).reshape(micro * rows, depth) for k in range(dp)]
    own[1], own[3] = after([own[1], own[3]], cot2)
    piece1, piece3 = swap(own[1], "dp", 1), swap(own[3], "dp", 3)
    pair = swap(jnp.stack([cot, cot2]), "dp", 1)
    cots = [cot, pair[0], cot2, pair[1]]
    own[0], w2 = after([own[0], w2], w2)
    across0 = swap(own[0], "tensor", 2)
    w13 = swap(jnp.concatenate([weights, w2], 1), "tensor", 1)
    theirs = [
        jnp.stack([c[:, order.index(j) * cols : (order.index(j) + 1) * cols] for c in cots[1:]])
        for j in range(tensor)
    ]
    whole_w = jnp.concatenate([weights, w2, w13], 1)
    d_part = dot(jnp.concatenate(cots), whole_w, ((1,), (1,))).astype(bf16)
    d_part = d_part.reshape(dp, micro * rows, depth)
    d_send = [d_part[k] for k in range(dp)]
    piece1, piece3, own[2], across0, far_cot = after(
        [piece1, piece3, own[2], across0, jnp.concatenate(theirs[2:])], d_send[1]
    )
    piece2 = swap(own[2], "dp", 2)
    across1, across3 = swap(piece1, "tensor", 2), swap(piece3, "tensor", 2)
    got = swap(far_cot, "tensor", 2)
    got2, got3 = got[: dp - 1], got[dp - 1 :]
    near_rows = swap(jnp.concatenate([theirs[1], got3]), "tensor", 1)
    got1, got3 = near_rows[: dp - 1], near_rows[dp - 1 :]
    rows_of = [jnp.concatenate([blocks[j][None], x]) for j, x in enumerate((theirs[0], got1, got2, got3))]
    near01 = jnp.concatenate([own[0], across0, piece1, across1])
    piece2, d_send[2] = after([piece2, d_send[2]], across1, across3)
    across2 = swap(piece2, "tensor", 2)
    d_recv = [d_send[0], None, swap(d_send[2], "dp", 2), None]
    far01 = swap(near01, "tensor", 1)
    near3 = jnp.concatenate([piece3, across3])
    far3 = swap(near3, "tensor", 1)
    across2, d_send[1], d_send[3] = after([across2, d_send[1], d_send[3]], d_recv[2])
    near2 = jnp.concatenate([piece2, across2])
    far2 = swap(near2, "tensor", 1)
    d_recv[1], d_recv[3] = swap(d_send[1], "dp", 1), swap(d_send[3], "dp", 3)
    tokens = [near01, far01, near2, far2, near3, far3]
    layout = ((0, 0, 2), (0, 1, 2), (2, 0, 1), (2, 1, 1), (3, 0, 1), (3, 1, 1))
    cot_all = jnp.concatenate(
        [
            rows_of[j + side][k]
            for first, side, replicas in layout
            for k in range(first, first + replicas)
            for j in (0, 2)
        ]
    ).T
    block = tensor * micro * rows

    def place(x):
        x = x.reshape(tensor, micro, rows, cols)
        return jnp.stack(reorder([x[j] for j in order], t), 1).reshape(
            1, micro, tensor * rows, cols
        )

    own_depth = master_kv.shape[1]
    part_shape = [jax.ShapeDtypeStruct((dp // 2, block, cols), bf16)] * 2
    count = len(tokens)
    master_new, keep, send = pl.pallas_call(
        functools.partial(update_kernel, layout=layout, tile=min(own_depth, 256)),
        out_shape=[jax.ShapeDtypeStruct((own_depth, cols), f32)] + part_shape,
        in_specs=[anywhere] + [vmem] * (4 + count),
        out_specs=[vmem] * 3,
        scratch_shapes=[pltpu.VMEM((own_depth, cols), bf16)],
        compiler_params=params,
        cost_estimate=light,
        name="update",
    )(mark(d_send[3]), cot_all, master_kv[0], moment_m[0], moment_v[0], *tokens)
    total, other = scatter_sum(keep, send)
    mine = place(total.astype(bf16))
    kv_next = from_behind(mine, "segment", -1)
    own_keep, own_send = pl.pallas_call(
        functools.partial(project_kernel, layout=layout),
        out_shape=part_shape,
        in_specs=[anywhere] + [vmem] * (1 + count),
        out_specs=[vmem] * 2,
        compiler_params=params,
        cost_estimate=light,
        name="project",
    )(mark(send), weights, *tokens)
    kv_own = place(scatter_sum(own_keep, own_send)[0].astype(bf16))

    d_recv[1], d_recv[3] = after([d_recv[1], d_recv[3]], own_send, other)
    d_normed = jnp.concatenate(reorder(d_recv, z), -1).astype(f32).reshape(widened.shape)
    upper = d_normed * gain_row
    grad_in = (
        scaling * upper - widened * scaling**3 * jnp.mean(upper * widened, axis=-1, keepdims=True)
    ).astype(bf16)

    return (kv_own, grad_in[None], master_new[None], kv_next)


def solution(mesh):
    in_specs = (
        P("segment", None, ("dp", "tensor"), None),
        P("segment", None),
        P("segment", None, "dp", "tensor"),
        P("segment", "dp", "tensor"),
        P("segment", "dp", "tensor"),
        P("segment", "dp", "tensor"),
    )
    out_specs = (
        P("segment", None, "dp", "tensor"),
        P("segment", None, ("dp", "tensor"), None),
        P("segment", "dp", "tensor"),
        P("segment", None, "dp", "tensor"),
    )
    return jax.shard_map(shards, mesh=mesh, in_specs=in_specs, out_specs=out_specs, check_vma=False)
```

time: 244 us -> 232 us (0.951)
  waiting for transfers between devices: 147 us -> 102 us
  local copies, waits for them, and re-layouts: 25.4 us -> 61.3 us
  Pallas kernels: 0.01 us -> 16.3 us
  matrix products: 19.8 us -> 4.48 us
  starting transfers between devices: 29.2 us -> 25.9 us
    ppermute x27 -> x26, waiting for transfers between devices: 142 us -> 97.5 us  [swap(): return lax.ppermute(x, axis, [(i, i ^ bits) for i in range(peers)])]
    unnamed x67 -> x87, local copies, waits for them, and re-layouts: 17.8 us -> 34.7 us
    pallas_call x2 -> x8, Pallas kernels: 0.01 us -> 16.3 us  [the longest x1 11.3 us: shards(): pl.pallas_call(functools.partial(update_kernel, layout=layout, tile=min(o...]
    dot_general x4 -> x1, matrix products: 19.8 us -> 4.48 us  [dot(): lax.dot_general(a, b, (contract, ((), ())), preferred_element_type=f32)]
    slice x3 -> x13, local copies, waits for them, and re-layouts: 2.06 us -> 10.1 us  [the longest x11 8.91 us: mark(): return x[tuple((slice(0, 1) for _ in x.shape[:-2]))][..., :16, :128]]
    concatenate x2 -> x6, local copies, waits for them, and re-layouts: 0.73 us -> 7.35 us  [the longest x1 1.97 us: shards(): near2 = jnp.concatenate([piece2, across2])]
    convert_element_type x4, other arithmetic: 1.38 us -> 5.24 us  [the longest x2 2.97 us: scatter_sum(): other = (keep[1].astype(f32) + got[1].astype(f32)).astype(bf16)]
    ppermute x27 -> x26, starting transfers between devices: 27.6 us -> 24.4 us  [swap(): return lax.ppermute(x, axis, [(i, i ^ bits) for i in range(peers)])]
  transfers between devices with their start and end apart: 28 -> 27, of which waited for: 13 -> 9; matrix products, arithmetic and copies ran while one was open for 21% -> 31% of each run, Pallas kernels for 0% -> 2%
where the time goes in v3:
time: 232 us; the launch traced here: 230 us
  waiting for transfers between devices  102 us (44%)
  local copies, waits for them, and re-layouts  61.3 us (26%)
  starting transfers between devices  25.9 us (11%)
  other arithmetic  18.9 us (8%)
  Pallas kernels  16.3 us (7%)
  matrix products  4.48 us (2%)
    ppermute x26, waiting for transfers between devices, swap(): return lax.ppermute(x, axis, [(i, i ^ bits) for i in range(peers)])  97.5 us
    unnamed x87, local copies, waits for them, and re-layouts  34.7 us
    ppermute x26, starting transfers between devices, swap(): return lax.ppermute(x, axis, [(i, i ^ bits) for i in range(peers)])  24.4 us
    pallas_call x1, Pallas kernels, shards(): pl.pallas_call(functools.partial(update_kernel, layout=layout, tile=min(o...  11.3 us
    slice x11, local copies, waits for them, and re-layouts, mark(): return x[tuple((slice(0, 1) for _ in x.shape[:-2]))][..., :16, :128]  8.91 us
    pallas_call x1, Pallas kernels, shards(): pl.pallas_call(functools.partial(project_kernel, layout=layout), out_shap...  4.99 us
  transfers between devices with their start and end apart: 27, of which 9 were waited for; matrix products, arithmetic and copies ran while one was open for 31% of the time, Pallas kernels for 2%

profile of v3, /device:TPU:0, one launch (start us, length us, event | category | flops | bytes accessed | tf_op | source)
XLA Modules:
  0.0 230.0 jit_solution(15889248179099956074)
XLA Ops:
  1.9 2.5 %collective-permute-start.2 = (bf16[128,256]{0,1:T(8,128)(2,1)S(1)}, bf16[128,256]{0,1:T(8,128)(2,1)}, u32[]{:S(2)}, u32[]{:S(2)}) collective-permute-start(bf16[128,256]{0,1:T(8,128)(2,1)S(1)} %copy.50), channel_id=1, source_target_pairs={{0,3},{1,2},{2,1},{3,0},{4,7},{5,6},{6,5},{7,4},{8,11},{9,10},{10,... | collective-permute-start | bytes 196616 | tf_op jit(solution)/shard_map/ppermute | solution.py:24
  5.5 1.7 bitcast_convert_fusion.weights_ref
  7.2 2.1 collective-permute-start.6
  9.8 1.9 fusion.5
  13.4 2.7 %collective-permute-start.3 = (bf16[128,1024]{0,1:T(8,128)(2,1)S(1)}, bf16[128,1024]{0,1:T(8,128)(2,1)S(1)}, u32[]{:S(2)}, u32[]{:S(2)}) collective-permute-start(bf16[128,1024]{0,1:T(8,128)(2,1)S(1)} %get-tuple-element.70), channel_id=1, source_target_pairs={{0,8},{4,12},{8,0},{12,4},{1,9},{5,13},{9,1},{13,5},{2,10},{6,14},... | collective-permute-start | bytes 786440 | tf_op jit(solution)/shard_map/ppermute | solution.py:24
  16.1 2.9 %constant_dynamic-slice_fusion = (bf16[2,64,2048]{2,1,0:T(8,128)(2,1)}, bf16[2,64,2048]{2,1,0:T(8,128)(2,1)}, bf16[2,64,2048]{2,1,0:T(8,128)(2,1)}, bf16[2,64,2048]{2,1,0:T(8,128)(2,1)}) fusion(bf16[2,64,8192]{2,1,0:T(8,128)(2,1)} %fusion.5, s32[]{:T(128)S(6)} %select_n.317, s32[]{:T(128)S(6)} %select_n.316, s32[]{:T(128)S(6)} %select_n.311, s32[]{:T(128)S(6)} %select_n.310), kind=kLoop, calls=%fused_computation.120 | loop fusion | bytes 4194320 | tf_op jit(solution)/shard_map/dynamic_slice | solution.py:129
  19.0 8.7 %collective-permute-done.3 = bf16[128,1024]{0,1:T(8,128)(2,1)S(1)} collective-permute-done((bf16[128,1024]{0,1:T(8,128)(2,1)S(1)}, bf16[128,1024]{0,1:T(8,128)(2,1)S(1)}, u32[]{:S(2)}, u32[]{:S(2)}) %collective-permute-start.3) | collective-permute-done | bytes 262176 | tf_op jit(solution)/shard_map/ppermute | solution.py:24
  31.1 3.5 %collective-permute-start.5 = (bf16[128,2048]{1,0:T(8,128)(2,1)}, bf16[128,2048]{1,0:T(8,128)(2,1)}, u32[]{:S(2)}, u32[]{:S(2)}) collective-permute-start(bf16[128,2048]{1,0:T(8,128)(2,1)} %get-tuple-element.26), channel_id=1, source_target_pairs={{0,12},{4,8},{8,4},{12,0},{1,13},{5,9},{9,5},{13,1},{2,14},{6,10},... | collective-permute-start | bytes 1572872 | tf_op jit(solution)/shard_map/ppermute | solution.py:24
  36.5 2.7 %pad_maximum_fusion = bf16[2048,512]{1,0:T(8,128)(2,1)} fusion(bf16[2048,256]{1,0:T(8,128)(2,1)} %get-tuple-element.28, bf16[2048,256]{1,0:T(8,128)(2,1)S(1)} %bitcast_convert_fusion.weights_ref), kind=kLoop, calls=%fused_computation.19 | loop fusion | flops 4194304 | bytes 4194304 | tf_op jit(solution)/shard_map/concatenate | solution.py:148
  39.2 3.4 %collective-permute-done.8 = bf16[2,128,1024]{1,2,0:T(8,128)(2,1)S(1)} collective-permute-done((bf16[2,128,1024]{1,2,0:T(8,128)(2,1)S(1)}, bf16[2,128,1024]{1,2,0:T(8,128)(2,1)S(1)}, u32[]{:S(2)}, u32[]{:S(2)}) %collective-permute-start.8) | collective-permute-done | bytes 524320 | tf_op jit(solution)/shard_map/ppermute | solution.py:24
  46.7 4.5 %fusion.16 = bf16[512,2048]{1,0:T(8,128)(2,1)S(1)} fusion(bf16[2048,512]{1,0:T(8,128)(2,1)} %collective-permute-done.9, bf16[2048,256]{1,0:T(8,128)(2,1)} %get-tuple-element.28, bf16[2048,256]{1,0:T(8,128)(2,1)S(1)} %bitcast_convert_fusion.weights_ref, bf16[128,1024]{0,1:T(8,128)(2,1)} %copy-done.15, bf16[128,1024]{0,1:T(8,128)(2,1)S(1)} %collective-permute-done.3, ...), kind=kOutput, calls=%fused_computation.18 | convolution fusion | flops 2168455168 | bytes 7340032 | tf_op jit(solution)/shard_map/dot_general | solution.py:51
  53.1 12.9 %collective-permute-done.5.refs_1_ = bf16[128,2048]{1,0:T(8,128)(2,1)} collective-permute-done((bf16[128,2048]{1,0:T(8,128)(2,1)}, bf16[128,2048]{1,0:T(8,128)(2,1)}, u32[]{:S(2)}, u32[]{:S(2)}) %collective-permute-start.5) | collective-permute-done | bytes 524320 | tf_op jit(solution)/shard_map/ppermute | solution.py:24
  66.5 1.9 constant_dynamic-update-slice_fusion.11
  69.9 1.9 copy.54
  76.0 23.2 %collective-permute-done.15 = bf16[6,128,256]{1,2,0:T(8,128)(2,1)S(1)} collective-permute-done((bf16[6,128,256]{1,2,0:T(8,128)(2,1)}, bf16[6,128,256]{1,2,0:T(8,128)(2,1)S(1)}, u32[]{:S(2)}, u32[]{:S(2)}) %collective-permute-start.15) | collective-permute-done | bytes 393248 | tf_op jit(solution)/shard_map/ppermute | solution.py:24
  106.5 1.9 constant_dynamic-update-slice_fusion.10.rest_4_
  108.7 1.9 constant_dynamic-update-slice_fusion.9
  117.2 12.1 %collective-permute-done.14 = bf16[128,2048]{1,0:T(8,128)(2,1)S(1)} collective-permute-done((bf16[128,2048]{1,0:T(8,128)(2,1)}, bf16[128,2048]{1,0:T(8,128)(2,1)S(1)}, u32[]{:S(2)}, u32[]{:S(2)}) %collective-permute-start.14) | collective-permute-done | bytes 524320 | tf_op jit(solution)/shard_map/ppermute | solution.py:24
  130.6 2.0 constant_dynamic-update-slice_fusion.8.rest_2_
  143.5 1.6 copy-done.3
  145.1 1.6 copy-done.4
  146.7 11.3 %update.1 = (f32[2048,256]{1,0:T(8,128)}, bf16[2,512,256]{2,1,0:T(8,128)(2,1)S(1)}, bf16[2,512,256]{2,1,0:T(8,128)(2,1)}) custom-call(bf16[16,128]{1,0:T(8,128)(2,1)S(1)} %slice.208.mark_ref, bf16[256,2048]{1,0:T(8,128)(2,1)} %bitcast.34.cot_ref, f32[2048,256]{1,0:T(8,128)S(1)} %bitcast.135, f32[2048,256]{1,0:T(8,128)S(1)} %bitcast.136, ...), custom_call_target="tpu_custom_call" | custom-call | flops 1000 | bytes 1000 | tf_op jit(solution)/shard_map/update/pallas_call | solution.py:199
  158.7 5.0 %project.1 = (bf16[2,512,256]{2,1,0:T(8,128)(2,1)S(1)}, bf16[2,512,256]{2,1,0:T(8,128)(2,1)}) custom-call(bf16[1,16,128]{2,1,0:T(8,128)(2,1)S(1)} %slice.225.mark_ref, bf16[2048,256]{1,0:T(8,128)(2,1)S(1)} %bitcast_convert_fusion.weights_ref, bf16[512,2048]{1,0:T(8,128)(2,1)S(1)} %constant_dynamic-update-slice_fusion.4.rest_0_, ...), custom_call_target="tpu_custom_call" | custom-call | flops 1000 | bytes 1000 | tf_op jit(solution)/shard_map/project/pallas_call | solution.py:212
  164.5 2.0 collective-permute-start.20
  166.6 2.6 %collective-permute-start.23 = (bf16[128,2048]{1,0:T(8,128)(2,1)}, bf16[128,2048]{1,0:T(8,128)(2,1)S(1)}, u32[]{:S(2)}, u32[]{:S(2)}) collective-permute-start(bf16[128,2048]{1,0:T(8,128)(2,1)} %get-tuple-element.34), channel_id=1, source_target_pairs={{0,12},{4,8},{8,4},{12,0},{1,13},{5,9},{9,5},{13,1},{2,14},{6,10},... | collective-permute-start | bytes 1572872 | tf_op jit(solution)/shard_map/ppermute | solution.py:24
  170.5 2.6 %collective-permute-done.24 = bf16[2,512,256]{2,1,0:T(8,128)(2,1)} collective-permute-done((bf16[2,512,256]{2,1,0:T(8,128)(2,1)}, bf16[2,512,256]{2,1,0:T(8,128)(2,1)}, u32[]{:S(2)}, u32[]{:S(2)}) %collective-permute-start.24) | collective-permute-done | bytes 524320 | tf_op jit(solution)/shard_map/ppermute | solution.py:24
  176.0 13.8 %collective-permute-done.20 = bf16[2,512,256]{2,1,0:T(8,128)(2,1)S(1)} collective-permute-done((bf16[2,512,256]{2,1,0:T(8,128)(2,1)}, bf16[2,512,256]{2,1,0:T(8,128)(2,1)S(1)}, u32[]{:S(2)}, u32[]{:S(2)}) %collective-permute-start.20) | collective-permute-done | bytes 524320 | tf_op jit(solution)/shard_map/ppermute | solution.py:24
  189.8 1.9 fusion.34
  192.5 20.7 %collective-permute-done.22.refs_0_ = bf16[128,2048]{1,0:T(8,128)(2,1)S(1)} collective-permute-done((bf16[128,2048]{1,0:T(8,128)(2,1)}, bf16[128,2048]{1,0:T(8,128)(2,1)S(1)}, u32[]{:S(2)}, u32[]{:S(2)}) %collective-permute-start.22) | collective-permute-done | bytes 524320 | tf_op jit(solution)/shard_map/ppermute | solution.py:24
  214.8 1.8 broadcast_select_fusion.7
  217.9 2.1 fusion.9
  224.8 4.5 %collective-permute-done.26 = bf16[1,2,256,256]{3,2,1,0:T(8,128)(2,1)S(1)} collective-permute-done((bf16[1,2,256,256]{3,2,1,0:T(8,128)(2,1)S(1)}, bf16[1,2,256,256]{3,2,1,0:T(8,128)(2,1)S(1)}, u32[]{:S(2)}, u32[]{:S(2)}) %collective-permute-start.26) | collective-permute-done | bytes 262176 | tf_op jit(solution)/shard_map/ppermute | solution.py:47
  (170 shorter events, 63.1 us)
Async XLA Ops:
  1.9 10.6 %collective-permute-start.2 = (bf16[128,256]{0,1:T(8,128)(2,1)S(1)}, bf16[128,256]{0,1:T(8,128)(2,1)}, u32[]{:S(2)}, u32[]{:S(2)}) collective-permute-start(bf16[128,256]{0,1:T(8,128)(2,1)S(1)} %copy.50), channel_id=1, source_target_pairs={{0,3},{1,2},{2,1},{3,0},{4,7},{5,6},{6,5},{7,4},{8,11},{9,10},{10,... | collective-permute-start | bytes 196616 | tf_op jit(solution)/shard_map/ppermute | solution.py:24
  4.5 8.0 %collective-permute-start.1 = (bf16[128,256]{0,1:T(8,128)(2,1)S(1)}, bf16[128,256]{0,1:T(8,128)(2,1)}, u32[]{:S(2)}, u32[]{:S(2)}) collective-permute-start(bf16[128,256]{0,1:T(8,128)(2,1)S(1)} %copy.49), channel_id=1, source_target_pairs={{0,1},{1,0},{2,3},{3,2},{4,5},{5,4},{6,7},{7,6},{8,9},{9,8},{10,11... | collective-permute-start | bytes 196616 | tf_op jit(solution)/shard_map/ppermute | solution.py:24
  5.4 7.1 %collective-permute-start = (bf16[128,256]{0,1:T(8,128)(2,1)S(1)}, bf16[128,256]{0,1:T(8,128)(2,1)}, u32[]{:S(2)}, u32[]{:S(2)}) collective-permute-start(bf16[128,256]{0,1:T(8,128)(2,1)S(1)} %copy.48), channel_id=1, source_target_pairs={{0,2},{1,3},{2,0},{3,1},{4,6},{5,7},{6,4},{7,5},{8,10},{9,11},{10,... | collective-permute-start | bytes 196616 | tf_op jit(solution)/shard_map/ppermute | solution.py:24
  7.2 28.1 %collective-permute-start.6 = (bf16[2048,256]{1,0:T(8,128)(2,1)S(1)}, bf16[2048,256]{1,0:T(8,128)(2,1)}, u32[]{:S(2)}, u32[]{:S(2)}) collective-permute-start(bf16[2048,256]{1,0:T(8,128)(2,1)S(1)} %bitcast_convert_fusion.weights_ref), channel_id=1, source_target_pairs={{0,2},{1,3},{2,0},{3,1},{4,6},{5,7},{6,4},{7,5},{8,10},{9,11},{10,... | collective-permute-start | bytes 3145736 | tf_op jit(solution)/shard_map/ppermute | solution.py:24
  13.4 14.2 %collective-permute-start.3 = (bf16[128,1024]{0,1:T(8,128)(2,1)S(1)}, bf16[128,1024]{0,1:T(8,128)(2,1)S(1)}, u32[]{:S(2)}, u32[]{:S(2)}) collective-permute-start(bf16[128,1024]{0,1:T(8,128)(2,1)S(1)} %get-tuple-element.70), channel_id=1, source_target_pairs={{0,8},{4,12},{8,0},{12,4},{1,9},{5,13},{9,1},{13,5},{2,10},{6,14},... | collective-permute-start | bytes 786440 | tf_op jit(solution)/shard_map/ppermute | solution.py:24
  27.7 14.9 %collective-permute-start.8 = (bf16[2,128,1024]{1,2,0:T(8,128)(2,1)S(1)}, bf16[2,128,1024]{1,2,0:T(8,128)(2,1)S(1)}, u32[]{:S(2)}, u32[]{:S(2)}) collective-permute-start(bf16[2,128,1024]{1,2,0:T(8,128)(2,1)S(1)} %pad_maximum_fusion.1), channel_id=1, source_target_pairs={{0,4},{4,0},{8,12},{12,8},{1,5},{5,1},{9,13},{13,9},{2,6},{6,2},{1... | collective-permute-start | bytes 1572872 | tf_op jit(solution)/shard_map/ppermute | solution.py:24
  29.8 23.3 %collective-permute-start.4 = (bf16[128,2048]{1,0:T(8,128)(2,1)}, bf16[128,2048]{1,0:T(8,128)(2,1)}, u32[]{:S(2)}, u32[]{:S(2)}) collective-permute-start(bf16[128,2048]{1,0:T(8,128)(2,1)} %get-tuple-element.25), channel_id=1, source_target_pairs={{0,4},{4,0},{8,12},{12,8},{1,5},{5,1},{9,13},{13,9},{2,6},{6,2},{1... | collective-permute-start | bytes 1572872 | tf_op jit(solution)/shard_map/ppermute | solution.py:24
  31.1 34.8 %collective-permute-start.5 = (bf16[128,2048]{1,0:T(8,128)(2,1)}, bf16[128,2048]{1,0:T(8,128)(2,1)}, u32[]{:S(2)}, u32[]{:S(2)}) collective-permute-start(bf16[128,2048]{1,0:T(8,128)(2,1)} %get-tuple-element.26), channel_id=1, source_target_pairs={{0,12},{4,8},{8,4},{12,0},{1,13},{5,9},{9,5},{13,1},{2,14},{6,10},... | collective-permute-start | bytes 1572872 | tf_op jit(solution)/shard_map/ppermute | solution.py:24
  39.2 7.4 %collective-permute-start.9 = (bf16[2048,512]{1,0:T(8,128)(2,1)}, bf16[2048,512]{1,0:T(8,128)(2,1)}, u32[]{:S(2)}, u32[]{:S(2)}) collective-permute-start(bf16[2048,512]{1,0:T(8,128)(2,1)} %pad_maximum_fusion), channel_id=1, source_target_pairs={{0,1},{1,0},{2,3},{3,2},{4,5},{5,4},{6,7},{7,6},{8,9},{9,8},{10,11... | collective-permute-start | bytes 6291464 | tf_op jit(solution)/shard_map/ppermute | solution.py:24
  45.1 20.9 %collective-permute-start.7 = (bf16[128,2048]{1,0:T(8,128)(2,1)}, bf16[128,2048]{1,0:T(8,128)(2,1)}, u32[]{:S(2)}, u32[]{:S(2)}) collective-permute-start(bf16[128,2048]{1,0:T(8,128)(2,1)} %get-tuple-element.27), channel_id=1, source_target_pairs={{0,2},{1,3},{2,0},{3,1},{4,6},{5,7},{6,4},{7,5},{8,10},{9,11},{10,... | collective-permute-start | bytes 1572872 | tf_op jit(solution)/shard_map/ppermute | solution.py:24
  66.0 37.3 %collective-permute-start.12 = (bf16[128,2048]{1,0:T(8,128)(2,1)}, bf16[128,2048]{1,0:T(8,128)(2,1)}, u32[]{:S(2)}, u32[]{:S(2)}) collective-permute-start(bf16[128,2048]{1,0:T(8,128)(2,1)} %get-tuple-element.31), channel_id=1, source_target_pairs={{0,2},{1,3},{2,0},{3,1},{4,6},{5,7},{6,4},{7,5},{8,10},{9,11},{10,... | collective-permute-start | bytes 1572872 | tf_op jit(solution)/shard_map/ppermute | solution.py:24
  68.4 36.2 %collective-permute-start.10 = (bf16[128,2048]{1,0:T(8,128)(2,1)}, bf16[128,2048]{1,0:T(8,128)(2,1)}, u32[]{:S(2)}, u32[]{:S(2)}) collective-permute-start(bf16[128,2048]{1,0:T(8,128)(2,1)} %get-tuple-element.29), channel_id=1, source_target_pairs={{0,8},{4,12},{8,0},{12,4},{1,9},{5,13},{9,1},{13,5},{2,10},{6,14},... | collective-permute-start | bytes 1572872 | tf_op jit(solution)/shard_map/ppermute | solution.py:24
  68.4 33.6 %collective-permute-start.11 = (bf16[128,2048]{1,0:T(8,128)(2,1)}, bf16[128,2048]{1,0:T(8,128)(2,1)}, u32[]{:S(2)}, u32[]{:S(2)}) collective-permute-start(bf16[128,2048]{1,0:T(8,128)(2,1)} %get-tuple-element.30), channel_id=1, source_target_pairs={{0,2},{1,3},{2,0},{3,1},{4,6},{5,7},{6,4},{7,5},{8,10},{9,11},{10,... | collective-permute-start | bytes 1572872 | tf_op jit(solution)/shard_map/ppermute | solution.py:24
  71.9 27.3 %collective-permute-start.15 = (bf16[6,128,256]{1,2,0:T(8,128)(2,1)}, bf16[6,128,256]{1,2,0:T(8,128)(2,1)S(1)}, u32[]{:S(2)}, u32[]{:S(2)}) collective-permute-start(bf16[6,128,256]{1,2,0:T(8,128)(2,1)} %copy.54), channel_id=1, source_target_pairs={{0,2},{1,3},{2,0},{3,1},{4,6},{5,7},{6,4},{7,5},{8,10},{9,11},{10,... | collective-permute-start | bytes 1179656 | tf_op jit(solution)/shard_map/ppermute | solution.py:24
  73.6 25.6 %copy-start.22 = (bf16[1,128,256]{1,2,0:T(8,128)(2,1)S(1)}, bf16[1,128,256]{1,2,0:T(8,128)(2,1)}, u32[]{:S(2)}) copy-start(bf16[1,128,256]{1,2,0:T(8,128)(2,1)} %slice_bitcast_fusion.11) | copy-start | bytes 196612
  73.6 25.6 %copy-start.23 = (bf16[1,128,256]{1,2,0:T(8,128)(2,1)S(1)}, bf16[1,128,256]{1,2,0:T(8,128)(2,1)}, u32[]{:S(2)}) copy-start(bf16[1,128,256]{1,2,0:T(8,128)(2,1)} %slice_bitcast_fusion.10) | copy-start | bytes 196612
  73.6 25.6 %copy-start.30 = (bf16[1,128,256]{1,2,0:T(8,128)(2,1)S(1)}, bf16[1,128,256]{1,2,0:T(8,128)(2,1)}, u32[]{:S(2)}) copy-start(bf16[1,128,256]{1,2,0:T(8,128)(2,1)} %get-tuple-element.67) | copy-start | bytes 196612
  74.7 26.0 %copy-start.27 = (bf16[128,256]{0,1:T(8,128)(2,1)S(1)}, bf16[128,256]{0,1:T(8,128)(2,1)}, u32[]{:S(2)}) copy-start(bf16[128,256]{0,1:T(8,128)(2,1)} %copy-done.26) | copy-start | bytes 196612
  74.8 26.6 %copy-start.25 = (bf16[128,256]{0,1:T(8,128)(2,1)S(1)}, bf16[128,256]{0,1:T(8,128)(2,1)}, u32[]{:S(2)}) copy-start(bf16[128,256]{0,1:T(8,128)(2,1)} %copy-done.24) | copy-start | bytes 196612
  100.1 10.5 %collective-permute-start.16 = (bf16[6,128,256]{1,2,0:T(8,128)(2,1)}, bf16[6,128,256]{1,2,0:T(8,128)(2,1)}, u32[]{:S(2)}, u32[]{:S(2)}) collective-permute-start(bf16[6,128,256]{1,2,0:T(8,128)(2,1)} %pad_maximum_fusion.2), channel_id=1, source_target_pairs={{0,1},{1,0},{2,3},{3,2},{4,5},{5,4},{6,7},{7,6},{8,9},{9,8},{10,11... | collective-permute-start | bytes 1179656 | tf_op jit(solution)/shard_map/ppermute | solution.py:24
  104.6 26.0 %collective-permute-start.13 = (bf16[128,2048]{1,0:T(8,128)(2,1)}, bf16[128,2048]{1,0:T(8,128)(2,1)}, u32[]{:S(2)}, u32[]{:S(2)}) collective-permute-start(bf16[128,2048]{1,0:T(8,128)(2,1)} %get-tuple-element.32), channel_id=1, source_target_pairs={{0,2},{1,3},{2,0},{3,1},{4,6},{5,7},{6,4},{7,5},{8,10},{9,11},{10,... | collective-permute-start | bytes 1572872 | tf_op jit(solution)/shard_map/ppermute | solution.py:24
  105.1 24.2 %collective-permute-start.14 = (bf16[128,2048]{1,0:T(8,128)(2,1)}, bf16[128,2048]{1,0:T(8,128)(2,1)S(1)}, u32[]{:S(2)}, u32[]{:S(2)}) collective-permute-start(bf16[128,2048]{1,0:T(8,128)(2,1)} %get-tuple-element.33), channel_id=1, source_target_pairs={{0,8},{4,12},{8,0},{12,4},{1,9},{5,13},{9,1},{13,5},{2,10},{6,14},... | collective-permute-start | bytes 1572872 | tf_op jit(solution)/shard_map/ppermute | solution.py:24
  106.2 34.5 %collective-permute-start.17 = (bf16[512,2048]{1,0:T(8,128)(2,1)S(1)}, bf16[512,2048]{1,0:T(8,128)(2,1)}, u32[]{:S(2)}, u32[]{:S(2)}) collective-permute-start(bf16[512,2048]{1,0:T(8,128)(2,1)S(1)} %constant_dynamic-update-slice_fusion.4.rest_0_), channel_id=1, source_target_pairs={{0,1},{1,0},{2,3},{3,2},{4,5},{5,4},{6,7},{7,6},{8,9},{9,8},{10,11... | collective-permute-start | bytes 6291464 | tf_op jit(solution)/shard_map/ppermute | solution.py:24
  108.4 32.3 %collective-permute-start.19 = (bf16[256,2048]{1,0:T(8,128)(2,1)}, bf16[256,2048]{1,0:T(8,128)(2,1)}, u32[]{:S(2)}, u32[]{:S(2)}) collective-permute-start(bf16[256,2048]{1,0:T(8,128)(2,1)} %constant_dynamic-update-slice_fusion.10.rest_4_), channel_id=1, source_target_pairs={{0,1},{1,0},{2,3},{3,2},{4,5},{5,4},{6,7},{7,6},{8,9},{9,8},{10,11... | collective-permute-start | bytes 3145736 | tf_op jit(solution)/shard_map/ppermute | solution.py:24
  132.6 8.1 %collective-permute-start.18 = (bf16[256,2048]{1,0:T(8,128)(2,1)}, bf16[256,2048]{1,0:T(8,128)(2,1)S(1)}, u32[]{:S(2)}, u32[]{:S(2)}) collective-permute-start(bf16[256,2048]{1,0:T(8,128)(2,1)} %constant_dynamic-update-slice_fusion.8.rest_2_), channel_id=1, source_target_pairs={{0,1},{1,0},{2,3},{3,2},{4,5},{5,4},{6,7},{7,6},{8,9},{9,8},{10,11... | collective-permute-start | bytes 3145736 | tf_op jit(solution)/shard_map/ppermute | solution.py:24
  158.0 15.0 %collective-permute-start.24 = (bf16[2,512,256]{2,1,0:T(8,128)(2,1)}, bf16[2,512,256]{2,1,0:T(8,128)(2,1)}, u32[]{:S(2)}, u32[]{:S(2)}) collective-permute-start(bf16[2,512,256]{2,1,0:T(8,128)(2,1)} %get-tuple-element.38), channel_id=1, source_target_pairs={{0,4},{4,0},{8,12},{12,8},{1,5},{5,1},{9,13},{13,9},{2,6},{6,2},{1... | collective-permute-start | bytes 1572872 | tf_op jit(solution)/shard_map/ppermute | solution.py:24
  164.5 25.3 %collective-permute-start.20 = (bf16[2,512,256]{2,1,0:T(8,128)(2,1)}, bf16[2,512,256]{2,1,0:T(8,128)(2,1)S(1)}, u32[]{:S(2)}, u32[]{:S(2)}) collective-permute-start(bf16[2,512,256]{2,1,0:T(8,128)(2,1)} %get-tuple-element.40), channel_id=1, source_target_pairs={{0,4},{4,0},{8,12},{12,8},{1,5},{5,1},{9,13},{13,9},{2,6},{6,2},{1... | collective-permute-start | bytes 1572872 | tf_op jit(solution)/shard_map/ppermute | solution.py:24
  166.6 46.6 %collective-permute-start.22 = (bf16[128,2048]{1,0:T(8,128)(2,1)}, bf16[128,2048]{1,0:T(8,128)(2,1)S(1)}, u32[]{:S(2)}, u32[]{:S(2)}) collective-permute-start(bf16[128,2048]{1,0:T(8,128)(2,1)} %get-tuple-element.41), channel_id=1, source_target_pairs={{0,4},{4,0},{8,12},{12,8},{1,5},{5,1},{9,13},{13,9},{2,6},{6,2},{1... | collective-permute-start | bytes 1572872 | tf_op jit(solution)/shard_map/ppermute | solution.py:24
  166.6 46.6 %collective-permute-start.23 = (bf16[128,2048]{1,0:T(8,128)(2,1)}, bf16[128,2048]{1,0:T(8,128)(2,1)S(1)}, u32[]{:S(2)}, u32[]{:S(2)}) collective-permute-start(bf16[128,2048]{1,0:T(8,128)(2,1)} %get-tuple-element.34), channel_id=1, source_target_pairs={{0,12},{4,8},{8,4},{12,0},{1,13},{5,9},{9,5},{13,1},{2,14},{6,10},... | collective-permute-start | bytes 1572872 | tf_op jit(solution)/shard_map/ppermute | solution.py:24
  174.8 45.3 %collective-permute-start.25 = (bf16[512,256]{1,0:T(8,128)(2,1)S(1)}, bf16[512,256]{1,0:T(8,128)(2,1)}, u32[]{:S(2)}, u32[]{:S(2)}) collective-permute-start(bf16[512,256]{1,0:T(8,128)(2,1)S(1)} %fusion.35), channel_id=1, source_target_pairs={{0,8},{4,12},{8,0},{12,4},{1,9},{5,13},{9,1},{13,5},{2,10},{6,14},... | collective-permute-start | bytes 786440 | tf_op jit(solution)/shard_map/ppermute | solution.py:24
  191.7 31.2 %collective-permute-start.21 = (bf16[512,256]{1,0:T(8,128)(2,1)}, bf16[512,256]{1,0:T(8,128)(2,1)}, u32[]{:S(2)}, u32[]{:S(2)}) collective-permute-start(bf16[512,256]{1,0:T(8,128)(2,1)} %fusion.34), channel_id=1, source_target_pairs={{0,8},{4,12},{8,0},{12,4},{1,9},{5,13},{9,1},{13,5},{2,10},{6,14},... | collective-permute-start | bytes 786440 | tf_op jit(solution)/shard_map/ppermute | solution.py:24
  221.3 8.0 %collective-permute-start.26 = (bf16[1,2,256,256]{3,2,1,0:T(8,128)(2,1)S(1)}, bf16[1,2,256,256]{3,2,1,0:T(8,128)(2,1)S(1)}, u32[]{:S(2)}, u32[]{:S(2)}) collective-permute-start(bf16[1,2,256,256]{3,2,1,0:T(8,128)(2,1)S(1)} %bitcast.154), channel_id=1, source_target_pairs={{0,16},{16,0},{1,17},{17,1},{2,18},{18,2},{3,19},{19,3},{4,20},{20... | collective-permute-start | bytes 786440 | tf_op jit(solution)/shard_map/ppermute | solution.py:47
  (26 other events, 115.5 us)

commit v4 on v3

--- a/solution.py
+++ b/solution.py
@@ -37,6 +37,8 @@
         in_specs=[hbm] * (len(values) + len(marks)),
         out_specs=[hbm] * len(values),
         input_output_aliases={i: i for i in range(len(values))},
+        compiler_params=pltpu.CompilerParams(vmem_limit_bytes=256 * 1024),
+        cost_estimate=light,
         name="after",
     )(*values, *marks)
     return list(tied)
@@ -110,7 +112,7 @@
 
 vmem = pl.BlockSpec(memory_space=pltpu.VMEM)
 anywhere = pl.BlockSpec(memory_space=pl.ANY)
-params = pltpu.CompilerParams(vmem_limit_bytes=28 * 1024 * 1024)
+params = pltpu.CompilerParams(vmem_limit_bytes=24 * 1024 * 1024)
 light = pl.CostEstimate(flops=1000, bytes_accessed=1000, transcendentals=0)
 
 

time: 232 us -> 216 us (0.931)
  local copies, waits for them, and re-layouts: 61.3 us -> 37.9 us
  waiting for transfers between devices: 102 us -> 115 us
  Pallas kernels: 16.3 us -> 13.4 us
    unnamed x87, local copies, waits for them, and re-layouts: 34.7 us -> 20.2 us
    ppermute x26, waiting for transfers between devices: 97.5 us -> 109 us  [swap(): return lax.ppermute(x, axis, [(i, i ^ bits) for i in range(peers)])]
    slice x11, local copies, waits for them, and re-layouts: 8.91 us -> 4.17 us  [mark(): return x[tuple((slice(0, 1) for _ in x.shape[:-2]))][..., :16, :128]]
  transfers between devices with their start and end apart: 27 -> 27, of which waited for: 9 -> 11; matrix products, arithmetic and copies ran while one was open for 31% -> 26% of each run, Pallas kernels for 2% -> 1%
where the time goes in v4:
time: 216 us; the launch traced here: 215 us
  waiting for transfers between devices  115 us (53%)
  local copies, waits for them, and re-layouts  37.9 us (18%)
  starting transfers between devices  26.3 us (12%)
  other arithmetic  16.9 us (8%)
  Pallas kernels  13.4 us (6%)
  matrix products  4.58 us (2%)
    ppermute x26, waiting for transfers between devices, swap(): return lax.ppermute(x, axis, [(i, i ^ bits) for i in range(peers)])  109 us
    ppermute x26, starting transfers between devices, swap(): return lax.ppermute(x, axis, [(i, i ^ bits) for i in range(peers)])  24.8 us
    unnamed x87, local copies, waits for them, and re-layouts  20.2 us
    pallas_call x1, Pallas kernels, shards(): pl.pallas_call(functools.partial(update_kernel, layout=layout, tile=min(o...  10.3 us
    ppermute x1, waiting for transfers between devices, from_behind(): return lax.ppermute(x, axis, [(i, (i + by) % peers) for i in range(peers)])  5.32 us
    dot_general x1, matrix products, dot(): lax.dot_general(a, b, (contract, ((), ())), preferred_element_type=f32)  4.58 us
  transfers between devices with their start and end apart: 27, of which 11 were waited for; matrix products, arithmetic and copies ran while one was open for 26% of the time, Pallas kernels for 1%

profile of v4, /device:TPU:0, one launch (start us, length us, event | category | flops | bytes accessed | tf_op | source)
XLA Modules:
  0.0 215.0 jit_solution(7173342436209288568)
XLA Ops:
  1.9 2.5 %collective-permute-start.2 = (bf16[128,256]{0,1:T(8,128)(2,1)S(1)}, bf16[128,256]{0,1:T(8,128)(2,1)S(1)}, u32[]{:S(2)}, u32[]{:S(2)}) collective-permute-start(bf16[128,256]{0,1:T(8,128)(2,1)S(1)} %copy.50), channel_id=1, source_target_pairs={{0,3},{1,2},{2,1},{3,0},{4,7},{5,6},{6,5},{7,4},{8,11},{9,10},{10,... | collective-permute-start | bytes 196616 | tf_op jit(solution)/shard_map/ppermute | solution.py:24
  5.4 1.7 bitcast_convert_fusion.weights_ref
  7.1 2.1 collective-permute-start.6
  9.8 1.9 fusion.5
  13.4 2.7 %collective-permute-start.3 = (bf16[128,1024]{0,1:T(8,128)(2,1)S(1)}, bf16[128,1024]{0,1:T(8,128)(2,1)S(1)}, u32[]{:S(2)}, u32[]{:S(2)}) collective-permute-start(bf16[128,1024]{0,1:T(8,128)(2,1)S(1)} %get-tuple-element.70), channel_id=1, source_target_pairs={{0,8},{4,12},{8,0},{12,4},{1,9},{5,13},{9,1},{13,5},{2,10},{6,14},... | collective-permute-start | bytes 786440 | tf_op jit(solution)/shard_map/ppermute | solution.py:24
  16.1 2.9 %constant_dynamic-slice_fusion = (bf16[2,64,2048]{2,1,0:T(8,128)(2,1)}, bf16[2,64,2048]{2,1,0:T(8,128)(2,1)}, bf16[2,64,2048]{2,1,0:T(8,128)(2,1)}, bf16[2,64,2048]{2,1,0:T(8,128)(2,1)}) fusion(bf16[2,64,8192]{2,1,0:T(8,128)(2,1)} %fusion.5, s32[]{:T(128)S(6)} %select_n.317, s32[]{:T(128)S(6)} %select_n.316, s32[]{:T(128)S(6)} %select_n.311, s32[]{:T(128)S(6)} %select_n.310), kind=kLoop, calls=%fused_computation.120 | loop fusion | bytes 4194320 | tf_op jit(solution)/shard_map/dynamic_slice | solution.py:131
  19.0 8.7 %collective-permute-done.3 = bf16[128,1024]{0,1:T(8,128)(2,1)S(1)} collective-permute-done((bf16[128,1024]{0,1:T(8,128)(2,1)S(1)}, bf16[128,1024]{0,1:T(8,128)(2,1)S(1)}, u32[]{:S(2)}, u32[]{:S(2)}) %collective-permute-start.3) | collective-permute-done | bytes 262176 | tf_op jit(solution)/shard_map/ppermute | solution.py:24
  30.0 1.4 collective-permute-start.4
  31.3 3.5 %collective-permute-start.5 = (bf16[128,2048]{1,0:T(8,128)(2,1)}, bf16[128,2048]{1,0:T(8,128)(2,1)}, u32[]{:S(2)}, u32[]{:S(2)}) collective-permute-start(bf16[128,2048]{1,0:T(8,128)(2,1)} %get-tuple-element.26), channel_id=1, source_target_pairs={{0,12},{4,8},{8,4},{12,0},{1,13},{5,9},{9,5},{13,1},{2,14},{6,10},... | collective-permute-start | bytes 1572872 | tf_op jit(solution)/shard_map/ppermute | solution.py:24
  36.2 2.7 %pad_maximum_fusion = bf16[2048,512]{1,0:T(8,128)(2,1)} fusion(bf16[2048,256]{1,0:T(8,128)(2,1)} %get-tuple-element.28, bf16[2048,256]{1,0:T(8,128)(2,1)S(1)} %bitcast_convert_fusion.weights_ref), kind=kLoop, calls=%fused_computation.19 | loop fusion | flops 4194304 | bytes 4194304 | tf_op jit(solution)/shard_map/concatenate | solution.py:150
  38.9 4.9 %collective-permute-done.8 = bf16[2,128,1024]{1,2,0:T(8,128)(2,1)} collective-permute-done((bf16[2,128,1024]{1,2,0:T(8,128)(2,1)}, bf16[2,128,1024]{1,2,0:T(8,128)(2,1)}, u32[]{:S(2)}, u32[]{:S(2)}) %collective-permute-start.8) | collective-permute-done | bytes 524320 | tf_op jit(solution)/shard_map/ppermute | solution.py:24
  48.0 4.6 %fusion.16 = bf16[512,2048]{1,0:T(8,128)(2,1)S(1)} fusion(bf16[2048,512]{1,0:T(8,128)(2,1)} %collective-permute-done.9, bf16[2048,256]{1,0:T(8,128)(2,1)} %get-tuple-element.28, bf16[2048,256]{1,0:T(8,128)(2,1)S(1)} %bitcast_convert_fusion.weights_ref, bf16[128,1024]{0,1:T(8,128)(2,1)} %copy-done.14, bf16[128,1024]{0,1:T(8,128)(2,1)} %copy-done.13, ...), kind=kOutput, calls=%fused_computation.18 | convolution fusion | flops 2168455168 | bytes 7340032 | tf_op jit(solution)/shard_map/dot_general | solution.py:53
  53.1 13.9 %collective-permute-done.5.refs_1_ = bf16[128,2048]{1,0:T(8,128)(2,1)} collective-permute-done((bf16[128,2048]{1,0:T(8,128)(2,1)}, bf16[128,2048]{1,0:T(8,128)(2,1)}, u32[]{:S(2)}, u32[]{:S(2)}) %collective-permute-start.5) | collective-permute-done | bytes 524320 | tf_op jit(solution)/shard_map/ppermute | solution.py:24
  68.2 1.9 constant_dynamic-update-slice_fusion.11
  70.2 1.5 collective-permute-start.11
  76.8 24.2 %collective-permute-done.15 = bf16[6,128,256]{1,2,0:T(8,128)(2,1)S(1)} collective-permute-done((bf16[6,128,256]{1,2,0:T(8,128)(2,1)}, bf16[6,128,256]{1,2,0:T(8,128)(2,1)S(1)}, u32[]{:S(2)}, u32[]{:S(2)}) %collective-permute-start.15) | collective-permute-done | bytes 393248 | tf_op jit(solution)/shard_map/ppermute | solution.py:24
  104.9 1.2 constant_dynamic-update-slice_fusion.4.rest_0_
  110.5 1.5 slice_dynamic-update-slice_fusion.1
  113.2 15.7 %collective-permute-done.14 = bf16[128,2048]{1,0:T(8,128)(2,1)S(1)} collective-permute-done((bf16[128,2048]{1,0:T(8,128)(2,1)S(1)}, bf16[128,2048]{1,0:T(8,128)(2,1)S(1)}, u32[]{:S(2)}, u32[]{:S(2)}) %collective-permute-start.14) | collective-permute-done | bytes 524320 | tf_op jit(solution)/shard_map/ppermute | solution.py:24
  129.7 1.5 slice_dynamic-update-slice_fusion
  133.9 10.3 %update.1 = (f32[2048,256]{1,0:T(8,128)}, bf16[2,512,256]{2,1,0:T(8,128)(2,1)S(1)}, bf16[2,512,256]{2,1,0:T(8,128)(2,1)}) custom-call(bf16[16,128]{1,0:T(8,128)(2,1)S(1)} %slice.208.mark_ref, bf16[256,2048]{1,0:T(8,128)(2,1)} %bitcast.34.cot_ref, f32[2048,256]{1,0:T(8,128)S(1)} %bitcast.135, f32[2048,256]{1,0:T(8,128)S(1)} %bitcast.136, ...), custom_call_target="tpu_custom_call" | custom-call | flops 1000 | bytes 1000 | tf_op jit(solution)/shard_map/update/pallas_call | solution.py:201
  144.9 3.1 %project.1 = (bf16[2,512,256]{2,1,0:T(8,128)(2,1)S(1)}, bf16[2,512,256]{2,1,0:T(8,128)(2,1)}) custom-call(bf16[1,16,128]{2,1,0:T(8,128)(2,1)S(1)} %slice.225.mark_ref, bf16[2048,256]{1,0:T(8,128)(2,1)S(1)} %bitcast_convert_fusion.weights_ref, bf16[512,2048]{1,0:T(8,128)(2,1)S(1)} %constant_dynamic-update-slice_fusion.4.rest_0_, ...), custom_call_target="tpu_custom_call" | custom-call | flops 1000 | bytes 1000 | tf_op jit(solution)/shard_map/project/pallas_call | solution.py:214
  148.8 2.0 collective-permute-start.20
  150.8 2.6 %collective-permute-start.23 = (bf16[128,2048]{1,0:T(8,128)(2,1)}, bf16[128,2048]{1,0:T(8,128)(2,1)S(1)}, u32[]{:S(2)}, u32[]{:S(2)}) collective-permute-start(bf16[128,2048]{1,0:T(8,128)(2,1)} %get-tuple-element.34), channel_id=1, source_target_pairs={{0,12},{4,8},{8,4},{12,0},{1,13},{5,9},{9,5},{13,1},{2,14},{6,10},... | collective-permute-start | bytes 1572872 | tf_op jit(solution)/shard_map/ppermute | solution.py:24
  154.2 5.0 %collective-permute-done.24 = bf16[2,512,256]{2,1,0:T(8,128)(2,1)} collective-permute-done((bf16[2,512,256]{2,1,0:T(8,128)(2,1)}, bf16[2,512,256]{2,1,0:T(8,128)(2,1)}, u32[]{:S(2)}, u32[]{:S(2)}) %collective-permute-start.24) | collective-permute-done | bytes 524320 | tf_op jit(solution)/shard_map/ppermute | solution.py:24
  160.3 1.3 collective-permute-start.25
  161.6 14.3 %collective-permute-done.20 = bf16[2,512,256]{2,1,0:T(8,128)(2,1)S(1)} collective-permute-done((bf16[2,512,256]{2,1,0:T(8,128)(2,1)}, bf16[2,512,256]{2,1,0:T(8,128)(2,1)S(1)}, u32[]{:S(2)}, u32[]{:S(2)}) %collective-permute-start.20) | collective-permute-done | bytes 524320 | tf_op jit(solution)/shard_map/ppermute | solution.py:24
  178.0 22.1 %collective-permute-done.22.refs_0_ = bf16[128,2048]{1,0:T(8,128)(2,1)S(1)} collective-permute-done((bf16[128,2048]{1,0:T(8,128)(2,1)}, bf16[128,2048]{1,0:T(8,128)(2,1)S(1)}, u32[]{:S(2)}, u32[]{:S(2)}) %collective-permute-start.22) | collective-permute-done | bytes 524320 | tf_op jit(solution)/shard_map/ppermute | solution.py:24
  200.1 1.5 broadcast_select_fusion.7
  203.0 2.1 fusion.9
  206.3 1.5 collective-permute-start.26
  208.9 5.3 %collective-permute-done.26 = bf16[1,2,256,256]{3,2,1,0:T(8,128)(2,1)S(1)} collective-permute-done((bf16[1,2,256,256]{3,2,1,0:T(8,128)(2,1)S(1)}, bf16[1,2,256,256]{3,2,1,0:T(8,128)(2,1)S(1)}, u32[]{:S(2)}, u32[]{:S(2)}) %collective-permute-start.26) | collective-permute-done | bytes 262176 | tf_op jit(solution)/shard_map/ppermute | solution.py:49
  (170 shorter events, 41.7 us)
Async XLA Ops:
  1.9 10.6 %collective-permute-start.2 = (bf16[128,256]{0,1:T(8,128)(2,1)S(1)}, bf16[128,256]{0,1:T(8,128)(2,1)S(1)}, u32[]{:S(2)}, u32[]{:S(2)}) collective-permute-start(bf16[128,256]{0,1:T(8,128)(2,1)S(1)} %copy.50), channel_id=1, source_target_pairs={{0,3},{1,2},{2,1},{3,0},{4,7},{5,6},{6,5},{7,4},{8,11},{9,10},{10,... | collective-permute-start | bytes 196616 | tf_op jit(solution)/shard_map/ppermute | solution.py:24
  4.5 8.0 %collective-permute-start.1 = (bf16[128,256]{0,1:T(8,128)(2,1)S(1)}, bf16[128,256]{0,1:T(8,128)(2,1)S(1)}, u32[]{:S(2)}, u32[]{:S(2)}) collective-permute-start(bf16[128,256]{0,1:T(8,128)(2,1)S(1)} %copy.49), channel_id=1, source_target_pairs={{0,1},{1,0},{2,3},{3,2},{4,5},{5,4},{6,7},{7,6},{8,9},{9,8},{10,11... | collective-permute-start | bytes 196616 | tf_op jit(solution)/shard_map/ppermute | solution.py:24
  5.4 7.1 %collective-permute-start = (bf16[128,256]{0,1:T(8,128)(2,1)S(1)}, bf16[128,256]{0,1:T(8,128)(2,1)}, u32[]{:S(2)}, u32[]{:S(2)}) collective-permute-start(bf16[128,256]{0,1:T(8,128)(2,1)S(1)} %copy.48), channel_id=1, source_target_pairs={{0,2},{1,3},{2,0},{3,1},{4,6},{5,7},{6,4},{7,5},{8,10},{9,11},{10,... | collective-permute-start | bytes 196616 | tf_op jit(solution)/shard_map/ppermute | solution.py:24
  7.1 28.3 %collective-permute-start.6 = (bf16[2048,256]{1,0:T(8,128)(2,1)S(1)}, bf16[2048,256]{1,0:T(8,128)(2,1)}, u32[]{:S(2)}, u32[]{:S(2)}) collective-permute-start(bf16[2048,256]{1,0:T(8,128)(2,1)S(1)} %bitcast_convert_fusion.weights_ref), channel_id=1, source_target_pairs={{0,2},{1,3},{2,0},{3,1},{4,6},{5,7},{6,4},{7,5},{8,10},{9,11},{10,... | collective-permute-start | bytes 3145736 | tf_op jit(solution)/shard_map/ppermute | solution.py:24
  13.4 14.2 %collective-permute-start.3 = (bf16[128,1024]{0,1:T(8,128)(2,1)S(1)}, bf16[128,1024]{0,1:T(8,128)(2,1)S(1)}, u32[]{:S(2)}, u32[]{:S(2)}) collective-permute-start(bf16[128,1024]{0,1:T(8,128)(2,1)S(1)} %get-tuple-element.70), channel_id=1, source_target_pairs={{0,8},{4,12},{8,0},{12,4},{1,9},{5,13},{9,1},{13,5},{2,10},{6,14},... | collective-permute-start | bytes 786440 | tf_op jit(solution)/shard_map/ppermute | solution.py:24
  28.6 15.2 %collective-permute-start.8 = (bf16[2,128,1024]{1,2,0:T(8,128)(2,1)}, bf16[2,128,1024]{1,2,0:T(8,128)(2,1)}, u32[]{:S(2)}, u32[]{:S(2)}) collective-permute-start(bf16[2,128,1024]{1,2,0:T(8,128)(2,1)} %pad_maximum_fusion.1), channel_id=1, source_target_pairs={{0,4},{4,0},{8,12},{12,8},{1,5},{5,1},{9,13},{13,9},{2,6},{6,2},{1... | collective-permute-start | bytes 1572872 | tf_op jit(solution)/shard_map/ppermute | solution.py:24
  30.0 23.1 %collective-permute-start.4 = (bf16[128,2048]{1,0:T(8,128)(2,1)}, bf16[128,2048]{1,0:T(8,128)(2,1)}, u32[]{:S(2)}, u32[]{:S(2)}) collective-permute-start(bf16[128,2048]{1,0:T(8,128)(2,1)} %get-tuple-element.25), channel_id=1, source_target_pairs={{0,4},{4,0},{8,12},{12,8},{1,5},{5,1},{9,13},{13,9},{2,6},{6,2},{1... | collective-permute-start | bytes 1572872 | tf_op jit(solution)/shard_map/ppermute | solution.py:24
  31.3 35.6 %collective-permute-start.5 = (bf16[128,2048]{1,0:T(8,128)(2,1)}, bf16[128,2048]{1,0:T(8,128)(2,1)}, u32[]{:S(2)}, u32[]{:S(2)}) collective-permute-start(bf16[128,2048]{1,0:T(8,128)(2,1)} %get-tuple-element.26), channel_id=1, source_target_pairs={{0,12},{4,8},{8,4},{12,0},{1,13},{5,9},{9,5},{13,1},{2,14},{6,10},... | collective-permute-start | bytes 1572872 | tf_op jit(solution)/shard_map/ppermute | solution.py:24
  38.8 9.2 %collective-permute-start.9 = (bf16[2048,512]{1,0:T(8,128)(2,1)}, bf16[2048,512]{1,0:T(8,128)(2,1)}, u32[]{:S(2)}, u32[]{:S(2)}) collective-permute-start(bf16[2048,512]{1,0:T(8,128)(2,1)} %pad_maximum_fusion), channel_id=1, source_target_pairs={{0,1},{1,0},{2,3},{3,2},{4,5},{5,4},{6,7},{7,6},{8,9},{9,8},{10,11... | collective-permute-start | bytes 6291464 | tf_op jit(solution)/shard_map/ppermute | solution.py:24
  46.4 20.5 %collective-permute-start.7 = (bf16[128,2048]{1,0:T(8,128)(2,1)}, bf16[128,2048]{1,0:T(8,128)(2,1)S(1)}, u32[]{:S(2)}, u32[]{:S(2)}) collective-permute-start(bf16[128,2048]{1,0:T(8,128)(2,1)} %get-tuple-element.27), channel_id=1, source_target_pairs={{0,2},{1,3},{2,0},{3,1},{4,6},{5,7},{6,4},{7,5},{8,10},{9,11},{10,... | collective-permute-start | bytes 1572872 | tf_op jit(solution)/shard_map/ppermute | solution.py:24
  67.7 36.0 %collective-permute-start.12 = (bf16[128,2048]{1,0:T(8,128)(2,1)}, bf16[128,2048]{1,0:T(8,128)(2,1)}, u32[]{:S(2)}, u32[]{:S(2)}) collective-permute-start(bf16[128,2048]{1,0:T(8,128)(2,1)} %get-tuple-element.31), channel_id=1, source_target_pairs={{0,2},{1,3},{2,0},{3,1},{4,6},{5,7},{6,4},{7,5},{8,10},{9,11},{10,... | collective-permute-start | bytes 1572872 | tf_op jit(solution)/shard_map/ppermute | solution.py:24
  70.2 34.3 %collective-permute-start.10 = (bf16[128,2048]{1,0:T(8,128)(2,1)}, bf16[128,2048]{1,0:T(8,128)(2,1)}, u32[]{:S(2)}, u32[]{:S(2)}) collective-permute-start(bf16[128,2048]{1,0:T(8,128)(2,1)} %get-tuple-element.29), channel_id=1, source_target_pairs={{0,8},{4,12},{8,0},{12,4},{1,9},{5,13},{9,1},{13,5},{2,10},{6,14},... | collective-permute-start | bytes 1572872 | tf_op jit(solution)/shard_map/ppermute | solution.py:24
  70.2 32.9 %collective-permute-start.11 = (bf16[128,2048]{1,0:T(8,128)(2,1)}, bf16[128,2048]{1,0:T(8,128)(2,1)}, u32[]{:S(2)}, u32[]{:S(2)}) collective-permute-start(bf16[128,2048]{1,0:T(8,128)(2,1)} %get-tuple-element.30), channel_id=1, source_target_pairs={{0,2},{1,3},{2,0},{3,1},{4,6},{5,7},{6,4},{7,5},{8,10},{9,11},{10,... | collective-permute-start | bytes 1572872 | tf_op jit(solution)/shard_map/ppermute | solution.py:24
  72.6 28.3 %collective-permute-start.15 = (bf16[6,128,256]{1,2,0:T(8,128)(2,1)}, bf16[6,128,256]{1,2,0:T(8,128)(2,1)S(1)}, u32[]{:S(2)}, u32[]{:S(2)}) collective-permute-start(bf16[6,128,256]{1,2,0:T(8,128)(2,1)} %copy.54), channel_id=1, source_target_pairs={{0,2},{1,3},{2,0},{3,1},{4,6},{5,7},{6,4},{7,5},{8,10},{9,11},{10,... | collective-permute-start | bytes 1179656 | tf_op jit(solution)/shard_map/ppermute | solution.py:24
  74.4 26.6 %copy-start.22 = (bf16[1,128,256]{1,2,0:T(8,128)(2,1)S(1)}, bf16[1,128,256]{1,2,0:T(8,128)(2,1)}, u32[]{:S(2)}) copy-start(bf16[1,128,256]{1,2,0:T(8,128)(2,1)} %slice_bitcast_fusion.11) | copy-start | bytes 196612
  74.4 26.6 %copy-start.23 = (bf16[1,128,256]{1,2,0:T(8,128)(2,1)S(1)}, bf16[1,128,256]{1,2,0:T(8,128)(2,1)}, u32[]{:S(2)}) copy-start(bf16[1,128,256]{1,2,0:T(8,128)(2,1)} %slice_bitcast_fusion.10) | copy-start | bytes 196612
  75.5 26.9 %copy-start.25 = (bf16[128,256]{0,1:T(8,128)(2,1)S(1)}, bf16[128,256]{0,1:T(8,128)(2,1)}, u32[]{:S(2)}) copy-start(bf16[128,256]{0,1:T(8,128)(2,1)} %copy-done.24) | copy-start | bytes 196612
  76.8 29.7 %copy-start.1 = (bf16[256,2048]{1,0:T(8,128)(2,1)S(1)}, bf16[256,2048]{1,0:T(8,128)(2,1)}, u32[]{:S(2)}) copy-start(bf16[256,2048]{1,0:T(8,128)(2,1)} %constant_dynamic-update-slice_fusion.11) | copy-start | bytes 3145732
  101.0 8.1 %collective-permute-start.16 = (bf16[6,128,256]{1,2,0:T(8,128)(2,1)S(1)}, bf16[6,128,256]{1,2,0:T(8,128)(2,1)S(1)}, u32[]{:S(2)}, u32[]{:S(2)}) collective-permute-start(bf16[6,128,256]{1,2,0:T(8,128)(2,1)S(1)} %pad_maximum_fusion.2), channel_id=1, source_target_pairs={{0,1},{1,0},{2,3},{3,2},{4,5},{5,4},{6,7},{7,6},{8,9},{9,8},{10,11... | collective-permute-start | bytes 1179656 | tf_op jit(solution)/shard_map/ppermute | solution.py:24
  104.4 24.5 %collective-permute-start.13 = (bf16[128,2048]{1,0:T(8,128)(2,1)}, bf16[128,2048]{1,0:T(8,128)(2,1)S(1)}, u32[]{:S(2)}, u32[]{:S(2)}) collective-permute-start(bf16[128,2048]{1,0:T(8,128)(2,1)} %get-tuple-element.32), channel_id=1, source_target_pairs={{0,2},{1,3},{2,0},{3,1},{4,6},{5,7},{6,4},{7,5},{8,10},{9,11},{10,... | collective-permute-start | bytes 1572872 | tf_op jit(solution)/shard_map/ppermute | solution.py:24
  104.9 23.9 %collective-permute-start.14 = (bf16[128,2048]{1,0:T(8,128)(2,1)S(1)}, bf16[128,2048]{1,0:T(8,128)(2,1)S(1)}, u32[]{:S(2)}, u32[]{:S(2)}) collective-permute-start(bf16[128,2048]{1,0:T(8,128)(2,1)S(1)} %get-tuple-element.33), channel_id=1, source_target_pairs={{0,8},{4,12},{8,0},{12,4},{1,9},{5,13},{9,1},{13,5},{2,10},{6,14},... | collective-permute-start | bytes 1572872 | tf_op jit(solution)/shard_map/ppermute | solution.py:24
  104.9 28.9 %copy-start.3 = (f32[1,2048,256]{2,1,0:T(8,128)S(1)}, f32[1,2048,256]{2,1,0:T(8,128)}, u32[]{:S(2)}) copy-start(f32[1,2048,256]{2,1,0:T(8,128)} %param.11) | copy-start | bytes 6291460
  106.2 27.6 %collective-permute-start.17 = (bf16[512,2048]{1,0:T(8,128)(2,1)S(1)}, bf16[512,2048]{1,0:T(8,128)(2,1)S(1)}, u32[]{:S(2)}, u32[]{:S(2)}) collective-permute-start(bf16[512,2048]{1,0:T(8,128)(2,1)S(1)} %constant_dynamic-update-slice_fusion.4.rest_0_), channel_id=1, source_target_pairs={{0,1},{1,0},{2,3},{3,2},{4,5},{5,4},{6,7},{7,6},{8,9},{9,8},{10,11... | collective-permute-start | bytes 6291464 | tf_op jit(solution)/shard_map/ppermute | solution.py:24
  107.5 26.3 %collective-permute-start.19 = (bf16[256,2048]{1,0:T(8,128)(2,1)S(1)}, bf16[256,2048]{1,0:T(8,128)(2,1)S(1)}, u32[]{:S(2)}, u32[]{:S(2)}) collective-permute-start(bf16[256,2048]{1,0:T(8,128)(2,1)S(1)} %constant_dynamic-update-slice_fusion.10.rest_4_), channel_id=1, source_target_pairs={{0,1},{1,0},{2,3},{3,2},{4,5},{5,4},{6,7},{7,6},{8,9},{9,8},{10,11... | collective-permute-start | bytes 3145736 | tf_op jit(solution)/shard_map/ppermute | solution.py:24
  128.9 4.9 %collective-permute-start.18 = (bf16[256,2048]{1,0:T(8,128)(2,1)S(1)}, bf16[256,2048]{1,0:T(8,128)(2,1)S(1)}, u32[]{:S(2)}, u32[]{:S(2)}) collective-permute-start(bf16[256,2048]{1,0:T(8,128)(2,1)S(1)} %constant_dynamic-update-slice_fusion.8.rest_2_), channel_id=1, source_target_pairs={{0,1},{1,0},{2,3},{3,2},{4,5},{5,4},{6,7},{7,6},{8,9},{9,8},{10,11... | collective-permute-start | bytes 3145736 | tf_op jit(solution)/shard_map/ppermute | solution.py:24
  144.1 15.0 %collective-permute-start.24 = (bf16[2,512,256]{2,1,0:T(8,128)(2,1)}, bf16[2,512,256]{2,1,0:T(8,128)(2,1)}, u32[]{:S(2)}, u32[]{:S(2)}) collective-permute-start(bf16[2,512,256]{2,1,0:T(8,128)(2,1)} %get-tuple-element.38), channel_id=1, source_target_pairs={{0,4},{4,0},{8,12},{12,8},{1,5},{5,1},{9,13},{13,9},{2,6},{6,2},{1... | collective-permute-start | bytes 1572872 | tf_op jit(solution)/shard_map/ppermute | solution.py:24
  148.8 27.1 %collective-permute-start.20 = (bf16[2,512,256]{2,1,0:T(8,128)(2,1)}, bf16[2,512,256]{2,1,0:T(8,128)(2,1)S(1)}, u32[]{:S(2)}, u32[]{:S(2)}) collective-permute-start(bf16[2,512,256]{2,1,0:T(8,128)(2,1)} %get-tuple-element.40), channel_id=1, source_target_pairs={{0,4},{4,0},{8,12},{12,8},{1,5},{5,1},{9,13},{13,9},{2,6},{6,2},{1... | collective-permute-start | bytes 1572872 | tf_op jit(solution)/shard_map/ppermute | solution.py:24
  150.8 49.3 %collective-permute-start.22 = (bf16[128,2048]{1,0:T(8,128)(2,1)}, bf16[128,2048]{1,0:T(8,128)(2,1)S(1)}, u32[]{:S(2)}, u32[]{:S(2)}) collective-permute-start(bf16[128,2048]{1,0:T(8,128)(2,1)} %get-tuple-element.41), channel_id=1, source_target_pairs={{0,4},{4,0},{8,12},{12,8},{1,5},{5,1},{9,13},{13,9},{2,6},{6,2},{1... | collective-permute-start | bytes 1572872 | tf_op jit(solution)/shard_map/ppermute | solution.py:24
  150.8 49.3 %collective-permute-start.23 = (bf16[128,2048]{1,0:T(8,128)(2,1)}, bf16[128,2048]{1,0:T(8,128)(2,1)S(1)}, u32[]{:S(2)}, u32[]{:S(2)}) collective-permute-start(bf16[128,2048]{1,0:T(8,128)(2,1)} %get-tuple-element.34), channel_id=1, source_target_pairs={{0,12},{4,8},{8,4},{12,0},{1,13},{5,9},{9,5},{13,1},{2,14},{6,10},... | collective-permute-start | bytes 1572872 | tf_op jit(solution)/shard_map/ppermute | solution.py:24
  160.3 44.8 %collective-permute-start.25 = (bf16[512,256]{1,0:T(8,128)(2,1)S(1)}, bf16[512,256]{1,0:T(8,128)(2,1)S(1)}, u32[]{:S(2)}, u32[]{:S(2)}) collective-permute-start(bf16[512,256]{1,0:T(8,128)(2,1)S(1)} %fusion.35), channel_id=1, source_target_pairs={{0,8},{4,12},{8,0},{12,4},{1,9},{5,13},{9,1},{13,5},{2,10},{6,14},... | collective-permute-start | bytes 786440 | tf_op jit(solution)/shard_map/ppermute | solution.py:24
  177.1 30.9 %collective-permute-start.21 = (bf16[512,256]{1,0:T(8,128)(2,1)S(1)}, bf16[512,256]{1,0:T(8,128)(2,1)S(1)}, u32[]{:S(2)}, u32[]{:S(2)}) collective-permute-start(bf16[512,256]{1,0:T(8,128)(2,1)S(1)} %fusion.34), channel_id=1, source_target_pairs={{0,8},{4,12},{8,0},{12,4},{1,9},{5,13},{9,1},{13,5},{2,10},{6,14},... | collective-permute-start | bytes 786440 | tf_op jit(solution)/shard_map/ppermute | solution.py:24
  206.3 7.9 %collective-permute-start.26 = (bf16[1,2,256,256]{3,2,1,0:T(8,128)(2,1)S(1)}, bf16[1,2,256,256]{3,2,1,0:T(8,128)(2,1)S(1)}, u32[]{:S(2)}, u32[]{:S(2)}) collective-permute-start(bf16[1,2,256,256]{3,2,1,0:T(8,128)(2,1)S(1)} %bitcast.151), channel_id=1, source_target_pairs={{0,16},{16,0},{1,17},{17,1},{2,18},{18,2},{3,19},{19,3},{4,20},{20... | collective-permute-start | bytes 786440 | tf_op jit(solution)/shard_map/ppermute | solution.py:49
  (26 other events, 233.9 us)

commit v5 on v1

v5 whole, which is shorter than its diff:
```python
import functools

import jax
import jax.numpy as jnp
from jax import lax
from jax.experimental import pallas as pl
from jax.experimental.pallas import tpu as pltpu
from jax.sharding import PartitionSpec as P

beta_first = 0.9
beta_second = 0.95
learn_rate = 0.03
weight_decay = 0.1
adam_eps = 1e-08
norm_eps = 1e-05
step_count = 20.0

f32 = jnp.float32
bf16 = jnp.bfloat16

vmem = pl.BlockSpec(memory_space=pltpu.VMEM)
smem = pl.BlockSpec(memory_space=pltpu.SMEM)
anywhere = pl.BlockSpec(memory_space=pl.ANY)
light = pl.CostEstimate(flops=1000, bytes_accessed=1000, transcendentals=0)


def swap(x, axis, bits):
    peers = lax.axis_size(axis)
    return lax.ppermute(x, axis, [(i, i ^ bits) for i in range(peers)])


def from_behind(x, axis, by):
    peers = lax.axis_size(axis)
    return lax.ppermute(x, axis, [(i, (i + by) % peers) for i in range(peers)])


def dot(a, b, contract):
    return lax.dot_general(a, b, (contract, ((), ())), preferred_element_type=f32)


def like(*shape, dtype=bf16):
    return jax.ShapeDtypeStruct(shape, dtype)


def call(body, out_shape, in_specs, out_specs, mib, name, scratch=(), **more):
    return pl.pallas_call(
        body,
        out_shape=out_shape,
        in_specs=in_specs,
        out_specs=out_specs,
        scratch_shapes=list(scratch),
        compiler_params=pltpu.CompilerParams(vmem_limit_bytes=int(mib * 1024 * 1024)),
        cost_estimate=light,
        name=name,
        **more,
    )


def after(values, *earlier):
    tied = call(
        lambda *refs: None,
        [like(*x.shape, dtype=x.dtype) for x in values],
        [anywhere] * (len(values) + len(earlier)),
        [anywhere] * len(values),
        0.25,
        "after",
        input_output_aliases={i: i for i in range(len(values))},
    )(*values, *earlier)
    return list(tied)


def lanes(index, size):
    return pl.ds(pl.multiple_of(index * size, size), size)


def norm_kernel(where_ref, hidden_ref, gain_ref, *own_refs, tile):
    z = where_ref[0]
    rows, width = hidden_ref.shape
    depth = width // len(own_refs)

    @pl.loop(0, rows // tile)
    def _(i):
        at = pl.ds(pl.multiple_of(i * tile, tile), tile)
        total = jnp.zeros((tile, 1), f32)
        for k in range(len(own_refs)):
            part = hidden_ref[at, k * depth : (k + 1) * depth].astype(f32)
            total += jnp.sum(part * part, axis=-1, keepdims=True)
        scaling = lax.rsqrt(total * (1.0 / width) + norm_eps)
        for k, own_ref in enumerate(own_refs):
            cut = lanes(z ^ k, depth)
            own_ref[at, :] = (
                hidden_ref[at, cut].astype(f32) * scaling * gain_ref[:, cut]
            ).astype(bf16)


def grad_kernel(where_ref, hidden_ref, gain_ref, *rest, tile):
    d_refs, out_ref = rest[:-1], rest[-1]
    z = where_ref[0]
    rows, width = hidden_ref.shape
    depth = width // len(d_refs)

    @pl.loop(0, rows // tile)
    def _(i):
        at = pl.ds(pl.multiple_of(i * tile, tile), tile)
        squares = jnp.zeros((tile, 1), f32)
        cross = jnp.zeros((tile, 1), f32)
        for k, d_ref in enumerate(d_refs):
            cut = lanes(z ^ k, depth)
            hidden = hidden_ref[at, cut].astype(f32)
            squares += jnp.sum(hidden * hidden, axis=-1, keepdims=True)
            upper = d_ref[at, :].astype(f32) * gain_ref[:, cut]
            cross += jnp.sum(upper * hidden, axis=-1, keepdims=True)
        scaling = lax.rsqrt(squares * (1.0 / width) + norm_eps)
        factor = scaling * scaling * scaling * (cross * (1.0 / width))
        for k, d_ref in enumerate(d_refs):
            cut = lanes(z ^ k, depth)
            upper = d_ref[at, :].astype(f32) * gain_ref[:, cut]
            hidden = hidden_ref[at, cut].astype(f32)
            out_ref[at, cut] = (scaling * upper - hidden * factor).astype(bf16)


def arrange_kernel(where_ref, *refs, dp, layout):
    cots, (zero_ref, one_ref, far_ref, turned_ref) = refs[:dp], refs[dp:]
    t = where_ref[1]
    micro, rows, cols = cots[0].shape
    rows //= 4
    piece = micro * rows

    def block(k, j):
        at = pl.ds(pl.multiple_of((t ^ j) * rows, rows), rows)
        return jnp.concatenate([cots[k][m, at, :] for m in range(micro)])

    for k in range(dp):
        zero_ref[k * piece : (k + 1) * piece, :] = block(k, 0)
        one_ref[k * piece : (k + 1) * piece, :] = block(k, 1)
        far_ref[0, k * piece : (k + 1) * piece, :] = block(k, 2)
        far_ref[1, k * piece : (k + 1) * piece, :] = block(k, 3)
    for p, (k, j) in enumerate(layout):
        turned_ref[:, p * piece : (p + 1) * piece] = block(k, j).astype(f32).T.astype(bf16)


def d_kernel(c0_ref, c1_ref, c2_ref, c3_ref, w0_ref, w1_ref, w2_ref, w3_ref, *d_refs):
    rows = d_refs[0].shape[0]
    depth = d_refs[0].shape[1]
    tile = min(depth, 512)
    for k, d_ref in enumerate(d_refs):
        at = slice(k * rows, (k + 1) * rows)
        cot = jnp.concatenate(
            [c0_ref[at, :], c1_ref[at, :], c2_ref[0, at, :], c3_ref[at, :]], axis=1
        )
        for i in range(depth // tile):
            cut = slice(i * tile, (i + 1) * tile)
            whole = jnp.concatenate([w[cut, :] for w in (w0_ref, w1_ref, w2_ref, w3_ref)], axis=1)
            d_ref[:, cut] = dot(cot, whole, ((1,), (1,))).astype(bf16)


def pack_kernel(*refs):
    pieces, packed_ref, sem = refs[:-2], refs[-2], refs[-1]
    rows = pieces[0].shape[0]
    copies = [
        pltpu.make_async_copy(x, packed_ref.at[pl.ds(p * rows, rows), :], sem.at[p])
        for p, x in enumerate(pieces)
    ]
    for copy in copies:
        copy.start()
    for copy in copies:
        copy.wait()


def token_copies(token_refs, tokens_ref, sems, cut, first):
    copies, row = [], 0
    for p, x in enumerate(token_refs):
        rows = x.shape[0]
        copies.append(
            pltpu.make_async_copy(
                x.at[:, cut], tokens_ref.at[pl.ds(row, rows), cut], sems.at[first + p]
            )
        )
        row += rows
    return copies


def update_kernel(turned_ref, master_hbm, m_hbm, v_hbm, *rest, count, tile, layout):
    token_refs = rest[:count]
    new_hbm, keep_ref, send_ref = rest[count : count + 3]
    tokens, master, m, v, updated, new, sems, out_sems = rest[count + 3 :]
    depth = master.shape[0]
    tiles = depth // tile
    each = count + 3
    groups = []
    for i in range(tiles):
        cut = pl.ds(i * tile, tile)
        group = token_copies(token_refs, tokens, sems, cut, i * each)
        for p, (source, target) in enumerate(((master_hbm, master), (m_hbm, m), (v_hbm, v))):
            group.append(
                pltpu.make_async_copy(
                    source.at[cut, :], target.at[cut, :], sems.at[i * each + count + p]
                )
            )
        for copy in group:
            copy.start()
        groups.append(group)
    outs = []
    for i in range(tiles):
        cut = slice(i * tile, (i + 1) * tile)
        for copy in groups[i]:
            copy.wait()
        grad = dot(turned_ref[...], tokens[:, cut], ((1,), (0,))).T
        m_new = beta_first * m[cut, :] + (1.0 - beta_first) * grad
        v_new = beta_second * v[cut, :] + (1.0 - beta_second) * grad * grad
        m_hat = m_new / (1.0 - beta_first**step_count)
        v_hat = v_new / (1.0 - beta_second**step_count)
        old = master[cut, :]
        master_new = old - learn_rate * (
            m_hat / (jnp.sqrt(v_hat) + adam_eps) + weight_decay * old
        )
        new[cut, :] = master_new
        out = pltpu.make_async_copy(
            new.at[pl.ds(i * tile, tile), :], new_hbm.at[pl.ds(i * tile, tile), :], out_sems.at[i]
        )
        out.start()
        outs.append(out)
        updated[cut, :] = master_new.astype(bf16)
    project(tokens, updated, keep_ref, send_ref, layout)
    for out in outs:
        out.wait()


def project(tokens, weights, keep_ref, send_ref, layout):
    piece = tokens.shape[0] // len(layout)
    slot = {0: 0, 2: 1, 1: 2, 3: 3}
    p = 0
    while p < len(layout):
        k, j = layout[p]
        span = 2 if layout[p + 1 : p + 2] == ((k, j + 2),) else 1
        part_ref = send_ref if k % 2 else keep_ref
        part_ref[k // 2, slot[j] * piece : (slot[j] + span) * piece, :] = dot(
            tokens[p * piece : (p + span) * piece, :], weights[...], ((1,), (0,))
        ).astype(bf16)
        p += span


def project_kernel(mark_ref, weights_ref, *rest, count, layout):
    token_refs = rest[:count]
    keep_ref, send_ref, tokens, sems = rest[count:]
    copies = token_copies(token_refs, tokens, sems, slice(None), 0)
    for copy in copies:
        copy.start()
    for copy in copies:
        copy.wait()
    project(tokens, weights_ref, keep_ref, send_ref, layout)


def reorder(blocks, me):
    bit = 1
    while bit < len(blocks):
        flip = (me & bit) != 0
        blocks = [jnp.where(flip, blocks[i ^ bit], blocks[i]) for i in range(len(blocks))]
        bit *= 2
    return blocks


def scatter_sum(keep, send):
    got = swap(send, "dp", 1)
    mine = keep[0].astype(f32) + got[0].astype(f32)
    other = (keep[1].astype(f32) + got[1].astype(f32)).astype(bf16)
    return mine + swap(other, "dp", 2).astype(f32)


def shards(hidden_in, norm_gain, kv_cot, master_kv, moment_m, moment_v):
    dp, tensor = lax.axis_size("dp"), lax.axis_size("tensor")
    assert dp == 4 and tensor == 4
    z, t = lax.axis_index("dp"), lax.axis_index("tensor")
    where = jnp.stack([z, t]).astype(jnp.int32)
    _, micro, rows, width = hidden_in.shape
    piece = micro * rows
    hidden = hidden_in.reshape(piece, width)
    own_depth, cols = master_kv.shape[1:]
    depth = width // dp
    tile = min(piece, 16)

    weights = master_kv[0].astype(bf16)
    w2 = swap(weights, "tensor", 2)
    w1 = swap(weights, "tensor", 1)
    cot0 = kv_cot[0]
    cot2 = swap(cot0, "dp", 2)
    cot1 = swap(cot0, "dp", 1)
    cot3 = swap(cot2, "dp", 1)
    own = call(
        functools.partial(norm_kernel, tile=tile),
        [like(piece, depth)] * dp,
        [smem, vmem, vmem],
        [vmem] * dp,
        8,
        "norm",
    )(where, hidden, norm_gain)
    n1, n3 = swap(own[1], "dp", 1), swap(own[3], "dp", 3)
    a0 = swap(own[0], "tensor", 2)
    w3 = swap(w2, "tensor", 1)
    layout = (
        (0, 0), (0, 2), (1, 0), (1, 2), (0, 1), (0, 3), (1, 1), (1, 3),
        (3, 0), (3, 2), (3, 1), (3, 3), (2, 0), (2, 2), (2, 1), (2, 3),
    )
    zero, one, far, turned = call(
        functools.partial(arrange_kernel, dp=dp, layout=layout),
        [like(dp * piece, cols)] * 2
        + [like(2, dp * piece, cols), like(cols, dp * tensor * piece)],
        [smem] + [vmem] * dp,
        [vmem] * 4,
        8,
        "arrange",
    )(where, cot0, cot1, cot2, cot3)
    got1 = swap(one, "tensor", 1)
    got2 = swap(far, "tensor", 2)
    got3 = swap(got2[1], "tensor", 1)
    d = list(
        call(
            d_kernel,
            [like(piece, depth)] * dp,
            [vmem] * 8,
            [vmem] * dp,
            16,
            "d_normed",
        )(zero, got1, got2, got3, weights, w1, w2, w3)
    )
    n3, own2 = after([n3, own[2]], d[0])
    n2 = swap(own2, "dp", 2)
    a1, a3 = swap(n1, "tensor", 2), swap(n3, "tensor", 2)
    near = call(
        pack_kernel,
        like(4 * piece, depth),
        [anywhere] * 4,
        anywhere,
        0.25,
        "pack",
        scratch=[pltpu.SemaphoreType.DMA((4,))],
    )(own[0], a0, n1, a1)
    n2, d[2] = after([n2, d[2]], near)
    d2 = swap(d[2], "dp", 2)
    a2 = swap(n2, "tensor", 2)
    a2, d[1], d[3] = after([a2, d[1], d[3]], d2)
    d1, d3 = swap(d[1], "dp", 1), swap(d[3], "dp", 3)
    tokens = [near, swap(near, "tensor", 1)]
    tokens += [n3, a3, swap(n3, "tensor", 1), swap(a3, "tensor", 1)]
    tokens += [n2, a2, swap(n2, "tensor", 1), swap(a2, "tensor", 1)]
    count = len(tokens)
    block = tensor * piece
    part_shape = [like(dp // 2, block, cols)] * 2
    step = min(own_depth, 512)
    tiles = own_depth // step
    whole = pltpu.VMEM((own_depth, cols), f32)
    all_tokens = pltpu.VMEM((dp * block, depth), bf16)
    master_new, keep, send = call(
        functools.partial(update_kernel, count=count, tile=step, layout=layout),
        [like(own_depth, cols, dtype=f32)] + part_shape,
        [vmem] + [anywhere] * (3 + count),
        [anywhere, vmem, vmem],
        24,
        "update",
        scratch=[
            all_tokens,
            whole,
            whole,
            whole,
            pltpu.VMEM((own_depth, cols), bf16),
            whole,
            pltpu.SemaphoreType.DMA((tiles * (count + 3),)),
            pltpu.SemaphoreType.DMA((tiles,)),
        ],
    )(turned, master_kv[0], moment_m[0], moment_v[0], *tokens)

    def place(x):
        x = x.reshape(tensor, micro, rows, cols)
        return jnp.stack(reorder([x[j] for j in (0, 2, 1, 3)], t), 1).reshape(
            1, micro, tensor * rows, cols
        )

    mine = place(scatter_sum(keep, send).astype(bf16))
    kv_next = from_behind(mine, "segment", -1)
    own_keep, own_send = call(
        functools.partial(project_kernel, count=count, layout=layout),
        part_shape,
        [anywhere, vmem] + [anywhere] * count,
        [vmem] * 2,
        16,
        "project",
        scratch=[all_tokens, pltpu.SemaphoreType.DMA((count,))],
    )(send, weights, *tokens)
    kv_own = place(scatter_sum(own_keep, own_send).astype(bf16))
    d1, d3 = after([d1, d3], send)
    grad_in = call(
        functools.partial(grad_kernel, tile=tile),
        like(piece, width),
        [smem] + [vmem] * (2 + dp),
        vmem,
        12,
        "grad_in",
    )(where, hidden, norm_gain, d[0], d1, d2, d3)
    return (kv_own, grad_in.reshape(hidden_in.shape), master_new[None], kv_next)


def solution(mesh):
    in_specs = (
        P("segment", None, ("dp", "tensor"), None),
        P("segment", None),
        P("segment", None, "dp", "tensor"),
        P("segment", "dp", "tensor"),
        P("segment", "dp", "tensor"),
        P("segment", "dp", "tensor"),
    )
    out_specs = (
        P("segment", None, "dp", "tensor"),
        P("segment", None, ("dp", "tensor"), None),
        P("segment", "dp", "tensor"),
        P("segment", None, "dp", "tensor"),
    )
    return jax.shard_map(shards, mesh=mesh, in_specs=in_specs, out_specs=out_specs, check_vma=False)
```

time: 225 us -> 211 us (0.938)
  Pallas kernels: 0 us -> 28.9 us
  starting transfers between devices: 41.1 us -> 24.3 us
  matrix products: 13.2 us -> 0 us
  other arithmetic: 10.6 us -> 5.26 us
  waiting for transfers between devices: 150 us -> 145 us
  local copies, waits for them, and re-layouts: 9.34 us -> 5.85 us
    pallas_call x0 -> x11, Pallas kernels: none -> 28.9 us  [the longest x1 9.74 us: shards(): call(functools.partial(update_kernel, count=count, tile=step, layout=layo...]
    ppermute x33 -> x28, starting transfers between devices: 39.5 us -> 22.7 us  [swap(): return lax.ppermute(x, axis, [(i, i ^ bits) for i in range(peers)])]
    dot_general x4 -> x0, matrix products: 13.2 us -> none  [dot(): lax.dot_general(a, b, (contract, ((), ())), preferred_element_type=f32)]
    ppermute x33 -> x28, waiting for transfers between devices: 150 us -> 145 us  [swap(): return lax.ppermute(x, axis, [(i, i ^ bits) for i in range(peers)])]
    broadcast_in_dim x1 -> x0, other arithmetic: 2.88 us -> none  [shards(): return (kv_own, grad_in[None], master_new[None], kv_next)]
    unnamed x36 -> x37, local copies, waits for them, and re-layouts: 5.32 us -> 5.1 us
  transfers between devices with their start and end apart: 34 -> 29, of which waited for: 16 -> 15; matrix products, arithmetic and copies ran while one was open for 7% -> 2% of each run, Pallas kernels for 0% -> 9%
where the time goes in v5:
time: 211 us; the launch traced here: 210 us
  waiting for transfers between devices  145 us (69%)
  Pallas kernels  28.9 us (14%)
  starting transfers between devices  24.3 us (12%)
  local copies, waits for them, and re-layouts  5.85 us (3%)
  other arithmetic  5.26 us (2%)
    ppermute x28, waiting for transfers between devices, swap(): return lax.ppermute(x, axis, [(i, i ^ bits) for i in range(peers)])  145 us
    ppermute x28, starting transfers between devices, swap(): return lax.ppermute(x, axis, [(i, i ^ bits) for i in range(peers)])  22.7 us
    pallas_call x1, Pallas kernels, shards(): call(functools.partial(update_kernel, count=count, tile=step, layout=layo...  9.74 us
    pallas_call x1, Pallas kernels, shards(): call(d_kernel, [like(piece, depth)] * dp, [vmem] * 8, [vmem] * dp, 16, 'd...  7.49 us
    unnamed x37, local copies, waits for them, and re-layouts  5.1 us
    pallas_call x1, Pallas kernels, shards(): call(functools.partial(grad_kernel, tile=tile), like(piece, width), [smem...  4.74 us
  transfers between devices with their start and end apart: 29, of which 15 were waited for; matrix products, arithmetic and copies ran while one was open for 2% of the time, Pallas kernels for 9%

profile of v5, /device:TPU:0, one launch (start us, length us, event | category | flops | bytes accessed | tf_op | source)
XLA Modules:
  0.0 210.4 jit_solution(12644264653478614888)
XLA Ops:
  0.7 1.8 bitcast_convert_fusion.w0_ref.weights_ref
  2.5 3.0 %collective-permute-start.12 = (bf16[2048,256]{1,0:T(8,128)(2,1)S(1)}, bf16[2048,256]{1,0:T(8,128)(2,1)}, u32[]{:S(2)}, u32[]{:S(2)}) collective-permute-start(bf16[2048,256]{1,0:T(8,128)(2,1)S(1)} %bitcast_convert_fusion.w0_ref.weights_ref), channel_id=1, source_target_pairs={{0,2},{1,3},{2,0},{3,1},{4,6},{5,7},{6,4},{7,5},{8,10},{9,11},{10,... | collective-permute-start | bytes 3145736 | tf_op jit(solution)/shard_map/ppermute | solution.py:29
  5.6 2.1 %norm.1 = (bf16[128,2048]{1,0:T(8,128)(2,1)S(1)}, bf16[128,2048]{1,0:T(8,128)(2,1)S(1)}, bf16[128,2048]{1,0:T(8,128)(2,1)S(1)}, bf16[128,2048]{1,0:T(8,128)(2,1)S(1)}) custom-call(s32[2]{0:T(128)S(1)} %pad_add_fusion.where_ref, bf16[128,8192]{1,0:T(8,128)(2,1)S(1)} %bitcast.35, f32[1,8192]{1,0:T(1,128)S(1)} %copy-done.15), custom_call_target="tpu_custom_call" | custom-call | flops 1000 | bytes 1000 | tf_op jit(solution)/shard_map/norm/pallas_call | solution.py:289
  7.8 1.6 collective-permute-start.4
  9.4 2.6 %collective-permute-start.1 = (bf16[2,256,256]{2,1,0:T(8,128)(2,1)S(1)}, bf16[2,256,256]{2,1,0:T(8,128)(2,1)S(1)}, u32[]{:S(2)}, u32[]{:S(2)}) collective-permute-start(bf16[2,256,256]{2,1,0:T(8,128)(2,1)S(1)} %bitcast.39), channel_id=1, source_target_pairs={{0,8},{4,12},{8,0},{12,4},{1,9},{5,13},{9,1},{13,5},{2,10},{6,14},... | collective-permute-start | bytes 786440 | tf_op jit(solution)/shard_map/ppermute | solution.py:29
  12.4 14.9 %collective-permute-done.1.refs_2_ = bf16[2,256,256]{2,1,0:T(8,128)(2,1)S(1)} collective-permute-done((bf16[2,256,256]{2,1,0:T(8,128)(2,1)S(1)}, bf16[2,256,256]{2,1,0:T(8,128)(2,1)S(1)}, u32[]{:S(2)}, u32[]{:S(2)}) %collective-permute-start.1) | collective-permute-done | bytes 262176 | tf_op jit(solution)/shard_map/ppermute | solution.py:29
  27.4 3.5 %collective-permute-start.2 = (bf16[2,256,256]{2,1,0:T(8,128)(2,1)S(1)}, bf16[2,256,256]{2,1,0:T(8,128)(2,1)S(1)}, u32[]{:S(2)}, u32[]{:S(2)}) collective-permute-start(bf16[2,256,256]{2,1,0:T(8,128)(2,1)S(1)} %collective-permute-done.1.refs_2_), channel_id=1, source_target_pairs={{0,4},{4,0},{8,12},{12,8},{1,5},{5,1},{9,13},{13,9},{2,6},{6,2},{1... | collective-permute-start | bytes 786440 | tf_op jit(solution)/shard_map/ppermute | solution.py:29
  31.4 2.5 %collective-permute-done.refs_1_ = bf16[2,256,256]{2,1,0:T(8,128)(2,1)S(1)} collective-permute-done((bf16[2,256,256]{2,1,0:T(8,128)(2,1)S(1)}, bf16[2,256,256]{2,1,0:T(8,128)(2,1)S(1)}, u32[]{:S(2)}, u32[]{:S(2)}) %collective-permute-start) | collective-permute-done | bytes 262176 | tf_op jit(solution)/shard_map/ppermute | solution.py:29
  34.6 3.5 %collective-permute-done.2.refs_3_ = bf16[2,256,256]{2,1,0:T(8,128)(2,1)S(1)} collective-permute-done((bf16[2,256,256]{2,1,0:T(8,128)(2,1)S(1)}, bf16[2,256,256]{2,1,0:T(8,128)(2,1)S(1)}, u32[]{:S(2)}, u32[]{:S(2)}) %collective-permute-start.2) | collective-permute-done | bytes 262176 | tf_op jit(solution)/shard_map/ppermute | solution.py:29
  39.5 6.2 %collective-permute-done.3.refs_1_ = bf16[128,2048]{1,0:T(8,128)(2,1)S(1)} collective-permute-done((bf16[128,2048]{1,0:T(8,128)(2,1)S(1)}, bf16[128,2048]{1,0:T(8,128)(2,1)S(1)}, u32[]{:S(2)}, u32[]{:S(2)}) %collective-permute-start.3) | collective-permute-done | bytes 524320 | tf_op jit(solution)/shard_map/ppermute | solution.py:29
  45.7 11.2 %collective-permute-done.5.refs_3_ = bf16[128,2048]{1,0:T(8,128)(2,1)S(1)} collective-permute-done((bf16[128,2048]{1,0:T(8,128)(2,1)S(1)}, bf16[128,2048]{1,0:T(8,128)(2,1)S(1)}, u32[]{:S(2)}, u32[]{:S(2)}) %collective-permute-start.5) | collective-permute-done | bytes 524320 | tf_op jit(solution)/shard_map/ppermute | solution.py:29
  57.0 1.3 collective-permute-start.7
  58.4 5.6 %collective-permute-done.9.c2_ref = bf16[2,512,256]{2,1,0:T(8,128)(2,1)S(1)} collective-permute-done((bf16[2,512,256]{2,1,0:T(8,128)(2,1)S(1)}, bf16[2,512,256]{2,1,0:T(8,128)(2,1)S(1)}, u32[]{:S(2)}, u32[]{:S(2)}) %collective-permute-start.9) | collective-permute-done | bytes 524320 | tf_op jit(solution)/shard_map/ppermute | solution.py:29
  64.7 3.9 %collective-permute-done.10.c3_ref = bf16[512,256]{1,0:T(8,128)(2,1)S(1)} collective-permute-done((bf16[512,256]{1,0:T(8,128)(2,1)S(1)}, bf16[512,256]{1,0:T(8,128)(2,1)S(1)}, u32[]{:S(2)}, u32[]{:S(2)}) %collective-permute-start.10) | collective-permute-done | bytes 262176 | tf_op jit(solution)/shard_map/ppermute | solution.py:29
  68.6 7.5 %d_normed.1 = (bf16[128,2048]{1,0:T(8,128)(2,1)S(1)}, bf16[128,2048]{1,0:T(8,128)(2,1)}, bf16[128,2048]{1,0:T(8,128)(2,1)S(1)}, bf16[128,2048]{1,0:T(8,128)(2,1)}) custom-call(bf16[512,256]{1,0:T(8,128)(2,1)S(1)} %get-tuple-element.35.c0_ref, bf16[512,256]{1,0:T(8,128)(2,1)S(1)} %collective-permute-done.8.c1_ref, ...), custom_call_target="tpu_custom_call" | custom-call | flops 1000 | bytes 1000 | tf_op jit(solution)/shard_map/d_normed/pallas_call | solution.py:317
  76.1 1.2 collective-permute-start.17
  77.3 1.5 collective-permute-start.14
  78.9 23.1 %collective-permute-done.17.refs_0_ = bf16[128,2048]{1,0:T(8,128)(2,1)S(1)} collective-permute-done((bf16[128,2048]{1,0:T(8,128)(2,1)S(1)}, bf16[128,2048]{1,0:T(8,128)(2,1)S(1)}, u32[]{:S(2)}, u32[]{:S(2)}) %collective-permute-start.17) | collective-permute-done | bytes 524320 | tf_op jit(solution)/shard_map/ppermute | solution.py:29
  103.5 24.3 %collective-permute-done.19.refs_3_.rest_2_ = bf16[128,2048]{1,0:T(8,128)(2,1)S(1)} collective-permute-done((bf16[128,2048]{1,0:T(8,128)(2,1)S(1)}, bf16[128,2048]{1,0:T(8,128)(2,1)S(1)}, u32[]{:S(2)}, u32[]{:S(2)}) %collective-permute-start.19) | collective-permute-done | bytes 524320 | tf_op jit(solution)/shard_map/ppermute | solution.py:29
  128.6 1.1 collective-permute-done.16.rest_5_
  130.5 9.7 %update.1 = (f32[2048,256]{1,0:T(8,128)}, bf16[2,512,256]{2,1,0:T(8,128)(2,1)S(1)}, bf16[2,512,256]{2,1,0:T(8,128)(2,1)S(1)}) custom-call(bf16[256,2048]{1,0:T(8,128)(2,1)S(1)} %get-tuple-element.30.turned_ref, f32[2048,256]{1,0:T(8,128)S(1)} %bitcast.34, f32[2048,256]{1,0:T(8,128)S(1)} %bitcast.37, f32[2048,256]{1,0:T(8,128)S(1)} %bitcast.38, ...), custom_call_target="tpu_custom_call" | custom-call | flops 1000 | bytes 1000 | tf_op jit(solution)/shard_map/update/pallas_call | solution.py:353
  140.3 2.0 collective-permute-start.24
  142.4 1.5 collective-permute-start.25
  143.8 3.7 %project.1 = (bf16[2,512,256]{2,1,0:T(8,128)(2,1)S(1)}, bf16[2,512,256]{2,1,0:T(8,128)(2,1)}) custom-call(bf16[2,512,256]{2,1,0:T(8,128)(2,1)S(1)} %get-tuple-element.47.mark_ref.refs_2_, bf16[2048,256]{1,0:T(8,128)(2,1)S(1)} %bitcast_convert_fusion.w0_ref.weights_ref, bf16[512,2048]{1,0:T(8,128)(2,1)S(1)} %pack.1.refs_2_.rest_0_, ...), custom_call_target="tpu_custom_call" | custom-call | flops 1000 | bytes 1000 | tf_op jit(solution)/shard_map/project/pallas_call | solution.py:380
  148.4 6.7 %collective-permute-done.26 = bf16[2,512,256]{2,1,0:T(8,128)(2,1)S(1)} collective-permute-done((bf16[2,512,256]{2,1,0:T(8,128)(2,1)S(1)}, bf16[2,512,256]{2,1,0:T(8,128)(2,1)S(1)}, u32[]{:S(2)}, u32[]{:S(2)}) %collective-permute-start.26) | collective-permute-done | bytes 524320 | tf_op jit(solution)/shard_map/ppermute | solution.py:29
  155.9 27.4 %collective-permute-done.24.refs_0_ = bf16[128,2048]{1,0:T(8,128)(2,1)} collective-permute-done((bf16[128,2048]{1,0:T(8,128)(2,1)}, bf16[128,2048]{1,0:T(8,128)(2,1)}, u32[]{:S(2)}, u32[]{:S(2)}) %collective-permute-start.24) | collective-permute-done | bytes 524320 | tf_op jit(solution)/shard_map/ppermute | solution.py:29
  185.4 4.7 %grad_in.1 = bf16[128,8192]{1,0:T(8,128)(2,1)} custom-call(s32[2]{0:T(128)S(1)} %pad_add_fusion.where_ref, bf16[128,8192]{1,0:T(8,128)(2,1)S(1)} %bitcast.36, f32[1,8192]{1,0:T(1,128)S(1)} %copy-done.15, bf16[128,2048]{1,0:T(8,128)(2,1)S(1)} %copy-done.5, bf16[128,2048]{1,0:T(8,128)(2,1)} %get-tuple-element.52.rest_1_, bf16[128,2048]{1,0:T(8,128)(2,1)S(1)} %copy-done.9, ...), custom_call_target="tpu_custom_call" | custom-call | flops 1000 | bytes 1000 | tf_op jit(solution)/shard_map/grad_in/pallas_call | solution.py:391
  190.1 3.6 %collective-permute-done.22 = bf16[2,512,256]{2,1,0:T(8,128)(2,1)} collective-permute-done((bf16[2,512,256]{2,1,0:T(8,128)(2,1)}, bf16[2,512,256]{2,1,0:T(8,128)(2,1)}, u32[]{:S(2)}, u32[]{:S(2)}) %collective-permute-start.22) | collective-permute-done | bytes 524320 | tf_op jit(solution)/shard_map/ppermute | solution.py:29
  194.9 1.1 fusion
  196.0 1.6 collective-permute-start.28
  197.6 10.2 %collective-permute-done.23 = bf16[512,256]{1,0:T(8,128)(2,1)S(1)} collective-permute-done((bf16[512,256]{1,0:T(8,128)(2,1)S(1)}, bf16[512,256]{1,0:T(8,128)(2,1)S(1)}, u32[]{:S(2)}, u32[]{:S(2)}) %collective-permute-start.23) | collective-permute-done | bytes 262176 | tf_op jit(solution)/shard_map/ppermute | solution.py:29
  207.8 1.1 fusion.1
  (87 shorter events, 13.5 us)
Async XLA Ops:
  2.5 31.4 %collective-permute-start.12 = (bf16[2048,256]{1,0:T(8,128)(2,1)S(1)}, bf16[2048,256]{1,0:T(8,128)(2,1)}, u32[]{:S(2)}, u32[]{:S(2)}) collective-permute-start(bf16[2048,256]{1,0:T(8,128)(2,1)S(1)} %bitcast_convert_fusion.w0_ref.weights_ref), channel_id=1, source_target_pairs={{0,2},{1,3},{2,0},{3,1},{4,6},{5,7},{6,4},{7,5},{8,10},{9,11},{10,... | collective-permute-start | bytes 3145736 | tf_op jit(solution)/shard_map/ppermute | solution.py:29
  7.8 26.7 %collective-permute-start.4 = (bf16[128,2048]{1,0:T(8,128)(2,1)S(1)}, bf16[128,2048]{1,0:T(8,128)(2,1)S(1)}, u32[]{:S(2)}, u32[]{:S(2)}) collective-permute-start(bf16[128,2048]{1,0:T(8,128)(2,1)S(1)} %get-tuple-element.32), channel_id=1, source_target_pairs={{0,4},{4,0},{8,12},{12,8},{1,5},{5,1},{9,13},{13,9},{2,6},{6,2},{1... | collective-permute-start | bytes 1572872 | tf_op jit(solution)/shard_map/ppermute | solution.py:29
  9.4 18.0 %collective-permute-start.1 = (bf16[2,256,256]{2,1,0:T(8,128)(2,1)S(1)}, bf16[2,256,256]{2,1,0:T(8,128)(2,1)S(1)}, u32[]{:S(2)}, u32[]{:S(2)}) collective-permute-start(bf16[2,256,256]{2,1,0:T(8,128)(2,1)S(1)} %bitcast.39), channel_id=1, source_target_pairs={{0,8},{4,12},{8,0},{12,4},{1,9},{5,13},{9,1},{13,5},{2,10},{6,14},... | collective-permute-start | bytes 786440 | tf_op jit(solution)/shard_map/ppermute | solution.py:29
  12.0 21.9 %collective-permute-start = (bf16[2,256,256]{2,1,0:T(8,128)(2,1)S(1)}, bf16[2,256,256]{2,1,0:T(8,128)(2,1)S(1)}, u32[]{:S(2)}, u32[]{:S(2)}) collective-permute-start(bf16[2,256,256]{2,1,0:T(8,128)(2,1)S(1)} %bitcast.40), channel_id=1, source_target_pairs={{0,4},{4,0},{8,12},{12,8},{1,5},{5,1},{9,13},{13,9},{2,6},{6,2},{1... | collective-permute-start | bytes 786440 | tf_op jit(solution)/shard_map/ppermute | solution.py:29
  27.4 10.7 %collective-permute-start.2 = (bf16[2,256,256]{2,1,0:T(8,128)(2,1)S(1)}, bf16[2,256,256]{2,1,0:T(8,128)(2,1)S(1)}, u32[]{:S(2)}, u32[]{:S(2)}) collective-permute-start(bf16[2,256,256]{2,1,0:T(8,128)(2,1)S(1)} %collective-permute-done.1.refs_2_), channel_id=1, source_target_pairs={{0,4},{4,0},{8,12},{12,8},{1,5},{5,1},{9,13},{13,9},{2,6},{6,2},{1... | collective-permute-start | bytes 786440 | tf_op jit(solution)/shard_map/ppermute | solution.py:29
  30.9 14.9 %collective-permute-start.3 = (bf16[128,2048]{1,0:T(8,128)(2,1)S(1)}, bf16[128,2048]{1,0:T(8,128)(2,1)S(1)}, u32[]{:S(2)}, u32[]{:S(2)}) collective-permute-start(bf16[128,2048]{1,0:T(8,128)(2,1)S(1)} %get-tuple-element.31.refs_0_), channel_id=1, source_target_pairs={{0,2},{1,3},{2,0},{3,1},{4,6},{5,7},{6,4},{7,5},{8,10},{9,11},{10,... | collective-permute-start | bytes 1572872 | tf_op jit(solution)/shard_map/ppermute | solution.py:29
  33.9 30.8 %collective-permute-start.11 = (bf16[2048,256]{1,0:T(8,128)(2,1)S(1)}, bf16[2048,256]{1,0:T(8,128)(2,1)S(1)}, u32[]{:S(2)}, u32[]{:S(2)}) collective-permute-start(bf16[2048,256]{1,0:T(8,128)(2,1)S(1)} %bitcast_convert_fusion.w0_ref.weights_ref), channel_id=1, source_target_pairs={{0,1},{1,0},{2,3},{3,2},{4,5},{5,4},{6,7},{7,6},{8,9},{9,8},{10,11... | collective-permute-start | bytes 3145736 | tf_op jit(solution)/shard_map/ppermute | solution.py:29
  33.9 34.7 %collective-permute-start.13 = (bf16[2048,256]{1,0:T(8,128)(2,1)}, bf16[2048,256]{1,0:T(8,128)(2,1)S(1)}, u32[]{:S(2)}, u32[]{:S(2)}) collective-permute-start(bf16[2048,256]{1,0:T(8,128)(2,1)} %collective-permute-done.12.w2_ref), channel_id=1, source_target_pairs={{0,1},{1,0},{2,3},{3,2},{4,5},{5,4},{6,7},{7,6},{8,9},{9,8},{10,11... | collective-permute-start | bytes 3145736 | tf_op jit(solution)/shard_map/ppermute | solution.py:29
  34.4 22.5 %collective-permute-start.5 = (bf16[128,2048]{1,0:T(8,128)(2,1)S(1)}, bf16[128,2048]{1,0:T(8,128)(2,1)S(1)}, u32[]{:S(2)}, u32[]{:S(2)}) collective-permute-start(bf16[128,2048]{1,0:T(8,128)(2,1)S(1)} %collective-permute-done.4.refs_2_), channel_id=1, source_target_pairs={{0,2},{1,3},{2,0},{3,1},{4,6},{5,7},{6,4},{7,5},{8,10},{9,11},{10,... | collective-permute-start | bytes 1572872 | tf_op jit(solution)/shard_map/ppermute | solution.py:29
  39.0 25.1 %collective-permute-start.9 = (bf16[2,512,256]{2,1,0:T(8,128)(2,1)S(1)}, bf16[2,512,256]{2,1,0:T(8,128)(2,1)S(1)}, u32[]{:S(2)}, u32[]{:S(2)}) collective-permute-start(bf16[2,512,256]{2,1,0:T(8,128)(2,1)S(1)} %get-tuple-element.37), channel_id=1, source_target_pairs={{0,2},{1,3},{2,0},{3,1},{4,6},{5,7},{6,4},{7,5},{8,10},{9,11},{10,... | collective-permute-start | bytes 1572872 | tf_op jit(solution)/shard_map/ppermute | solution.py:29
  45.7 18.4 %collective-permute-start.8 = (bf16[512,256]{1,0:T(8,128)(2,1)S(1)}, bf16[512,256]{1,0:T(8,128)(2,1)S(1)}, u32[]{:S(2)}, u32[]{:S(2)}) collective-permute-start(bf16[512,256]{1,0:T(8,128)(2,1)S(1)} %get-tuple-element.36), channel_id=1, source_target_pairs={{0,1},{1,0},{2,3},{3,2},{4,5},{5,4},{6,7},{7,6},{8,9},{9,8},{10,11... | collective-permute-start | bytes 786440 | tf_op jit(solution)/shard_map/ppermute | solution.py:29
  57.0 19.1 %collective-permute-start.7 = (bf16[128,2048]{1,0:T(8,128)(2,1)S(1)}, bf16[128,2048]{1,0:T(8,128)(2,1)S(1)}, u32[]{:S(2)}, u32[]{:S(2)}) collective-permute-start(bf16[128,2048]{1,0:T(8,128)(2,1)S(1)} %get-tuple-element.33), channel_id=1, source_target_pairs={{0,12},{4,8},{8,4},{12,0},{1,13},{5,9},{9,5},{13,1},{2,14},{6,10},... | collective-permute-start | bytes 1572872 | tf_op jit(solution)/shard_map/ppermute | solution.py:29
  64.1 64.5 %collective-permute-start.6 = (bf16[512,2048]{1,0:T(8,128)(2,1)S(1)}, bf16[512,2048]{1,0:T(8,128)(2,1)S(1)}, u32[]{:S(2)}, u32[]{:S(2)}) collective-permute-start(bf16[512,2048]{1,0:T(8,128)(2,1)S(1)} %pack.1.refs_2_.rest_0_), channel_id=1, source_target_pairs={{0,1},{1,0},{2,3},{3,2},{4,5},{5,4},{6,7},{7,6},{8,9},{9,8},{10,11... | collective-permute-start | bytes 6291464 | tf_op jit(solution)/shard_map/ppermute | solution.py:29
  64.1 4.5 %collective-permute-start.10 = (bf16[512,256]{1,0:T(8,128)(2,1)S(1)}, bf16[512,256]{1,0:T(8,128)(2,1)S(1)}, u32[]{:S(2)}, u32[]{:S(2)}) collective-permute-start(bf16[512,256]{1,0:T(8,128)(2,1)S(1)} %slice_bitcast_fusion), channel_id=1, source_target_pairs={{0,1},{1,0},{2,3},{3,2},{4,5},{5,4},{6,7},{7,6},{8,9},{9,8},{10,11... | collective-permute-start | bytes 786440 | tf_op jit(solution)/shard_map/ppermute | solution.py:29
  76.1 54.4 %copy-start.3 = (f32[1,2048,256]{2,1,0:T(8,128)S(1)}, f32[1,2048,256]{2,1,0:T(8,128)}, u32[]{:S(2)}) copy-start(f32[1,2048,256]{2,1,0:T(8,128)} %param.11) | copy-start | bytes 6291460
  76.1 25.9 %collective-permute-start.17 = (bf16[128,2048]{1,0:T(8,128)(2,1)S(1)}, bf16[128,2048]{1,0:T(8,128)(2,1)S(1)}, u32[]{:S(2)}, u32[]{:S(2)}) collective-permute-start(bf16[128,2048]{1,0:T(8,128)(2,1)S(1)} %get-tuple-element.40), channel_id=1, source_target_pairs={{0,8},{4,12},{8,0},{12,4},{1,9},{5,13},{9,1},{13,5},{2,10},{6,14},... | collective-permute-start | bytes 1572872 | tf_op jit(solution)/shard_map/ppermute | solution.py:29
  77.3 25.6 %collective-permute-start.14 = (bf16[128,2048]{1,0:T(8,128)(2,1)S(1)}, bf16[128,2048]{1,0:T(8,128)(2,1)S(1)}, u32[]{:S(2)}, u32[]{:S(2)}) collective-permute-start(bf16[128,2048]{1,0:T(8,128)(2,1)S(1)} %get-tuple-element.39.rest_2_), channel_id=1, source_target_pairs={{0,2},{1,3},{2,0},{3,1},{4,6},{5,7},{6,4},{7,5},{8,10},{9,11},{10,... | collective-permute-start | bytes 1572872 | tf_op jit(solution)/shard_map/ppermute | solution.py:29
  102.0 28.5 %copy-start.2 = (f32[1,2048,256]{2,1,0:T(8,128)S(1)}, f32[1,2048,256]{2,1,0:T(8,128)}, u32[]{:S(2)}) copy-start(f32[1,2048,256]{2,1,0:T(8,128)} %param.10) | copy-start | bytes 6291460
  102.0 25.8 %collective-permute-start.19 = (bf16[128,2048]{1,0:T(8,128)(2,1)S(1)}, bf16[128,2048]{1,0:T(8,128)(2,1)S(1)}, u32[]{:S(2)}, u32[]{:S(2)}) collective-permute-start(bf16[128,2048]{1,0:T(8,128)(2,1)S(1)} %get-tuple-element.45), channel_id=1, source_target_pairs={{0,8},{4,12},{8,0},{12,4},{1,9},{5,13},{9,1},{13,5},{2,10},{6,14},... | collective-permute-start | bytes 1572872 | tf_op jit(solution)/shard_map/ppermute | solution.py:29
  102.1 25.7 %collective-permute-start.18 = (bf16[128,2048]{1,0:T(8,128)(2,1)S(1)}, bf16[128,2048]{1,0:T(8,128)(2,1)S(1)}, u32[]{:S(2)}, u32[]{:S(2)}) collective-permute-start(bf16[128,2048]{1,0:T(8,128)(2,1)S(1)} %get-tuple-element.42.rest_6_), channel_id=1, source_target_pairs={{0,2},{1,3},{2,0},{3,1},{4,6},{5,7},{6,4},{7,5},{8,10},{9,11},{10,... | collective-permute-start | bytes 1572872 | tf_op jit(solution)/shard_map/ppermute | solution.py:29
  103.0 25.7 %collective-permute-start.15 = (bf16[128,2048]{1,0:T(8,128)(2,1)S(1)}, bf16[128,2048]{1,0:T(8,128)(2,1)S(1)}, u32[]{:S(2)}, u32[]{:S(2)}) collective-permute-start(bf16[128,2048]{1,0:T(8,128)(2,1)S(1)} %get-tuple-element.39.rest_2_), channel_id=1, source_target_pairs={{0,1},{1,0},{2,3},{3,2},{4,5},{5,4},{6,7},{7,6},{8,9},{9,8},{10,11... | collective-permute-start | bytes 1572872 | tf_op jit(solution)/shard_map/ppermute | solution.py:29
  103.0 26.7 %collective-permute-start.20 = (bf16[128,2048]{1,0:T(8,128)(2,1)S(1)}, bf16[128,2048]{1,0:T(8,128)(2,1)S(1)}, u32[]{:S(2)}, u32[]{:S(2)}) collective-permute-start(bf16[128,2048]{1,0:T(8,128)(2,1)S(1)} %get-tuple-element.42.rest_6_), channel_id=1, source_target_pairs={{0,1},{1,0},{2,3},{3,2},{4,5},{5,4},{6,7},{7,6},{8,9},{9,8},{10,11... | collective-permute-start | bytes 1572872 | tf_op jit(solution)/shard_map/ppermute | solution.py:29
  127.8 1.9 collective-permute-start.16
  128.6 1.9 collective-permute-start.21
  140.3 14.8 %collective-permute-start.26 = (bf16[2,512,256]{2,1,0:T(8,128)(2,1)S(1)}, bf16[2,512,256]{2,1,0:T(8,128)(2,1)S(1)}, u32[]{:S(2)}, u32[]{:S(2)}) collective-permute-start(bf16[2,512,256]{2,1,0:T(8,128)(2,1)S(1)} %get-tuple-element.47.mark_ref.refs_2_), channel_id=1, source_target_pairs={{0,4},{4,0},{8,12},{12,8},{1,5},{5,1},{9,13},{13,9},{2,6},{6,2},{1... | collective-permute-start | bytes 1572872 | tf_op jit(solution)/shard_map/ppermute | solution.py:29
  140.3 43.0 %collective-permute-start.24 = (bf16[128,2048]{1,0:T(8,128)(2,1)}, bf16[128,2048]{1,0:T(8,128)(2,1)}, u32[]{:S(2)}, u32[]{:S(2)}) collective-permute-start(bf16[128,2048]{1,0:T(8,128)(2,1)} %get-tuple-element.50), channel_id=1, source_target_pairs={{0,4},{4,0},{8,12},{12,8},{1,5},{5,1},{9,13},{13,9},{2,6},{6,2},{1... | collective-permute-start | bytes 1572872 | tf_op jit(solution)/shard_map/ppermute | solution.py:29
  142.4 40.9 %collective-permute-start.25 = (bf16[128,2048]{1,0:T(8,128)(2,1)}, bf16[128,2048]{1,0:T(8,128)(2,1)}, u32[]{:S(2)}, u32[]{:S(2)}) collective-permute-start(bf16[128,2048]{1,0:T(8,128)(2,1)} %get-tuple-element.51), channel_id=1, source_target_pairs={{0,12},{4,8},{8,4},{12,0},{1,13},{5,9},{9,5},{13,1},{2,14},{6,10},... | collective-permute-start | bytes 1572872 | tf_op jit(solution)/shard_map/ppermute | solution.py:29
  148.4 36.0 %copy-start.5 = (bf16[128,2048]{1,0:T(8,128)(2,1)S(1)}, bf16[128,2048]{1,0:T(8,128)(2,1)}, u32[]{:S(2)}) copy-start(bf16[128,2048]{1,0:T(8,128)(2,1)} %copy-done.4) | copy-start | bytes 1572868
  148.4 45.3 %collective-permute-start.22 = (bf16[2,512,256]{2,1,0:T(8,128)(2,1)}, bf16[2,512,256]{2,1,0:T(8,128)(2,1)}, u32[]{:S(2)}, u32[]{:S(2)}) collective-permute-start(bf16[2,512,256]{2,1,0:T(8,128)(2,1)} %get-tuple-element.49), channel_id=1, source_target_pairs={{0,4},{4,0},{8,12},{12,8},{1,5},{5,1},{9,13},{13,9},{2,6},{6,2},{1... | collective-permute-start | bytes 1572872 | tf_op jit(solution)/shard_map/ppermute | solution.py:29
  155.9 38.9 %collective-permute-start.27 = (bf16[512,256]{1,0:T(8,128)(2,1)S(1)}, bf16[512,256]{1,0:T(8,128)(2,1)}, u32[]{:S(2)}, u32[]{:S(2)}) collective-permute-start(bf16[512,256]{1,0:T(8,128)(2,1)S(1)} %fusion.3), channel_id=1, source_target_pairs={{0,8},{4,12},{8,0},{12,4},{1,9},{5,13},{9,1},{13,5},{2,10},{6,14},... | collective-permute-start | bytes 786440 | tf_op jit(solution)/shard_map/ppermute | solution.py:29
  194.7 13.1 %collective-permute-start.23 = (bf16[512,256]{1,0:T(8,128)(2,1)S(1)}, bf16[512,256]{1,0:T(8,128)(2,1)S(1)}, u32[]{:S(2)}, u32[]{:S(2)}) collective-permute-start(bf16[512,256]{1,0:T(8,128)(2,1)S(1)} %fusion.2), channel_id=1, source_target_pairs={{0,8},{4,12},{8,0},{12,4},{1,9},{5,13},{9,1},{13,5},{2,10},{6,14},... | collective-permute-start | bytes 786440 | tf_op jit(solution)/shard_map/ppermute | solution.py:29
  196.0 13.7 %collective-permute-start.28 = (bf16[1,2,256,256]{3,2,1,0:T(8,128)(2,1)S(1)}, bf16[1,2,256,256]{3,2,1,0:T(8,128)(2,1)S(1)}, u32[]{:S(2)}, u32[]{:S(2)}) collective-permute-start(bf16[1,2,256,256]{3,2,1,0:T(8,128)(2,1)S(1)} %bitcast.43), channel_id=1, source_target_pairs={{0,16},{16,0},{1,17},{17,1},{2,18},{18,2},{3,19},{19,3},{4,20},{20... | collective-permute-start | bytes 786440 | tf_op jit(solution)/shard_map/ppermute | solution.py:34
  (15 other events, 127.0 us)

commit v6 on v5

--- a/solution.py
+++ b/solution.py
@@ -73,7 +73,7 @@
     return pl.ds(pl.multiple_of(index * size, size), size)
 
 
-def norm_kernel(where_ref, hidden_ref, gain_ref, *own_refs, tile):
+def norm_kernel(mark_ref, other_ref, where_ref, hidden_ref, gain_ref, *own_refs, tile):
     z = where_ref[0]
     rows, width = hidden_ref.shape
     depth = width // len(own_refs)
@@ -94,7 +94,8 @@
 
 
 def grad_kernel(where_ref, hidden_ref, gain_ref, *rest, tile):
-    d_refs, out_ref = rest[:-1], rest[-1]
+    d0_ref, d1_ref, d23_ref, d3_ref, out_ref = rest
+    d_refs = (d0_ref, d1_ref, d23_ref.at[0], d3_ref)
     z = where_ref[0]
     rows, width = hidden_ref.shape
     depth = width // len(d_refs)
@@ -120,38 +121,40 @@
 
 
 def arrange_kernel(where_ref, *refs, dp, layout):
-    cots, (zero_ref, one_ref, far_ref, turned_ref) = refs[:dp], refs[dp:]
+    cots, (send_ref, turned_ref) = refs[:dp], refs[dp:]
     t = where_ref[1]
+    tensor = send_ref.shape[0]
     micro, rows, cols = cots[0].shape
-    rows //= 4
+    rows //= tensor
     piece = micro * rows
-
-    def block(k, j):
+    for k in range(dp):
+        for b in range(tensor):
+            for m in range(micro):
+                at = k * piece + m * rows
+                send_ref[b, at : at + rows, :] = cots[k][m, b * rows : (b + 1) * rows, :]
+    for p, (k, j) in enumerate(layout):
         at = pl.ds(pl.multiple_of((t ^ j) * rows, rows), rows)
-        return jnp.concatenate([cots[k][m, at, :] for m in range(micro)])
-
-    for k in range(dp):
-        zero_ref[k * piece : (k + 1) * piece, :] = block(k, 0)
-        one_ref[k * piece : (k + 1) * piece, :] = block(k, 1)
-        far_ref[0, k * piece : (k + 1) * piece, :] = block(k, 2)
-        far_ref[1, k * piece : (k + 1) * piece, :] = block(k, 3)
-    for p, (k, j) in enumerate(layout):
-        turned_ref[:, p * piece : (p + 1) * piece] = block(k, j).astype(f32).T.astype(bf16)
-
-
-def d_kernel(c0_ref, c1_ref, c2_ref, c3_ref, w0_ref, w1_ref, w2_ref, w3_ref, *d_refs):
-    rows = d_refs[0].shape[0]
-    depth = d_refs[0].shape[1]
-    tile = min(depth, 512)
-    for k, d_ref in enumerate(d_refs):
-        at = slice(k * rows, (k + 1) * rows)
-        cot = jnp.concatenate(
-            [c0_ref[at, :], c1_ref[at, :], c2_ref[0, at, :], c3_ref[at, :]], axis=1
-        )
-        for i in range(depth // tile):
+        block = jnp.concatenate([cots[k][m, at, :] for m in range(micro)])
+        turned_ref[:, p * piece : (p + 1) * piece] = block.astype(f32).T.astype(bf16)
+
+
+def d_kernel(where_ref, cot_ref, *rest):
+    w_refs, (d0_ref, d1_ref, d23_ref) = rest[:8], rest[8:]
+    rows = d0_ref.shape[0]
+    half = w_refs[0].shape[0]
+    tile = min(half, 512)
+    targets = (d0_ref, d1_ref, d23_ref.at[0], d23_ref.at[1])
+    t = where_ref[1]
+    cot = jnp.concatenate([cot_ref[t ^ j] for j in range(cot_ref.shape[0])], axis=1)
+    for side in range(2):
+        for i in range(half // tile):
             cut = slice(i * tile, (i + 1) * tile)
-            whole = jnp.concatenate([w[cut, :] for w in (w0_ref, w1_ref, w2_ref, w3_ref)], axis=1)
-            d_ref[:, cut] = dot(cot, whole, ((1,), (1,))).astype(bf16)
+            whole = jnp.concatenate([w[cut, :] for w in w_refs[side::2]], axis=1)
+            part = dot(cot, whole, ((1,), (1,))).astype(bf16)
+            for k, target in enumerate(targets):
+                target[:, side * half + i * tile : side * half + (i + 1) * tile] = part[
+                    k * rows : (k + 1) * rows
+                ]
 
 
 def pack_kernel(*refs):
@@ -182,8 +185,8 @@
 
 def update_kernel(turned_ref, master_hbm, m_hbm, v_hbm, *rest, count, tile, layout):
     token_refs = rest[:count]
-    new_hbm, keep_ref, send_ref = rest[count : count + 3]
-    tokens, master, m, v, updated, new, sems, out_sems = rest[count + 3 :]
+    new_hbm, part_refs = rest[count], rest[count + 1 : -8]
+    tokens, master, m, v, updated, new, sems, out_sems = rest[-8:]
     depth = master.shape[0]
     tiles = depth // tile
     each = count + 3
@@ -221,20 +224,19 @@
         out.start()
         outs.append(out)
         updated[cut, :] = master_new.astype(bf16)
-    project(tokens, updated, keep_ref, send_ref, layout)
+    project(tokens, updated, part_refs, layout)
     for out in outs:
         out.wait()
 
 
-def project(tokens, weights, keep_ref, send_ref, layout):
+def project(tokens, weights, part_refs, layout):
     piece = tokens.shape[0] // len(layout)
     slot = {0: 0, 2: 1, 1: 2, 3: 3}
     p = 0
     while p < len(layout):
         k, j = layout[p]
         span = 2 if layout[p + 1 : p + 2] == ((k, j + 2),) else 1
-        part_ref = send_ref if k % 2 else keep_ref
-        part_ref[k // 2, slot[j] * piece : (slot[j] + span) * piece, :] = dot(
+        part_refs[k][slot[j] * piece : (slot[j] + span) * piece, :] = dot(
             tokens[p * piece : (p + span) * piece, :], weights[...], ((1,), (0,))
         ).astype(bf16)
         p += span
@@ -242,13 +244,13 @@
 
 def project_kernel(mark_ref, weights_ref, *rest, count, layout):
     token_refs = rest[:count]
-    keep_ref, send_ref, tokens, sems = rest[count:]
+    part_refs, (tokens, sems) = rest[count:-2], rest[-2:]
     copies = token_copies(token_refs, tokens, sems, slice(None), 0)
     for copy in copies:
         copy.start()
     for copy in copies:
         copy.wait()
-    project(tokens, weights_ref, keep_ref, send_ref, layout)
+    project(tokens, weights_ref, part_refs, layout)
 
 
 def reorder(blocks, me):
@@ -260,10 +262,12 @@
     return blocks
 
 
-def scatter_sum(keep, send):
-    got = swap(send, "dp", 1)
-    mine = keep[0].astype(f32) + got[0].astype(f32)
-    other = (keep[1].astype(f32) + got[1].astype(f32)).astype(bf16)
+def scatter_sum(parts, *earlier):
+    got1, got3 = swap(parts[1], "dp", 1), swap(parts[3], "dp", 1)
+    if earlier:
+        got1, got3 = after([got1, got3], *earlier)
+    mine = parts[0].astype(f32) + got1.astype(f32)
+    other = (parts[2].astype(f32) + got3.astype(f32)).astype(bf16)
     return mine + swap(other, "dp", 2).astype(f32)
 
 
@@ -279,9 +283,10 @@
     depth = width // dp
     tile = min(piece, 16)
 
-    weights = master_kv[0].astype(bf16)
-    w2 = swap(weights, "tensor", 2)
-    w1 = swap(weights, "tensor", 1)
+    half = own_depth // 2
+    w0 = [master_kv[0, :half].astype(bf16), master_kv[0, half:].astype(bf16)]
+    w2 = [swap(w, "tensor", 2) for w in w0]
+    w1 = [swap(w, "tensor", 1) for w in w0]
     cot0 = kv_cot[0]
     cot2 = swap(cot0, "dp", 2)
     cot1 = swap(cot0, "dp", 1)
@@ -289,72 +294,67 @@
     own = call(
         functools.partial(norm_kernel, tile=tile),
         [like(piece, depth)] * dp,
-        [smem, vmem, vmem],
+        [anywhere, anywhere, smem, vmem, vmem],
         [vmem] * dp,
         8,
         "norm",
-    )(where, hidden, norm_gain)
+    )(cot2, cot1, where, hidden, norm_gain)
     n1, n3 = swap(own[1], "dp", 1), swap(own[3], "dp", 3)
-    a0 = swap(own[0], "tensor", 2)
-    w3 = swap(w2, "tensor", 1)
-    layout = (
-        (0, 0), (0, 2), (1, 0), (1, 2), (0, 1), (0, 3), (1, 1), (1, 3),
-        (3, 0), (3, 2), (3, 1), (3, 3), (2, 0), (2, 2), (2, 1), (2, 3),
-    )
-    zero, one, far, turned = call(
+    w3 = [swap(w, "tensor", 1) for w in w2]
+    layout = tuple((k, j) for k in (0, 1, 3, 2) for j in (0, 2, 1, 3))
+    send, turned = call(
         functools.partial(arrange_kernel, dp=dp, layout=layout),
-        [like(dp * piece, cols)] * 2
-        + [like(2, dp * piece, cols), like(cols, dp * tensor * piece)],
+        [like(tensor, dp * piece, cols), like(cols, dp * tensor * piece)],
         [smem] + [vmem] * dp,
-        [vmem] * 4,
+        [vmem] * 2,
         8,
         "arrange",
     )(where, cot0, cot1, cot2, cot3)
-    got1 = swap(one, "tensor", 1)
-    got2 = swap(far, "tensor", 2)
-    got3 = swap(got2[1], "tensor", 1)
-    d = list(
-        call(
-            d_kernel,
-            [like(piece, depth)] * dp,
-            [vmem] * 8,
-            [vmem] * dp,
-            16,
-            "d_normed",
-        )(zero, got1, got2, got3, weights, w1, w2, w3)
-    )
-    n3, own2 = after([n3, own[2]], d[0])
+    own2, n3 = after([own[2], n3])
     n2 = swap(own2, "dp", 2)
-    a1, a3 = swap(n1, "tensor", 2), swap(n3, "tensor", 2)
-    near = call(
-        pack_kernel,
-        like(4 * piece, depth),
-        [anywhere] * 4,
-        anywhere,
-        0.25,
-        "pack",
-        scratch=[pltpu.SemaphoreType.DMA((4,))],
-    )(own[0], a0, n1, a1)
-    n2, d[2] = after([n2, d[2]], near)
-    d2 = swap(d[2], "dp", 2)
-    a2 = swap(n2, "tensor", 2)
-    a2, d[1], d[3] = after([a2, d[1], d[3]], d2)
-    d1, d3 = swap(d[1], "dp", 1), swap(d[3], "dp", 3)
-    tokens = [near, swap(near, "tensor", 1)]
-    tokens += [n3, a3, swap(n3, "tensor", 1), swap(a3, "tensor", 1)]
-    tokens += [n2, a2, swap(n2, "tensor", 1), swap(a2, "tensor", 1)]
+    (send,) = after([send], own2)
+    mine_cot = lax.all_to_all(send, "tensor", 0, 0, tiled=True)
+    d0, d1, d23 = call(
+        d_kernel,
+        [like(piece, depth)] * 2 + [like(2, piece, depth)],
+        [smem] + [vmem] * 9,
+        [vmem] * 3,
+        20,
+        "d_normed",
+    )(where, mine_cot, *w0, *w1, *w2, *w3)
+    def pack(*pieces):
+        return call(
+            pack_kernel,
+            like(len(pieces) * piece, depth),
+            [anywhere] * len(pieces),
+            anywhere,
+            0.25,
+            "pack",
+            scratch=[pltpu.SemaphoreType.DMA((len(pieces),))],
+        )(*pieces)
+
+    tokens = []
+    for x in (own[0], n1, n3):
+        near = pack(x, swap(x, "tensor", 2))
+        tokens += [near, swap(near, "tensor", 1)]
+    n2, d23 = after([n2, d23], tokens[1])
+    d23 = swap(d23, "dp", 2)
+    d1 = swap(d1, "dp", 1)
+
+    across = swap(n2, "tensor", 2)
+    tokens += [n2, across, swap(n2, "tensor", 1), swap(across, "tensor", 1)]
     count = len(tokens)
     block = tensor * piece
-    part_shape = [like(dp // 2, block, cols)] * 2
+    part_shape = [like(block, cols)] * dp
     step = min(own_depth, 512)
     tiles = own_depth // step
     whole = pltpu.VMEM((own_depth, cols), f32)
     all_tokens = pltpu.VMEM((dp * block, depth), bf16)
-    master_new, keep, send = call(
+    master_new, *parts = call(
         functools.partial(update_kernel, count=count, tile=step, layout=layout),
         [like(own_depth, cols, dtype=f32)] + part_shape,
         [vmem] + [anywhere] * (3 + count),
-        [anywhere, vmem, vmem],
+        [anywhere] + [vmem] * dp,
         24,
         "update",
         scratch=[
@@ -375,27 +375,28 @@
             1, micro, tensor * rows, cols
         )
 
-    mine = place(scatter_sum(keep, send).astype(bf16))
+    mine = place(scatter_sum(parts, d23).astype(bf16))
     kv_next = from_behind(mine, "segment", -1)
-    own_keep, own_send = call(
+    own_parts = call(
         functools.partial(project_kernel, count=count, layout=layout),
         part_shape,
         [anywhere, vmem] + [anywhere] * count,
-        [vmem] * 2,
+        [vmem] * dp,
         16,
         "project",
         scratch=[all_tokens, pltpu.SemaphoreType.DMA((count,))],
-    )(send, weights, *tokens)
-    kv_own = place(scatter_sum(own_keep, own_send).astype(bf16))
-    d1, d3 = after([d1, d3], send)
+    )(parts[1], jnp.concatenate(w0), *tokens)
+    kv_own = place(scatter_sum(own_parts).astype(bf16))
+    d3 = swap(after([d23[1]], parts[1])[0], "dp", 1)
+    d1, d3 = after([d1, d3], mine, kv_own)
     grad_in = call(
         functools.partial(grad_kernel, tile=tile),
         like(piece, width),
-        [smem] + [vmem] * (2 + dp),
+        [smem] + [vmem] * 6,
         vmem,
         12,
         "grad_in",
-    )(where, hidden, norm_gain, d[0], d1, d2, d3)
+    )(where, hidden, norm_gain, d0, d1, d23, d3)
     return (kv_own, grad_in.reshape(hidden_in.shape), master_new[None], kv_next)
 
 

time: 211 us -> 228 us (1.081)
  waiting for transfers between devices: 145 us -> 125 us
  Pallas kernels: 28.9 us -> 46.1 us
  local copies, waits for them, and re-layouts: 5.85 us -> 16.2 us
  starting transfers between devices: 24.3 us -> 33.5 us
    ppermute x28 -> x30, waiting for transfers between devices: 145 us -> 125 us  [swap(): return lax.ppermute(x, axis, [(i, i ^ bits) for i in range(peers)])]
    pallas_call x3 -> x5, Pallas kernels: 8.59 us -> 24.4 us  [the longest x3 18.3 us: pack(): call(pack_kernel, like(len(pieces) * piece, depth), [anywhere] * len(piec...]
    unnamed x37 -> x79, local copies, waits for them, and re-layouts: 5.1 us -> 14.3 us
    ppermute x28 -> x30, starting transfers between devices: 22.7 us -> 27.7 us  [swap(): return lax.ppermute(x, axis, [(i, i ^ bits) for i in range(peers)])]
    all_to_all x0 -> x1, starting transfers between devices: none -> 4.26 us  [shards(): mine_cot = lax.all_to_all(send, 'tensor', 0, 0, tiled=True)]
    convert_element_type x5 -> x4, other arithmetic: 5.05 us -> 2.31 us  [the longest x2 1.14 us: scatter_sum(): other = (parts[2].astype(f32) + got3.astype(f32)).astype(bf16)]
  transfers between devices with their start and end apart: 29 -> 32, of which waited for: 15 -> 18; matrix products, arithmetic and copies ran while one was open for 2% -> 3% of each run, Pallas kernels for 9% -> 19%
where the time goes in v6:
time: 228 us
  waiting for transfers between devices  125 us (55%)
  Pallas kernels  46.1 us (20%)
  starting transfers between devices  33.5 us (15%)
  local copies, waits for them, and re-layouts  16.2 us (7%)
  other arithmetic  5.63 us (2%)
    ppermute x30, waiting for transfers between devices, swap(): return lax.ppermute(x, axis, [(i, i ^ bits) for i in range(peers)])  125 us
    ppermute x30, starting transfers between devices, swap(): return lax.ppermute(x, axis, [(i, i ^ bits) for i in range(peers)])  27.7 us
    pallas_call x3, Pallas kernels, pack(): call(pack_kernel, like(len(pieces) * piece, depth), [anywhere] * len(piec...  18.3 us
    unnamed x79, local copies, waits for them, and re-layouts  14.3 us
    pallas_call x1, Pallas kernels, shards(): call(functools.partial(update_kernel, count=count, tile=step, layout=layo...  9.37 us
    pallas_call x1, Pallas kernels, shards(): call(d_kernel, [like(piece, depth)] * 2 + [like(2, piece, depth)], [smem]...  5.2 us
    pallas_call x1, Pallas kernels, shards(): call(functools.partial(grad_kernel, tile=tile), like(piece, width), [smem...  4.69 us
    pallas_call x1, Pallas kernels, shards(): call(functools.partial(project_kernel, count=count, layout=layout), part_...  4.66 us
  transfers between devices with their start and end apart: 32, of which 18 were waited for; matrix products, arithmetic and copies ran while one was open for 3% of the time, Pallas kernels for 19%

profile of v6, /device:TPU:0, one launch (start us, length us, event | category | flops | bytes accessed | tf_op | source)
XLA Modules:
  0.0 227.8 jit_solution(6328926351310604409)
XLA Ops:
  0.7 3.1 %collective-permute-start = (bf16[2,256,256]{2,1,0:T(8,128)(2,1)}, bf16[2,256,256]{2,1,0:T(8,128)(2,1)S(1)}, u32[]{:S(2)}, u32[]{:S(2)}) collective-permute-start(bf16[2,256,256]{2,1,0:T(8,128)(2,1)} %bitcast.50), channel_id=1, source_target_pairs={{0,4},{4,0},{8,12},{12,8},{1,5},{5,1},{9,13},{13,9},{2,6},{6,2},{1... | collective-permute-start | bytes 786440 | tf_op jit(solution)/shard_map/ppermute | solution.py:29
  3.7 2.6 %collective-permute-start.1 = (bf16[2,256,256]{2,1,0:T(8,128)(2,1)}, bf16[2,256,256]{2,1,0:T(8,128)(2,1)S(1)}, u32[]{:S(2)}, u32[]{:S(2)}) collective-permute-start(bf16[2,256,256]{2,1,0:T(8,128)(2,1)} %bitcast.51), channel_id=1, source_target_pairs={{0,8},{4,12},{8,0},{12,4},{1,9},{5,13},{9,1},{13,5},{2,10},{6,14},... | collective-permute-start | bytes 786440 | tf_op jit(solution)/shard_map/ppermute | solution.py:29
  6.3 1.7 convert.4
  8.1 7.6 %collective-permute-done.refs_1_.other_ref = bf16[2,256,256]{2,1,0:T(8,128)(2,1)S(1)} collective-permute-done((bf16[2,256,256]{2,1,0:T(8,128)(2,1)}, bf16[2,256,256]{2,1,0:T(8,128)(2,1)S(1)}, u32[]{:S(2)}, u32[]{:S(2)}) %collective-permute-start) | collective-permute-done | bytes 262176 | tf_op jit(solution)/shard_map/ppermute | solution.py:29
  15.7 2.5 %collective-permute-done.1.refs_2_.mark_ref = bf16[2,256,256]{2,1,0:T(8,128)(2,1)S(1)} collective-permute-done((bf16[2,256,256]{2,1,0:T(8,128)(2,1)}, bf16[2,256,256]{2,1,0:T(8,128)(2,1)S(1)}, u32[]{:S(2)}, u32[]{:S(2)}) %collective-permute-start.1) | collective-permute-done | bytes 262176 | tf_op jit(solution)/shard_map/ppermute | solution.py:29
  18.3 2.9 %norm.1 = (bf16[128,2048]{1,0:T(8,128)(2,1)S(1)}, bf16[128,2048]{1,0:T(8,128)(2,1)S(1)}, bf16[128,2048]{1,0:T(8,128)(2,1)}, bf16[128,2048]{1,0:T(8,128)(2,1)S(1)}) custom-call(bf16[2,256,256]{2,1,0:T(8,128)(2,1)S(1)} %collective-permute-done.1.refs_2_.mark_ref, bf16[2,256,256]{2,1,0:T(8,128)(2,1)S(1)} %collective-permute-done.refs_1_.other_ref, ...), custom_call_target="tpu_custom_call" | custom-call | flops 1000 | bytes 1000 | tf_op jit(solution)/shard_map/norm/pallas_call | solution.py:294
  23.2 2.0 collective-permute-start.8
  27.3 5.9 %collective-permute-done.3.refs_1_ = bf16[128,2048]{1,0:T(8,128)(2,1)S(1)} collective-permute-done((bf16[128,2048]{1,0:T(8,128)(2,1)S(1)}, bf16[128,2048]{1,0:T(8,128)(2,1)S(1)}, u32[]{:S(2)}, u32[]{:S(2)}) %collective-permute-start.3) | collective-permute-done | bytes 524320 | tf_op jit(solution)/shard_map/ppermute | solution.py:29
  34.8 11.8 %collective-permute-done.5.refs_0_ = bf16[128,2048]{1,0:T(8,128)(2,1)} collective-permute-done((bf16[128,2048]{1,0:T(8,128)(2,1)S(1)}, bf16[128,2048]{1,0:T(8,128)(2,1)}, u32[]{:S(2)}, u32[]{:S(2)}) %collective-permute-start.5) | collective-permute-done | bytes 524320 | tf_op jit(solution)/shard_map/ppermute | solution.py:29
  47.2 1.9 collective-permute-done.8.refs_1_
  55.0 4.3 %all-to-all-start = ((bf16[4,512,256]{2,1,0:T(8,128)(2,1)}), bf16[4,512,256]{2,1,0:T(8,128)(2,1)}, u32[]{:S(2)}, u32[]{:S(2)}) async-start(bf16[4,512,256]{2,1,0:T(8,128)(2,1)} %copy-done.5), calls=%async_computation | async-start | bytes 2097152 | tf_op jit(solution)/shard_map/all_to_all | solution.py:316
  59.8 2.0 collective-permute-done.15.rest_5_
  61.8 11.2 %collective-permute-done.6.refs_1_ = bf16[128,2048]{1,0:T(8,128)(2,1)} collective-permute-done((bf16[128,2048]{1,0:T(8,128)(2,1)}, bf16[128,2048]{1,0:T(8,128)(2,1)}, u32[]{:S(2)}, u32[]{:S(2)}) %collective-permute-start.6) | collective-permute-done | bytes 524320 | tf_op jit(solution)/shard_map/ppermute | solution.py:29
  73.1 9.4 %collective-permute-done.9.refs_1_ = bf16[128,2048]{1,0:T(8,128)(2,1)} collective-permute-done((bf16[128,2048]{1,0:T(8,128)(2,1)S(1)}, bf16[128,2048]{1,0:T(8,128)(2,1)}, u32[]{:S(2)}, u32[]{:S(2)}) %collective-permute-start.9) | collective-permute-done | bytes 524320 | tf_op jit(solution)/shard_map/ppermute | solution.py:29
  84.6 17.0 %pack.5.rest_4_ = bf16[256,2048]{1,0:T(8,128)(2,1)} custom-call(bf16[128,2048]{1,0:T(8,128)(2,1)S(1)} %copy-done.15, bf16[128,2048]{1,0:T(8,128)(2,1)} %collective-permute-done.9.refs_1_), custom_call_target="tpu_custom_call" | custom-call | flops 1000 | bytes 1000 | tf_op jit(solution)/shard_map/pack/pallas_call | solution.py:326
  109.8 5.2 %d_normed.1 = (bf16[128,2048]{1,0:T(8,128)(2,1)S(1)}, bf16[128,2048]{1,0:T(8,128)(2,1)S(1)}, bf16[2,128,2048]{2,1,0:T(8,128)(2,1)}) custom-call(s32[2]{0:T(128)S(1)} %pad_add_fusion.where_ref, bf16[4,512,256]{2,1,0:T(8,128)(2,1)} %all-to-all-done.cot_ref, bf16[1024,256]{1,0:T(8,128)(2,1)S(1)} %copy-done.4, bf16[1024,256]{1,0:T(8,128)(2,1)} %get-tuple-element.56.rest_1_, ...), custom_call_target="tpu_custom_call" | custom-call | flops 1000 | bytes 1000 | tf_op jit(solution)/shard_map/d_normed/pallas_call | solution.py:317
  117.9 2.3 %collective-permute-start.25 = (bf16[2,128,2048]{2,1,0:T(8,128)(2,1)}, bf16[2,128,2048]{2,1,0:T(8,128)(2,1)}, u32[]{:S(2)}, u32[]{:S(2)}) collective-permute-start(bf16[2,128,2048]{2,1,0:T(8,128)(2,1)} %get-tuple-element.47), channel_id=1, source_target_pairs={{0,8},{4,12},{8,0},{12,4},{1,9},{5,13},{9,1},{13,5},{2,10},{6,14},... | collective-permute-start | bytes 3145736 | tf_op jit(solution)/shard_map/ppermute | solution.py:29
  120.1 10.7 %collective-permute-done.18.rest_7_ = bf16[128,2048]{1,0:T(8,128)(2,1)S(1)} collective-permute-done((bf16[128,2048]{1,0:T(8,128)(2,1)}, bf16[128,2048]{1,0:T(8,128)(2,1)S(1)}, u32[]{:S(2)}, u32[]{:S(2)}) %collective-permute-start.18) | collective-permute-done | bytes 524320 | tf_op jit(solution)/shard_map/ppermute | solution.py:29
  130.8 1.9 collective-permute-done.20.rest_9_
  132.7 9.4 %update.1 = (f32[2048,256]{1,0:T(8,128)}, bf16[512,256]{1,0:T(8,128)(2,1)S(1)}, bf16[512,256]{1,0:T(8,128)(2,1)S(1)}, bf16[512,256]{1,0:T(8,128)(2,1)S(1)}, bf16[512,256]{1,0:T(8,128)(2,1)}) custom-call(bf16[256,2048]{1,0:T(8,128)(2,1)S(1)} %copy-done.20, f32[2048,256]{1,0:T(8,128)S(1)} %bitcast.41, f32[2048,256]{1,0:T(8,128)S(1)} %bitcast.44, ...), custom_call_target="tpu_custom_call" | custom-call | flops 1000 | bytes 1000 | tf_op jit(solution)/shard_map/update/pallas_call | solution.py:353
  143.5 2.0 collective-permute-start.27
  147.0 2.1 collective-permute-start.24
  149.1 4.7 %project.1 = (bf16[512,256]{1,0:T(8,128)(2,1)S(1)}, bf16[512,256]{1,0:T(8,128)(2,1)S(1)}, bf16[512,256]{1,0:T(8,128)(2,1)S(1)}, bf16[512,256]{1,0:T(8,128)(2,1)S(1)}) custom-call(bf16[512,256]{1,0:T(8,128)(2,1)S(1)} %get-tuple-element.40.mark_ref.refs_1_, bf16[2048,256]{1,0:T(8,128)(2,1)S(1)} %pad_maximum_fusion.weights_ref, ...), custom_call_target="tpu_custom_call" | custom-call | flops 1000 | bytes 1000 | tf_op jit(solution)/shard_map/project/pallas_call | solution.py:380
  154.1 12.3 %collective-permute-done.25.refs_2_.rest_2_ = bf16[2,128,2048]{2,1,0:T(8,128)(2,1)} collective-permute-done((bf16[2,128,2048]{2,1,0:T(8,128)(2,1)}, bf16[2,128,2048]{2,1,0:T(8,128)(2,1)}, u32[]{:S(2)}, u32[]{:S(2)}) %collective-permute-start.25) | collective-permute-done | bytes 1048608 | tf_op jit(solution)/shard_map/ppermute | solution.py:29
  166.4 5.6 %collective-permute-done.27.refs_0_ = bf16[512,256]{1,0:T(8,128)(2,1)} collective-permute-done((bf16[512,256]{1,0:T(8,128)(2,1)S(1)}, bf16[512,256]{1,0:T(8,128)(2,1)}, u32[]{:S(2)}, u32[]{:S(2)}) %collective-permute-start.27) | collective-permute-done | bytes 262176 | tf_op jit(solution)/shard_map/ppermute | solution.py:29
  172.0 5.6 %collective-permute-done.28.refs_1_ = bf16[512,256]{1,0:T(8,128)(2,1)} collective-permute-done((bf16[512,256]{1,0:T(8,128)(2,1)}, bf16[512,256]{1,0:T(8,128)(2,1)}, u32[]{:S(2)}, u32[]{:S(2)}) %collective-permute-start.28) | collective-permute-done | bytes 262176 | tf_op jit(solution)/shard_map/ppermute | solution.py:29
  180.4 2.5 %collective-permute-start.21 = (bf16[512,256]{1,0:T(8,128)(2,1)S(1)}, bf16[512,256]{1,0:T(8,128)(2,1)S(1)}, u32[]{:S(2)}, u32[]{:S(2)}) collective-permute-start(bf16[512,256]{1,0:T(8,128)(2,1)S(1)} %get-tuple-element.42), channel_id=1, source_target_pairs={{0,4},{4,0},{8,12},{12,8},{1,5},{5,1},{9,13},{13,9},{2,6},{6,2},{1... | collective-permute-start | bytes 786440 | tf_op jit(solution)/shard_map/ppermute | solution.py:29
  183.1 16.9 %collective-permute-done.22 = bf16[512,256]{1,0:T(8,128)(2,1)S(1)} collective-permute-done((bf16[512,256]{1,0:T(8,128)(2,1)S(1)}, bf16[512,256]{1,0:T(8,128)(2,1)S(1)}, u32[]{:S(2)}, u32[]{:S(2)}) %collective-permute-start.22) | collective-permute-done | bytes 262176 | tf_op jit(solution)/shard_map/ppermute | solution.py:29
  203.4 3.2 %collective-permute-done.21 = bf16[512,256]{1,0:T(8,128)(2,1)S(1)} collective-permute-done((bf16[512,256]{1,0:T(8,128)(2,1)S(1)}, bf16[512,256]{1,0:T(8,128)(2,1)S(1)}, u32[]{:S(2)}, u32[]{:S(2)}) %collective-permute-start.21) | collective-permute-done | bytes 262176 | tf_op jit(solution)/shard_map/ppermute | solution.py:29
  206.7 8.3 %collective-permute-done.23 = bf16[512,256]{1,0:T(8,128)(2,1)S(1)} collective-permute-done((bf16[512,256]{1,0:T(8,128)(2,1)S(1)}, bf16[512,256]{1,0:T(8,128)(2,1)S(1)}, u32[]{:S(2)}, u32[]{:S(2)}) %collective-permute-start.23) | collective-permute-done | bytes 262176 | tf_op jit(solution)/shard_map/ppermute | solution.py:29
  215.2 7.2 %collective-permute-done.26.refs_1_ = bf16[128,2048]{1,0:T(8,128)(2,1)S(1)} collective-permute-done((bf16[128,2048]{1,0:T(8,128)(2,1)S(1)}, bf16[128,2048]{1,0:T(8,128)(2,1)S(1)}, u32[]{:S(2)}, u32[]{:S(2)}) %collective-permute-start.26) | collective-permute-done | bytes 524320 | tf_op jit(solution)/shard_map/ppermute | solution.py:29
  222.4 4.7 %grad_in.1 = bf16[128,8192]{1,0:T(8,128)(2,1)} custom-call(s32[2]{0:T(128)S(1)} %pad_add_fusion.where_ref, bf16[128,8192]{1,0:T(8,128)(2,1)S(1)} %bitcast.43, f32[1,8192]{1,0:T(1,128)S(1)} %copy-done.36, bf16[128,2048]{1,0:T(8,128)(2,1)S(1)} %copy-done.22, bf16[128,2048]{1,0:T(8,128)(2,1)S(1)} %get-tuple-element.53.rest_1_, ...), custom_call_target="tpu_custom_call" | custom-call | flops 1000 | bytes 1000 | tf_op jit(solution)/shard_map/grad_in/pallas_call | solution.py:392
  (139 shorter events, 36.2 us)
Async XLA Ops:
  0.7 15.1 %collective-permute-start = (bf16[2,256,256]{2,1,0:T(8,128)(2,1)}, bf16[2,256,256]{2,1,0:T(8,128)(2,1)S(1)}, u32[]{:S(2)}, u32[]{:S(2)}) collective-permute-start(bf16[2,256,256]{2,1,0:T(8,128)(2,1)} %bitcast.50), channel_id=1, source_target_pairs={{0,4},{4,0},{8,12},{12,8},{1,5},{5,1},{9,13},{13,9},{2,6},{6,2},{1... | collective-permute-start | bytes 786440 | tf_op jit(solution)/shard_map/ppermute | solution.py:29
  3.7 14.6 %collective-permute-start.1 = (bf16[2,256,256]{2,1,0:T(8,128)(2,1)}, bf16[2,256,256]{2,1,0:T(8,128)(2,1)S(1)}, u32[]{:S(2)}, u32[]{:S(2)}) collective-permute-start(bf16[2,256,256]{2,1,0:T(8,128)(2,1)} %bitcast.51), channel_id=1, source_target_pairs={{0,8},{4,12},{8,0},{12,4},{1,9},{5,13},{9,1},{13,5},{2,10},{6,14},... | collective-permute-start | bytes 786440 | tf_op jit(solution)/shard_map/ppermute | solution.py:29
  21.2 12.0 %collective-permute-start.3 = (bf16[128,2048]{1,0:T(8,128)(2,1)S(1)}, bf16[128,2048]{1,0:T(8,128)(2,1)S(1)}, u32[]{:S(2)}, u32[]{:S(2)}) collective-permute-start(bf16[128,2048]{1,0:T(8,128)(2,1)S(1)} %get-tuple-element.31.refs_0_), channel_id=1, source_target_pairs={{0,2},{1,3},{2,0},{3,1},{4,6},{5,7},{6,4},{7,5},{8,10},{9,11},{10,... | collective-permute-start | bytes 1572872 | tf_op jit(solution)/shard_map/ppermute | solution.py:29
  22.8 23.9 %collective-permute-start.5 = (bf16[128,2048]{1,0:T(8,128)(2,1)S(1)}, bf16[128,2048]{1,0:T(8,128)(2,1)}, u32[]{:S(2)}, u32[]{:S(2)}) collective-permute-start(bf16[128,2048]{1,0:T(8,128)(2,1)S(1)} %get-tuple-element.32), channel_id=1, source_target_pairs={{0,4},{4,0},{8,12},{12,8},{1,5},{5,1},{9,13},{13,9},{2,6},{6,2},{1... | collective-permute-start | bytes 1572872 | tf_op jit(solution)/shard_map/ppermute | solution.py:29
  23.2 25.9 %collective-permute-start.8 = (bf16[128,2048]{1,0:T(8,128)(2,1)S(1)}, bf16[128,2048]{1,0:T(8,128)(2,1)S(1)}, u32[]{:S(2)}, u32[]{:S(2)}) collective-permute-start(bf16[128,2048]{1,0:T(8,128)(2,1)S(1)} %get-tuple-element.34), channel_id=1, source_target_pairs={{0,12},{4,8},{8,4},{12,0},{1,13},{5,9},{9,5},{13,1},{2,14},{6,10},... | collective-permute-start | bytes 1572872 | tf_op jit(solution)/shard_map/ppermute | solution.py:29
  26.1 25.2 %collective-permute-start.12 = (bf16[1024,256]{1,0:T(8,128)(2,1)S(1)}, bf16[1024,256]{1,0:T(8,128)(2,1)S(1)}, u32[]{:S(2)}, u32[]{:S(2)}) collective-permute-start(bf16[1024,256]{1,0:T(8,128)(2,1)S(1)} %get-tuple-element.57.rest_0_), channel_id=1, source_target_pairs={{0,1},{1,0},{2,3},{3,2},{4,5},{5,4},{6,7},{7,6},{8,9},{9,8},{10,11... | collective-permute-start | bytes 1572872 | tf_op jit(solution)/shard_map/ppermute | solution.py:29
  26.2 24.6 %collective-permute-start.2 = (bf16[2,256,256]{2,1,0:T(8,128)(2,1)S(1)}, bf16[2,256,256]{2,1,0:T(8,128)(2,1)S(1)}, u32[]{:S(2)}, u32[]{:S(2)}) collective-permute-start(bf16[2,256,256]{2,1,0:T(8,128)(2,1)S(1)} %copy-done.17), channel_id=1, source_target_pairs={{0,4},{4,0},{8,12},{12,8},{1,5},{5,1},{9,13},{13,9},{2,6},{6,2},{1... | collective-permute-start | bytes 786440 | tf_op jit(solution)/shard_map/ppermute | solution.py:29
  33.2 26.0 %collective-permute-start.14 = (bf16[1024,256]{1,0:T(8,128)(2,1)S(1)}, bf16[1024,256]{1,0:T(8,128)(2,1)}, u32[]{:S(2)}, u32[]{:S(2)}) collective-permute-start(bf16[1024,256]{1,0:T(8,128)(2,1)S(1)} %get-tuple-element.57.rest_0_), channel_id=1, source_target_pairs={{0,2},{1,3},{2,0},{3,1},{4,6},{5,7},{6,4},{7,5},{8,10},{9,11},{10,... | collective-permute-start | bytes 1572872 | tf_op jit(solution)/shard_map/ppermute | solution.py:29
  46.7 15.2 %collective-permute-start.15 = (bf16[1024,256]{1,0:T(8,128)(2,1)}, bf16[1024,256]{1,0:T(8,128)(2,1)}, u32[]{:S(2)}, u32[]{:S(2)}) collective-permute-start(bf16[1024,256]{1,0:T(8,128)(2,1)} %get-tuple-element.56.rest_1_), channel_id=1, source_target_pairs={{0,2},{1,3},{2,0},{3,1},{4,6},{5,7},{6,4},{7,5},{8,10},{9,11},{10,... | collective-permute-start | bytes 1572872 | tf_op jit(solution)/shard_map/ppermute | solution.py:29
  49.1 24.0 %collective-permute-start.6 = (bf16[128,2048]{1,0:T(8,128)(2,1)}, bf16[128,2048]{1,0:T(8,128)(2,1)}, u32[]{:S(2)}, u32[]{:S(2)}) collective-permute-start(bf16[128,2048]{1,0:T(8,128)(2,1)} %collective-permute-done.5.refs_0_), channel_id=1, source_target_pairs={{0,2},{1,3},{2,0},{3,1},{4,6},{5,7},{6,4},{7,5},{8,10},{9,11},{10,... | collective-permute-start | bytes 1572872 | tf_op jit(solution)/shard_map/ppermute | solution.py:29
  50.8 31.7 %collective-permute-start.9 = (bf16[128,2048]{1,0:T(8,128)(2,1)S(1)}, bf16[128,2048]{1,0:T(8,128)(2,1)}, u32[]{:S(2)}, u32[]{:S(2)}) collective-permute-start(bf16[128,2048]{1,0:T(8,128)(2,1)S(1)} %get-tuple-element.35.refs_0_), channel_id=1, source_target_pairs={{0,2},{1,3},{2,0},{3,1},{4,6},{5,7},{6,4},{7,5},{8,10},{9,11},{10,... | collective-permute-start | bytes 1572872 | tf_op jit(solution)/shard_map/ppermute | solution.py:29
  52.1 64.6 %collective-permute-start.4 = (bf16[256,2048]{1,0:T(8,128)(2,1)S(1)}, bf16[256,2048]{1,0:T(8,128)(2,1)S(1)}, u32[]{:S(2)}, u32[]{:S(2)}) collective-permute-start(bf16[256,2048]{1,0:T(8,128)(2,1)S(1)} %pack.3.rest_0_), channel_id=1, source_target_pairs={{0,1},{1,0},{2,3},{3,2},{4,5},{5,4},{6,7},{7,6},{8,9},{9,8},{10,11... | collective-permute-start | bytes 3145736 | tf_op jit(solution)/shard_map/ppermute | solution.py:29
  55.0 49.6 %all-to-all-start = ((bf16[4,512,256]{2,1,0:T(8,128)(2,1)}), bf16[4,512,256]{2,1,0:T(8,128)(2,1)}, u32[]{:S(2)}, u32[]{:S(2)}) async-start(bf16[4,512,256]{2,1,0:T(8,128)(2,1)} %copy-done.5), calls=%async_computation | async-start | bytes 2097152 | tf_op jit(solution)/shard_map/all_to_all | solution.py:316
  59.2 42.4 %collective-permute-start.13 = (bf16[1024,256]{1,0:T(8,128)(2,1)}, bf16[1024,256]{1,0:T(8,128)(2,1)S(1)}, u32[]{:S(2)}, u32[]{:S(2)}) collective-permute-start(bf16[1024,256]{1,0:T(8,128)(2,1)} %get-tuple-element.56.rest_1_), channel_id=1, source_target_pairs={{0,1},{1,0},{2,3},{3,2},{4,5},{5,4},{6,7},{7,6},{8,9},{9,8},{10,11... | collective-permute-start | bytes 1572872 | tf_op jit(solution)/shard_map/ppermute | solution.py:29
  61.8 40.6 %collective-permute-start.16 = (bf16[1024,256]{1,0:T(8,128)(2,1)}, bf16[1024,256]{1,0:T(8,128)(2,1)S(1)}, u32[]{:S(2)}, u32[]{:S(2)}) collective-permute-start(bf16[1024,256]{1,0:T(8,128)(2,1)} %collective-permute-done.14.rest_4_), channel_id=1, source_target_pairs={{0,1},{1,0},{2,3},{3,2},{4,5},{5,4},{6,7},{7,6},{8,9},{9,8},{10,11... | collective-permute-start | bytes 1572872 | tf_op jit(solution)/shard_map/ppermute | solution.py:29
  73.1 30.7 %collective-permute-start.17 = (bf16[1024,256]{1,0:T(8,128)(2,1)}, bf16[1024,256]{1,0:T(8,128)(2,1)S(1)}, u32[]{:S(2)}, u32[]{:S(2)}) collective-permute-start(bf16[1024,256]{1,0:T(8,128)(2,1)} %collective-permute-done.15.rest_5_), channel_id=1, source_target_pairs={{0,1},{1,0},{2,3},{3,2},{4,5},{5,4},{6,7},{7,6},{8,9},{9,8},{10,11... | collective-permute-start | bytes 1572872 | tf_op jit(solution)/shard_map/ppermute | solution.py:29
  82.5 34.2 %collective-permute-start.11 = (bf16[128,2048]{1,0:T(8,128)(2,1)}, bf16[128,2048]{1,0:T(8,128)(2,1)}, u32[]{:S(2)}, u32[]{:S(2)}) collective-permute-start(bf16[128,2048]{1,0:T(8,128)(2,1)} %get-tuple-element.36.refs_1_), channel_id=1, source_target_pairs={{0,8},{4,12},{8,0},{12,4},{1,9},{5,13},{9,1},{13,5},{2,10},{6,14},... | collective-permute-start | bytes 1572872 | tf_op jit(solution)/shard_map/ppermute | solution.py:29
  102.5 28.3 %collective-permute-start.7 = (bf16[256,2048]{1,0:T(8,128)(2,1)S(1)}, bf16[256,2048]{1,0:T(8,128)(2,1)}, u32[]{:S(2)}, u32[]{:S(2)}) collective-permute-start(bf16[256,2048]{1,0:T(8,128)(2,1)S(1)} %pack.4.rest_2_), channel_id=1, source_target_pairs={{0,1},{1,0},{2,3},{3,2},{4,5},{5,4},{6,7},{7,6},{8,9},{9,8},{10,11... | collective-permute-start | bytes 3145736 | tf_op jit(solution)/shard_map/ppermute | solution.py:29
  103.3 27.5 %collective-permute-start.10 = (bf16[256,2048]{1,0:T(8,128)(2,1)}, bf16[256,2048]{1,0:T(8,128)(2,1)}, u32[]{:S(2)}, u32[]{:S(2)}) collective-permute-start(bf16[256,2048]{1,0:T(8,128)(2,1)} %pack.5.rest_4_), channel_id=1, source_target_pairs={{0,1},{1,0},{2,3},{3,2},{4,5},{5,4},{6,7},{7,6},{8,9},{9,8},{10,11... | collective-permute-start | bytes 3145736 | tf_op jit(solution)/shard_map/ppermute | solution.py:29
  116.7 14.1 %collective-permute-start.18 = (bf16[128,2048]{1,0:T(8,128)(2,1)}, bf16[128,2048]{1,0:T(8,128)(2,1)S(1)}, u32[]{:S(2)}, u32[]{:S(2)}) collective-permute-start(bf16[128,2048]{1,0:T(8,128)(2,1)} %get-tuple-element.39.rest_6_), channel_id=1, source_target_pairs={{0,2},{1,3},{2,0},{3,1},{4,6},{5,7},{6,4},{7,5},{8,10},{9,11},{10,... | collective-permute-start | bytes 1572872 | tf_op jit(solution)/shard_map/ppermute | solution.py:29
  117.9 48.6 %collective-permute-start.25 = (bf16[2,128,2048]{2,1,0:T(8,128)(2,1)}, bf16[2,128,2048]{2,1,0:T(8,128)(2,1)}, u32[]{:S(2)}, u32[]{:S(2)}) collective-permute-start(bf16[2,128,2048]{2,1,0:T(8,128)(2,1)} %get-tuple-element.47), channel_id=1, source_target_pairs={{0,8},{4,12},{8,0},{12,4},{1,9},{5,13},{9,1},{13,5},{2,10},{6,14},... | collective-permute-start | bytes 3145736 | tf_op jit(solution)/shard_map/ppermute | solution.py:29
  120.1 10.7 %collective-permute-start.19 = (bf16[128,2048]{1,0:T(8,128)(2,1)}, bf16[128,2048]{1,0:T(8,128)(2,1)S(1)}, u32[]{:S(2)}, u32[]{:S(2)}) collective-permute-start(bf16[128,2048]{1,0:T(8,128)(2,1)} %get-tuple-element.39.rest_6_), channel_id=1, source_target_pairs={{0,1},{1,0},{2,3},{3,2},{4,5},{5,4},{6,7},{7,6},{8,9},{9,8},{10,11... | collective-permute-start | bytes 1572872 | tf_op jit(solution)/shard_map/ppermute | solution.py:29
  130.8 1.9 collective-permute-start.20
  143.5 28.4 %collective-permute-start.27 = (bf16[512,256]{1,0:T(8,128)(2,1)S(1)}, bf16[512,256]{1,0:T(8,128)(2,1)}, u32[]{:S(2)}, u32[]{:S(2)}) collective-permute-start(bf16[512,256]{1,0:T(8,128)(2,1)S(1)} %get-tuple-element.40.mark_ref.refs_1_), channel_id=1, source_target_pairs={{0,4},{4,0},{8,12},{12,8},{1,5},{5,1},{9,13},{13,9},{2,6},{6,2},{1... | collective-permute-start | bytes 786440 | tf_op jit(solution)/shard_map/ppermute | solution.py:29
  145.5 32.1 %collective-permute-start.28 = (bf16[512,256]{1,0:T(8,128)(2,1)}, bf16[512,256]{1,0:T(8,128)(2,1)}, u32[]{:S(2)}, u32[]{:S(2)}) collective-permute-start(bf16[512,256]{1,0:T(8,128)(2,1)} %get-tuple-element.49), channel_id=1, source_target_pairs={{0,4},{4,0},{8,12},{12,8},{1,5},{5,1},{9,13},{13,9},{2,6},{6,2},{1... | collective-permute-start | bytes 786440 | tf_op jit(solution)/shard_map/ppermute | solution.py:29
  147.0 68.1 %collective-permute-start.24 = (bf16[128,2048]{1,0:T(8,128)(2,1)S(1)}, bf16[128,2048]{1,0:T(8,128)(2,1)S(1)}, u32[]{:S(2)}, u32[]{:S(2)}) collective-permute-start(bf16[128,2048]{1,0:T(8,128)(2,1)S(1)} %copy-done.38), channel_id=1, source_target_pairs={{0,4},{4,0},{8,12},{12,8},{1,5},{5,1},{9,13},{13,9},{2,6},{6,2},{1... | collective-permute-start | bytes 1572872 | tf_op jit(solution)/shard_map/ppermute | solution.py:29
  153.8 46.2 %collective-permute-start.22 = (bf16[512,256]{1,0:T(8,128)(2,1)S(1)}, bf16[512,256]{1,0:T(8,128)(2,1)S(1)}, u32[]{:S(2)}, u32[]{:S(2)}) collective-permute-start(bf16[512,256]{1,0:T(8,128)(2,1)S(1)} %get-tuple-element.44), channel_id=1, source_target_pairs={{0,4},{4,0},{8,12},{12,8},{1,5},{5,1},{9,13},{13,9},{2,6},{6,2},{1... | collective-permute-start | bytes 786440 | tf_op jit(solution)/shard_map/ppermute | solution.py:29
  178.7 22.0 %collective-permute-start.29 = (bf16[512,256]{1,0:T(8,128)(2,1)S(1)}, bf16[512,256]{1,0:T(8,128)(2,1)S(1)}, u32[]{:S(2)}, u32[]{:S(2)}) collective-permute-start(bf16[512,256]{1,0:T(8,128)(2,1)S(1)} %add_convert_fusion.1), channel_id=1, source_target_pairs={{0,8},{4,12},{8,0},{12,4},{1,9},{5,13},{9,1},{13,5},{2,10},{6,14},... | collective-permute-start | bytes 786440 | tf_op jit(solution)/shard_map/ppermute | solution.py:29
  180.4 26.2 %collective-permute-start.21 = (bf16[512,256]{1,0:T(8,128)(2,1)S(1)}, bf16[512,256]{1,0:T(8,128)(2,1)S(1)}, u32[]{:S(2)}, u32[]{:S(2)}) collective-permute-start(bf16[512,256]{1,0:T(8,128)(2,1)S(1)} %get-tuple-element.42), channel_id=1, source_target_pairs={{0,4},{4,0},{8,12},{12,8},{1,5},{5,1},{9,13},{13,9},{2,6},{6,2},{1... | collective-permute-start | bytes 786440 | tf_op jit(solution)/shard_map/ppermute | solution.py:29
  183.0 39.4 %collective-permute-start.26 = (bf16[128,2048]{1,0:T(8,128)(2,1)S(1)}, bf16[128,2048]{1,0:T(8,128)(2,1)S(1)}, u32[]{:S(2)}, u32[]{:S(2)}) collective-permute-start(bf16[128,2048]{1,0:T(8,128)(2,1)S(1)} %after.9), channel_id=1, source_target_pairs={{0,4},{4,0},{8,12},{12,8},{1,5},{5,1},{9,13},{13,9},{2,6},{6,2},{1... | collective-permute-start | bytes 1572872 | tf_op jit(solution)/shard_map/ppermute | solution.py:29
  200.1 14.9 %collective-permute-start.23 = (bf16[512,256]{1,0:T(8,128)(2,1)S(1)}, bf16[512,256]{1,0:T(8,128)(2,1)S(1)}, u32[]{:S(2)}, u32[]{:S(2)}) collective-permute-start(bf16[512,256]{1,0:T(8,128)(2,1)S(1)} %add_convert_fusion.3), channel_id=1, source_target_pairs={{0,8},{4,12},{8,0},{12,4},{1,9},{5,13},{9,1},{13,5},{2,10},{6,14},... | collective-permute-start | bytes 786440 | tf_op jit(solution)/shard_map/ppermute | solution.py:29
  201.9 25.2 %collective-permute-start.30 = (bf16[1,2,256,256]{3,2,1,0:T(8,128)(2,1)S(1)}, bf16[1,2,256,256]{3,2,1,0:T(8,128)(2,1)S(1)}, u32[]{:S(2)}, u32[]{:S(2)}) collective-permute-start(bf16[1,2,256,256]{3,2,1,0:T(8,128)(2,1)S(1)} %bitcast.46), channel_id=1, source_target_pairs={{0,16},{16,0},{1,17},{17,1},{2,18},{18,2},{3,19},{19,3},{4,20},{20... | collective-permute-start | bytes 786440 | tf_op jit(solution)/shard_map/ppermute | solution.py:34
  (39 other events, 373.8 us)

commit v7 on v6

--- a/solution.py
+++ b/solution.py
@@ -93,29 +93,27 @@
             ).astype(bf16)
 
 
-def grad_kernel(where_ref, hidden_ref, gain_ref, *rest, tile):
-    d0_ref, d1_ref, d23_ref, d3_ref, out_ref = rest
-    d_refs = (d0_ref, d1_ref, d23_ref.at[0], d3_ref)
-    z = where_ref[0]
+def grad_kernel(hidden_ref, gain_ref, d_ref, out_ref, *, tile):
     rows, width = hidden_ref.shape
-    depth = width // len(d_refs)
+    blocks = d_ref.shape[0]
+    depth = width // blocks
 
     @pl.loop(0, rows // tile)
     def _(i):
         at = pl.ds(pl.multiple_of(i * tile, tile), tile)
         squares = jnp.zeros((tile, 1), f32)
         cross = jnp.zeros((tile, 1), f32)
-        for k, d_ref in enumerate(d_refs):
-            cut = lanes(z ^ k, depth)
+        for k in range(blocks):
+            cut = slice(k * depth, (k + 1) * depth)
             hidden = hidden_ref[at, cut].astype(f32)
             squares += jnp.sum(hidden * hidden, axis=-1, keepdims=True)
-            upper = d_ref[at, :].astype(f32) * gain_ref[:, cut]
+            upper = d_ref[k, at, :].astype(f32) * gain_ref[:, cut]
             cross += jnp.sum(upper * hidden, axis=-1, keepdims=True)
         scaling = lax.rsqrt(squares * (1.0 / width) + norm_eps)
         factor = scaling * scaling * scaling * (cross * (1.0 / width))
-        for k, d_ref in enumerate(d_refs):
-            cut = lanes(z ^ k, depth)
-            upper = d_ref[at, :].astype(f32) * gain_ref[:, cut]
+        for k in range(blocks):
+            cut = slice(k * depth, (k + 1) * depth)
+            upper = d_ref[k, at, :].astype(f32) * gain_ref[:, cut]
             hidden = hidden_ref[at, cut].astype(f32)
             out_ref[at, cut] = (scaling * upper - hidden * factor).astype(bf16)
 
@@ -139,20 +137,19 @@
 
 
 def d_kernel(where_ref, cot_ref, *rest):
-    w_refs, (d0_ref, d1_ref, d23_ref) = rest[:8], rest[8:]
-    rows = d0_ref.shape[0]
+    w_refs, d_ref = rest[:8], rest[8]
+    z, t = where_ref[0], where_ref[1]
+    dp, rows = d_ref.shape[:2]
     half = w_refs[0].shape[0]
     tile = min(half, 512)
-    targets = (d0_ref, d1_ref, d23_ref.at[0], d23_ref.at[1])
-    t = where_ref[1]
     cot = jnp.concatenate([cot_ref[t ^ j] for j in range(cot_ref.shape[0])], axis=1)
     for side in range(2):
         for i in range(half // tile):
             cut = slice(i * tile, (i + 1) * tile)
             whole = jnp.concatenate([w[cut, :] for w in w_refs[side::2]], axis=1)
             part = dot(cot, whole, ((1,), (1,))).astype(bf16)
-            for k, target in enumerate(targets):
-                target[:, side * half + i * tile : side * half + (i + 1) * tile] = part[
+            for k in range(dp):
+                d_ref[z ^ k, :, side * half + i * tile : side * half + (i + 1) * tile] = part[
                     k * rows : (k + 1) * rows
                 ]
 
@@ -314,14 +311,6 @@
     n2 = swap(own2, "dp", 2)
     (send,) = after([send], own2)
     mine_cot = lax.all_to_all(send, "tensor", 0, 0, tiled=True)
-    d0, d1, d23 = call(
-        d_kernel,
-        [like(piece, depth)] * 2 + [like(2, piece, depth)],
-        [smem] + [vmem] * 9,
-        [vmem] * 3,
-        20,
-        "d_normed",
-    )(where, mine_cot, *w0, *w1, *w2, *w3)
     def pack(*pieces):
         return call(
             pack_kernel,
@@ -337,10 +326,16 @@
     for x in (own[0], n1, n3):
         near = pack(x, swap(x, "tensor", 2))
         tokens += [near, swap(near, "tensor", 1)]
-    n2, d23 = after([n2, d23], tokens[1])
-    d23 = swap(d23, "dp", 2)
-    d1 = swap(d1, "dp", 1)
-
+    d = call(
+        d_kernel,
+        like(dp, piece, depth),
+        [smem] + [vmem] * 9,
+        vmem,
+        20,
+        "d_normed",
+    )(where, mine_cot, *w0, *w1, *w2, *w3)
+    n2, d = after([n2, d], tokens[1])
+    d = lax.all_to_all(d, "dp", 0, 0, tiled=True)
     across = swap(n2, "tensor", 2)
     tokens += [n2, across, swap(n2, "tensor", 1), swap(across, "tensor", 1)]
     count = len(tokens)
@@ -375,7 +370,7 @@
             1, micro, tensor * rows, cols
         )
 
-    mine = place(scatter_sum(parts, d23).astype(bf16))
+    mine = place(scatter_sum(parts).astype(bf16))
     kv_next = from_behind(mine, "segment", -1)
     own_parts = call(
         functools.partial(project_kernel, count=count, layout=layout),
@@ -387,16 +382,15 @@
         scratch=[all_tokens, pltpu.SemaphoreType.DMA((count,))],
     )(parts[1], jnp.concatenate(w0), *tokens)
     kv_own = place(scatter_sum(own_parts).astype(bf16))
-    d3 = swap(after([d23[1]], parts[1])[0], "dp", 1)
-    d1, d3 = after([d1, d3], mine, kv_own)
+    (d,) = after([d], mine, kv_own)
     grad_in = call(
         functools.partial(grad_kernel, tile=tile),
         like(piece, width),
-        [smem] + [vmem] * 6,
+        [vmem] * 3,
         vmem,
         12,
         "grad_in",
-    )(where, hidden, norm_gain, d0, d1, d23, d3)
+    )(hidden, norm_gain, d)
     return (kv_own, grad_in.reshape(hidden_in.shape), master_new[None], kv_next)
 
 

time: 228 us -> 184 us (0.81)
  waiting for transfers between devices: 125 us -> 99.4 us
  Pallas kernels: 46.1 us -> 28.9 us
    ppermute x30 -> x27, waiting for transfers between devices: 125 us -> 90.4 us  [swap(): return lax.ppermute(x, axis, [(i, i ^ bits) for i in range(peers)])]
    pallas_call x3, Pallas kernels: 18.3 us -> 3.51 us  [pack(): call(pack_kernel, like(len(pieces) * piece, depth), [anywhere] * len(piec...]
    all_to_all x1, waiting for transfers between devices: 0.01 us -> 9.02 us  [shards(): mine_cot = lax.all_to_all(send, 'tensor', 0, 0, tiled=True)]
    all_to_all x0 -> x1, starting transfers between devices: none -> 3.79 us  [shards(): d = lax.all_to_all(d, 'dp', 0, 0, tiled=True)]
    pallas_call x2, Pallas kernels: 9.9 us -> 7.38 us  [the longest x1 4.04 us: shards(): call(d_kernel, like(dp, piece, depth), [smem] + [vmem] * 9, vmem, 20, 'd_...]
    ppermute x30 -> x27, starting transfers between devices: 27.7 us -> 26.3 us  [swap(): return lax.ppermute(x, axis, [(i, i ^ bits) for i in range(peers)])]
    unnamed x79 -> x59, local copies, waits for them, and re-layouts: 14.3 us -> 14.7 us
  transfers between devices with their start and end apart: 32 -> 30, of which waited for: 18 -> 16; matrix products, arithmetic and copies ran while one was open for 3% -> 2% of each run, Pallas kernels for 19% -> 12%
where the time goes in v7:
time: 184 us
  waiting for transfers between devices  99.4 us (54%)
  starting transfers between devices  35.1 us (19%)
  Pallas kernels  28.9 us (16%)
  local copies, waits for them, and re-layouts  14.8 us (8%)
  other arithmetic  4.36 us (2%)
    ppermute x27, waiting for transfers between devices, swap(): return lax.ppermute(x, axis, [(i, i ^ bits) for i in range(peers)])  90.4 us
    ppermute x27, starting transfers between devices, swap(): return lax.ppermute(x, axis, [(i, i ^ bits) for i in range(peers)])  26.3 us
    unnamed x59, local copies, waits for them, and re-layouts  14.7 us
    all_to_all x1, waiting for transfers between devices, shards(): mine_cot = lax.all_to_all(send, 'tensor', 0, 0, tiled=True)  9.02 us
    pallas_call x1, Pallas kernels, shards(): call(functools.partial(update_kernel, count=count, tile=step, layout=layo...  8.86 us
    pallas_call x1, Pallas kernels, shards(): call(functools.partial(project_kernel, count=count, layout=layout), part_...  4.37 us
    pallas_call x1, Pallas kernels, shards(): call(d_kernel, like(dp, piece, depth), [smem] + [vmem] * 9, vmem, 20, 'd_...  4.04 us
    all_to_all x1, starting transfers between devices, shards(): d = lax.all_to_all(d, 'dp', 0, 0, tiled=True)  3.79 us
  transfers between devices with their start and end apart: 30, of which 16 were waited for; matrix products, arithmetic and copies ran while one was open for 2% of the time, Pallas kernels for 12%

profile of v7, /device:TPU:0, one launch (start us, length us, event | category | flops | bytes accessed | tf_op | source)
XLA Modules:
  0.0 183.6 jit_solution(6701789899764548559)
XLA Ops:
  0.7 4.1 %collective-permute-start.1 = (bf16[2,256,256]{2,1,0:T(8,128)(2,1)}, bf16[2,256,256]{2,1,0:T(8,128)(2,1)S(1)}, u32[]{:S(2)}, u32[]{:S(2)}) collective-permute-start(bf16[2,256,256]{2,1,0:T(8,128)(2,1)} %bitcast.48), channel_id=1, source_target_pairs={{0,8},{4,12},{8,0},{12,4},{1,9},{5,13},{9,1},{13,5},{2,10},{6,14},... | collective-permute-start | bytes 786440 | tf_op jit(solution)/shard_map/ppermute | solution.py:29
  6.3 1.7 convert.4
  8.1 8.9 %collective-permute-done.1.refs_2_.mark_ref = bf16[2,256,256]{2,1,0:T(8,128)(2,1)S(1)} collective-permute-done((bf16[2,256,256]{2,1,0:T(8,128)(2,1)}, bf16[2,256,256]{2,1,0:T(8,128)(2,1)S(1)}, u32[]{:S(2)}, u32[]{:S(2)}) %collective-permute-start.1) | collective-permute-done | bytes 262176 | tf_op jit(solution)/shard_map/ppermute | solution.py:29
  17.2 2.9 %norm.1 = (bf16[128,2048]{1,0:T(8,128)(2,1)S(1)}, bf16[128,2048]{1,0:T(8,128)(2,1)}, bf16[128,2048]{1,0:T(8,128)(2,1)S(1)}, bf16[128,2048]{1,0:T(8,128)(2,1)S(1)}) custom-call(bf16[2,256,256]{2,1,0:T(8,128)(2,1)S(1)} %collective-permute-done.1.refs_2_.mark_ref, bf16[2,256,256]{2,1,0:T(8,128)(2,1)S(1)} %collective-permute-done.refs_1_.other_ref, ...), custom_call_target="tpu_custom_call" | custom-call | flops 1000 | bytes 1000 | tf_op jit(solution)/shard_map/norm/pallas_call | solution.py:291
  20.1 1.6 collective-permute-start.3
  22.3 1.6 collective-permute-start.15
  23.9 3.2 %collective-permute-start.8 = (bf16[128,2048]{1,0:T(8,128)(2,1)S(1)}, bf16[128,2048]{1,0:T(8,128)(2,1)S(1)}, u32[]{:S(2)}, u32[]{:S(2)}) collective-permute-start(bf16[128,2048]{1,0:T(8,128)(2,1)S(1)} %get-tuple-element.27), channel_id=1, source_target_pairs={{0,12},{4,8},{8,4},{12,0},{1,13},{5,9},{9,5},{13,1},{2,14},{6,10},... | collective-permute-start | bytes 1572872 | tf_op jit(solution)/shard_map/ppermute | solution.py:29
  27.1 7.9 %collective-permute-done.3.refs_1_ = bf16[128,2048]{1,0:T(8,128)(2,1)S(1)} collective-permute-done((bf16[128,2048]{1,0:T(8,128)(2,1)S(1)}, bf16[128,2048]{1,0:T(8,128)(2,1)S(1)}, u32[]{:S(2)}, u32[]{:S(2)}) %collective-permute-start.3) | collective-permute-done | bytes 524320 | tf_op jit(solution)/shard_map/ppermute | solution.py:29
  36.0 8.1 %collective-permute-done.2.refs_3_ = bf16[2,256,256]{2,1,0:T(8,128)(2,1)S(1)} collective-permute-done((bf16[2,256,256]{2,1,0:T(8,128)(2,1)S(1)}, bf16[2,256,256]{2,1,0:T(8,128)(2,1)S(1)}, u32[]{:S(2)}, u32[]{:S(2)}) %collective-permute-start.2) | collective-permute-done | bytes 262176 | tf_op jit(solution)/shard_map/ppermute | solution.py:29
  44.2 2.1 %collective-permute-done.14.rest_4_ = bf16[1024,256]{1,0:T(8,128)(2,1)} collective-permute-done((bf16[1024,256]{1,0:T(8,128)(2,1)S(1)}, bf16[1024,256]{1,0:T(8,128)(2,1)}, u32[]{:S(2)}, u32[]{:S(2)}) %collective-permute-start.14) | collective-permute-done | bytes 524320 | tf_op jit(solution)/shard_map/ppermute | solution.py:29
  46.3 9.2 %collective-permute-done.15.rest_5_ = bf16[1024,256]{1,0:T(8,128)(2,1)} collective-permute-done((bf16[1024,256]{1,0:T(8,128)(2,1)S(1)}, bf16[1024,256]{1,0:T(8,128)(2,1)}, u32[]{:S(2)}, u32[]{:S(2)}) %collective-permute-start.15) | collective-permute-done | bytes 524320 | tf_op jit(solution)/shard_map/ppermute | solution.py:29
  57.1 1.9 %arrange.1 = (bf16[4,512,256]{2,1,0:T(8,128)(2,1)}, bf16[256,2048]{1,0:T(8,128)(2,1)S(1)}) custom-call(s32[2]{0:T(128)S(1)} %pad_add_fusion.where_ref, bf16[2,256,256]{2,1,0:T(8,128)(2,1)S(1)} %bitcast.50, bf16[2,256,256]{2,1,0:T(8,128)(2,1)S(1)} %copy-done.19, bf16[2,256,256]{2,1,0:T(8,128)(2,1)S(1)} %collective-permute-done.1.refs_2_.mark_ref, ...), custom_call_target="tpu_custom_call" | custom-call | flops 1000 | bytes 1000 | tf_op jit(solution)/shard_map/arrange/pallas_call | solution.py:302
  60.9 3.5 %all-to-all-start = ((bf16[4,512,256]{2,1,0:T(8,128)(2,1)}), bf16[4,512,256]{2,1,0:T(8,128)(2,1)S(1)}, u32[]{:S(2)}, u32[]{:S(2)}) async-start(bf16[4,512,256]{2,1,0:T(8,128)(2,1)} %after.5), calls=%async_computation | async-start | bytes 2097152 | tf_op jit(solution)/shard_map/all_to_all | solution.py:313
  65.0 3.3 %collective-permute-start.11 = (bf16[128,2048]{1,0:T(8,128)(2,1)}, bf16[128,2048]{1,0:T(8,128)(2,1)}, u32[]{:S(2)}, u32[]{:S(2)}) collective-permute-start(bf16[128,2048]{1,0:T(8,128)(2,1)} %copy-done.14), channel_id=1, source_target_pairs={{0,8},{4,12},{8,0},{12,4},{1,9},{5,13},{9,1},{13,5},{2,10},{6,14},... | collective-permute-start | bytes 1572872 | tf_op jit(solution)/shard_map/ppermute | solution.py:29
  68.3 1.6 collective-permute-start.9
  70.4 9.0 %all-to-all-done.cot_ref = bf16[4,512,256]{2,1,0:T(8,128)(2,1)S(1)} async-done(((bf16[4,512,256]{2,1,0:T(8,128)(2,1)}), bf16[4,512,256]{2,1,0:T(8,128)(2,1)S(1)}, u32[]{:S(2)}, u32[]{:S(2)}) %all-to-all-start) | async-done | bytes 1048608 | tf_op jit(solution)/shard_map/all_to_all | solution.py:313
  83.6 4.0 %d_normed.1.refs_1_ = bf16[4,128,2048]{2,1,0:T(8,128)(2,1)S(1)} custom-call(s32[2]{0:T(128)S(1)} %pad_add_fusion.where_ref, bf16[4,512,256]{2,1,0:T(8,128)(2,1)S(1)} %copy-done.11, bf16[1024,256]{1,0:T(8,128)(2,1)S(1)} %copy-done.8, bf16[1024,256]{1,0:T(8,128)(2,1)S(1)} %copy-done.5, bf16[1024,256]{1,0:T(8,128)(2,1)} %collective-permute-done.12.rest_2_, ...), custom_call_target="tpu_custom_call" | custom-call | flops 1000 | bytes 1000 | tf_op jit(solution)/shard_map/d_normed/pallas_call | solution.py:329
  87.7 4.3 %collective-permute-done.11.refs_0_ = bf16[128,2048]{1,0:T(8,128)(2,1)} collective-permute-done((bf16[128,2048]{1,0:T(8,128)(2,1)}, bf16[128,2048]{1,0:T(8,128)(2,1)}, u32[]{:S(2)}, u32[]{:S(2)}) %collective-permute-start.11) | collective-permute-done | bytes 524320 | tf_op jit(solution)/shard_map/ppermute | solution.py:29
  93.4 3.8 %all-to-all-start.1 = ((bf16[4,128,2048]{2,1,0:T(8,128)(2,1)}), bf16[4,128,2048]{2,1,0:T(8,128)(2,1)S(1)}, u32[]{:S(2)}, u32[]{:S(2)}) async-start(bf16[4,128,2048]{2,1,0:T(8,128)(2,1)} %copy-done), calls=%async_computation.1 | async-start | bytes 4194304 | tf_op jit(solution)/shard_map/all_to_all | solution.py:338
  99.7 1.7 collective-permute-done.6.refs_1_
  103.4 14.0 %collective-permute-done.18.rest_7_ = bf16[128,2048]{1,0:T(8,128)(2,1)S(1)} collective-permute-done((bf16[128,2048]{1,0:T(8,128)(2,1)}, bf16[128,2048]{1,0:T(8,128)(2,1)S(1)}, u32[]{:S(2)}, u32[]{:S(2)}) %collective-permute-start.18) | collective-permute-done | bytes 524320 | tf_op jit(solution)/shard_map/ppermute | solution.py:29
  117.3 1.9 %collective-permute-done.20.rest_9_ = bf16[128,2048]{1,0:T(8,128)(2,1)S(1)} collective-permute-done((bf16[128,2048]{1,0:T(8,128)(2,1)S(1)}, bf16[128,2048]{1,0:T(8,128)(2,1)S(1)}, u32[]{:S(2)}, u32[]{:S(2)}) %collective-permute-start.20) | collective-permute-done | bytes 524320 | tf_op jit(solution)/shard_map/ppermute | solution.py:29
  119.2 1.6 copy-done.13
  122.1 8.9 %update.1 = (f32[2048,256]{1,0:T(8,128)}, bf16[512,256]{1,0:T(8,128)(2,1)S(1)}, bf16[512,256]{1,0:T(8,128)(2,1)S(1)}, bf16[512,256]{1,0:T(8,128)(2,1)S(1)}, bf16[512,256]{1,0:T(8,128)(2,1)S(1)}) custom-call(bf16[256,2048]{1,0:T(8,128)(2,1)S(1)} %copy-done.21, f32[2048,256]{1,0:T(8,128)S(1)} %bitcast.39, f32[2048,256]{1,0:T(8,128)S(1)} %bitcast.42, ...), custom_call_target="tpu_custom_call" | custom-call | flops 1000 | bytes 1000 | tf_op jit(solution)/shard_map/update/pallas_call | solution.py:348
  131.6 4.4 %project.1 = (bf16[512,256]{1,0:T(8,128)(2,1)S(1)}, bf16[512,256]{1,0:T(8,128)(2,1)S(1)}, bf16[512,256]{1,0:T(8,128)(2,1)S(1)}, bf16[512,256]{1,0:T(8,128)(2,1)}) custom-call(bf16[512,256]{1,0:T(8,128)(2,1)S(1)} %get-tuple-element.32.mark_ref, bf16[2048,256]{1,0:T(8,128)(2,1)S(1)} %pad_maximum_fusion.weights_ref, bf16[256,2048]{1,0:T(8,128)(2,1)} %pack.3.rest_0_, ...), custom_call_target="tpu_custom_call" | custom-call | flops 1000 | bytes 1000 | tf_op jit(solution)/shard_map/project/pallas_call | solution.py:375
  138.7 11.6 %collective-permute-done.25 = bf16[512,256]{1,0:T(8,128)(2,1)S(1)} collective-permute-done((bf16[512,256]{1,0:T(8,128)(2,1)S(1)}, bf16[512,256]{1,0:T(8,128)(2,1)S(1)}, u32[]{:S(2)}, u32[]{:S(2)}) %collective-permute-start.25) | collective-permute-done | bytes 262176 | tf_op jit(solution)/shard_map/ppermute | solution.py:29
  150.8 2.5 %collective-permute-start.21 = (bf16[512,256]{1,0:T(8,128)(2,1)}, bf16[512,256]{1,0:T(8,128)(2,1)S(1)}, u32[]{:S(2)}, u32[]{:S(2)}) collective-permute-start(bf16[512,256]{1,0:T(8,128)(2,1)} %copy-done.28), channel_id=1, source_target_pairs={{0,4},{4,0},{8,12},{12,8},{1,5},{5,1},{9,13},{13,9},{2,6},{6,2},{1... | collective-permute-start | bytes 786440 | tf_op jit(solution)/shard_map/ppermute | solution.py:29
  153.2 3.7 %collective-permute-done.22 = bf16[512,256]{1,0:T(8,128)(2,1)S(1)} collective-permute-done((bf16[512,256]{1,0:T(8,128)(2,1)}, bf16[512,256]{1,0:T(8,128)(2,1)S(1)}, u32[]{:S(2)}, u32[]{:S(2)}) %collective-permute-start.22) | collective-permute-done | bytes 262176 | tf_op jit(solution)/shard_map/ppermute | solution.py:29
  158.1 10.2 %collective-permute-done.24 = bf16[512,256]{1,0:T(8,128)(2,1)} collective-permute-done((bf16[512,256]{1,0:T(8,128)(2,1)S(1)}, bf16[512,256]{1,0:T(8,128)(2,1)}, u32[]{:S(2)}, u32[]{:S(2)}) %collective-permute-start.24) | collective-permute-done | bytes 262176 | tf_op jit(solution)/shard_map/ppermute | solution.py:29
  168.3 2.4 %collective-permute-done.26 = bf16[512,256]{1,0:T(8,128)(2,1)} collective-permute-done((bf16[512,256]{1,0:T(8,128)(2,1)S(1)}, bf16[512,256]{1,0:T(8,128)(2,1)}, u32[]{:S(2)}, u32[]{:S(2)}) %collective-permute-start.26) | collective-permute-done | bytes 262176 | tf_op jit(solution)/shard_map/ppermute | solution.py:29
  173.5 4.1 %collective-permute-done.21 = bf16[512,256]{1,0:T(8,128)(2,1)S(1)} collective-permute-done((bf16[512,256]{1,0:T(8,128)(2,1)}, bf16[512,256]{1,0:T(8,128)(2,1)S(1)}, u32[]{:S(2)}, u32[]{:S(2)}) %collective-permute-start.21) | collective-permute-done | bytes 262176 | tf_op jit(solution)/shard_map/ppermute | solution.py:29
  179.6 3.3 %grad_in.1 = bf16[128,8192]{1,0:T(8,128)(2,1)} custom-call(bf16[128,8192]{1,0:T(8,128)(2,1)S(1)} %bitcast.41, f32[1,8192]{1,0:T(1,128)S(1)} %copy-done.27, bf16[4,128,2048]{2,1,0:T(8,128)(2,1)S(1)} %after.7.d_ref), custom_call_target="tpu_custom_call" | custom-call | flops 1000 | bytes 1000 | tf_op jit(solution)/shard_map/grad_in/pallas_call | solution.py:386
  (112 shorter events, 29.5 us)
Async XLA Ops:
  0.7 16.3 %collective-permute-start.1 = (bf16[2,256,256]{2,1,0:T(8,128)(2,1)}, bf16[2,256,256]{2,1,0:T(8,128)(2,1)S(1)}, u32[]{:S(2)}, u32[]{:S(2)}) collective-permute-start(bf16[2,256,256]{2,1,0:T(8,128)(2,1)} %bitcast.48), channel_id=1, source_target_pairs={{0,8},{4,12},{8,0},{12,4},{1,9},{5,13},{9,1},{13,5},{2,10},{6,14},... | collective-permute-start | bytes 786440 | tf_op jit(solution)/shard_map/ppermute | solution.py:29
  4.8 12.4 %collective-permute-start = (bf16[2,256,256]{2,1,0:T(8,128)(2,1)}, bf16[2,256,256]{2,1,0:T(8,128)(2,1)S(1)}, u32[]{:S(2)}, u32[]{:S(2)}) collective-permute-start(bf16[2,256,256]{2,1,0:T(8,128)(2,1)} %bitcast.49), channel_id=1, source_target_pairs={{0,4},{4,0},{8,12},{12,8},{1,5},{5,1},{9,13},{13,9},{2,6},{6,2},{1... | collective-permute-start | bytes 786440 | tf_op jit(solution)/shard_map/ppermute | solution.py:29
  20.1 14.9 %collective-permute-start.3 = (bf16[128,2048]{1,0:T(8,128)(2,1)S(1)}, bf16[128,2048]{1,0:T(8,128)(2,1)S(1)}, u32[]{:S(2)}, u32[]{:S(2)}) collective-permute-start(bf16[128,2048]{1,0:T(8,128)(2,1)S(1)} %get-tuple-element.24.refs_0_), channel_id=1, source_target_pairs={{0,2},{1,3},{2,0},{3,1},{4,6},{5,7},{6,4},{7,5},{8,10},{9,11},{10,... | collective-permute-start | bytes 1572872 | tf_op jit(solution)/shard_map/ppermute | solution.py:29
  21.8 37.2 %copy-start.4 = (bf16[1024,256]{1,0:T(8,128)(2,1)}, bf16[1024,256]{1,0:T(8,128)(2,1)S(1)}, u32[]{:S(2)}) copy-start(bf16[1024,256]{1,0:T(8,128)(2,1)S(1)} %get-tuple-element.42.rest_1_) | copy-start | bytes 1572868
  21.8 37.2 %copy-start.7 = (bf16[1024,256]{1,0:T(8,128)(2,1)}, bf16[1024,256]{1,0:T(8,128)(2,1)S(1)}, u32[]{:S(2)}) copy-start(bf16[1024,256]{1,0:T(8,128)(2,1)S(1)} %get-tuple-element.43.rest_0_) | copy-start | bytes 1572868
  21.8 24.5 %collective-permute-start.14 = (bf16[1024,256]{1,0:T(8,128)(2,1)S(1)}, bf16[1024,256]{1,0:T(8,128)(2,1)}, u32[]{:S(2)}, u32[]{:S(2)}) collective-permute-start(bf16[1024,256]{1,0:T(8,128)(2,1)S(1)} %get-tuple-element.43.rest_0_), channel_id=1, source_target_pairs={{0,2},{1,3},{2,0},{3,1},{4,6},{5,7},{6,4},{7,5},{8,10},{9,11},{10,... | collective-permute-start | bytes 1572872 | tf_op jit(solution)/shard_map/ppermute | solution.py:29
  22.3 33.2 %collective-permute-start.15 = (bf16[1024,256]{1,0:T(8,128)(2,1)S(1)}, bf16[1024,256]{1,0:T(8,128)(2,1)}, u32[]{:S(2)}, u32[]{:S(2)}) collective-permute-start(bf16[1024,256]{1,0:T(8,128)(2,1)S(1)} %get-tuple-element.42.rest_1_), channel_id=1, source_target_pairs={{0,2},{1,3},{2,0},{3,1},{4,6},{5,7},{6,4},{7,5},{8,10},{9,11},{10,... | collective-permute-start | bytes 1572872 | tf_op jit(solution)/shard_map/ppermute | solution.py:29
  23.9 33.2 %collective-permute-start.8 = (bf16[128,2048]{1,0:T(8,128)(2,1)S(1)}, bf16[128,2048]{1,0:T(8,128)(2,1)S(1)}, u32[]{:S(2)}, u32[]{:S(2)}) collective-permute-start(bf16[128,2048]{1,0:T(8,128)(2,1)S(1)} %get-tuple-element.27), channel_id=1, source_target_pairs={{0,12},{4,8},{8,4},{12,0},{1,13},{5,9},{9,5},{13,1},{2,14},{6,10},... | collective-permute-start | bytes 1572872 | tf_op jit(solution)/shard_map/ppermute | solution.py:29
  27.1 17.0 %collective-permute-start.2 = (bf16[2,256,256]{2,1,0:T(8,128)(2,1)S(1)}, bf16[2,256,256]{2,1,0:T(8,128)(2,1)S(1)}, u32[]{:S(2)}, u32[]{:S(2)}) collective-permute-start(bf16[2,256,256]{2,1,0:T(8,128)(2,1)S(1)} %collective-permute-done.1.refs_2_.mark_ref), channel_id=1, source_target_pairs={{0,4},{4,0},{8,12},{12,8},{1,5},{5,1},{9,13},{13,9},{2,6},{6,2},{1... | collective-permute-start | bytes 786440 | tf_op jit(solution)/shard_map/ppermute | solution.py:29
  35.0 29.5 %collective-permute-start.12 = (bf16[1024,256]{1,0:T(8,128)(2,1)S(1)}, bf16[1024,256]{1,0:T(8,128)(2,1)}, u32[]{:S(2)}, u32[]{:S(2)}) collective-permute-start(bf16[1024,256]{1,0:T(8,128)(2,1)S(1)} %get-tuple-element.43.rest_0_), channel_id=1, source_target_pairs={{0,1},{1,0},{2,3},{3,2},{4,5},{5,4},{6,7},{7,6},{8,9},{9,8},{10,11... | collective-permute-start | bytes 1572872 | tf_op jit(solution)/shard_map/ppermute | solution.py:29
  44.1 21.0 %collective-permute-start.13 = (bf16[1024,256]{1,0:T(8,128)(2,1)S(1)}, bf16[1024,256]{1,0:T(8,128)(2,1)}, u32[]{:S(2)}, u32[]{:S(2)}) collective-permute-start(bf16[1024,256]{1,0:T(8,128)(2,1)S(1)} %get-tuple-element.42.rest_1_), channel_id=1, source_target_pairs={{0,1},{1,0},{2,3},{3,2},{4,5},{5,4},{6,7},{7,6},{8,9},{9,8},{10,11... | collective-permute-start | bytes 1572872 | tf_op jit(solution)/shard_map/ppermute | solution.py:29
  46.3 45.7 %collective-permute-start.4 = (bf16[256,2048]{1,0:T(8,128)(2,1)}, bf16[256,2048]{1,0:T(8,128)(2,1)S(1)}, u32[]{:S(2)}, u32[]{:S(2)}) collective-permute-start(bf16[256,2048]{1,0:T(8,128)(2,1)} %pack.3.rest_0_), channel_id=1, source_target_pairs={{0,1},{1,0},{2,3},{3,2},{4,5},{5,4},{6,7},{7,6},{8,9},{9,8},{10,11... | collective-permute-start | bytes 3145736 | tf_op jit(solution)/shard_map/ppermute | solution.py:29
  55.6 12.8 %collective-permute-start.5 = (bf16[128,2048]{1,0:T(8,128)(2,1)}, bf16[128,2048]{1,0:T(8,128)(2,1)}, u32[]{:S(2)}, u32[]{:S(2)}) collective-permute-start(bf16[128,2048]{1,0:T(8,128)(2,1)} %get-tuple-element.25), channel_id=1, source_target_pairs={{0,4},{4,0},{8,12},{12,8},{1,5},{5,1},{9,13},{13,9},{2,6},{6,2},{1... | collective-permute-start | bytes 1572872 | tf_op jit(solution)/shard_map/ppermute | solution.py:29
  57.1 12.8 %collective-permute-start.16 = (bf16[1024,256]{1,0:T(8,128)(2,1)}, bf16[1024,256]{1,0:T(8,128)(2,1)}, u32[]{:S(2)}, u32[]{:S(2)}) collective-permute-start(bf16[1024,256]{1,0:T(8,128)(2,1)} %collective-permute-done.14.rest_4_), channel_id=1, source_target_pairs={{0,1},{1,0},{2,3},{3,2},{4,5},{5,4},{6,7},{7,6},{8,9},{9,8},{10,11... | collective-permute-start | bytes 1572872 | tf_op jit(solution)/shard_map/ppermute | solution.py:29
  60.9 18.4 %all-to-all-start = ((bf16[4,512,256]{2,1,0:T(8,128)(2,1)}), bf16[4,512,256]{2,1,0:T(8,128)(2,1)S(1)}, u32[]{:S(2)}, u32[]{:S(2)}) async-start(bf16[4,512,256]{2,1,0:T(8,128)(2,1)} %after.5), calls=%async_computation | async-start | bytes 2097152 | tf_op jit(solution)/shard_map/all_to_all | solution.py:313
  64.5 5.9 %collective-permute-start.17 = (bf16[1024,256]{1,0:T(8,128)(2,1)}, bf16[1024,256]{1,0:T(8,128)(2,1)S(1)}, u32[]{:S(2)}, u32[]{:S(2)}) collective-permute-start(bf16[1024,256]{1,0:T(8,128)(2,1)} %collective-permute-done.15.rest_5_), channel_id=1, source_target_pairs={{0,1},{1,0},{2,3},{3,2},{4,5},{5,4},{6,7},{7,6},{8,9},{9,8},{10,11... | collective-permute-start | bytes 1572872 | tf_op jit(solution)/shard_map/ppermute | solution.py:29
  65.0 27.0 %collective-permute-start.11 = (bf16[128,2048]{1,0:T(8,128)(2,1)}, bf16[128,2048]{1,0:T(8,128)(2,1)}, u32[]{:S(2)}, u32[]{:S(2)}) collective-permute-start(bf16[128,2048]{1,0:T(8,128)(2,1)} %copy-done.14), channel_id=1, source_target_pairs={{0,8},{4,12},{8,0},{12,4},{1,9},{5,13},{9,1},{13,5},{2,10},{6,14},... | collective-permute-start | bytes 1572872 | tf_op jit(solution)/shard_map/ppermute | solution.py:29
  68.3 28.9 %collective-permute-start.9 = (bf16[128,2048]{1,0:T(8,128)(2,1)}, bf16[128,2048]{1,0:T(8,128)(2,1)}, u32[]{:S(2)}, u32[]{:S(2)}) collective-permute-start(bf16[128,2048]{1,0:T(8,128)(2,1)} %copy-done.15), channel_id=1, source_target_pairs={{0,2},{1,3},{2,0},{3,1},{4,6},{5,7},{6,4},{7,5},{8,10},{9,11},{10,... | collective-permute-start | bytes 1572872 | tf_op jit(solution)/shard_map/ppermute | solution.py:29
  69.9 31.6 %collective-permute-start.6 = (bf16[128,2048]{1,0:T(8,128)(2,1)}, bf16[128,2048]{1,0:T(8,128)(2,1)}, u32[]{:S(2)}, u32[]{:S(2)}) collective-permute-start(bf16[128,2048]{1,0:T(8,128)(2,1)} %collective-permute-done.5.refs_0_), channel_id=1, source_target_pairs={{0,2},{1,3},{2,0},{3,1},{4,6},{5,7},{6,4},{7,5},{8,10},{9,11},{10,... | collective-permute-start | bytes 1572872 | tf_op jit(solution)/shard_map/ppermute | solution.py:29
  93.4 84.5 %all-to-all-start.1 = ((bf16[4,128,2048]{2,1,0:T(8,128)(2,1)}), bf16[4,128,2048]{2,1,0:T(8,128)(2,1)S(1)}, u32[]{:S(2)}, u32[]{:S(2)}) async-start(bf16[4,128,2048]{2,1,0:T(8,128)(2,1)} %copy-done), calls=%async_computation.1 | async-start | bytes 4194304 | tf_op jit(solution)/shard_map/all_to_all | solution.py:338
  99.7 17.7 %collective-permute-start.10 = (bf16[256,2048]{1,0:T(8,128)(2,1)S(1)}, bf16[256,2048]{1,0:T(8,128)(2,1)S(1)}, u32[]{:S(2)}, u32[]{:S(2)}) collective-permute-start(bf16[256,2048]{1,0:T(8,128)(2,1)S(1)} %pack.5.rest_4_), channel_id=1, source_target_pairs={{0,1},{1,0},{2,3},{3,2},{4,5},{5,4},{6,7},{7,6},{8,9},{9,8},{10,11... | collective-permute-start | bytes 3145736 | tf_op jit(solution)/shard_map/ppermute | solution.py:29
  102.7 14.6 %collective-permute-start.7 = (bf16[256,2048]{1,0:T(8,128)(2,1)S(1)}, bf16[256,2048]{1,0:T(8,128)(2,1)S(1)}, u32[]{:S(2)}, u32[]{:S(2)}) collective-permute-start(bf16[256,2048]{1,0:T(8,128)(2,1)S(1)} %pack.4.rest_2_), channel_id=1, source_target_pairs={{0,1},{1,0},{2,3},{3,2},{4,5},{5,4},{6,7},{7,6},{8,9},{9,8},{10,11... | collective-permute-start | bytes 3145736 | tf_op jit(solution)/shard_map/ppermute | solution.py:29
  102.8 14.6 %collective-permute-start.18 = (bf16[128,2048]{1,0:T(8,128)(2,1)}, bf16[128,2048]{1,0:T(8,128)(2,1)S(1)}, u32[]{:S(2)}, u32[]{:S(2)}) collective-permute-start(bf16[128,2048]{1,0:T(8,128)(2,1)} %get-tuple-element.31.rest_6_), channel_id=1, source_target_pairs={{0,2},{1,3},{2,0},{3,1},{4,6},{5,7},{6,4},{7,5},{8,10},{9,11},{10,... | collective-permute-start | bytes 1572872 | tf_op jit(solution)/shard_map/ppermute | solution.py:29
  103.3 14.0 %collective-permute-start.19 = (bf16[128,2048]{1,0:T(8,128)(2,1)}, bf16[128,2048]{1,0:T(8,128)(2,1)S(1)}, u32[]{:S(2)}, u32[]{:S(2)}) collective-permute-start(bf16[128,2048]{1,0:T(8,128)(2,1)} %get-tuple-element.31.rest_6_), channel_id=1, source_target_pairs={{0,1},{1,0},{2,3},{3,2},{4,5},{5,4},{6,7},{7,6},{8,9},{9,8},{10,11... | collective-permute-start | bytes 1572872 | tf_op jit(solution)/shard_map/ppermute | solution.py:29
  117.3 1.9 %collective-permute-start.20 = (bf16[128,2048]{1,0:T(8,128)(2,1)S(1)}, bf16[128,2048]{1,0:T(8,128)(2,1)S(1)}, u32[]{:S(2)}, u32[]{:S(2)}) collective-permute-start(bf16[128,2048]{1,0:T(8,128)(2,1)S(1)} %collective-permute-done.18.rest_7_), channel_id=1, source_target_pairs={{0,1},{1,0},{2,3},{3,2},{4,5},{5,4},{6,7},{7,6},{8,9},{9,8},{10,11... | collective-permute-start | bytes 1572872 | tf_op jit(solution)/shard_map/ppermute | solution.py:29
  130.9 19.4 %collective-permute-start.25 = (bf16[512,256]{1,0:T(8,128)(2,1)S(1)}, bf16[512,256]{1,0:T(8,128)(2,1)S(1)}, u32[]{:S(2)}, u32[]{:S(2)}) collective-permute-start(bf16[512,256]{1,0:T(8,128)(2,1)S(1)} %get-tuple-element.40), channel_id=1, source_target_pairs={{0,4},{4,0},{8,12},{12,8},{1,5},{5,1},{9,13},{13,9},{2,6},{6,2},{1... | collective-permute-start | bytes 786440 | tf_op jit(solution)/shard_map/ppermute | solution.py:29
  136.7 20.3 %collective-permute-start.22 = (bf16[512,256]{1,0:T(8,128)(2,1)}, bf16[512,256]{1,0:T(8,128)(2,1)S(1)}, u32[]{:S(2)}, u32[]{:S(2)}) collective-permute-start(bf16[512,256]{1,0:T(8,128)(2,1)} %get-tuple-element.36), channel_id=1, source_target_pairs={{0,4},{4,0},{8,12},{12,8},{1,5},{5,1},{9,13},{13,9},{2,6},{6,2},{1... | collective-permute-start | bytes 786440 | tf_op jit(solution)/shard_map/ppermute | solution.py:29
  138.2 30.1 %collective-permute-start.24 = (bf16[512,256]{1,0:T(8,128)(2,1)S(1)}, bf16[512,256]{1,0:T(8,128)(2,1)}, u32[]{:S(2)}, u32[]{:S(2)}) collective-permute-start(bf16[512,256]{1,0:T(8,128)(2,1)S(1)} %get-tuple-element.32.mark_ref), channel_id=1, source_target_pairs={{0,4},{4,0},{8,12},{12,8},{1,5},{5,1},{9,13},{13,9},{2,6},{6,2},{1... | collective-permute-start | bytes 786440 | tf_op jit(solution)/shard_map/ppermute | solution.py:29
  150.4 20.2 %collective-permute-start.26 = (bf16[512,256]{1,0:T(8,128)(2,1)S(1)}, bf16[512,256]{1,0:T(8,128)(2,1)}, u32[]{:S(2)}, u32[]{:S(2)}) collective-permute-start(bf16[512,256]{1,0:T(8,128)(2,1)S(1)} %add_convert_fusion.1), channel_id=1, source_target_pairs={{0,8},{4,12},{8,0},{12,4},{1,9},{5,13},{9,1},{13,5},{2,10},{6,14},... | collective-permute-start | bytes 786440 | tf_op jit(solution)/shard_map/ppermute | solution.py:29
  150.8 26.9 %collective-permute-start.21 = (bf16[512,256]{1,0:T(8,128)(2,1)}, bf16[512,256]{1,0:T(8,128)(2,1)S(1)}, u32[]{:S(2)}, u32[]{:S(2)}) collective-permute-start(bf16[512,256]{1,0:T(8,128)(2,1)} %copy-done.28), channel_id=1, source_target_pairs={{0,4},{4,0},{8,12},{12,8},{1,5},{5,1},{9,13},{13,9},{2,6},{6,2},{1... | collective-permute-start | bytes 786440 | tf_op jit(solution)/shard_map/ppermute | solution.py:29
  158.0 19.7 %collective-permute-start.23 = (bf16[512,256]{1,0:T(8,128)(2,1)S(1)}, bf16[512,256]{1,0:T(8,128)(2,1)S(1)}, u32[]{:S(2)}, u32[]{:S(2)}) collective-permute-start(bf16[512,256]{1,0:T(8,128)(2,1)S(1)} %add_convert_fusion.3), channel_id=1, source_target_pairs={{0,8},{4,12},{8,0},{12,4},{1,9},{5,13},{9,1},{13,5},{2,10},{6,14},... | collective-permute-start | bytes 786440 | tf_op jit(solution)/shard_map/ppermute | solution.py:29
  172.0 6.6 %collective-permute-start.27 = (bf16[1,2,256,256]{3,2,1,0:T(8,128)(2,1)S(1)}, bf16[1,2,256,256]{3,2,1,0:T(8,128)(2,1)S(1)}, u32[]{:S(2)}, u32[]{:S(2)}) collective-permute-start(bf16[1,2,256,256]{3,2,1,0:T(8,128)(2,1)S(1)} %bitcast.44), channel_id=1, source_target_pairs={{0,16},{16,0},{1,17},{17,1},{2,18},{18,2},{3,19},{19,3},{4,20},{20... | collective-permute-start | bytes 786440 | tf_op jit(solution)/shard_map/ppermute | solution.py:34
  (27 other events, 248.0 us)

commit v8 on v7

v8 whole, which is shorter than its diff:
```python
import functools

import jax
import jax.numpy as jnp
from jax import lax
from jax.experimental import pallas as pl
from jax.experimental.pallas import tpu as pltpu
from jax.sharding import PartitionSpec as P

beta_first = 0.9
beta_second = 0.95
learn_rate = 0.03
weight_decay = 0.1
adam_eps = 1e-08
norm_eps = 1e-05
step_count = 20.0

f32 = jnp.float32
bf16 = jnp.bfloat16

vmem = pl.BlockSpec(memory_space=pltpu.VMEM)
smem = pl.BlockSpec(memory_space=pltpu.SMEM)
anywhere = pl.BlockSpec(memory_space=pl.ANY)
light = pl.CostEstimate(flops=1000, bytes_accessed=1000, transcendentals=0)


def swap(x, axis, bits):
    peers = lax.axis_size(axis)
    return lax.ppermute(x, axis, [(i, i ^ bits) for i in range(peers)])


def from_behind(x, axis, by):
    peers = lax.axis_size(axis)
    return lax.ppermute(x, axis, [(i, (i + by) % peers) for i in range(peers)])


def dot(a, b, contract):
    return lax.dot_general(a, b, (contract, ((), ())), preferred_element_type=f32)


def like(*shape, dtype=bf16):
    return jax.ShapeDtypeStruct(shape, dtype)


def call(body, out_shape, in_specs, out_specs, mib, name, scratch=(), **more):
    return pl.pallas_call(
        body,
        out_shape=out_shape,
        in_specs=in_specs,
        out_specs=out_specs,
        scratch_shapes=list(scratch),
        compiler_params=pltpu.CompilerParams(vmem_limit_bytes=int(mib * 1024 * 1024)),
        cost_estimate=light,
        name=name,
        **more,
    )


def after(values, *earlier):
    tied = call(
        lambda *refs: None,
        [like(*x.shape, dtype=x.dtype) for x in values],
        [anywhere] * (len(values) + len(earlier)),
        [anywhere] * len(values),
        0.25,
        "after",
        input_output_aliases={i: i for i in range(len(values))},
    )(*values, *earlier)
    return list(tied)


def lanes(index, size):
    return pl.ds(pl.multiple_of(index * size, size), size)


def norm_kernel(hidden_ref, gain_ref, *own_refs, tile):
    blocks, rows = own_refs[0].shape[:2]
    width = hidden_ref.shape[1]
    depth = width // blocks
    for m, own_ref in enumerate(own_refs):

        @pl.loop(0, rows // tile)
        def _(i, m=m, own_ref=own_ref):
            row = pl.multiple_of(i * tile, tile)
            at, to = pl.ds(m * rows + row, tile), pl.ds(row, tile)
            total = jnp.zeros((tile, 1), f32)
            for k in range(blocks):
                part = hidden_ref[at, k * depth : (k + 1) * depth].astype(f32)
                total += jnp.sum(part * part, axis=-1, keepdims=True)
            scaling = lax.rsqrt(total * (1.0 / width) + norm_eps)
            for k in range(blocks):
                cut = slice(k * depth, (k + 1) * depth)
                own_ref[k, to, :] = (
                    hidden_ref[at, cut].astype(f32) * scaling * gain_ref[:, cut]
                ).astype(bf16)


def grad_kernel(hidden_ref, gain_ref, d_ref, out_ref, *, tile):
    rows, width = hidden_ref.shape
    blocks = d_ref.shape[0]
    depth = width // blocks

    @pl.loop(0, rows // tile)
    def _(i):
        at = pl.ds(pl.multiple_of(i * tile, tile), tile)
        squares = jnp.zeros((tile, 1), f32)
        cross = jnp.zeros((tile, 1), f32)
        for k in range(blocks):
            cut = slice(k * depth, (k + 1) * depth)
            hidden = hidden_ref[at, cut].astype(f32)
            squares += jnp.sum(hidden * hidden, axis=-1, keepdims=True)
            upper = d_ref[k, at, :].astype(f32) * gain_ref[:, cut]
            cross += jnp.sum(upper * hidden, axis=-1, keepdims=True)
        scaling = lax.rsqrt(squares * (1.0 / width) + norm_eps)
        factor = scaling * scaling * scaling * (cross * (1.0 / width))
        for k in range(blocks):
            cut = slice(k * depth, (k + 1) * depth)
            upper = d_ref[k, at, :].astype(f32) * gain_ref[:, cut]
            hidden = hidden_ref[at, cut].astype(f32)
            out_ref[at, cut] = (scaling * upper - hidden * factor).astype(bf16)


def arrange_kernel(mark_ref, where_ref, *refs, dp, layout):
    cots, send_refs, (turned_ref, held) = refs[:dp], refs[dp:-2], refs[-2:]
    z, t = where_ref[0], where_ref[1]
    micro, rows, cols = cots[0].shape
    rows //= len(send_refs)
    for k in range(dp):
        held[z ^ k] = cots[k][...]

    def block(k, m, j):
        return held[k, m, pl.ds(pl.multiple_of((t ^ j) * rows, rows), rows), :]

    for j, send_ref in enumerate(send_refs):
        for k in range(dp):
            for m in range(micro):
                at = (k * micro + m) * rows
                send_ref[at : at + rows, :] = block(k, m, j)
    for p, (m, j) in enumerate(layout):
        part = jnp.concatenate([block(k, m, j) for k in range(dp)])
        turned_ref[:, p * dp * rows : (p + 1) * dp * rows] = part.astype(f32).T.astype(bf16)


def d_kernel(*refs):
    cot_refs, w_refs, d_ref = refs[:4], refs[4:8], refs[8]
    dp, rows, depth = d_ref.shape
    tile = min(depth, 512)
    cot = jnp.concatenate([x[...] for x in cot_refs], axis=1)
    for i in range(depth // tile):
        cut = slice(i * tile, (i + 1) * tile)
        whole = jnp.concatenate([w[cut, :] for w in w_refs], axis=1)
        part = dot(cot, whole, ((1,), (1,))).astype(bf16)
        for k in range(dp):
            d_ref[k, :, cut] = part[k * rows : (k + 1) * rows]


def token_copies(token_refs, tokens, sems, cut, first):
    copies, row = [], 0
    for p, x in enumerate(token_refs):
        for k in range(x.shape[0]):
            copies.append(
                pltpu.make_async_copy(
                    x.at[k, :, cut],
                    tokens.at[pl.ds(row, x.shape[1]), cut],
                    sems.at[first + p * x.shape[0] + k],
                )
            )
            row += x.shape[1]
    return copies


def update_kernel(where_ref, turned_ref, master_hbm, m_hbm, v_hbm, *rest, count, tile):
    token_refs, (new_hbm, keep_ref, send_ref) = rest[:count], rest[count : count + 3]
    tokens, master, m, v, updated, new, product, sems, out_sems = rest[count + 3 :]
    tiles = master.shape[0] // tile
    each = count * token_refs[0].shape[0] + 3
    groups = []
    for i in range(tiles):
        cut = pl.ds(i * tile, tile)
        group = token_copies(token_refs, tokens, sems, cut, i * each)
        for p, (source, target) in enumerate(((master_hbm, master), (m_hbm, m), (v_hbm, v))):
            group.append(
                pltpu.make_async_copy(
                    source.at[cut, :], target.at[cut, :], sems.at[(i + 1) * each - 3 + p]
                )
            )
        for copy in group:
            copy.start()
        groups.append(group)
    outs = []
    for i in range(tiles):
        cut = slice(i * tile, (i + 1) * tile)
        for copy in groups[i]:
            copy.wait()
        grad = dot(turned_ref[...], tokens[:, cut], ((1,), (0,))).T
        m_new = beta_first * m[cut, :] + (1.0 - beta_first) * grad
        v_new = beta_second * v[cut, :] + (1.0 - beta_second) * grad * grad
        m_hat = m_new / (1.0 - beta_first**step_count)
        v_hat = v_new / (1.0 - beta_second**step_count)
        old = master[cut, :]
        master_new = old - learn_rate * (
            m_hat / (jnp.sqrt(v_hat) + adam_eps) + weight_decay * old
        )
        new[cut, :] = master_new
        out = pltpu.make_async_copy(
            new.at[pl.ds(i * tile, tile), :], new_hbm.at[pl.ds(i * tile, tile), :], out_sems.at[i]
        )
        out.start()
        outs.append(out)
        updated[cut, :] = master_new.astype(bf16)
    project(where_ref, tokens, updated, keep_ref, send_ref, product, count)
    for out in outs:
        out.wait()


def project(where_ref, tokens, weights, keep_ref, send_ref, product, count):
    z = where_ref[0]
    dp, rows = product.shape[1:3]
    size = dp * rows
    for p in range(count):
        part = dot(tokens[p * size : (p + 1) * size, :], weights[...], ((1,), (0,)))
        product[p] = part.astype(bf16).reshape(product.shape[1:])
    for k in range(dp):
        part_ref = send_ref if k % 2 else keep_ref
        for p in range(count):
            part_ref[k // 2, p * rows : (p + 1) * rows, :] = product[p, z ^ k]


def project_kernel(mark_ref, where_ref, weights_ref, *rest, count):
    token_refs = rest[:count]
    keep_ref, send_ref, tokens, product, sems = rest[count:]
    copies = token_copies(token_refs, tokens, sems, slice(None), 0)
    for copy in copies:
        copy.start()
    for copy in copies:
        copy.wait()
    project(where_ref, tokens, weights_ref, keep_ref, send_ref, product, count)


def reorder(blocks, me):
    bit = 1
    while bit < len(blocks):
        flip = (me & bit) != 0
        blocks = [jnp.where(flip, blocks[i ^ bit], blocks[i]) for i in range(len(blocks))]
        bit *= 2
    return blocks


def scatter_sum(keep, send, *earlier):
    got = swap(send, "dp", 1)
    if earlier:
        got = after([got], *earlier)[0]
    mine = keep[0].astype(f32) + got[0].astype(f32)
    other = (keep[1].astype(f32) + got[1].astype(f32)).astype(bf16)
    return mine + swap(other, "dp", 2).astype(f32)


def shards(hidden_in, norm_gain, kv_cot, master_kv, moment_m, moment_v):
    dp, tensor = lax.axis_size("dp"), lax.axis_size("tensor")
    assert dp == 4 and tensor == 4
    z, t = lax.axis_index("dp"), lax.axis_index("tensor")
    where = jnp.stack([z, t]).astype(jnp.int32)
    _, micro, rows, width = hidden_in.shape
    piece = micro * rows
    hidden = hidden_in.reshape(piece, width)
    own_depth, cols = master_kv.shape[1:]
    depth = width // dp
    tile = min(piece, 16)

    w0 = master_kv[0].astype(bf16)
    w2, w1 = swap(w0, "tensor", 2), swap(w0, "tensor", 1)
    cot0 = kv_cot[0]
    cot2, cot1 = swap(cot0, "dp", 2), swap(cot0, "dp", 1)
    cot3 = swap(cot2, "dp", 1)
    own = call(
        functools.partial(norm_kernel, tile=tile),
        [like(dp, rows, depth)] * micro,
        [vmem, vmem],
        [vmem] * micro,
        8,
        "norm",
    )(hidden, norm_gain)
    token0 = lax.all_to_all(own[0], "dp", 0, 0, tiled=True)
    layout = tuple((m, j) for m in range(micro) for j in (0, 1, 2, 3))
    *blocks, turned = call(
        functools.partial(arrange_kernel, dp=dp, layout=layout),
        [like(dp * piece, cols)] * tensor + [like(cols, dp * tensor * piece)],
        [anywhere, smem] + [vmem] * dp,
        [vmem] * (tensor + 1),
        8,
        "arrange",
        scratch=[pltpu.VMEM((dp,) + cot0.shape, bf16)],
    )(w2, where, cot0, cot1, cot2, cot3)
    own1, token0 = after([own[1], token0], blocks[0])
    token1 = lax.all_to_all(own1, "dp", 0, 0, tiled=True)
    across0 = swap(token0, "tensor", 2)
    mine_cot = [blocks[0]] + [swap(blocks[j], "tensor", j) for j in range(1, tensor)]
    w3 = swap(w2, "tensor", 1)
    d = call(
        d_kernel,
        like(dp, piece, depth),
        [vmem] * 8,
        vmem,
        20,
        "d_normed",
    )(*mine_cot, w0, w1, w2, w3)
    token1, d = after([token1, d], across0)
    d = lax.all_to_all(d, "dp", 0, 0, tiled=True)
    tokens = []
    for x, across in ((token0, across0), (token1, swap(token1, "tensor", 2))):
        tokens += [x, swap(x, "tensor", 1), across, swap(across, "tensor", 1)]
    count = len(tokens)
    block = tensor * piece
    part_shape = [like(dp // 2, block, cols)] * 2
    step = min(own_depth, 512)
    tiles = own_depth // step
    whole = pltpu.VMEM((own_depth, cols), f32)
    all_tokens = pltpu.VMEM((dp * block, depth), bf16)
    product = pltpu.VMEM((count, dp, rows, cols), bf16)
    master_new, keep, send = call(
        functools.partial(update_kernel, count=count, tile=step),
        [like(own_depth, cols, dtype=f32)] + part_shape,
        [smem, vmem] + [anywhere] * (3 + count),
        [anywhere] + [vmem] * 2,
        25,
        "update",
        scratch=[
            all_tokens,
            whole,
            whole,
            whole,
            pltpu.VMEM((own_depth, cols), bf16),
            whole,
            product,
            pltpu.SemaphoreType.DMA((tiles * (count * dp + 3),)),
            pltpu.SemaphoreType.DMA((tiles,)),
        ],
    )(where, turned, master_kv[0], moment_m[0], moment_v[0], *tokens)

    def place(x):
        x = x.reshape(micro, tensor, rows, cols)
        return jnp.stack(reorder([x[:, j] for j in range(tensor)], t), 1).reshape(
            1, micro, tensor * rows, cols
        )

    mine = place(scatter_sum(keep, send, d).astype(bf16))
    kv_next = from_behind(mine, "segment", -1)
    own_keep, own_send = call(
        functools.partial(project_kernel, count=count),
        part_shape,
        [anywhere, smem, vmem] + [anywhere] * count,
        [vmem] * 2,
        17,
        "project",
        scratch=[all_tokens, product, pltpu.SemaphoreType.DMA((count * dp,))],
    )(send, where, w0, *tokens)
    kv_own = place(scatter_sum(own_keep, own_send).astype(bf16))
    (d,) = after([d], mine, kv_own)
    grad_in = call(
        functools.partial(grad_kernel, tile=tile),
        like(piece, width),
        [vmem] * 3,
        vmem,
        12,
        "grad_in",
    )(hidden, norm_gain, d)
    return (kv_own, grad_in.reshape(hidden_in.shape), master_new[None], kv_next)


def solution(mesh):
    in_specs = (
        P("segment", None, ("dp", "tensor"), None),
        P("segment", None),
        P("segment", None, "dp", "tensor"),
        P("segment", "dp", "tensor"),
        P("segment", "dp", "tensor"),
        P("segment", "dp", "tensor"),
    )
    out_specs = (
        P("segment", None, "dp", "tensor"),
        P("segment", None, ("dp", "tensor"), None),
        P("segment", "dp", "tensor"),
        P("segment", None, "dp", "tensor"),
    )
    return jax.shard_map(shards, mesh=mesh, in_specs=in_specs, out_specs=out_specs, check_vma=False)
```

time: 184 us -> 226 us (1.23)
  waiting for transfers between devices: 99.4 us -> 133 us
  local copies, waits for them, and re-layouts: 14.8 us -> 25.1 us
  Pallas kernels: 28.9 us -> 25.2 us
    ppermute x27 -> x19, waiting for transfers between devices: 90.4 us -> 133 us  [swap(): return lax.ppermute(x, axis, [(i, i ^ bits) for i in range(peers)])]
    unnamed x59 -> x63, local copies, waits for them, and re-layouts: 14.7 us -> 25.1 us
    all_to_all x1 -> x2, waiting for transfers between devices: 9.02 us -> 0.01 us  [the longest x1 0.01 us: shards(): token0 = lax.all_to_all(own[0], 'dp', 0, 0, tiled=True)]
    ppermute x27 -> x19, starting transfers between devices: 26.3 us -> 18.4 us  [swap(): return lax.ppermute(x, axis, [(i, i ^ bits) for i in range(peers)])]
    all_to_all x1 -> x2, starting transfers between devices: 3.52 us -> 10.6 us  [the longest x1 6.32 us: shards(): token0 = lax.all_to_all(own[0], 'dp', 0, 0, tiled=True)]
    pallas_call x8 -> x5, Pallas kernels: 25.6 us -> 21.9 us  [the longest x1 10.6 us: shards(): call(functools.partial(update_kernel, count=count, tile=step), [like(own_...]
    convert_element_type x4 -> x5, other arithmetic: 2.39 us -> 4.83 us  [the longest x1 1.74 us: shards(): w0 = master_kv[0].astype(bf16)]
  transfers between devices with their start and end apart: 30 -> 23, of which waited for: 16 -> 12; matrix products, arithmetic and copies ran while one was open for 2% -> 2% of each run, Pallas kernels for 12% -> 10%
where the time goes in v8:
time: 226 us; the launch traced here: 225 us
  waiting for transfers between devices  133 us (59%)
  starting transfers between devices  35.5 us (16%)
  Pallas kernels  25.2 us (11%)
  local copies, waits for them, and re-layouts  25.1 us (11%)
  other arithmetic  5.03 us (2%)
    ppermute x19, waiting for transfers between devices, swap(): return lax.ppermute(x, axis, [(i, i ^ bits) for i in range(peers)])  133 us
    unnamed x63, local copies, waits for them, and re-layouts  25.1 us
    ppermute x19, starting transfers between devices, swap(): return lax.ppermute(x, axis, [(i, i ^ bits) for i in range(peers)])  18.4 us
    pallas_call x1, Pallas kernels, shards(): call(functools.partial(update_kernel, count=count, tile=step), [like(own_...  10.6 us
    all_to_all x1, starting transfers between devices, shards(): token0 = lax.all_to_all(own[0], 'dp', 0, 0, tiled=True)  6.32 us
    all_to_all x1, starting transfers between devices, shards(): d = lax.all_to_all(d, 'dp', 0, 0, tiled=True)  4.96 us
    pallas_call x1, Pallas kernels, shards(): call(functools.partial(project_kernel, count=count), part_shape, [anywher...  4.73 us
  transfers between devices with their start and end apart: 23, of which 12 were waited for; matrix products, arithmetic and copies ran while one was open for 2% of the time, Pallas kernels for 10%

profile of v8, /device:TPU:0, one launch (start us, length us, event | category | flops | bytes accessed | tf_op | source)
XLA Modules:
  0.0 225.3 jit_solution(7463812997638313929)
XLA Ops:
  0.6 1.6 copy-done.8
  3.0 2.3 %norm.1 = (bf16[4,64,2048]{2,1,0:T(8,128)(2,1)}, bf16[4,64,2048]{2,1,0:T(8,128)(2,1)S(1)}) custom-call(bf16[128,8192]{1,0:T(8,128)(2,1)S(1)} %bitcast.27, f32[1,8192]{1,0:T(1,128)S(1)} %copy-done.25), custom_call_target="tpu_custom_call" | custom-call | flops 1000 | bytes 1000 | tf_op jit(solution)/shard_map/norm/pallas_call | solution.py:275
  6.3 6.3 %all-to-all-start = ((bf16[4,64,2048]{2,1,0:T(8,128)(2,1)}), bf16[4,64,2048]{2,1,0:T(8,128)(2,1)S(1)}, u32[]{:S(2)}, u32[]{:S(2)}) async-start(bf16[4,64,2048]{2,1,0:T(8,128)(2,1)} %get-tuple-element.22), calls=%async_computation | async-start | bytes 2097152 | tf_op jit(solution)/shard_map/all_to_all | solution.py:283
  12.6 1.7 bitcast_convert_fusion.refs_4_.weights_ref
  14.4 1.6 collective-permute-start
  15.9 2.9 %collective-permute-start.2 = (bf16[2,256,256]{2,1,0:T(8,128)(2,1)S(1)}, bf16[2,256,256]{2,1,0:T(8,128)(2,1)}, u32[]{:S(2)}, u32[]{:S(2)}) collective-permute-start(bf16[2,256,256]{2,1,0:T(8,128)(2,1)S(1)} %bitcast.35), channel_id=1, source_target_pairs={{0,8},{4,12},{8,0},{12,4},{1,9},{5,13},{9,1},{13,5},{2,10},{6,14},... | collective-permute-start | bytes 786440 | tf_op jit(solution)/shard_map/ppermute | solution.py:29
  18.9 1.5 collective-permute-start.1
  20.3 29.3 %collective-permute-done.2.refs_2_ = bf16[2,256,256]{2,1,0:T(8,128)(2,1)} collective-permute-done((bf16[2,256,256]{2,1,0:T(8,128)(2,1)S(1)}, bf16[2,256,256]{2,1,0:T(8,128)(2,1)}, u32[]{:S(2)}, u32[]{:S(2)}) %collective-permute-start.2) | collective-permute-done | bytes 262176 | tf_op jit(solution)/shard_map/ppermute | solution.py:29
  49.8 7.5 %collective-permute-done.3.refs_3_ = bf16[2,256,256]{2,1,0:T(8,128)(2,1)} collective-permute-done((bf16[2,256,256]{2,1,0:T(8,128)(2,1)}, bf16[2,256,256]{2,1,0:T(8,128)(2,1)}, u32[]{:S(2)}, u32[]{:S(2)}) %collective-permute-start.3) | collective-permute-done | bytes 262176 | tf_op jit(solution)/shard_map/ppermute | solution.py:29
  58.2 1.9 arrange.1
  65.4 4.3 %all-to-all-start.1 = ((bf16[4,64,2048]{2,1,0:T(8,128)(2,1)}), bf16[4,64,2048]{2,1,0:T(8,128)(2,1)}, u32[]{:S(2)}, u32[]{:S(2)}) async-start(bf16[4,64,2048]{2,1,0:T(8,128)(2,1)} %copy-done.14), calls=%async_computation.1 | async-start | bytes 2097152 | tf_op jit(solution)/shard_map/all_to_all | solution.py:295
  70.3 1.5 collective-permute-start.5
  74.5 27.4 %collective-permute-done.8.refs_2_ = bf16[512,256]{1,0:T(8,128)(2,1)S(1)} collective-permute-done((bf16[512,256]{1,0:T(8,128)(2,1)}, bf16[512,256]{1,0:T(8,128)(2,1)S(1)}, u32[]{:S(2)}, u32[]{:S(2)}) %collective-permute-start.8) | collective-permute-done | bytes 262176 | tf_op jit(solution)/shard_map/ppermute | solution.py:29
  101.9 3.9 %collective-permute-done.9.refs_3_ = bf16[512,256]{1,0:T(8,128)(2,1)S(1)} collective-permute-done((bf16[512,256]{1,0:T(8,128)(2,1)}, bf16[512,256]{1,0:T(8,128)(2,1)S(1)}, u32[]{:S(2)}, u32[]{:S(2)}) %collective-permute-start.9) | collective-permute-done | bytes 262176 | tf_op jit(solution)/shard_map/ppermute | solution.py:29
  108.3 2.4 %d_normed.1.refs_1_ = bf16[4,128,2048]{2,1,0:T(8,128)(2,1)S(1)} custom-call(bf16[512,256]{1,0:T(8,128)(2,1)S(1)} %get-tuple-element.23.refs_2_.refs_0_, bf16[512,256]{1,0:T(8,128)(2,1)S(1)} %collective-permute-done.7.refs_1_, bf16[512,256]{1,0:T(8,128)(2,1)S(1)} %collective-permute-done.8.refs_2_, bf16[512,256]{1,0:T(8,128)(2,1)S(1)} %collective-permute-done.9.refs_3_, ...), custom_call_target="tpu_custom_call" | custom-call | flops 1000 | bytes 1000 | tf_op jit(solution)/shard_map/d_normed/pallas_call | solution.py:299
  114.2 5.0 %all-to-all-start.2 = ((bf16[4,128,2048]{2,1,0:T(8,128)(2,1)}), bf16[4,128,2048]{2,1,0:T(8,128)(2,1)S(1)}, u32[]{:S(2)}, u32[]{:S(2)}) async-start(bf16[4,128,2048]{2,1,0:T(8,128)(2,1)} %copy-done), calls=%async_computation.2 | async-start | bytes 4194304 | tf_op jit(solution)/shard_map/all_to_all | solution.py:308
  119.1 1.5 collective-permute-start.13
  121.3 23.5 %collective-permute-done.13.rest_6_ = bf16[4,64,2048]{2,1,0:T(8,128)(2,1)S(1)} collective-permute-done((bf16[4,64,2048]{2,1,0:T(8,128)(2,1)}, bf16[4,64,2048]{2,1,0:T(8,128)(2,1)S(1)}, u32[]{:S(2)}, u32[]{:S(2)}) %collective-permute-start.13) | collective-permute-done | bytes 1048608 | tf_op jit(solution)/shard_map/ppermute | solution.py:29
  144.9 2.6 %collective-permute-done.14.rest_7_ = bf16[4,64,2048]{2,1,0:T(8,128)(2,1)S(1)} collective-permute-done((bf16[4,64,2048]{2,1,0:T(8,128)(2,1)S(1)}, bf16[4,64,2048]{2,1,0:T(8,128)(2,1)S(1)}, u32[]{:S(2)}, u32[]{:S(2)}) %collective-permute-start.14) | collective-permute-done | bytes 1048608 | tf_op jit(solution)/shard_map/ppermute | solution.py:29
  148.7 1.6 copy-done.7
  150.3 1.6 copy-done.15
  151.9 1.6 copy-done.16
  154.7 10.6 %update.1 = (f32[2048,256]{1,0:T(8,128)}, bf16[2,512,256]{2,1,0:T(8,128)(2,1)S(1)}, bf16[2,512,256]{2,1,0:T(8,128)(2,1)S(1)}) custom-call(s32[2]{0:T(128)S(1)} %pad_add_fusion.where_ref, bf16[256,2048]{1,0:T(8,128)(2,1)S(1)} %copy-done.18, f32[2048,256]{1,0:T(8,128)S(1)} %bitcast.26, f32[2048,256]{1,0:T(8,128)S(1)} %bitcast.29, f32[2048,256]{1,0:T(8,128)S(1)} %bitcast.30, ...), custom_call_target="tpu_custom_call" | custom-call | flops 1000 | bytes 1000 | tf_op jit(solution)/shard_map/update/pallas_call | solution.py:320
  165.3 4.7 %project.1 = (bf16[2,512,256]{2,1,0:T(8,128)(2,1)S(1)}, bf16[2,512,256]{2,1,0:T(8,128)(2,1)S(1)}) custom-call(bf16[2,512,256]{2,1,0:T(8,128)(2,1)S(1)} %get-tuple-element.30.mark_ref, s32[2]{0:T(128)S(1)} %pad_add_fusion.where_ref, bf16[2048,256]{1,0:T(8,128)(2,1)S(1)} %copy-done.3, bf16[4,64,2048]{2,1,0:T(8,128)(2,1)S(1)} %get-tuple-element.24.rest_0_, ...), custom_call_target="tpu_custom_call" | custom-call | flops 1000 | bytes 1000 | tf_op jit(solution)/shard_map/project/pallas_call | solution.py:348
  170.1 1.8 collective-permute-start.15
  172.2 12.7 %collective-permute-done.15 = bf16[2,512,256]{2,1,0:T(8,128)(2,1)S(1)} collective-permute-done((bf16[2,512,256]{2,1,0:T(8,128)(2,1)S(1)}, bf16[2,512,256]{2,1,0:T(8,128)(2,1)S(1)}, u32[]{:S(2)}, u32[]{:S(2)}) %collective-permute-start.15) | collective-permute-done | bytes 524320 | tf_op jit(solution)/shard_map/ppermute | solution.py:29
  185.0 2.7 %collective-permute-start.16 = (bf16[512,256]{1,0:T(8,128)(2,1)S(1)}, bf16[512,256]{1,0:T(8,128)(2,1)}, u32[]{:S(2)}, u32[]{:S(2)}) collective-permute-start(bf16[512,256]{1,0:T(8,128)(2,1)S(1)} %fusion.2), channel_id=1, source_target_pairs={{0,8},{4,12},{8,0},{12,4},{1,9},{5,13},{9,1},{13,5},{2,10},{6,14},... | collective-permute-start | bytes 786440 | tf_op jit(solution)/shard_map/ppermute | solution.py:29
  187.7 13.3 %collective-permute-done.17.refs_0_ = bf16[2,512,256]{2,1,0:T(8,128)(2,1)S(1)} collective-permute-done((bf16[2,512,256]{2,1,0:T(8,128)(2,1)S(1)}, bf16[2,512,256]{2,1,0:T(8,128)(2,1)S(1)}, u32[]{:S(2)}, u32[]{:S(2)}) %collective-permute-start.17) | collective-permute-done | bytes 524320 | tf_op jit(solution)/shard_map/ppermute | solution.py:29
  201.7 1.6 collective-permute-start.18
  204.6 11.5 %collective-permute-done.18 = bf16[512,256]{1,0:T(8,128)(2,1)} collective-permute-done((bf16[512,256]{1,0:T(8,128)(2,1)}, bf16[512,256]{1,0:T(8,128)(2,1)}, u32[]{:S(2)}, u32[]{:S(2)}) %collective-permute-start.18) | collective-permute-done | bytes 262176 | tf_op jit(solution)/shard_map/ppermute | solution.py:29
  217.2 1.5 collective-permute-start.19
  220.6 3.3 %grad_in.1 = bf16[128,8192]{1,0:T(8,128)(2,1)} custom-call(bf16[128,8192]{1,0:T(8,128)(2,1)S(1)} %bitcast.28, f32[1,8192]{1,0:T(1,128)S(1)} %copy-done.26, bf16[4,128,2048]{2,1,0:T(8,128)(2,1)S(1)} %after.7.d_ref), custom_call_target="tpu_custom_call" | custom-call | flops 1000 | bytes 1000 | tf_op jit(solution)/shard_map/grad_in/pallas_call | solution.py:359
  (97 shorter events, 27.0 us)
Async XLA Ops:
  6.3 56.9 %all-to-all-start = ((bf16[4,64,2048]{2,1,0:T(8,128)(2,1)}), bf16[4,64,2048]{2,1,0:T(8,128)(2,1)S(1)}, u32[]{:S(2)}, u32[]{:S(2)}) async-start(bf16[4,64,2048]{2,1,0:T(8,128)(2,1)} %get-tuple-element.22), calls=%async_computation | async-start | bytes 2097152 | tf_op jit(solution)/shard_map/all_to_all | solution.py:283
  12.6 3.3 %copy-start.23 = (bf16[1,2,256,256]{3,2,1,0:T(8,128)(2,1)S(1)}, bf16[1,2,256,256]{3,2,1,0:T(8,128)(2,1)}, u32[]{:S(2)}) copy-start(bf16[1,2,256,256]{3,2,1,0:T(8,128)(2,1)} %param.8) | copy-start | bytes 786436
  14.3 55.4 %copy-start.1 = (bf16[2048,256]{1,0:T(8,128)(2,1)}, bf16[2048,256]{1,0:T(8,128)(2,1)S(1)}, u32[]{:S(2)}) copy-start(bf16[2048,256]{1,0:T(8,128)(2,1)S(1)} %bitcast_convert_fusion.refs_4_.weights_ref) | copy-start | bytes 3145732
  14.4 42.9 %collective-permute-start = (bf16[2048,256]{1,0:T(8,128)(2,1)S(1)}, bf16[2048,256]{1,0:T(8,128)(2,1)S(1)}, u32[]{:S(2)}, u32[]{:S(2)}) collective-permute-start(bf16[2048,256]{1,0:T(8,128)(2,1)S(1)} %bitcast_convert_fusion.refs_4_.weights_ref), channel_id=1, source_target_pairs={{0,2},{1,3},{2,0},{3,1},{4,6},{5,7},{6,4},{7,5},{8,10},{9,11},{10,... | collective-permute-start | bytes 3145736 | tf_op jit(solution)/shard_map/ppermute | solution.py:29
  15.9 33.7 %collective-permute-start.2 = (bf16[2,256,256]{2,1,0:T(8,128)(2,1)S(1)}, bf16[2,256,256]{2,1,0:T(8,128)(2,1)}, u32[]{:S(2)}, u32[]{:S(2)}) collective-permute-start(bf16[2,256,256]{2,1,0:T(8,128)(2,1)S(1)} %bitcast.35), channel_id=1, source_target_pairs={{0,8},{4,12},{8,0},{12,4},{1,9},{5,13},{9,1},{13,5},{2,10},{6,14},... | collective-permute-start | bytes 786440 | tf_op jit(solution)/shard_map/ppermute | solution.py:29
  18.9 30.9 %collective-permute-start.1 = (bf16[2,256,256]{2,1,0:T(8,128)(2,1)S(1)}, bf16[2,256,256]{2,1,0:T(8,128)(2,1)}, u32[]{:S(2)}, u32[]{:S(2)}) collective-permute-start(bf16[2,256,256]{2,1,0:T(8,128)(2,1)S(1)} %bitcast.36), channel_id=1, source_target_pairs={{0,4},{4,0},{8,12},{12,8},{1,5},{5,1},{9,13},{13,9},{2,6},{6,2},{1... | collective-permute-start | bytes 786440 | tf_op jit(solution)/shard_map/ppermute | solution.py:29
  49.7 7.6 %collective-permute-start.3 = (bf16[2,256,256]{2,1,0:T(8,128)(2,1)}, bf16[2,256,256]{2,1,0:T(8,128)(2,1)}, u32[]{:S(2)}, u32[]{:S(2)}) collective-permute-start(bf16[2,256,256]{2,1,0:T(8,128)(2,1)} %collective-permute-done.2.refs_2_), channel_id=1, source_target_pairs={{0,4},{4,0},{8,12},{12,8},{1,5},{5,1},{9,13},{13,9},{2,6},{6,2},{1... | collective-permute-start | bytes 786440 | tf_op jit(solution)/shard_map/ppermute | solution.py:29
  58.2 11.6 %copy-start.10 = (bf16[2048,256]{1,0:T(8,128)(2,1)}, bf16[2048,256]{1,0:T(8,128)(2,1)S(1)}, u32[]{:S(2)}) copy-start(bf16[2048,256]{1,0:T(8,128)(2,1)S(1)} %collective-permute-done.mark_ref.refs_6_) | copy-start | bytes 3145732
  65.4 46.2 %all-to-all-start.1 = ((bf16[4,64,2048]{2,1,0:T(8,128)(2,1)}), bf16[4,64,2048]{2,1,0:T(8,128)(2,1)}, u32[]{:S(2)}, u32[]{:S(2)}) async-start(bf16[4,64,2048]{2,1,0:T(8,128)(2,1)} %copy-done.14), calls=%async_computation.1 | async-start | bytes 2097152 | tf_op jit(solution)/shard_map/all_to_all | solution.py:295
  69.7 2.7 %collective-permute-start.10 = (bf16[2048,256]{1,0:T(8,128)(2,1)S(1)}, bf16[2048,256]{1,0:T(8,128)(2,1)S(1)}, u32[]{:S(2)}, u32[]{:S(2)}) collective-permute-start(bf16[2048,256]{1,0:T(8,128)(2,1)S(1)} %bitcast_convert_fusion.refs_4_.weights_ref), channel_id=1, source_target_pairs={{0,1},{1,0},{2,3},{3,2},{4,5},{5,4},{6,7},{7,6},{8,9},{9,8},{10,11... | collective-permute-start | bytes 3145736 | tf_op jit(solution)/shard_map/ppermute | solution.py:29
  69.8 36.0 %collective-permute-start.11 = (bf16[2048,256]{1,0:T(8,128)(2,1)S(1)}, bf16[2048,256]{1,0:T(8,128)(2,1)S(1)}, u32[]{:S(2)}, u32[]{:S(2)}) collective-permute-start(bf16[2048,256]{1,0:T(8,128)(2,1)S(1)} %collective-permute-done.mark_ref.refs_6_), channel_id=1, source_target_pairs={{0,1},{1,0},{2,3},{3,2},{4,5},{5,4},{6,7},{7,6},{8,9},{9,8},{10,11... | collective-permute-start | bytes 3145736 | tf_op jit(solution)/shard_map/ppermute | solution.py:29
  70.3 40.4 %collective-permute-start.5 = (bf16[4,64,2048]{2,1,0:T(8,128)(2,1)S(1)}, bf16[4,64,2048]{2,1,0:T(8,128)(2,1)S(1)}, u32[]{:S(2)}, u32[]{:S(2)}) collective-permute-start(bf16[4,64,2048]{2,1,0:T(8,128)(2,1)S(1)} %get-tuple-element.24.rest_0_), channel_id=1, source_target_pairs={{0,2},{1,3},{2,0},{3,1},{4,6},{5,7},{6,4},{7,5},{8,10},{9,11},{10,... | collective-permute-start | bytes 3145736 | tf_op jit(solution)/shard_map/ppermute | solution.py:29
  71.8 2.7 %collective-permute-start.7 = (bf16[512,256]{1,0:T(8,128)(2,1)}, bf16[512,256]{1,0:T(8,128)(2,1)S(1)}, u32[]{:S(2)}, u32[]{:S(2)}) collective-permute-start(bf16[512,256]{1,0:T(8,128)(2,1)} %copy-done.29), channel_id=1, source_target_pairs={{0,1},{1,0},{2,3},{3,2},{4,5},{5,4},{6,7},{7,6},{8,9},{9,8},{10,11... | collective-permute-start | bytes 786440 | tf_op jit(solution)/shard_map/ppermute | solution.py:29
  71.8 30.1 %collective-permute-start.8 = (bf16[512,256]{1,0:T(8,128)(2,1)}, bf16[512,256]{1,0:T(8,128)(2,1)S(1)}, u32[]{:S(2)}, u32[]{:S(2)}) collective-permute-start(bf16[512,256]{1,0:T(8,128)(2,1)} %copy-done.28), channel_id=1, source_target_pairs={{0,2},{1,3},{2,0},{3,1},{4,6},{5,7},{6,4},{7,5},{8,10},{9,11},{10,... | collective-permute-start | bytes 786440 | tf_op jit(solution)/shard_map/ppermute | solution.py:29
  72.4 33.4 %collective-permute-start.9 = (bf16[512,256]{1,0:T(8,128)(2,1)}, bf16[512,256]{1,0:T(8,128)(2,1)S(1)}, u32[]{:S(2)}, u32[]{:S(2)}) collective-permute-start(bf16[512,256]{1,0:T(8,128)(2,1)} %copy-done.27), channel_id=1, source_target_pairs={{0,3},{1,2},{2,1},{3,0},{4,7},{5,6},{6,5},{7,4},{8,11},{9,10},{10,... | collective-permute-start | bytes 786440 | tf_op jit(solution)/shard_map/ppermute | solution.py:29
  114.2 86.8 %all-to-all-start.2 = ((bf16[4,128,2048]{2,1,0:T(8,128)(2,1)}), bf16[4,128,2048]{2,1,0:T(8,128)(2,1)S(1)}, u32[]{:S(2)}, u32[]{:S(2)}) async-start(bf16[4,128,2048]{2,1,0:T(8,128)(2,1)} %copy-done), calls=%async_computation.2 | async-start | bytes 4194304 | tf_op jit(solution)/shard_map/all_to_all | solution.py:308
  119.1 25.7 %collective-permute-start.13 = (bf16[4,64,2048]{2,1,0:T(8,128)(2,1)}, bf16[4,64,2048]{2,1,0:T(8,128)(2,1)S(1)}, u32[]{:S(2)}, u32[]{:S(2)}) collective-permute-start(bf16[4,64,2048]{2,1,0:T(8,128)(2,1)} %get-tuple-element.29.rest_4_), channel_id=1, source_target_pairs={{0,2},{1,3},{2,0},{3,1},{4,6},{5,7},{6,4},{7,5},{8,10},{9,11},{10,... | collective-permute-start | bytes 3145736 | tf_op jit(solution)/shard_map/ppermute | solution.py:29
  120.6 24.2 %collective-permute-start.4 = (bf16[4,64,2048]{2,1,0:T(8,128)(2,1)S(1)}, bf16[4,64,2048]{2,1,0:T(8,128)(2,1)S(1)}, u32[]{:S(2)}, u32[]{:S(2)}) collective-permute-start(bf16[4,64,2048]{2,1,0:T(8,128)(2,1)S(1)} %get-tuple-element.24.rest_0_), channel_id=1, source_target_pairs={{0,1},{1,0},{2,3},{3,2},{4,5},{5,4},{6,7},{7,6},{8,9},{9,8},{10,11... | collective-permute-start | bytes 3145736 | tf_op jit(solution)/shard_map/ppermute | solution.py:29
  120.8 24.1 %collective-permute-start.6 = (bf16[4,64,2048]{2,1,0:T(8,128)(2,1)}, bf16[4,64,2048]{2,1,0:T(8,128)(2,1)S(1)}, u32[]{:S(2)}, u32[]{:S(2)}) collective-permute-start(bf16[4,64,2048]{2,1,0:T(8,128)(2,1)} %copy-done.4), channel_id=1, source_target_pairs={{0,1},{1,0},{2,3},{3,2},{4,5},{5,4},{6,7},{7,6},{8,9},{9,8},{10,11... | collective-permute-start | bytes 3145736 | tf_op jit(solution)/shard_map/ppermute | solution.py:29
  121.2 23.7 %collective-permute-start.12 = (bf16[4,64,2048]{2,1,0:T(8,128)(2,1)}, bf16[4,64,2048]{2,1,0:T(8,128)(2,1)S(1)}, u32[]{:S(2)}, u32[]{:S(2)}) collective-permute-start(bf16[4,64,2048]{2,1,0:T(8,128)(2,1)} %get-tuple-element.29.rest_4_), channel_id=1, source_target_pairs={{0,1},{1,0},{2,3},{3,2},{4,5},{5,4},{6,7},{7,6},{8,9},{9,8},{10,11... | collective-permute-start | bytes 3145736 | tf_op jit(solution)/shard_map/ppermute | solution.py:29
  144.9 2.7 %collective-permute-start.14 = (bf16[4,64,2048]{2,1,0:T(8,128)(2,1)S(1)}, bf16[4,64,2048]{2,1,0:T(8,128)(2,1)S(1)}, u32[]{:S(2)}, u32[]{:S(2)}) collective-permute-start(bf16[4,64,2048]{2,1,0:T(8,128)(2,1)S(1)} %collective-permute-done.13.rest_6_), channel_id=1, source_target_pairs={{0,1},{1,0},{2,3},{3,2},{4,5},{5,4},{6,7},{7,6},{8,9},{9,8},{10,11... | collective-permute-start | bytes 3145736 | tf_op jit(solution)/shard_map/ppermute | solution.py:29
  154.7 10.6 %copy-start.3 = (bf16[2048,256]{1,0:T(8,128)(2,1)S(1)}, bf16[2048,256]{1,0:T(8,128)(2,1)}, u32[]{:S(2)}) copy-start(bf16[2048,256]{1,0:T(8,128)(2,1)} %copy-done.1) | copy-start | bytes 3145732
  165.3 4.8 %copy-start.20 = (bf16[2,512,256]{2,1,0:T(8,128)(2,1)}, bf16[2,512,256]{2,1,0:T(8,128)(2,1)S(1)}, u32[]{:S(2)}) copy-start(bf16[2,512,256]{2,1,0:T(8,128)(2,1)S(1)} %get-tuple-element.34) | copy-start | bytes 1572868
  170.1 17.6 %copy-start.22 = (bf16[2,512,256]{2,1,0:T(8,128)(2,1)}, bf16[2,512,256]{2,1,0:T(8,128)(2,1)S(1)}, u32[]{:S(2)}) copy-start(bf16[2,512,256]{2,1,0:T(8,128)(2,1)S(1)} %get-tuple-element.31) | copy-start | bytes 1572868
  170.1 30.9 %copy-start.21 = (bf16[2,512,256]{2,1,0:T(8,128)(2,1)S(1)}, bf16[2,512,256]{2,1,0:T(8,128)(2,1)}, u32[]{:S(2)}) copy-start(bf16[2,512,256]{2,1,0:T(8,128)(2,1)} %copy-done.20) | copy-start | bytes 1572868
  170.1 14.8 %collective-permute-start.15 = (bf16[2,512,256]{2,1,0:T(8,128)(2,1)S(1)}, bf16[2,512,256]{2,1,0:T(8,128)(2,1)S(1)}, u32[]{:S(2)}, u32[]{:S(2)}) collective-permute-start(bf16[2,512,256]{2,1,0:T(8,128)(2,1)S(1)} %get-tuple-element.32), channel_id=1, source_target_pairs={{0,4},{4,0},{8,12},{12,8},{1,5},{5,1},{9,13},{13,9},{2,6},{6,2},{1... | collective-permute-start | bytes 1572872 | tf_op jit(solution)/shard_map/ppermute | solution.py:29
  171.9 29.1 %collective-permute-start.17 = (bf16[2,512,256]{2,1,0:T(8,128)(2,1)S(1)}, bf16[2,512,256]{2,1,0:T(8,128)(2,1)S(1)}, u32[]{:S(2)}, u32[]{:S(2)}) collective-permute-start(bf16[2,512,256]{2,1,0:T(8,128)(2,1)S(1)} %get-tuple-element.30.mark_ref), channel_id=1, source_target_pairs={{0,4},{4,0},{8,12},{12,8},{1,5},{5,1},{9,13},{13,9},{2,6},{6,2},{1... | collective-permute-start | bytes 1572872 | tf_op jit(solution)/shard_map/ppermute | solution.py:29
  184.9 2.8 %copy-start.30 = (bf16[2,512,256]{2,1,0:T(8,128)(2,1)}, bf16[2,512,256]{2,1,0:T(8,128)(2,1)S(1)}, u32[]{:S(2)}) copy-start(bf16[2,512,256]{2,1,0:T(8,128)(2,1)S(1)} %collective-permute-done.15) | copy-start | bytes 1572868
  185.0 18.4 %collective-permute-start.16 = (bf16[512,256]{1,0:T(8,128)(2,1)S(1)}, bf16[512,256]{1,0:T(8,128)(2,1)}, u32[]{:S(2)}, u32[]{:S(2)}) collective-permute-start(bf16[512,256]{1,0:T(8,128)(2,1)S(1)} %fusion.2), channel_id=1, source_target_pairs={{0,8},{4,12},{8,0},{12,4},{1,9},{5,13},{9,1},{13,5},{2,10},{6,14},... | collective-permute-start | bytes 786440 | tf_op jit(solution)/shard_map/ppermute | solution.py:29
  201.7 14.4 %collective-permute-start.18 = (bf16[512,256]{1,0:T(8,128)(2,1)}, bf16[512,256]{1,0:T(8,128)(2,1)}, u32[]{:S(2)}, u32[]{:S(2)}) collective-permute-start(bf16[512,256]{1,0:T(8,128)(2,1)} %fusion.3), channel_id=1, source_target_pairs={{0,8},{4,12},{8,0},{12,4},{1,9},{5,13},{9,1},{13,5},{2,10},{6,14},... | collective-permute-start | bytes 786440 | tf_op jit(solution)/shard_map/ppermute | solution.py:29
  217.2 7.3 %collective-permute-start.19 = (bf16[1,2,256,256]{3,2,1,0:T(8,128)(2,1)S(1)}, bf16[1,2,256,256]{3,2,1,0:T(8,128)(2,1)S(1)}, u32[]{:S(2)}, u32[]{:S(2)}) collective-permute-start(bf16[1,2,256,256]{3,2,1,0:T(8,128)(2,1)S(1)} %bitcast.31), channel_id=1, source_target_pairs={{0,16},{16,0},{1,17},{17,1},{2,18},{18,2},{3,19},{19,3},{4,20},{20... | collective-permute-start | bytes 786440 | tf_op jit(solution)/shard_map/ppermute | solution.py:34
  218.9 1.7 copy-start.9
  (22 other events, 25.1 us)

commit v9 on v8

--- a/solution.py
+++ b/solution.py
@@ -74,15 +74,16 @@
 
 
 def norm_kernel(hidden_ref, gain_ref, *own_refs, tile):
-    blocks, rows = own_refs[0].shape[:2]
+    blocks = own_refs[0].shape[0]
     width = hidden_ref.shape[1]
     depth = width // blocks
-    for m, own_ref in enumerate(own_refs):
-
-        @pl.loop(0, rows // tile)
-        def _(i, m=m, own_ref=own_ref):
+    start = 0
+    for own_ref in own_refs:
+
+        @pl.loop(0, own_ref.shape[1] // tile)
+        def _(i, start=start, own_ref=own_ref):
             row = pl.multiple_of(i * tile, tile)
-            at, to = pl.ds(m * rows + row, tile), pl.ds(row, tile)
+            at, to = pl.ds(start + row, tile), pl.ds(row, tile)
             total = jnp.zeros((tile, 1), f32)
             for k in range(blocks):
                 part = hidden_ref[at, k * depth : (k + 1) * depth].astype(f32)
@@ -93,6 +94,8 @@
                 own_ref[k, to, :] = (
                     hidden_ref[at, cut].astype(f32) * scaling * gain_ref[:, cut]
                 ).astype(bf16)
+
+        start += own_ref.shape[1]
 
 
 def grad_kernel(hidden_ref, gain_ref, d_ref, out_ref, *, tile):
@@ -120,25 +123,30 @@
             out_ref[at, cut] = (scaling * upper - hidden * factor).astype(bf16)
 
 
-def arrange_kernel(mark_ref, where_ref, *refs, dp, layout):
+def arrange_kernel(mark_ref, where_ref, *refs, dp, cuts):
     cots, send_refs, (turned_ref, held) = refs[:dp], refs[dp:-2], refs[-2:]
     z, t = where_ref[0], where_ref[1]
+    tensor = len(send_refs)
     micro, rows, cols = cots[0].shape
-    rows //= len(send_refs)
+    rows //= tensor
+    piece = micro * rows
     for k in range(dp):
         held[z ^ k] = cots[k][...]
-
-    def block(k, m, j):
-        return held[k, m, pl.ds(pl.multiple_of((t ^ j) * rows, rows), rows), :]
-
     for j, send_ref in enumerate(send_refs):
+        at = pl.ds(pl.multiple_of((t ^ j) * rows, rows), rows)
         for k in range(dp):
             for m in range(micro):
-                at = (k * micro + m) * rows
-                send_ref[at : at + rows, :] = block(k, m, j)
-    for p, (m, j) in enumerate(layout):
-        part = jnp.concatenate([block(k, m, j) for k in range(dp)])
-        turned_ref[:, p * dp * rows : (p + 1) * dp * rows] = part.astype(f32).T.astype(bf16)
+                start = k * piece + m * rows
+                send_ref[start : start + rows, :] = held[k, m, at, :]
+    position = 0
+    for low, high in zip(cuts[:-1], cuts[1:]):
+        for send_ref in send_refs:
+            part = jnp.concatenate(
+                [send_ref[k * piece + low : k * piece + high, :] for k in range(dp)]
+            )
+            width = dp * (high - low)
+            turned_ref[:, position : position + width] = part.astype(f32).T.astype(bf16)
+            position += width
 
 
 def d_kernel(*refs):
@@ -169,13 +177,15 @@
     return copies
 
 
-def update_kernel(where_ref, turned_ref, master_hbm, m_hbm, v_hbm, *rest, count, tile):
-    token_refs, (new_hbm, keep_ref, send_ref) = rest[:count], rest[count : count + 3]
-    tokens, master, m, v, updated, new, product, sems, out_sems = rest[count + 3 :]
-    tiles = master.shape[0] // tile
+def update_kernel(mark_ref, where_ref, turned_ref, weights_ref, master_hbm, m_hbm, v_hbm, *rest, cuts):
+    tensor = (len(rest) - 13) // (len(cuts) - 1)
+    count = tensor * (len(cuts) - 1)
+    token_refs, new_hbm, part_refs = rest[:count], rest[count], rest[count + 1 : count + 5]
+    tokens, master, m, v, updated, new, sems, out_sems = rest[count + 5 :]
+    tile = new.shape[0] // out_sems.shape[0]
     each = count * token_refs[0].shape[0] + 3
     groups = []
-    for i in range(tiles):
+    for i in range(out_sems.shape[0]):
         cut = pl.ds(i * tile, tile)
         group = token_copies(token_refs, tokens, sems, cut, i * each)
         for p, (source, target) in enumerate(((master_hbm, master), (m_hbm, m), (v_hbm, v))):
@@ -188,7 +198,7 @@
             copy.start()
         groups.append(group)
     outs = []
-    for i in range(tiles):
+    for i in range(out_sems.shape[0]):
         cut = slice(i * tile, (i + 1) * tile)
         for copy in groups[i]:
             copy.wait()
@@ -208,33 +218,42 @@
         out.start()
         outs.append(out)
         updated[cut, :] = master_new.astype(bf16)
-    project(where_ref, tokens, updated, keep_ref, send_ref, product, count)
+    project(where_ref, tokens, updated, *part_refs[:2], cuts, 0)
+    project(where_ref, tokens, weights_ref, *part_refs[2:], cuts, len(cuts) - 2)
     for out in outs:
         out.wait()
 
 
-def project(where_ref, tokens, weights, keep_ref, send_ref, product, count):
+def project(where_ref, tokens, weights, keep_ref, send_ref, cuts, first):
     z = where_ref[0]
-    dp, rows = product.shape[1:3]
-    size = dp * rows
-    for p in range(count):
-        part = dot(tokens[p * size : (p + 1) * size, :], weights[...], ((1,), (0,)))
-        product[p] = part.astype(bf16).reshape(product.shape[1:])
-    for k in range(dp):
-        part_ref = send_ref if k % 2 else keep_ref
-        for p in range(count):
-            part_ref[k // 2, p * rows : (p + 1) * rows, :] = product[p, z ^ k]
-
-
-def project_kernel(mark_ref, where_ref, weights_ref, *rest, count):
-    token_refs = rest[:count]
-    keep_ref, send_ref, tokens, product, sems = rest[count:]
+    dp = 4
+    tensor = tokens.shape[0] // (dp * cuts[-1])
+    stored = keep_ref.shape[1] // tensor
+    for c in range(first, len(cuts) - 1):
+        rows = cuts[c + 1] - cuts[c]
+        for j in range(tensor):
+            at = dp * (tensor * cuts[c] + j * rows)
+            part = dot(tokens[at : at + dp * rows, :], weights[...], ((1,), (0,))).astype(bf16)
+            to = j * stored + cuts[c] - cuts[first]
+            for k in range(dp):
+                piece = part[k * rows : (k + 1) * rows]
+                if k % 2 == 0:
+                    even = piece
+                else:
+                    odd = z % 2 == 1
+                    slot = (k // 2) ^ (z // 2)
+                    keep_ref[slot, to : to + rows, :] = jnp.where(odd, piece, even)
+                    send_ref[slot, to : to + rows, :] = jnp.where(odd, even, piece)
+
+
+def project_kernel(where_ref, weights_ref, *rest, cuts):
+    token_refs, (keep_ref, send_ref, tokens, sems) = rest[:-4], rest[-4:]
     copies = token_copies(token_refs, tokens, sems, slice(None), 0)
     for copy in copies:
         copy.start()
     for copy in copies:
         copy.wait()
-    project(where_ref, tokens, weights_ref, keep_ref, send_ref, product, count)
+    project(where_ref, tokens, weights_ref, keep_ref, send_ref, cuts, 0)
 
 
 def reorder(blocks, me):
@@ -252,7 +271,7 @@
         got = after([got], *earlier)[0]
     mine = keep[0].astype(f32) + got[0].astype(f32)
     other = (keep[1].astype(f32) + got[1].astype(f32)).astype(bf16)
-    return mine + swap(other, "dp", 2).astype(f32)
+    return mine + swap(other, "dp", 2).astype(f32), got
 
 
 def shards(hidden_in, norm_gain, kv_cot, master_kv, moment_m, moment_v):
@@ -271,97 +290,112 @@
     w2, w1 = swap(w0, "tensor", 2), swap(w0, "tensor", 1)
     cot0 = kv_cot[0]
     cot2, cot1 = swap(cot0, "dp", 2), swap(cot0, "dp", 1)
-    cot3 = swap(cot2, "dp", 1)
+    cot3 = swap(cot0, "dp", 3)
+    cuts = (0, 3 * piece // 8, 3 * piece // 4, piece)
     own = call(
         functools.partial(norm_kernel, tile=tile),
-        [like(dp, rows, depth)] * micro,
+        [like(dp, high - low, depth) for low, high in zip(cuts[:-1], cuts[1:])],
         [vmem, vmem],
-        [vmem] * micro,
-        8,
+        [vmem] * (len(cuts) - 1),
+        60,
         "norm",
     )(hidden, norm_gain)
-    token0 = lax.all_to_all(own[0], "dp", 0, 0, tiled=True)
-    layout = tuple((m, j) for m in range(micro) for j in (0, 1, 2, 3))
     *blocks, turned = call(
-        functools.partial(arrange_kernel, dp=dp, layout=layout),
+        functools.partial(arrange_kernel, dp=dp, cuts=cuts),
         [like(dp * piece, cols)] * tensor + [like(cols, dp * tensor * piece)],
         [anywhere, smem] + [vmem] * dp,
         [vmem] * (tensor + 1),
-        8,
+        60,
         "arrange",
         scratch=[pltpu.VMEM((dp,) + cot0.shape, bf16)],
     )(w2, where, cot0, cot1, cot2, cot3)
-    own1, token0 = after([own[1], token0], blocks[0])
+    (own0,) = after([own[0]], blocks[0])
+    token0 = lax.all_to_all(own0, "dp", 0, 0, tiled=True)
+    mine_cot = [blocks[0]] + [swap(blocks[j], "tensor", j) for j in range(1, tensor)]
+    w3 = swap(w2, "tensor", 1)
+    own1, token0 = after([own[1], token0], mine_cot[2], mine_cot[3])
     token1 = lax.all_to_all(own1, "dp", 0, 0, tiled=True)
     across0 = swap(token0, "tensor", 2)
-    mine_cot = [blocks[0]] + [swap(blocks[j], "tensor", j) for j in range(1, tensor)]
-    w3 = swap(w2, "tensor", 1)
     d = call(
         d_kernel,
         like(dp, piece, depth),
         [vmem] * 8,
         vmem,
-        20,
+        60,
         "d_normed",
     )(*mine_cot, w0, w1, w2, w3)
-    token1, d = after([token1, d], across0)
+    own2, token1 = after([own[2], token1], across0)
+    token2 = lax.all_to_all(own2, "dp", 0, 0, tiled=True)
+    across1 = swap(token1, "tensor", 2)
+    token2, d = after([token2, d], across1)
     d = lax.all_to_all(d, "dp", 0, 0, tiled=True)
+    across2 = swap(token2, "tensor", 2)
     tokens = []
-    for x, across in ((token0, across0), (token1, swap(token1, "tensor", 2))):
+    for x, across in ((token0, across0), (token1, across1), (token2, across2)):
         tokens += [x, swap(x, "tensor", 1), across, swap(across, "tensor", 1)]
     count = len(tokens)
     block = tensor * piece
+    first = cuts[-2]
     part_shape = [like(dp // 2, block, cols)] * 2
     step = min(own_depth, 512)
     tiles = own_depth // step
     whole = pltpu.VMEM((own_depth, cols), f32)
-    all_tokens = pltpu.VMEM((dp * block, depth), bf16)
-    product = pltpu.VMEM((count, dp, rows, cols), bf16)
-    master_new, keep, send = call(
-        functools.partial(update_kernel, count=count, tile=step),
-        [like(own_depth, cols, dtype=f32)] + part_shape,
-        [smem, vmem] + [anywhere] * (3 + count),
-        [anywhere] + [vmem] * 2,
-        25,
+    keep0, send0 = call(
+        functools.partial(project_kernel, cuts=cuts[:-1]),
+        [like(dp // 2, tensor * first, cols)] * 2,
+        [smem, vmem] + [anywhere] * (count - tensor),
+        [vmem] * 2,
+        60,
+        "project",
+        scratch=[
+            pltpu.VMEM((dp * tensor * first, depth), bf16),
+            pltpu.SemaphoreType.DMA(((count - tensor) * dp,)),
+        ],
+    )(where, w0, *tokens[:-tensor])
+    master_new, keep, send, keep1, send1 = call(
+        functools.partial(update_kernel, cuts=cuts),
+        [like(own_depth, cols, dtype=f32)] + part_shape
+        + [like(dp // 2, tensor * (piece - first), cols)] * 2,
+        [anywhere, smem, vmem, vmem] + [anywhere] * (3 + count),
+        [anywhere] + [vmem] * 4,
+        60,
         "update",
         scratch=[
-            all_tokens,
+            pltpu.VMEM((dp * block, depth), bf16),
             whole,
             whole,
             whole,
             pltpu.VMEM((own_depth, cols), bf16),
             whole,
-            product,
             pltpu.SemaphoreType.DMA((tiles * (count * dp + 3),)),
             pltpu.SemaphoreType.DMA((tiles,)),
         ],
-    )(where, turned, master_kv[0], moment_m[0], moment_v[0], *tokens)
+    )(send0, where, turned, w0, master_kv[0], moment_m[0], moment_v[0], *tokens)
 
     def place(x):
-        x = x.reshape(micro, tensor, rows, cols)
-        return jnp.stack(reorder([x[:, j] for j in range(tensor)], t), 1).reshape(
+        x = x.reshape(tensor, micro, rows, cols)
+        return jnp.stack(reorder([x[j] for j in range(tensor)], t), 1).reshape(
             1, micro, tensor * rows, cols
         )
 
-    mine = place(scatter_sum(keep, send, d).astype(bf16))
+    mine, got = scatter_sum(keep, send, d)
+    mine = place(mine.astype(bf16))
     kv_next = from_behind(mine, "segment", -1)
-    own_keep, own_send = call(
-        functools.partial(project_kernel, count=count),
-        part_shape,
-        [anywhere, smem, vmem] + [anywhere] * count,
-        [vmem] * 2,
-        17,
-        "project",
-        scratch=[all_tokens, product, pltpu.SemaphoreType.DMA((count * dp,))],
-    )(send, where, w0, *tokens)
-    kv_own = place(scatter_sum(own_keep, own_send).astype(bf16))
+    (send1,) = after([send1], got)
+    early, _ = scatter_sum(keep0, send0)
+    late, _ = scatter_sum(keep1, send1)
+    kv_own = place(
+        jnp.concatenate(
+            [x.reshape(tensor, -1, cols) for x in (early.astype(bf16), late.astype(bf16))], 1
+        )
+    )
     (d,) = after([d], mine, kv_own)
     grad_in = call(
         functools.partial(grad_kernel, tile=tile),
         like(piece, width),
         [vmem] * 3,
         vmem,
-        12,
+        60,
         "grad_in",
     )(hidden, norm_gain, d)
     return (kv_own, grad_in.reshape(hidden_in.shape), master_new[None], kv_next)

time: 226 us -> 203 us (0.90)
  waiting for transfers between devices: 133 us -> 102 us
  Pallas kernels: 25.2 us -> 40.3 us
  local copies, waits for them, and re-layouts: 25.1 us -> 11.6 us
  starting transfers between devices: 35.5 us -> 42.6 us
    ppermute x19 -> x24, waiting for transfers between devices: 133 us -> 91.9 us  [swap(): return lax.ppermute(x, axis, [(i, i ^ bits) for i in range(peers)])]
    unnamed x63 -> x59, local copies, waits for them, and re-layouts: 25.1 us -> 11.6 us
    pallas_call x5, Pallas kernels: 21.9 us -> 34.7 us  [the longest x1 14.2 us: shards(): call(functools.partial(update_kernel, cuts=cuts), [like(own_depth, cols,...]
    all_to_all x1 -> x2, waiting for transfers between devices: 0.01 us -> 8.65 us  [the longest x1 8.65 us: shards(): token0 = lax.all_to_all(own0, 'dp', 0, 0, tiled=True)]
    ppermute x19 -> x24, starting transfers between devices: 18.4 us -> 23.2 us  [swap(): return lax.ppermute(x, axis, [(i, i ^ bits) for i in range(peers)])]
    all_to_all x1 -> x2, starting transfers between devices: 6.32 us -> 10.6 us  [the longest x1 6.79 us: shards(): token0 = lax.all_to_all(own0, 'dp', 0, 0, tiled=True)]
  transfers between devices with their start and end apart: 23 -> 29, of which waited for: 12 -> 17; matrix products, arithmetic and copies ran while one was open for 2% -> 2% of each run, Pallas kernels for 10% -> 18%
where the time goes in v9:
time: 203 us; the launch traced here: 202 us
  waiting for transfers between devices  102 us (50%)
  starting transfers between devices  42.6 us (21%)
  Pallas kernels  40.3 us (20%)
  local copies, waits for them, and re-layouts  11.6 us (6%)
  other arithmetic  5.44 us (3%)
    ppermute x24, waiting for transfers between devices, swap(): return lax.ppermute(x, axis, [(i, i ^ bits) for i in range(peers)])  91.9 us
    ppermute x24, starting transfers between devices, swap(): return lax.ppermute(x, axis, [(i, i ^ bits) for i in range(peers)])  23.2 us
    pallas_call x1, Pallas kernels, shards(): call(functools.partial(update_kernel, cuts=cuts), [like(own_depth, cols,...  14.2 us
    unnamed x59, local copies, waits for them, and re-layouts  11.6 us
    all_to_all x1, waiting for transfers between devices, shards(): token0 = lax.all_to_all(own0, 'dp', 0, 0, tiled=True)  8.65 us
    pallas_call x1, Pallas kernels, shards(): call(functools.partial(project_kernel, cuts=cuts[:-1]), [like(dp // 2, te...  7.07 us
    all_to_all x1, starting transfers between devices, shards(): token0 = lax.all_to_all(own0, 'dp', 0, 0, tiled=True)  6.79 us
    pallas_call x1, Pallas kernels, shards(): call(d_kernel, like(dp, piece, depth), [vmem] * 8, vmem, 60, 'd_normed')  6.18 us
  transfers between devices with their start and end apart: 29, of which 17 were waited for; matrix products, arithmetic and copies ran while one was open for 2% of the time, Pallas kernels for 18%

profile of v9, /device:TPU:0, one launch (start us, length us, event | category | flops | bytes accessed | tf_op | source)
XLA Modules:
  0.0 202.5 jit_solution(12697826753526944990)
XLA Ops:
  0.6 1.7 bitcast_convert_fusion.weights_ref.refs_4_
  2.4 3.0 %collective-permute-start = (bf16[2048,256]{1,0:T(8,128)(2,1)S(1)}, bf16[2048,256]{1,0:T(8,128)(2,1)S(1)}, u32[]{:S(2)}, u32[]{:S(2)}) collective-permute-start(bf16[2048,256]{1,0:T(8,128)(2,1)S(1)} %bitcast_convert_fusion.weights_ref.refs_4_), channel_id=1, source_target_pairs={{0,2},{1,3},{2,0},{3,1},{4,6},{5,7},{6,4},{7,5},{8,10},{9,11},{10,... | collective-permute-start | bytes 3145736 | tf_op jit(solution)/shard_map/ppermute | solution.py:29
  5.4 1.6 collective-permute-start.1
  7.0 2.6 %collective-permute-start.2 = (bf16[2,256,256]{2,1,0:T(8,128)(2,1)S(1)}, bf16[2,256,256]{2,1,0:T(8,128)(2,1)S(1)}, u32[]{:S(2)}, u32[]{:S(2)}) collective-permute-start(bf16[2,256,256]{2,1,0:T(8,128)(2,1)S(1)} %bitcast.61), channel_id=1, source_target_pairs={{0,8},{4,12},{8,0},{12,4},{1,9},{5,13},{9,1},{13,5},{2,10},{6,14},... | collective-permute-start | bytes 786440 | tf_op jit(solution)/shard_map/ppermute | solution.py:29
  9.8 4.3 %norm.1 = (bf16[4,48,2048]{2,1,0:T(8,128)(2,1)}, bf16[4,48,2048]{2,1,0:T(8,128)(2,1)}, bf16[4,32,2048]{2,1,0:T(8,128)(2,1)}) custom-call(bf16[128,8192]{1,0:T(8,128)(2,1)} %bitcast.53, f32[1,8192]{1,0:T(1,128)} %gain_ref.3), custom_call_target="tpu_custom_call" | custom-call | flops 1000 | bytes 1000 | tf_op jit(solution)/shard_map/norm/pallas_call | solution.py:295
  14.8 3.1 %collective-permute-done.1.refs_1_ = bf16[2,256,256]{2,1,0:T(8,128)(2,1)S(1)} collective-permute-done((bf16[2,256,256]{2,1,0:T(8,128)(2,1)S(1)}, bf16[2,256,256]{2,1,0:T(8,128)(2,1)S(1)}, u32[]{:S(2)}, u32[]{:S(2)}) %collective-permute-start.1) | collective-permute-done | bytes 262176 | tf_op jit(solution)/shard_map/ppermute | solution.py:29
  17.9 10.5 %collective-permute-done.2.refs_2_ = bf16[2,256,256]{2,1,0:T(8,128)(2,1)S(1)} collective-permute-done((bf16[2,256,256]{2,1,0:T(8,128)(2,1)S(1)}, bf16[2,256,256]{2,1,0:T(8,128)(2,1)S(1)}, u32[]{:S(2)}, u32[]{:S(2)}) %collective-permute-start.2) | collective-permute-done | bytes 262176 | tf_op jit(solution)/shard_map/ppermute | solution.py:29
  30.1 3.0 %arrange.1 = (bf16[512,256]{1,0:T(8,128)(2,1)}, bf16[512,256]{1,0:T(8,128)(2,1)}, bf16[512,256]{1,0:T(8,128)(2,1)}, bf16[512,256]{1,0:T(8,128)(2,1)}, bf16[256,2048]{1,0:T(8,128)(2,1)}) custom-call(bf16[2048,256]{1,0:T(8,128)(2,1)} %copy-done.13, s32[2]{0:T(128)} %pad_add_fusion.where_ref, bf16[2,256,256]{2,1,0:T(8,128)(2,1)} %bitcast.59, ...), custom_call_target="tpu_custom_call" | custom-call | flops 1000 | bytes 1000 | tf_op jit(solution)/shard_map/arrange/pallas_call | solution.py:303
  34.1 6.8 %all-to-all-start = ((bf16[4,48,2048]{2,1,0:T(8,128)(2,1)}), bf16[4,48,2048]{2,1,0:T(8,128)(2,1)S(1)}, u32[]{:S(2)}, u32[]{:S(2)}) async-start(bf16[4,48,2048]{2,1,0:T(8,128)(2,1)} %after.7), calls=%async_computation | async-start | bytes 1572864 | tf_op jit(solution)/shard_map/all_to_all | solution.py:313
  41.4 8.6 %collective-permute-done.4.refs_2_ = bf16[512,256]{1,0:T(8,128)(2,1)S(1)} collective-permute-done((bf16[512,256]{1,0:T(8,128)(2,1)S(1)}, bf16[512,256]{1,0:T(8,128)(2,1)S(1)}, u32[]{:S(2)}, u32[]{:S(2)}) %collective-permute-start.4) | collective-permute-done | bytes 262176 | tf_op jit(solution)/shard_map/ppermute | solution.py:29
  50.9 8.6 %all-to-all-done.refs_1_ = bf16[4,48,2048]{2,1,0:T(8,128)(2,1)S(1)} async-done(((bf16[4,48,2048]{2,1,0:T(8,128)(2,1)}), bf16[4,48,2048]{2,1,0:T(8,128)(2,1)S(1)}, u32[]{:S(2)}, u32[]{:S(2)}) %all-to-all-start) | async-done | bytes 786464 | tf_op jit(solution)/shard_map/all_to_all | solution.py:313
  59.6 3.5 %all-to-all-start.1 = ((bf16[4,48,2048]{2,1,0:T(8,128)(2,1)}), bf16[4,48,2048]{2,1,0:T(8,128)(2,1)S(1)}, u32[]{:S(2)}, u32[]{:S(2)}) async-start(bf16[4,48,2048]{2,1,0:T(8,128)(2,1)} %get-tuple-element.32), calls=%async_computation.1 | async-start | bytes 1572864 | tf_op jit(solution)/shard_map/all_to_all | solution.py:317
  64.2 17.5 %collective-permute-done.7.refs_2_.rest_2_ = bf16[4,48,2048]{2,1,0:T(8,128)(2,1)S(1)} collective-permute-done((bf16[4,48,2048]{2,1,0:T(8,128)(2,1)S(1)}, bf16[4,48,2048]{2,1,0:T(8,128)(2,1)S(1)}, u32[]{:S(2)}, u32[]{:S(2)}) %collective-permute-start.7) | collective-permute-done | bytes 786464 | tf_op jit(solution)/shard_map/ppermute | solution.py:29
  83.2 3.8 %all-to-all-start.2 = ((bf16[4,32,2048]{2,1,0:T(8,128)(2,1)}), bf16[4,32,2048]{2,1,0:T(8,128)(2,1)S(1)}, u32[]{:S(2)}, u32[]{:S(2)}) async-start(bf16[4,32,2048]{2,1,0:T(8,128)(2,1)} %get-tuple-element.37), calls=%async_computation.2 | async-start | bytes 1048576 | tf_op jit(solution)/shard_map/all_to_all | solution.py:328
  87.0 1.7 collective-permute-done.14.refs_1_
  89.4 6.2 %d_normed.1.refs_1_ = bf16[4,128,2048]{2,1,0:T(8,128)(2,1)} custom-call(bf16[512,256]{1,0:T(8,128)(2,1)} %get-tuple-element.27.refs_1_.refs_0_, bf16[512,256]{1,0:T(8,128)(2,1)} %copy-done.25, bf16[512,256]{1,0:T(8,128)(2,1)} %copy-done.9, bf16[512,256]{1,0:T(8,128)(2,1)} %copy-done.10, bf16[2048,256]{1,0:T(8,128)(2,1)} %copy-done.12, ...), custom_call_target="tpu_custom_call" | custom-call | flops 1000 | bytes 1000 | tf_op jit(solution)/shard_map/d_normed/pallas_call | solution.py:319
  95.6 5.7 %collective-permute-done.10.rest_6_.refs_2_ = bf16[4,48,2048]{2,1,0:T(8,128)(2,1)} collective-permute-done((bf16[4,48,2048]{2,1,0:T(8,128)(2,1)S(1)}, bf16[4,48,2048]{2,1,0:T(8,128)(2,1)}, u32[]{:S(2)}, u32[]{:S(2)}) %collective-permute-start.10) | collective-permute-done | bytes 786464 | tf_op jit(solution)/shard_map/ppermute | solution.py:29
  101.3 1.6 copy-done.1
  104.2 3.8 %all-to-all-start.3 = ((bf16[4,128,2048]{2,1,0:T(8,128)(2,1)}), bf16[4,128,2048]{2,1,0:T(8,128)(2,1)S(1)}, u32[]{:S(2)}, u32[]{:S(2)}) async-start(bf16[4,128,2048]{2,1,0:T(8,128)(2,1)} %copy-done.2), calls=%async_computation.3 | async-start | bytes 4194304 | tf_op jit(solution)/shard_map/all_to_all | solution.py:331
  110.7 12.3 %collective-permute-done.18.rest_10_ = bf16[4,32,2048]{2,1,0:T(8,128)(2,1)S(1)} collective-permute-done((bf16[4,32,2048]{2,1,0:T(8,128)(2,1)S(1)}, bf16[4,32,2048]{2,1,0:T(8,128)(2,1)S(1)}, u32[]{:S(2)}, u32[]{:S(2)}) %collective-permute-start.18) | collective-permute-done | bytes 524320 | tf_op jit(solution)/shard_map/ppermute | solution.py:29
  124.9 7.1 %project.1 = (bf16[2,384,256]{2,1,0:T(8,128)(2,1)}, bf16[2,384,256]{2,1,0:T(8,128)(2,1)}) custom-call(s32[2]{0:T(128)} %pad_add_fusion.where_ref, bf16[2048,256]{1,0:T(8,128)(2,1)} %copy-done.12, bf16[4,48,2048]{2,1,0:T(8,128)(2,1)} %copy-done.4, bf16[4,48,2048]{2,1,0:T(8,128)(2,1)} %copy-done.14, bf16[4,48,2048]{2,1,0:T(8,128)(2,1)} %copy-done.5, ...), custom_call_target="tpu_custom_call" | custom-call | flops 1000 | bytes 1000 | tf_op jit(solution)/shard_map/project/pallas_call | solution.py:343
  131.9 1.7 collective-permute-start.12
  133.7 14.2 %update.1 = (f32[2048,256]{1,0:T(8,128)}, bf16[2,512,256]{2,1,0:T(8,128)(2,1)}, bf16[2,512,256]{2,1,0:T(8,128)(2,1)}, bf16[2,128,256]{2,1,0:T(8,128)(2,1)}, bf16[2,128,256]{2,1,0:T(8,128)(2,1)}) custom-call(bf16[2,384,256]{2,1,0:T(8,128)(2,1)} %get-tuple-element.35.mark_ref, s32[2]{0:T(128)} %pad_add_fusion.where_ref, ...), custom_call_target="tpu_custom_call" | custom-call | flops 1000 | bytes 1000 | tf_op jit(solution)/shard_map/update/pallas_call | solution.py:355
  149.0 1.6 fusion.3
  150.6 6.6 %collective-permute-start.13 = (bf16[384,256]{1,0:T(8,128)(2,1)}, bf16[384,256]{1,0:T(8,128)(2,1)S(1)}, u32[]{:S(2)}, u32[]{:S(2)}) collective-permute-start(bf16[384,256]{1,0:T(8,128)(2,1)} %fusion.3), channel_id=1, source_target_pairs={{0,8},{4,12},{8,0},{12,4},{1,9},{5,13},{9,1},{13,5},{2,10},{6,14},... | collective-permute-start | bytes 589832 | tf_op jit(solution)/shard_map/ppermute | solution.py:29
  157.2 12.8 %collective-permute-done.20.refs_0_ = bf16[2,512,256]{2,1,0:T(8,128)(2,1)S(1)} collective-permute-done((bf16[2,512,256]{2,1,0:T(8,128)(2,1)}, bf16[2,512,256]{2,1,0:T(8,128)(2,1)S(1)}, u32[]{:S(2)}, u32[]{:S(2)}) %collective-permute-start.20) | collective-permute-done | bytes 524320 | tf_op jit(solution)/shard_map/ppermute | solution.py:29
  172.0 3.5 %collective-permute-done.21 = bf16[2,128,256]{2,1,0:T(8,128)(2,1)S(1)} collective-permute-done((bf16[2,128,256]{2,1,0:T(8,128)(2,1)S(1)}, bf16[2,128,256]{2,1,0:T(8,128)(2,1)S(1)}, u32[]{:S(2)}, u32[]{:S(2)}) %collective-permute-start.21) | collective-permute-done | bytes 131104 | tf_op jit(solution)/shard_map/ppermute | solution.py:29
  176.5 2.1 %collective-permute-start.23 = (bf16[512,256]{1,0:T(8,128)(2,1)S(1)}, bf16[512,256]{1,0:T(8,128)(2,1)S(1)}, u32[]{:S(2)}, u32[]{:S(2)}) collective-permute-start(bf16[512,256]{1,0:T(8,128)(2,1)S(1)} %fusion.2), channel_id=1, source_target_pairs={{0,8},{4,12},{8,0},{12,4},{1,9},{5,13},{9,1},{13,5},{2,10},{6,14},... | collective-permute-start | bytes 786440 | tf_op jit(solution)/shard_map/ppermute | solution.py:29
  178.7 9.0 %collective-permute-done.22 = bf16[128,256]{1,0:T(8,128)(2,1)S(1)} collective-permute-done((bf16[128,256]{1,0:T(8,128)(2,1)S(1)}, bf16[128,256]{1,0:T(8,128)(2,1)S(1)}, u32[]{:S(2)}, u32[]{:S(2)}) %collective-permute-start.22) | collective-permute-done | bytes 65568 | tf_op jit(solution)/shard_map/ppermute | solution.py:29
  187.7 4.6 %collective-permute-done.23 = bf16[512,256]{1,0:T(8,128)(2,1)S(1)} collective-permute-done((bf16[512,256]{1,0:T(8,128)(2,1)S(1)}, bf16[512,256]{1,0:T(8,128)(2,1)S(1)}, u32[]{:S(2)}, u32[]{:S(2)}) %collective-permute-start.23) | collective-permute-done | bytes 262176 | tf_op jit(solution)/shard_map/ppermute | solution.py:29
  192.5 1.6 collective-permute-start.24
  196.2 5.6 %grad_in.1 = bf16[128,8192]{1,0:T(8,128)(2,1)} custom-call(bf16[128,8192]{1,0:T(8,128)(2,1)} %bitcast.54, f32[1,8192]{1,0:T(1,128)} %gain_ref.3, bf16[4,128,2048]{2,1,0:T(8,128)(2,1)} %copy-done), custom_call_target="tpu_custom_call" | custom-call | flops 1000 | bytes 1000 | tf_op jit(solution)/shard_map/grad_in/pallas_call | solution.py:393
  (111 shorter events, 21.3 us)
Async XLA Ops:
  2.4 30.8 %copy-start.12 = (bf16[2048,256]{1,0:T(8,128)(2,1)}, bf16[2048,256]{1,0:T(8,128)(2,1)S(1)}, u32[]{:S(2)}) copy-start(bf16[2048,256]{1,0:T(8,128)(2,1)S(1)} %bitcast_convert_fusion.weights_ref.refs_4_) | copy-start | bytes 3145732
  2.4 26.2 %collective-permute-start = (bf16[2048,256]{1,0:T(8,128)(2,1)S(1)}, bf16[2048,256]{1,0:T(8,128)(2,1)S(1)}, u32[]{:S(2)}, u32[]{:S(2)}) collective-permute-start(bf16[2048,256]{1,0:T(8,128)(2,1)S(1)} %bitcast_convert_fusion.weights_ref.refs_4_), channel_id=1, source_target_pairs={{0,2},{1,3},{2,0},{3,1},{4,6},{5,7},{6,4},{7,5},{8,10},{9,11},{10,... | collective-permute-start | bytes 3145736 | tf_op jit(solution)/shard_map/ppermute | solution.py:29
  5.4 12.5 %collective-permute-start.1 = (bf16[2,256,256]{2,1,0:T(8,128)(2,1)S(1)}, bf16[2,256,256]{2,1,0:T(8,128)(2,1)S(1)}, u32[]{:S(2)}, u32[]{:S(2)}) collective-permute-start(bf16[2,256,256]{2,1,0:T(8,128)(2,1)S(1)} %bitcast.60), channel_id=1, source_target_pairs={{0,4},{4,0},{8,12},{12,8},{1,5},{5,1},{9,13},{13,9},{2,6},{6,2},{1... | collective-permute-start | bytes 786440 | tf_op jit(solution)/shard_map/ppermute | solution.py:29
  7.0 21.4 %collective-permute-start.2 = (bf16[2,256,256]{2,1,0:T(8,128)(2,1)S(1)}, bf16[2,256,256]{2,1,0:T(8,128)(2,1)S(1)}, u32[]{:S(2)}, u32[]{:S(2)}) collective-permute-start(bf16[2,256,256]{2,1,0:T(8,128)(2,1)S(1)} %bitcast.61), channel_id=1, source_target_pairs={{0,8},{4,12},{8,0},{12,4},{1,9},{5,13},{9,1},{13,5},{2,10},{6,14},... | collective-permute-start | bytes 786440 | tf_op jit(solution)/shard_map/ppermute | solution.py:29
  9.6 18.8 %collective-permute-start.3 = (bf16[2,256,256]{2,1,0:T(8,128)(2,1)S(1)}, bf16[2,256,256]{2,1,0:T(8,128)(2,1)S(1)}, u32[]{:S(2)}, u32[]{:S(2)}) collective-permute-start(bf16[2,256,256]{2,1,0:T(8,128)(2,1)S(1)} %bitcast.62), channel_id=1, source_target_pairs={{0,12},{4,8},{8,4},{12,0},{1,13},{5,9},{9,5},{13,1},{2,14},{6,10},... | collective-permute-start | bytes 786440 | tf_op jit(solution)/shard_map/ppermute | solution.py:29
  34.1 25.5 %all-to-all-start = ((bf16[4,48,2048]{2,1,0:T(8,128)(2,1)}), bf16[4,48,2048]{2,1,0:T(8,128)(2,1)S(1)}, u32[]{:S(2)}, u32[]{:S(2)}) async-start(bf16[4,48,2048]{2,1,0:T(8,128)(2,1)} %after.7), calls=%async_computation | async-start | bytes 1572864 | tf_op jit(solution)/shard_map/all_to_all | solution.py:313
  40.9 9.1 %collective-permute-start.4 = (bf16[512,256]{1,0:T(8,128)(2,1)S(1)}, bf16[512,256]{1,0:T(8,128)(2,1)S(1)}, u32[]{:S(2)}, u32[]{:S(2)}) collective-permute-start(bf16[512,256]{1,0:T(8,128)(2,1)S(1)} %copy-done.28), channel_id=1, source_target_pairs={{0,2},{1,3},{2,0},{3,1},{4,6},{5,7},{6,4},{7,5},{8,10},{9,11},{10,... | collective-permute-start | bytes 786440 | tf_op jit(solution)/shard_map/ppermute | solution.py:29
  41.4 9.5 %collective-permute-start.5 = (bf16[512,256]{1,0:T(8,128)(2,1)S(1)}, bf16[512,256]{1,0:T(8,128)(2,1)S(1)}, u32[]{:S(2)}, u32[]{:S(2)}) collective-permute-start(bf16[512,256]{1,0:T(8,128)(2,1)S(1)} %copy-done.27), channel_id=1, source_target_pairs={{0,3},{1,2},{2,1},{3,0},{4,7},{5,6},{6,5},{7,4},{8,11},{9,10},{10,... | collective-permute-start | bytes 786440 | tf_op jit(solution)/shard_map/ppermute | solution.py:29
  59.6 23.6 %copy-start.4 = (bf16[4,48,2048]{2,1,0:T(8,128)(2,1)}, bf16[4,48,2048]{2,1,0:T(8,128)(2,1)S(1)}, u32[]{:S(2)}) copy-start(bf16[4,48,2048]{2,1,0:T(8,128)(2,1)S(1)} %get-tuple-element.30.rest_0_) | copy-start | bytes 2359300
  59.6 23.1 %all-to-all-start.1 = ((bf16[4,48,2048]{2,1,0:T(8,128)(2,1)}), bf16[4,48,2048]{2,1,0:T(8,128)(2,1)S(1)}, u32[]{:S(2)}, u32[]{:S(2)}) async-start(bf16[4,48,2048]{2,1,0:T(8,128)(2,1)} %get-tuple-element.32), calls=%async_computation.1 | async-start | bytes 1572864 | tf_op jit(solution)/shard_map/all_to_all | solution.py:317
  63.1 18.6 %collective-permute-start.7 = (bf16[4,48,2048]{2,1,0:T(8,128)(2,1)S(1)}, bf16[4,48,2048]{2,1,0:T(8,128)(2,1)S(1)}, u32[]{:S(2)}, u32[]{:S(2)}) collective-permute-start(bf16[4,48,2048]{2,1,0:T(8,128)(2,1)S(1)} %get-tuple-element.30.rest_0_), channel_id=1, source_target_pairs={{0,2},{1,3},{2,0},{3,1},{4,6},{5,7},{6,4},{7,5},{8,10},{9,11},{10,... | collective-permute-start | bytes 2359304 | tf_op jit(solution)/shard_map/ppermute | solution.py:29
  63.7 23.3 %collective-permute-start.15 = (bf16[2048,256]{1,0:T(8,128)(2,1)}, bf16[2048,256]{1,0:T(8,128)(2,1)}, u32[]{:S(2)}, u32[]{:S(2)}) collective-permute-start(bf16[2048,256]{1,0:T(8,128)(2,1)} %copy-done.12), channel_id=1, source_target_pairs={{0,1},{1,0},{2,3},{3,2},{4,5},{5,4},{6,7},{7,6},{8,9},{9,8},{10,11... | collective-permute-start | bytes 3145736 | tf_op jit(solution)/shard_map/ppermute | solution.py:29
  63.7 25.0 %collective-permute-start.16 = (bf16[2048,256]{1,0:T(8,128)(2,1)}, bf16[2048,256]{1,0:T(8,128)(2,1)}, u32[]{:S(2)}, u32[]{:S(2)}) collective-permute-start(bf16[2048,256]{1,0:T(8,128)(2,1)} %copy-done.13), channel_id=1, source_target_pairs={{0,1},{1,0},{2,3},{3,2},{4,5},{5,4},{6,7},{7,6},{8,9},{9,8},{10,11... | collective-permute-start | bytes 3145736 | tf_op jit(solution)/shard_map/ppermute | solution.py:29
  82.7 25.9 %copy-start.3 = (bf16[4,48,2048]{2,1,0:T(8,128)(2,1)}, bf16[4,48,2048]{2,1,0:T(8,128)(2,1)S(1)}, u32[]{:S(2)}) copy-start(bf16[4,48,2048]{2,1,0:T(8,128)(2,1)S(1)} %get-tuple-element.33.rest_4_) | copy-start | bytes 2359300
  82.7 18.6 %collective-permute-start.10 = (bf16[4,48,2048]{2,1,0:T(8,128)(2,1)S(1)}, bf16[4,48,2048]{2,1,0:T(8,128)(2,1)}, u32[]{:S(2)}, u32[]{:S(2)}) collective-permute-start(bf16[4,48,2048]{2,1,0:T(8,128)(2,1)S(1)} %get-tuple-element.33.rest_4_), channel_id=1, source_target_pairs={{0,2},{1,3},{2,0},{3,1},{4,6},{5,7},{6,4},{7,5},{8,10},{9,11},{10,... | collective-permute-start | bytes 2359304 | tf_op jit(solution)/shard_map/ppermute | solution.py:29
  83.2 18.1 %all-to-all-start.2 = ((bf16[4,32,2048]{2,1,0:T(8,128)(2,1)}), bf16[4,32,2048]{2,1,0:T(8,128)(2,1)S(1)}, u32[]{:S(2)}, u32[]{:S(2)}) async-start(bf16[4,32,2048]{2,1,0:T(8,128)(2,1)} %get-tuple-element.37), calls=%async_computation.2 | async-start | bytes 1048576 | tf_op jit(solution)/shard_map/all_to_all | solution.py:328
  87.0 1.7 collective-permute-start.14
  104.2 65.8 %all-to-all-start.3 = ((bf16[4,128,2048]{2,1,0:T(8,128)(2,1)}), bf16[4,128,2048]{2,1,0:T(8,128)(2,1)S(1)}, u32[]{:S(2)}, u32[]{:S(2)}) async-start(bf16[4,128,2048]{2,1,0:T(8,128)(2,1)} %copy-done.2), calls=%async_computation.3 | async-start | bytes 4194304 | tf_op jit(solution)/shard_map/all_to_all | solution.py:331
  108.0 2.6 %collective-permute-start.6 = (bf16[4,48,2048]{2,1,0:T(8,128)(2,1)}, bf16[4,48,2048]{2,1,0:T(8,128)(2,1)S(1)}, u32[]{:S(2)}, u32[]{:S(2)}) collective-permute-start(bf16[4,48,2048]{2,1,0:T(8,128)(2,1)} %copy-done.4), channel_id=1, source_target_pairs={{0,1},{1,0},{2,3},{3,2},{4,5},{5,4},{6,7},{7,6},{8,9},{9,8},{10,11... | collective-permute-start | bytes 2359304 | tf_op jit(solution)/shard_map/ppermute | solution.py:29
  108.0 14.9 %collective-permute-start.8 = (bf16[4,48,2048]{2,1,0:T(8,128)(2,1)}, bf16[4,48,2048]{2,1,0:T(8,128)(2,1)S(1)}, u32[]{:S(2)}, u32[]{:S(2)}) collective-permute-start(bf16[4,48,2048]{2,1,0:T(8,128)(2,1)} %copy-done.5), channel_id=1, source_target_pairs={{0,1},{1,0},{2,3},{3,2},{4,5},{5,4},{6,7},{7,6},{8,9},{9,8},{10,11... | collective-permute-start | bytes 2359304 | tf_op jit(solution)/shard_map/ppermute | solution.py:29
  108.5 14.4 %collective-permute-start.9 = (bf16[4,48,2048]{2,1,0:T(8,128)(2,1)S(1)}, bf16[4,48,2048]{2,1,0:T(8,128)(2,1)S(1)}, u32[]{:S(2)}, u32[]{:S(2)}) collective-permute-start(bf16[4,48,2048]{2,1,0:T(8,128)(2,1)S(1)} %get-tuple-element.33.rest_4_), channel_id=1, source_target_pairs={{0,1},{1,0},{2,3},{3,2},{4,5},{5,4},{6,7},{7,6},{8,9},{9,8},{10,11... | collective-permute-start | bytes 2359304 | tf_op jit(solution)/shard_map/ppermute | solution.py:29
  108.6 16.2 %collective-permute-start.11 = (bf16[4,48,2048]{2,1,0:T(8,128)(2,1)}, bf16[4,48,2048]{2,1,0:T(8,128)(2,1)}, u32[]{:S(2)}, u32[]{:S(2)}) collective-permute-start(bf16[4,48,2048]{2,1,0:T(8,128)(2,1)} %collective-permute-done.10.rest_6_.refs_2_), channel_id=1, source_target_pairs={{0,1},{1,0},{2,3},{3,2},{4,5},{5,4},{6,7},{7,6},{8,9},{9,8},{10,11... | collective-permute-start | bytes 2359304 | tf_op jit(solution)/shard_map/ppermute | solution.py:29
  109.1 13.9 %collective-permute-start.18 = (bf16[4,32,2048]{2,1,0:T(8,128)(2,1)S(1)}, bf16[4,32,2048]{2,1,0:T(8,128)(2,1)S(1)}, u32[]{:S(2)}, u32[]{:S(2)}) collective-permute-start(bf16[4,32,2048]{2,1,0:T(8,128)(2,1)S(1)} %get-tuple-element.39.rest_8_), channel_id=1, source_target_pairs={{0,2},{1,3},{2,0},{3,1},{4,6},{5,7},{6,4},{7,5},{8,10},{9,11},{10,... | collective-permute-start | bytes 1572872 | tf_op jit(solution)/shard_map/ppermute | solution.py:29
  110.5 23.1 %collective-permute-start.17 = (bf16[4,32,2048]{2,1,0:T(8,128)(2,1)S(1)}, bf16[4,32,2048]{2,1,0:T(8,128)(2,1)}, u32[]{:S(2)}, u32[]{:S(2)}) collective-permute-start(bf16[4,32,2048]{2,1,0:T(8,128)(2,1)S(1)} %get-tuple-element.39.rest_8_), channel_id=1, source_target_pairs={{0,1},{1,0},{2,3},{3,2},{4,5},{5,4},{6,7},{7,6},{8,9},{9,8},{10,11... | collective-permute-start | bytes 1572872 | tf_op jit(solution)/shard_map/ppermute | solution.py:29
  123.0 10.7 %collective-permute-start.19 = (bf16[4,32,2048]{2,1,0:T(8,128)(2,1)S(1)}, bf16[4,32,2048]{2,1,0:T(8,128)(2,1)}, u32[]{:S(2)}, u32[]{:S(2)}) collective-permute-start(bf16[4,32,2048]{2,1,0:T(8,128)(2,1)S(1)} %collective-permute-done.18.rest_10_), channel_id=1, source_target_pairs={{0,1},{1,0},{2,3},{3,2},{4,5},{5,4},{6,7},{7,6},{8,9},{9,8},{10,11... | collective-permute-start | bytes 1572872 | tf_op jit(solution)/shard_map/ppermute | solution.py:29
  131.9 17.0 %collective-permute-start.12 = (bf16[2,384,256]{2,1,0:T(8,128)(2,1)}, bf16[2,384,256]{2,1,0:T(8,128)(2,1)}, u32[]{:S(2)}, u32[]{:S(2)}) collective-permute-start(bf16[2,384,256]{2,1,0:T(8,128)(2,1)} %get-tuple-element.35.mark_ref), channel_id=1, source_target_pairs={{0,4},{4,0},{8,12},{12,8},{1,5},{5,1},{9,13},{13,9},{2,6},{6,2},{1... | collective-permute-start | bytes 1179656 | tf_op jit(solution)/shard_map/ppermute | solution.py:29
  147.9 22.1 %collective-permute-start.20 = (bf16[2,512,256]{2,1,0:T(8,128)(2,1)}, bf16[2,512,256]{2,1,0:T(8,128)(2,1)S(1)}, u32[]{:S(2)}, u32[]{:S(2)}) collective-permute-start(bf16[2,512,256]{2,1,0:T(8,128)(2,1)} %get-tuple-element.42), channel_id=1, source_target_pairs={{0,4},{4,0},{8,12},{12,8},{1,5},{5,1},{9,13},{13,9},{2,6},{6,2},{1... | collective-permute-start | bytes 1572872 | tf_op jit(solution)/shard_map/ppermute | solution.py:29
  150.6 19.5 %collective-permute-start.13 = (bf16[384,256]{1,0:T(8,128)(2,1)}, bf16[384,256]{1,0:T(8,128)(2,1)S(1)}, u32[]{:S(2)}, u32[]{:S(2)}) collective-permute-start(bf16[384,256]{1,0:T(8,128)(2,1)} %fusion.3), channel_id=1, source_target_pairs={{0,8},{4,12},{8,0},{12,4},{1,9},{5,13},{9,1},{13,5},{2,10},{6,14},... | collective-permute-start | bytes 589832 | tf_op jit(solution)/shard_map/ppermute | solution.py:29
  170.0 5.5 %collective-permute-start.21 = (bf16[2,128,256]{2,1,0:T(8,128)(2,1)S(1)}, bf16[2,128,256]{2,1,0:T(8,128)(2,1)S(1)}, u32[]{:S(2)}, u32[]{:S(2)}) collective-permute-start(bf16[2,128,256]{2,1,0:T(8,128)(2,1)S(1)} %after.12), channel_id=1, source_target_pairs={{0,4},{4,0},{8,12},{12,8},{1,5},{5,1},{9,13},{13,9},{2,6},{6,2},{1... | collective-permute-start | bytes 393224 | tf_op jit(solution)/shard_map/ppermute | solution.py:29
  175.5 12.1 %collective-permute-start.22 = (bf16[128,256]{1,0:T(8,128)(2,1)S(1)}, bf16[128,256]{1,0:T(8,128)(2,1)S(1)}, u32[]{:S(2)}, u32[]{:S(2)}) collective-permute-start(bf16[128,256]{1,0:T(8,128)(2,1)S(1)} %fusion.5), channel_id=1, source_target_pairs={{0,8},{4,12},{8,0},{12,4},{1,9},{5,13},{9,1},{13,5},{2,10},{6,14},... | collective-permute-start | bytes 196616 | tf_op jit(solution)/shard_map/ppermute | solution.py:29
  176.5 15.8 %collective-permute-start.23 = (bf16[512,256]{1,0:T(8,128)(2,1)S(1)}, bf16[512,256]{1,0:T(8,128)(2,1)S(1)}, u32[]{:S(2)}, u32[]{:S(2)}) collective-permute-start(bf16[512,256]{1,0:T(8,128)(2,1)S(1)} %fusion.2), channel_id=1, source_target_pairs={{0,8},{4,12},{8,0},{12,4},{1,9},{5,13},{9,1},{13,5},{2,10},{6,14},... | collective-permute-start | bytes 786440 | tf_op jit(solution)/shard_map/ppermute | solution.py:29
  192.5 9.2 %collective-permute-start.24 = (bf16[1,2,256,256]{3,2,1,0:T(8,128)(2,1)S(1)}, bf16[1,2,256,256]{3,2,1,0:T(8,128)(2,1)S(1)}, u32[]{:S(2)}, u32[]{:S(2)}) collective-permute-start(bf16[1,2,256,256]{3,2,1,0:T(8,128)(2,1)S(1)} %bitcast.48), channel_id=1, source_target_pairs={{0,16},{16,0},{1,17},{17,1},{2,18},{18,2},{3,19},{19,3},{4,20},{20... | collective-permute-start | bytes 786440 | tf_op jit(solution)/shard_map/ppermute | solution.py:34
  (26 other events, 172.4 us)

commit v10 on v7

--- a/solution.py
+++ b/solution.py
@@ -118,53 +118,35 @@
             out_ref[at, cut] = (scaling * upper - hidden * factor).astype(bf16)
 
 
-def arrange_kernel(where_ref, *refs, dp, layout):
-    cots, (send_ref, turned_ref) = refs[:dp], refs[dp:]
+def arrange_kernel(mark_ref, where_ref, *refs, dp, layout):
+    cots, send_refs, turned_ref = refs[:dp], refs[dp:-1], refs[-1]
     t = where_ref[1]
-    tensor = send_ref.shape[0]
+    tensor = len(send_refs)
     micro, rows, cols = cots[0].shape
     rows //= tensor
     piece = micro * rows
-    for k in range(dp):
-        for b in range(tensor):
+    for j, send_ref in enumerate(send_refs):
+        at = pl.ds(pl.multiple_of((t ^ j) * rows, rows), rows)
+        for k in range(dp):
             for m in range(micro):
-                at = k * piece + m * rows
-                send_ref[b, at : at + rows, :] = cots[k][m, b * rows : (b + 1) * rows, :]
+                start = k * piece + m * rows
+                send_ref[start : start + rows, :] = cots[k][m, at, :]
     for p, (k, j) in enumerate(layout):
-        at = pl.ds(pl.multiple_of((t ^ j) * rows, rows), rows)
-        block = jnp.concatenate([cots[k][m, at, :] for m in range(micro)])
+        block = send_refs[j][k * piece : (k + 1) * piece, :]
         turned_ref[:, p * piece : (p + 1) * piece] = block.astype(f32).T.astype(bf16)
 
 
-def d_kernel(where_ref, cot_ref, *rest):
-    w_refs, d_ref = rest[:8], rest[8]
+def d_kernel(where_ref, c0_ref, c1_ref, c2_ref, c3_ref, w_ref, d_ref):
     z, t = where_ref[0], where_ref[1]
-    dp, rows = d_ref.shape[:2]
-    half = w_refs[0].shape[0]
-    tile = min(half, 512)
-    cot = jnp.concatenate([cot_ref[t ^ j] for j in range(cot_ref.shape[0])], axis=1)
-    for side in range(2):
-        for i in range(half // tile):
-            cut = slice(i * tile, (i + 1) * tile)
-            whole = jnp.concatenate([w[cut, :] for w in w_refs[side::2]], axis=1)
-            part = dot(cot, whole, ((1,), (1,))).astype(bf16)
-            for k in range(dp):
-                d_ref[z ^ k, :, side * half + i * tile : side * half + (i + 1) * tile] = part[
-                    k * rows : (k + 1) * rows
-                ]
-
-
-def pack_kernel(*refs):
-    pieces, packed_ref, sem = refs[:-2], refs[-2], refs[-1]
-    rows = pieces[0].shape[0]
-    copies = [
-        pltpu.make_async_copy(x, packed_ref.at[pl.ds(p * rows, rows), :], sem.at[p])
-        for p, x in enumerate(pieces)
-    ]
-    for copy in copies:
-        copy.start()
-    for copy in copies:
-        copy.wait()
+    dp, rows, depth = d_ref.shape
+    tile = min(depth, 512)
+    cot = jnp.concatenate([x[...] for x in (c0_ref, c1_ref, c2_ref, c3_ref)], axis=1)
+    for i in range(depth // tile):
+        cut = slice(i * tile, (i + 1) * tile)
+        whole = jnp.concatenate([w_ref[t ^ j, cut, :] for j in range(w_ref.shape[0])], axis=1)
+        part = dot(cot, whole, ((1,), (1,))).astype(bf16)
+        for k in range(dp):
+            d_ref[z ^ k, :, cut] = part[k * rows : (k + 1) * rows]
 
 
 def token_copies(token_refs, tokens_ref, sems, cut, first):
@@ -180,9 +162,9 @@
     return copies
 
 
-def update_kernel(turned_ref, master_hbm, m_hbm, v_hbm, *rest, count, tile, layout):
+def update_kernel(mark_ref, turned_ref, weights_ref, master_hbm, m_hbm, v_hbm, *rest, count, tile, layout):
     token_refs = rest[:count]
-    new_hbm, part_refs = rest[count], rest[count + 1 : -8]
+    new_hbm, part_refs, last_ref = rest[count], rest[count + 1 : -9], rest[-9]
     tokens, master, m, v, updated, new, sems, out_sems = rest[-8:]
     depth = master.shape[0]
     tiles = depth // tile
@@ -222,6 +204,14 @@
         outs.append(out)
         updated[cut, :] = master_new.astype(bf16)
     project(tokens, updated, part_refs, layout)
+    late = [p for p, (k, _) in enumerate(layout) if k == 3]
+    rows = tokens.shape[0] // len(layout)
+    project(
+        tokens.at[pl.ds(late[0] * rows, len(late) * rows), :],
+        weights_ref,
+        {3: last_ref},
+        [layout[p] for p in late],
+    )
     for out in outs:
         out.wait()
 
@@ -239,7 +229,7 @@
         p += span
 
 
-def project_kernel(mark_ref, weights_ref, *rest, count, layout):
+def project_kernel(weights_ref, *rest, count, layout):
     token_refs = rest[:count]
     part_refs, (tokens, sems) = rest[count:-2], rest[-2:]
     copies = token_copies(token_refs, tokens, sems, slice(None), 0)
@@ -280,10 +270,10 @@
     depth = width // dp
     tile = min(piece, 16)
 
-    half = own_depth // 2
-    w0 = [master_kv[0, :half].astype(bf16), master_kv[0, half:].astype(bf16)]
-    w2 = [swap(w, "tensor", 2) for w in w0]
-    w1 = [swap(w, "tensor", 1) for w in w0]
+    w0 = master_kv[0].astype(bf16)
+    whole_w = lax.all_to_all(
+        jnp.broadcast_to(w0, (tensor, own_depth, cols)), "tensor", 0, 0, tiled=True
+    )
     cot0 = kv_cot[0]
     cot2 = swap(cot0, "dp", 2)
     cot1 = swap(cot0, "dp", 1)
@@ -297,47 +287,33 @@
         "norm",
     )(cot2, cot1, where, hidden, norm_gain)
     n1, n3 = swap(own[1], "dp", 1), swap(own[3], "dp", 3)
-    w3 = [swap(w, "tensor", 1) for w in w2]
-    layout = tuple((k, j) for k in (0, 1, 3, 2) for j in (0, 2, 1, 3))
-    send, turned = call(
+    n2 = swap(own[2], "dp", 2)
+    layout = tuple((k, j) for k in range(dp) for j in (0, 2, 1, 3))
+    *blocks, turned = call(
         functools.partial(arrange_kernel, dp=dp, layout=layout),
-        [like(tensor, dp * piece, cols), like(cols, dp * tensor * piece)],
-        [smem] + [vmem] * dp,
-        [vmem] * 2,
+        [like(dp * piece, cols)] * tensor + [like(cols, dp * tensor * piece)],
+        [anywhere, smem] + [vmem] * dp,
+        [vmem] * (tensor + 1),
         8,
         "arrange",
-    )(where, cot0, cot1, cot2, cot3)
-    own2, n3 = after([own[2], n3])
-    n2 = swap(own2, "dp", 2)
-    (send,) = after([send], own2)
-    mine_cot = lax.all_to_all(send, "tensor", 0, 0, tiled=True)
-    def pack(*pieces):
-        return call(
-            pack_kernel,
-            like(len(pieces) * piece, depth),
-            [anywhere] * len(pieces),
-            anywhere,
-            0.25,
-            "pack",
-            scratch=[pltpu.SemaphoreType.DMA((len(pieces),))],
-        )(*pieces)
-
-    tokens = []
-    for x in (own[0], n1, n3):
-        near = pack(x, swap(x, "tensor", 2))
-        tokens += [near, swap(near, "tensor", 1)]
+    )(own[1], where, cot0, cot1, cot2, cot3)
+    got1 = swap(blocks[1], "tensor", 1)
+    got1, blocks[2], blocks[3] = after([got1, blocks[2], blocks[3]])
+    mine_cot = [blocks[0], got1] + [swap(blocks[j], "tensor", j) for j in (2, 3)]
     d = call(
         d_kernel,
         like(dp, piece, depth),
-        [smem] + [vmem] * 9,
+        [smem] + [vmem] * 5,
         vmem,
         20,
         "d_normed",
-    )(where, mine_cot, *w0, *w1, *w2, *w3)
-    n2, d = after([n2, d], tokens[1])
+    )(where, *mine_cot, whole_w)
+    n1, n2, n3, d = after([n1, n2, n3, d])
     d = lax.all_to_all(d, "dp", 0, 0, tiled=True)
-    across = swap(n2, "tensor", 2)
-    tokens += [n2, across, swap(n2, "tensor", 1), swap(across, "tensor", 1)]
+    tokens = []
+    for x in (own[0], n1, n2, n3):
+        across = swap(x, "tensor", 2)
+        tokens += [x, across, swap(x, "tensor", 1), swap(across, "tensor", 1)]
     count = len(tokens)
     block = tensor * piece
     part_shape = [like(block, cols)] * dp
@@ -345,11 +321,24 @@
     tiles = own_depth // step
     whole = pltpu.VMEM((own_depth, cols), f32)
     all_tokens = pltpu.VMEM((dp * block, depth), bf16)
-    master_new, *parts = call(
+    early = count * 3 // 4
+    own_parts = call(
+        functools.partial(project_kernel, count=early, layout=layout[: 3 * tensor]),
+        part_shape[:3],
+        [vmem] + [anywhere] * early,
+        [vmem] * 3,
+        16,
+        "project",
+        scratch=[
+            pltpu.VMEM((3 * block, depth), bf16),
+            pltpu.SemaphoreType.DMA((early,)),
+        ],
+    )(w0, *tokens[:early])
+    master_new, *parts, last = call(
         functools.partial(update_kernel, count=count, tile=step, layout=layout),
-        [like(own_depth, cols, dtype=f32)] + part_shape,
-        [vmem] + [anywhere] * (3 + count),
-        [anywhere] + [vmem] * dp,
+        [like(own_depth, cols, dtype=f32)] + part_shape + part_shape[:1],
+        [anywhere, vmem, vmem] + [anywhere] * (3 + count),
+        [anywhere] + [vmem] * (dp + 1),
         24,
         "update",
         scratch=[
@@ -362,7 +351,7 @@
             pltpu.SemaphoreType.DMA((tiles * (count + 3),)),
             pltpu.SemaphoreType.DMA((tiles,)),
         ],
-    )(turned, master_kv[0], moment_m[0], moment_v[0], *tokens)
+    )(own_parts[0], turned, w0, master_kv[0], moment_m[0], moment_v[0], *tokens)
 
     def place(x):
         x = x.reshape(tensor, micro, rows, cols)
@@ -372,16 +361,7 @@
 
     mine = place(scatter_sum(parts).astype(bf16))
     kv_next = from_behind(mine, "segment", -1)
-    own_parts = call(
-        functools.partial(project_kernel, count=count, layout=layout),
-        part_shape,
-        [anywhere, vmem] + [anywhere] * count,
-        [vmem] * dp,
-        16,
-        "project",
-        scratch=[all_tokens, pltpu.SemaphoreType.DMA((count,))],
-    )(parts[1], jnp.concatenate(w0), *tokens)
-    kv_own = place(scatter_sum(own_parts).astype(bf16))
+    kv_own = place(scatter_sum([*own_parts, last]).astype(bf16))
     (d,) = after([d], mine, kv_own)
     grad_in = call(
         functools.partial(grad_kernel, tile=tile),

time: 184 us -> 192 us (1.043)
  starting transfers between devices: 35.1 us -> 49.4 us
  local copies, waits for them, and re-layouts: 14.8 us -> 9.31 us
    all_to_all x1, starting transfers between devices: 3.79 us -> 13.6 us  [shards(): d = lax.all_to_all(d, 'dp', 0, 0, tiled=True)]
    ppermute x27, waiting for transfers between devices: 90.4 us -> 99.9 us  [swap(): return lax.ppermute(x, axis, [(i, i ^ bits) for i in range(peers)])]
    all_to_all x1, waiting for transfers between devices: 9.02 us -> 0.01 us  [shards(): lax.all_to_all(jnp.broadcast_to(w0, (tensor, own_depth, cols)), 'tensor',...]
    unnamed x59 -> x33, local copies, waits for them, and re-layouts: 14.7 us -> 7.04 us
    pallas_call x6 -> x3, Pallas kernels: 13.8 us -> 9.58 us  [the longest x1 4.56 us: shards(): call(d_kernel, like(dp, piece, depth), [smem] + [vmem] * 5, vmem, 20, 'd_...]
    ppermute x27, starting transfers between devices: 26.3 us -> 29.3 us  [swap(): return lax.ppermute(x, axis, [(i, i ^ bits) for i in range(peers)])]
    broadcast_in_dim x0 -> x1, local copies, waits for them, and re-layouts: none -> 2.28 us  [shards(): jnp.broadcast_to(w0, (tensor, own_depth, cols))]
    pallas_call x1, Pallas kernels: 8.86 us -> 10.9 us  [shards(): call(functools.partial(update_kernel, count=count, tile=step, layout=layo...]
  transfers between devices with their start and end apart: 30 -> 30, of which waited for: 16 -> 13; matrix products, arithmetic and copies ran while one was open for 2% -> 1% of each run, Pallas kernels for 12% -> 13%
where the time goes in v10:
time: 192 us; the launch traced here: 191 us
  waiting for transfers between devices  99.9 us (52%)
  starting transfers between devices  49.4 us (26%)
  Pallas kernels  27.3 us (14%)
  local copies, waits for them, and re-layouts  9.31 us (5%)
  other arithmetic  4.3 us (2%)
    ppermute x27, waiting for transfers between devices, swap(): return lax.ppermute(x, axis, [(i, i ^ bits) for i in range(peers)])  99.9 us
    ppermute x27, starting transfers between devices, swap(): return lax.ppermute(x, axis, [(i, i ^ bits) for i in range(peers)])  29.3 us
    all_to_all x1, starting transfers between devices, shards(): d = lax.all_to_all(d, 'dp', 0, 0, tiled=True)  13.6 us
    pallas_call x1, Pallas kernels, shards(): call(functools.partial(update_kernel, count=count, tile=step, layout=layo...  10.9 us
    unnamed x33, local copies, waits for them, and re-layouts  7.04 us
    all_to_all x1, starting transfers between devices, shards(): lax.all_to_all(jnp.broadcast_to(w0, (tensor, own_depth, cols)), 'tensor',...  5 us
    pallas_call x1, Pallas kernels, shards(): call(d_kernel, like(dp, piece, depth), [smem] + [vmem] * 5, vmem, 20, 'd_...  4.56 us
  transfers between devices with their start and end apart: 30, of which 13 were waited for; matrix products, arithmetic and copies ran while one was open for 1% of the time, Pallas kernels for 13%

profile of v10, /device:TPU:0, one launch (start us, length us, event | category | flops | bytes accessed | tf_op | source)
XLA Modules:
  0.0 191.0 jit_solution(2057580337771698118)
XLA Ops:
  0.6 1.7 bitcast_convert_fusion.weights_ref
  2.3 2.3 %broadcast_in_dim.6 = bf16[4,2048,256]{2,1,0:T(8,128)(2,1)} broadcast(bf16[2048,256]{1,0:T(8,128)(2,1)S(1)} %bitcast_convert_fusion.weights_ref), dimensions={1,2} | broadcast | bytes 5242880 | tf_op jit(solution)/shard_map/broadcast_in_dim | solution.py:275
  4.6 5.0 %all-to-all-start = ((bf16[4,2048,256]{2,1,0:T(8,128)(2,1)}), bf16[4,2048,256]{2,1,0:T(8,128)(2,1)}, u32[]{:S(2)}, u32[]{:S(2)}) async-start(bf16[4,2048,256]{2,1,0:T(8,128)(2,1)} %broadcast_in_dim.6), calls=%async_computation | async-start | bytes 8388608 | tf_op jit(solution)/shard_map/all_to_all | solution.py:274
  9.6 4.1 %collective-permute-start = (bf16[2,256,256]{2,1,0:T(8,128)(2,1)}, bf16[2,256,256]{2,1,0:T(8,128)(2,1)S(1)}, u32[]{:S(2)}, u32[]{:S(2)}) collective-permute-start(bf16[2,256,256]{2,1,0:T(8,128)(2,1)} %bitcast.45), channel_id=1, source_target_pairs={{0,8},{4,12},{8,0},{12,4},{1,9},{5,13},{9,1},{13,5},{2,10},{6,14},... | collective-permute-start | bytes 786440 | tf_op jit(solution)/shard_map/ppermute | solution.py:29
  13.8 1.6 collective-permute-start.1
  15.3 11.2 %collective-permute-done.mark_ref.refs_2_ = bf16[2,256,256]{2,1,0:T(8,128)(2,1)S(1)} collective-permute-done((bf16[2,256,256]{2,1,0:T(8,128)(2,1)}, bf16[2,256,256]{2,1,0:T(8,128)(2,1)S(1)}, u32[]{:S(2)}, u32[]{:S(2)}) %collective-permute-start) | collective-permute-done | bytes 262176 | tf_op jit(solution)/shard_map/ppermute | solution.py:29
  27.3 3.4 %norm.1 = (bf16[128,2048]{1,0:T(8,128)(2,1)}, bf16[128,2048]{1,0:T(8,128)(2,1)}, bf16[128,2048]{1,0:T(8,128)(2,1)}, bf16[128,2048]{1,0:T(8,128)(2,1)}) custom-call(bf16[2,256,256]{2,1,0:T(8,128)(2,1)S(1)} %collective-permute-done.mark_ref.refs_2_, bf16[2,256,256]{2,1,0:T(8,128)(2,1)} %collective-permute-done.1.other_ref.refs_1_, ...), custom_call_target="tpu_custom_call" | custom-call | flops 1000 | bytes 1000 | tf_op jit(solution)/shard_map/norm/pallas_call | solution.py:281
  30.7 3.9 %collective-permute-done.8.refs_3_ = bf16[2,256,256]{2,1,0:T(8,128)(2,1)} collective-permute-done((bf16[2,256,256]{2,1,0:T(8,128)(2,1)S(1)}, bf16[2,256,256]{2,1,0:T(8,128)(2,1)}, u32[]{:S(2)}, u32[]{:S(2)}) %collective-permute-start.8) | collective-permute-done | bytes 262176 | tf_op jit(solution)/shard_map/ppermute | solution.py:29
  41.2 3.3 %collective-permute-start.6 = (bf16[128,2048]{1,0:T(8,128)(2,1)}, bf16[128,2048]{1,0:T(8,128)(2,1)}, u32[]{:S(2)}, u32[]{:S(2)}) collective-permute-start(bf16[128,2048]{1,0:T(8,128)(2,1)} %get-tuple-element.31), channel_id=1, source_target_pairs={{0,8},{4,12},{8,0},{12,4},{1,9},{5,13},{9,1},{13,5},{2,10},{6,14},... | collective-permute-start | bytes 1572872 | tf_op jit(solution)/shard_map/ppermute | solution.py:29
  44.5 20.3 %collective-permute-done.10.c2_ref = bf16[512,256]{1,0:T(8,128)(2,1)S(1)} collective-permute-done((bf16[512,256]{1,0:T(8,128)(2,1)S(1)}, bf16[512,256]{1,0:T(8,128)(2,1)S(1)}, u32[]{:S(2)}, u32[]{:S(2)}) %collective-permute-start.10) | collective-permute-done | bytes 262176 | tf_op jit(solution)/shard_map/ppermute | solution.py:29
  64.8 3.9 %collective-permute-done.11.c3_ref = bf16[512,256]{1,0:T(8,128)(2,1)S(1)} collective-permute-done((bf16[512,256]{1,0:T(8,128)(2,1)S(1)}, bf16[512,256]{1,0:T(8,128)(2,1)S(1)}, u32[]{:S(2)}, u32[]{:S(2)}) %collective-permute-start.11) | collective-permute-done | bytes 262176 | tf_op jit(solution)/shard_map/ppermute | solution.py:29
  68.8 1.9 collective-permute-start.3
  71.6 4.6 %d_normed.1.refs_3_ = bf16[4,128,2048]{2,1,0:T(8,128)(2,1)S(1)} custom-call(s32[2]{0:T(128)S(1)} %pad_add_fusion.where_ref, bf16[512,256]{1,0:T(8,128)(2,1)S(1)} %copy-done.13, bf16[512,256]{1,0:T(8,128)(2,1)S(1)} %get-tuple-element.37.c1_ref, bf16[512,256]{1,0:T(8,128)(2,1)S(1)} %collective-permute-done.10.c2_ref, ...), custom_call_target="tpu_custom_call" | custom-call | flops 1000 | bytes 1000 | tf_op jit(solution)/shard_map/d_normed/pallas_call | solution.py:303
  76.2 3.8 %collective-permute-done.6.refs_1_ = bf16[128,2048]{1,0:T(8,128)(2,1)} collective-permute-done((bf16[128,2048]{1,0:T(8,128)(2,1)}, bf16[128,2048]{1,0:T(8,128)(2,1)}, u32[]{:S(2)}, u32[]{:S(2)}) %collective-permute-start.6) | collective-permute-done | bytes 524320 | tf_op jit(solution)/shard_map/ppermute | solution.py:29
  81.3 13.6 %all-to-all-start.1 = ((bf16[4,128,2048]{2,1,0:T(8,128)(2,1)}), bf16[4,128,2048]{2,1,0:T(8,128)(2,1)S(1)}, u32[]{:S(2)}, u32[]{:S(2)}) async-start(bf16[4,128,2048]{2,1,0:T(8,128)(2,1)} %copy-done), calls=%async_computation.1 | async-start | bytes 4194304 | tf_op jit(solution)/shard_map/all_to_all | solution.py:312
  94.9 1.7 collective-permute-start.12
  97.0 1.7 collective-permute-start.19
  99.0 10.9 %collective-permute-done.12.rest_5_ = bf16[128,2048]{1,0:T(8,128)(2,1)S(1)} collective-permute-done((bf16[128,2048]{1,0:T(8,128)(2,1)}, bf16[128,2048]{1,0:T(8,128)(2,1)S(1)}, u32[]{:S(2)}, u32[]{:S(2)}) %collective-permute-start.12) | collective-permute-done | bytes 524320 | tf_op jit(solution)/shard_map/ppermute | solution.py:29
  109.9 11.2 %collective-permute-done.15.rest_9_ = bf16[128,2048]{1,0:T(8,128)(2,1)S(1)} collective-permute-done((bf16[128,2048]{1,0:T(8,128)(2,1)}, bf16[128,2048]{1,0:T(8,128)(2,1)S(1)}, u32[]{:S(2)}, u32[]{:S(2)}) %collective-permute-start.15) | collective-permute-done | bytes 524320 | tf_op jit(solution)/shard_map/ppermute | solution.py:29
  121.6 10.3 %collective-permute-done.19.rest_13_ = bf16[128,2048]{1,0:T(8,128)(2,1)S(1)} collective-permute-done((bf16[128,2048]{1,0:T(8,128)(2,1)}, bf16[128,2048]{1,0:T(8,128)(2,1)S(1)}, u32[]{:S(2)}, u32[]{:S(2)}) %collective-permute-start.19) | collective-permute-done | bytes 524320 | tf_op jit(solution)/shard_map/ppermute | solution.py:29
  131.9 3.6 %project.1 = (bf16[512,256]{1,0:T(8,128)(2,1)S(1)}, bf16[512,256]{1,0:T(8,128)(2,1)S(1)}, bf16[512,256]{1,0:T(8,128)(2,1)S(1)}) custom-call(bf16[2048,256]{1,0:T(8,128)(2,1)S(1)} %bitcast_convert_fusion.weights_ref, bf16[128,2048]{1,0:T(8,128)(2,1)} %get-tuple-element.29.rest_0_, bf16[128,2048]{1,0:T(8,128)(2,1)} %collective-permute-done.2.rest_1_, ...), custom_call_target="tpu_custom_call" | custom-call | flops 1000 | bytes 1000 | tf_op jit(solution)/shard_map/project/pallas_call | solution.py:325
  137.0 10.9 %update.1 = (f32[2048,256]{1,0:T(8,128)}, bf16[512,256]{1,0:T(8,128)(2,1)S(1)}, bf16[512,256]{1,0:T(8,128)(2,1)}, bf16[512,256]{1,0:T(8,128)(2,1)S(1)}, bf16[512...) custom-call(bf16[512,256]{1,0:T(8,128)(2,1)S(1)} %get-tuple-element.42.mark_ref, bf16[256,2048]{1,0:T(8,128)(2,1)S(1)} %copy-done.7, ...), custom_call_target="tpu_custom_call" | custom-call | flops 1000 | bytes 1000 | tf_op jit(solution)/shard_map/update/pallas_call | solution.py:337
  147.9 2.1 %collective-permute-start.25 = (bf16[512,256]{1,0:T(8,128)(2,1)S(1)}, bf16[512,256]{1,0:T(8,128)(2,1)S(1)}, u32[]{:S(2)}, u32[]{:S(2)}) collective-permute-start(bf16[512,256]{1,0:T(8,128)(2,1)S(1)} %get-tuple-element.52), channel_id=1, source_target_pairs={{0,4},{4,0},{8,12},{12,8},{1,5},{5,1},{9,13},{13,9},{2,6},{6,2},{1... | collective-permute-start | bytes 786440 | tf_op jit(solution)/shard_map/ppermute | solution.py:29
  150.1 1.9 %collective-permute-start.24 = (bf16[512,256]{1,0:T(8,128)(2,1)}, bf16[512,256]{1,0:T(8,128)(2,1)}, u32[]{:S(2)}, u32[]{:S(2)}) collective-permute-start(bf16[512,256]{1,0:T(8,128)(2,1)} %get-tuple-element.50), channel_id=1, source_target_pairs={{0,4},{4,0},{8,12},{12,8},{1,5},{5,1},{9,13},{13,9},{2,6},{6,2},{1... | collective-permute-start | bytes 786440 | tf_op jit(solution)/shard_map/ppermute | solution.py:29
  152.0 5.1 %collective-permute-done.25 = bf16[512,256]{1,0:T(8,128)(2,1)S(1)} collective-permute-done((bf16[512,256]{1,0:T(8,128)(2,1)S(1)}, bf16[512,256]{1,0:T(8,128)(2,1)S(1)}, u32[]{:S(2)}, u32[]{:S(2)}) %collective-permute-start.25) | collective-permute-done | bytes 262176 | tf_op jit(solution)/shard_map/ppermute | solution.py:29
  157.3 2.9 %collective-permute-start.26 = (bf16[512,256]{1,0:T(8,128)(2,1)S(1)}, bf16[512,256]{1,0:T(8,128)(2,1)}, u32[]{:S(2)}, u32[]{:S(2)}) collective-permute-start(bf16[512,256]{1,0:T(8,128)(2,1)S(1)} %add_convert_fusion.1), channel_id=1, source_target_pairs={{0,8},{4,12},{8,0},{12,4},{1,9},{5,13},{9,1},{13,5},{2,10},{6,14},... | collective-permute-start | bytes 786440 | tf_op jit(solution)/shard_map/ppermute | solution.py:29
  161.6 6.8 %collective-permute-done.22 = bf16[512,256]{1,0:T(8,128)(2,1)S(1)} collective-permute-done((bf16[512,256]{1,0:T(8,128)(2,1)}, bf16[512,256]{1,0:T(8,128)(2,1)S(1)}, u32[]{:S(2)}, u32[]{:S(2)}) %collective-permute-start.22) | collective-permute-done | bytes 262176 | tf_op jit(solution)/shard_map/ppermute | solution.py:29
  169.4 2.0 %collective-permute-start.23 = (bf16[512,256]{1,0:T(8,128)(2,1)S(1)}, bf16[512,256]{1,0:T(8,128)(2,1)S(1)}, u32[]{:S(2)}, u32[]{:S(2)}) collective-permute-start(bf16[512,256]{1,0:T(8,128)(2,1)S(1)} %add_convert_fusion.3), channel_id=1, source_target_pairs={{0,8},{4,12},{8,0},{12,4},{1,9},{5,13},{9,1},{13,5},{2,10},{6,14},... | collective-permute-start | bytes 786440 | tf_op jit(solution)/shard_map/ppermute | solution.py:29
  171.4 2.8 %collective-permute-done.24 = bf16[512,256]{1,0:T(8,128)(2,1)} collective-permute-done((bf16[512,256]{1,0:T(8,128)(2,1)}, bf16[512,256]{1,0:T(8,128)(2,1)}, u32[]{:S(2)}, u32[]{:S(2)}) %collective-permute-start.24) | collective-permute-done | bytes 262176 | tf_op jit(solution)/shard_map/ppermute | solution.py:29
  175.5 1.5 collective-permute-start.27
  177.1 8.0 %collective-permute-done.18 = bf16[512,256]{1,0:T(8,128)(2,1)S(1)} collective-permute-done((bf16[512,256]{1,0:T(8,128)(2,1)}, bf16[512,256]{1,0:T(8,128)(2,1)S(1)}, u32[]{:S(2)}, u32[]{:S(2)}) %collective-permute-start.18) | collective-permute-done | bytes 262176 | tf_op jit(solution)/shard_map/ppermute | solution.py:29
  187.0 3.3 %grad_in.1 = bf16[128,8192]{1,0:T(8,128)(2,1)} custom-call(bf16[128,8192]{1,0:T(8,128)(2,1)S(1)} %bitcast.37, f32[1,8192]{1,0:T(1,128)S(1)} %copy-done.14, bf16[4,128,2048]{2,1,0:T(8,128)(2,1)S(1)} %after.5.d_ref), custom_call_target="tpu_custom_call" | custom-call | flops 1000 | bytes 1000 | tf_op jit(solution)/shard_map/grad_in/pallas_call | solution.py:366
  (81 shorter events, 18.7 us)
Async XLA Ops:
  4.6 66.0 %all-to-all-start = ((bf16[4,2048,256]{2,1,0:T(8,128)(2,1)}), bf16[4,2048,256]{2,1,0:T(8,128)(2,1)}, u32[]{:S(2)}, u32[]{:S(2)}) async-start(bf16[4,2048,256]{2,1,0:T(8,128)(2,1)} %broadcast_in_dim.6), calls=%async_computation | async-start | bytes 8388608 | tf_op jit(solution)/shard_map/all_to_all | solution.py:274
  9.6 16.9 %collective-permute-start = (bf16[2,256,256]{2,1,0:T(8,128)(2,1)}, bf16[2,256,256]{2,1,0:T(8,128)(2,1)S(1)}, u32[]{:S(2)}, u32[]{:S(2)}) collective-permute-start(bf16[2,256,256]{2,1,0:T(8,128)(2,1)} %bitcast.45), channel_id=1, source_target_pairs={{0,8},{4,12},{8,0},{12,4},{1,9},{5,13},{9,1},{13,5},{2,10},{6,14},... | collective-permute-start | bytes 786440 | tf_op jit(solution)/shard_map/ppermute | solution.py:29
  13.8 13.6 %collective-permute-start.1 = (bf16[2,256,256]{2,1,0:T(8,128)(2,1)}, bf16[2,256,256]{2,1,0:T(8,128)(2,1)}, u32[]{:S(2)}, u32[]{:S(2)}) collective-permute-start(bf16[2,256,256]{2,1,0:T(8,128)(2,1)} %bitcast.46), channel_id=1, source_target_pairs={{0,4},{4,0},{8,12},{12,8},{1,5},{5,1},{9,13},{13,9},{2,6},{6,2},{1... | collective-permute-start | bytes 786440 | tf_op jit(solution)/shard_map/ppermute | solution.py:29
  26.5 8.1 %collective-permute-start.8 = (bf16[2,256,256]{2,1,0:T(8,128)(2,1)S(1)}, bf16[2,256,256]{2,1,0:T(8,128)(2,1)}, u32[]{:S(2)}, u32[]{:S(2)}) collective-permute-start(bf16[2,256,256]{2,1,0:T(8,128)(2,1)S(1)} %collective-permute-done.mark_ref.refs_2_), channel_id=1, source_target_pairs={{0,4},{4,0},{8,12},{12,8},{1,5},{5,1},{9,13},{13,9},{2,6},{6,2},{1... | collective-permute-start | bytes 786440 | tf_op jit(solution)/shard_map/ppermute | solution.py:29
  37.0 1.5 collective-permute-start.9
  38.5 26.3 %collective-permute-start.10 = (bf16[512,256]{1,0:T(8,128)(2,1)S(1)}, bf16[512,256]{1,0:T(8,128)(2,1)S(1)}, u32[]{:S(2)}, u32[]{:S(2)}) collective-permute-start(bf16[512,256]{1,0:T(8,128)(2,1)S(1)} %get-tuple-element.38), channel_id=1, source_target_pairs={{0,2},{1,3},{2,0},{3,1},{4,6},{5,7},{6,4},{7,5},{8,10},{9,11},{10,... | collective-permute-start | bytes 786440 | tf_op jit(solution)/shard_map/ppermute | solution.py:29
  40.0 28.7 %collective-permute-start.11 = (bf16[512,256]{1,0:T(8,128)(2,1)S(1)}, bf16[512,256]{1,0:T(8,128)(2,1)S(1)}, u32[]{:S(2)}, u32[]{:S(2)}) collective-permute-start(bf16[512,256]{1,0:T(8,128)(2,1)S(1)} %get-tuple-element.39), channel_id=1, source_target_pairs={{0,3},{1,2},{2,1},{3,0},{4,7},{5,6},{6,5},{7,4},{8,11},{9,10},{10,... | collective-permute-start | bytes 786440 | tf_op jit(solution)/shard_map/ppermute | solution.py:29
  40.0 36.2 %collective-permute-start.5 = (bf16[128,2048]{1,0:T(8,128)(2,1)}, bf16[128,2048]{1,0:T(8,128)(2,1)}, u32[]{:S(2)}, u32[]{:S(2)}) collective-permute-start(bf16[128,2048]{1,0:T(8,128)(2,1)} %get-tuple-element.30.mark_ref), channel_id=1, source_target_pairs={{0,4},{4,0},{8,12},{12,8},{1,5},{5,1},{9,13},{13,9},{2,6},{6,2},{1... | collective-permute-start | bytes 1572872 | tf_op jit(solution)/shard_map/ppermute | solution.py:29
  41.2 38.8 %collective-permute-start.6 = (bf16[128,2048]{1,0:T(8,128)(2,1)}, bf16[128,2048]{1,0:T(8,128)(2,1)}, u32[]{:S(2)}, u32[]{:S(2)}) collective-permute-start(bf16[128,2048]{1,0:T(8,128)(2,1)} %get-tuple-element.31), channel_id=1, source_target_pairs={{0,8},{4,12},{8,0},{12,4},{1,9},{5,13},{9,1},{13,5},{2,10},{6,14},... | collective-permute-start | bytes 1572872 | tf_op jit(solution)/shard_map/ppermute | solution.py:29
  44.5 35.5 %collective-permute-start.7 = (bf16[128,2048]{1,0:T(8,128)(2,1)}, bf16[128,2048]{1,0:T(8,128)(2,1)}, u32[]{:S(2)}, u32[]{:S(2)}) collective-permute-start(bf16[128,2048]{1,0:T(8,128)(2,1)} %get-tuple-element.32), channel_id=1, source_target_pairs={{0,12},{4,8},{8,4},{12,0},{1,13},{5,9},{9,5},{13,1},{2,14},{6,10},... | collective-permute-start | bytes 1572872 | tf_op jit(solution)/shard_map/ppermute | solution.py:29
  64.8 30.1 %collective-permute-start.2 = (bf16[128,2048]{1,0:T(8,128)(2,1)}, bf16[128,2048]{1,0:T(8,128)(2,1)}, u32[]{:S(2)}, u32[]{:S(2)}) collective-permute-start(bf16[128,2048]{1,0:T(8,128)(2,1)} %get-tuple-element.29.rest_0_), channel_id=1, source_target_pairs={{0,2},{1,3},{2,0},{3,1},{4,6},{5,7},{6,4},{7,5},{8,10},{9,11},{10,... | collective-permute-start | bytes 1572872 | tf_op jit(solution)/shard_map/ppermute | solution.py:29
  68.8 28.2 %collective-permute-start.3 = (bf16[128,2048]{1,0:T(8,128)(2,1)}, bf16[128,2048]{1,0:T(8,128)(2,1)}, u32[]{:S(2)}, u32[]{:S(2)}) collective-permute-start(bf16[128,2048]{1,0:T(8,128)(2,1)} %get-tuple-element.29.rest_0_), channel_id=1, source_target_pairs={{0,1},{1,0},{2,3},{3,2},{4,5},{5,4},{6,7},{7,6},{8,9},{9,8},{10,11... | collective-permute-start | bytes 1572872 | tf_op jit(solution)/shard_map/ppermute | solution.py:29
  81.3 104.0 %all-to-all-start.1 = ((bf16[4,128,2048]{2,1,0:T(8,128)(2,1)}), bf16[4,128,2048]{2,1,0:T(8,128)(2,1)S(1)}, u32[]{:S(2)}, u32[]{:S(2)}) async-start(bf16[4,128,2048]{2,1,0:T(8,128)(2,1)} %copy-done), calls=%async_computation.1 | async-start | bytes 4194304 | tf_op jit(solution)/shard_map/all_to_all | solution.py:312
  94.9 3.9 %collective-permute-start.4 = (bf16[128,2048]{1,0:T(8,128)(2,1)}, bf16[128,2048]{1,0:T(8,128)(2,1)S(1)}, u32[]{:S(2)}, u32[]{:S(2)}) collective-permute-start(bf16[128,2048]{1,0:T(8,128)(2,1)} %collective-permute-done.2.rest_1_), channel_id=1, source_target_pairs={{0,1},{1,0},{2,3},{3,2},{4,5},{5,4},{6,7},{7,6},{8,9},{9,8},{10,11... | collective-permute-start | bytes 1572872 | tf_op jit(solution)/shard_map/ppermute | solution.py:29
  94.9 15.0 %collective-permute-start.12 = (bf16[128,2048]{1,0:T(8,128)(2,1)}, bf16[128,2048]{1,0:T(8,128)(2,1)S(1)}, u32[]{:S(2)}, u32[]{:S(2)}) collective-permute-start(bf16[128,2048]{1,0:T(8,128)(2,1)} %get-tuple-element.40.rest_4_), channel_id=1, source_target_pairs={{0,2},{1,3},{2,0},{3,1},{4,6},{5,7},{6,4},{7,5},{8,10},{9,11},{10,... | collective-permute-start | bytes 1572872 | tf_op jit(solution)/shard_map/ppermute | solution.py:29
  96.6 24.5 %collective-permute-start.15 = (bf16[128,2048]{1,0:T(8,128)(2,1)}, bf16[128,2048]{1,0:T(8,128)(2,1)S(1)}, u32[]{:S(2)}, u32[]{:S(2)}) collective-permute-start(bf16[128,2048]{1,0:T(8,128)(2,1)} %get-tuple-element.41.rest_8_), channel_id=1, source_target_pairs={{0,2},{1,3},{2,0},{3,1},{4,6},{5,7},{6,4},{7,5},{8,10},{9,11},{10,... | collective-permute-start | bytes 1572872 | tf_op jit(solution)/shard_map/ppermute | solution.py:29
  97.0 24.2 %collective-permute-start.13 = (bf16[128,2048]{1,0:T(8,128)(2,1)}, bf16[128,2048]{1,0:T(8,128)(2,1)S(1)}, u32[]{:S(2)}, u32[]{:S(2)}) collective-permute-start(bf16[128,2048]{1,0:T(8,128)(2,1)} %get-tuple-element.40.rest_4_), channel_id=1, source_target_pairs={{0,1},{1,0},{2,3},{3,2},{4,5},{5,4},{6,7},{7,6},{8,9},{9,8},{10,11... | collective-permute-start | bytes 1572872 | tf_op jit(solution)/shard_map/ppermute | solution.py:29
  97.0 40.0 %copy-start.3 = (f32[1,2048,256]{2,1,0:T(8,128)S(1)}, f32[1,2048,256]{2,1,0:T(8,128)}, u32[]{:S(2)}) copy-start(f32[1,2048,256]{2,1,0:T(8,128)} %param.9) | copy-start | bytes 6291460
  97.0 40.0 %copy-start.4 = (f32[1,2048,256]{2,1,0:T(8,128)S(1)}, f32[1,2048,256]{2,1,0:T(8,128)}, u32[]{:S(2)}) copy-start(f32[1,2048,256]{2,1,0:T(8,128)} %param.10) | copy-start | bytes 6291460
  97.0 34.9 %collective-permute-start.19 = (bf16[128,2048]{1,0:T(8,128)(2,1)}, bf16[128,2048]{1,0:T(8,128)(2,1)S(1)}, u32[]{:S(2)}, u32[]{:S(2)}) collective-permute-start(bf16[128,2048]{1,0:T(8,128)(2,1)} %get-tuple-element.46.rest_12_), channel_id=1, source_target_pairs={{0,2},{1,3},{2,0},{3,1},{4,6},{5,7},{6,4},{7,5},{8,10},{9,11},{10,... | collective-permute-start | bytes 1572872 | tf_op jit(solution)/shard_map/ppermute | solution.py:29
  98.7 33.2 %collective-permute-start.16 = (bf16[128,2048]{1,0:T(8,128)(2,1)}, bf16[128,2048]{1,0:T(8,128)(2,1)S(1)}, u32[]{:S(2)}, u32[]{:S(2)}) collective-permute-start(bf16[128,2048]{1,0:T(8,128)(2,1)} %get-tuple-element.41.rest_8_), channel_id=1, source_target_pairs={{0,1},{1,0},{2,3},{3,2},{4,5},{5,4},{6,7},{7,6},{8,9},{9,8},{10,11... | collective-permute-start | bytes 1572872 | tf_op jit(solution)/shard_map/ppermute | solution.py:29
  109.9 22.0 %collective-permute-start.14 = (bf16[128,2048]{1,0:T(8,128)(2,1)S(1)}, bf16[128,2048]{1,0:T(8,128)(2,1)S(1)}, u32[]{:S(2)}, u32[]{:S(2)}) collective-permute-start(bf16[128,2048]{1,0:T(8,128)(2,1)S(1)} %collective-permute-done.12.rest_5_), channel_id=1, source_target_pairs={{0,1},{1,0},{2,3},{3,2},{4,5},{5,4},{6,7},{7,6},{8,9},{9,8},{10,11... | collective-permute-start | bytes 1572872 | tf_op jit(solution)/shard_map/ppermute | solution.py:29
  121.1 10.8 %collective-permute-start.17 = (bf16[128,2048]{1,0:T(8,128)(2,1)S(1)}, bf16[128,2048]{1,0:T(8,128)(2,1)S(1)}, u32[]{:S(2)}, u32[]{:S(2)}) collective-permute-start(bf16[128,2048]{1,0:T(8,128)(2,1)S(1)} %collective-permute-done.15.rest_9_), channel_id=1, source_target_pairs={{0,1},{1,0},{2,3},{3,2},{4,5},{5,4},{6,7},{7,6},{8,9},{9,8},{10,11... | collective-permute-start | bytes 1572872 | tf_op jit(solution)/shard_map/ppermute | solution.py:29
  121.1 15.1 %collective-permute-start.20 = (bf16[128,2048]{1,0:T(8,128)(2,1)}, bf16[128,2048]{1,0:T(8,128)(2,1)S(1)}, u32[]{:S(2)}, u32[]{:S(2)}) collective-permute-start(bf16[128,2048]{1,0:T(8,128)(2,1)} %get-tuple-element.46.rest_12_), channel_id=1, source_target_pairs={{0,1},{1,0},{2,3},{3,2},{4,5},{5,4},{6,7},{7,6},{8,9},{9,8},{10,11... | collective-permute-start | bytes 1572872 | tf_op jit(solution)/shard_map/ppermute | solution.py:29
  131.9 4.4 %collective-permute-start.21 = (bf16[128,2048]{1,0:T(8,128)(2,1)S(1)}, bf16[128,2048]{1,0:T(8,128)(2,1)S(1)}, u32[]{:S(2)}, u32[]{:S(2)}) collective-permute-start(bf16[128,2048]{1,0:T(8,128)(2,1)S(1)} %collective-permute-done.19.rest_13_), channel_id=1, source_target_pairs={{0,1},{1,0},{2,3},{3,2},{4,5},{5,4},{6,7},{7,6},{8,9},{9,8},{10,11... | collective-permute-start | bytes 1572872 | tf_op jit(solution)/shard_map/ppermute | solution.py:29
  147.9 9.2 %collective-permute-start.25 = (bf16[512,256]{1,0:T(8,128)(2,1)S(1)}, bf16[512,256]{1,0:T(8,128)(2,1)S(1)}, u32[]{:S(2)}, u32[]{:S(2)}) collective-permute-start(bf16[512,256]{1,0:T(8,128)(2,1)S(1)} %get-tuple-element.52), channel_id=1, source_target_pairs={{0,4},{4,0},{8,12},{12,8},{1,5},{5,1},{9,13},{13,9},{2,6},{6,2},{1... | collective-permute-start | bytes 786440 | tf_op jit(solution)/shard_map/ppermute | solution.py:29
  150.0 18.4 %collective-permute-start.22 = (bf16[512,256]{1,0:T(8,128)(2,1)}, bf16[512,256]{1,0:T(8,128)(2,1)S(1)}, u32[]{:S(2)}, u32[]{:S(2)}) collective-permute-start(bf16[512,256]{1,0:T(8,128)(2,1)} %get-tuple-element.47), channel_id=1, source_target_pairs={{0,4},{4,0},{8,12},{12,8},{1,5},{5,1},{9,13},{13,9},{2,6},{6,2},{1... | collective-permute-start | bytes 786440 | tf_op jit(solution)/shard_map/ppermute | solution.py:29
  150.1 24.1 %collective-permute-start.24 = (bf16[512,256]{1,0:T(8,128)(2,1)}, bf16[512,256]{1,0:T(8,128)(2,1)}, u32[]{:S(2)}, u32[]{:S(2)}) collective-permute-start(bf16[512,256]{1,0:T(8,128)(2,1)} %get-tuple-element.50), channel_id=1, source_target_pairs={{0,4},{4,0},{8,12},{12,8},{1,5},{5,1},{9,13},{13,9},{2,6},{6,2},{1... | collective-permute-start | bytes 786440 | tf_op jit(solution)/shard_map/ppermute | solution.py:29
  157.3 17.0 %collective-permute-start.26 = (bf16[512,256]{1,0:T(8,128)(2,1)S(1)}, bf16[512,256]{1,0:T(8,128)(2,1)}, u32[]{:S(2)}, u32[]{:S(2)}) collective-permute-start(bf16[512,256]{1,0:T(8,128)(2,1)S(1)} %add_convert_fusion.1), channel_id=1, source_target_pairs={{0,8},{4,12},{8,0},{12,4},{1,9},{5,13},{9,1},{13,5},{2,10},{6,14},... | collective-permute-start | bytes 786440 | tf_op jit(solution)/shard_map/ppermute | solution.py:29
  160.2 24.9 %collective-permute-start.18 = (bf16[512,256]{1,0:T(8,128)(2,1)}, bf16[512,256]{1,0:T(8,128)(2,1)S(1)}, u32[]{:S(2)}, u32[]{:S(2)}) collective-permute-start(bf16[512,256]{1,0:T(8,128)(2,1)} %copy-done.15), channel_id=1, source_target_pairs={{0,4},{4,0},{8,12},{12,8},{1,5},{5,1},{9,13},{13,9},{2,6},{6,2},{1... | collective-permute-start | bytes 786440 | tf_op jit(solution)/shard_map/ppermute | solution.py:29
  169.4 15.6 %collective-permute-start.23 = (bf16[512,256]{1,0:T(8,128)(2,1)S(1)}, bf16[512,256]{1,0:T(8,128)(2,1)S(1)}, u32[]{:S(2)}, u32[]{:S(2)}) collective-permute-start(bf16[512,256]{1,0:T(8,128)(2,1)S(1)} %add_convert_fusion.3), channel_id=1, source_target_pairs={{0,8},{4,12},{8,0},{12,4},{1,9},{5,13},{9,1},{13,5},{2,10},{6,14},... | collective-permute-start | bytes 786440 | tf_op jit(solution)/shard_map/ppermute | solution.py:29
  175.5 10.4 %collective-permute-start.27 = (bf16[1,2,256,256]{3,2,1,0:T(8,128)(2,1)S(1)}, bf16[1,2,256,256]{3,2,1,0:T(8,128)(2,1)S(1)}, u32[]{:S(2)}, u32[]{:S(2)}) collective-permute-start(bf16[1,2,256,256]{3,2,1,0:T(8,128)(2,1)S(1)} %bitcast.41), channel_id=1, source_target_pairs={{0,16},{16,0},{1,17},{17,1},{2,18},{18,2},{3,19},{19,3},{4,20},{20... | collective-permute-start | bytes 786440 | tf_op jit(solution)/shard_map/ppermute | solution.py:34
  (14 other events, 180.9 us)

commit v11 on v10

--- a/solution.py
+++ b/solution.py
@@ -73,7 +73,7 @@
     return pl.ds(pl.multiple_of(index * size, size), size)
 
 
-def norm_kernel(mark_ref, other_ref, where_ref, hidden_ref, gain_ref, *own_refs, tile):
+def norm_kernel(where_ref, hidden_ref, gain_ref, *own_refs, tile):
     z = where_ref[0]
     rows, width = hidden_ref.shape
     depth = width // len(own_refs)
@@ -149,6 +149,19 @@
             d_ref[z ^ k, :, cut] = part[k * rows : (k + 1) * rows]
 
 
+def pack_kernel(*refs):
+    pieces, packed_ref, sem = refs[:-2], refs[-2], refs[-1]
+    rows = pieces[0].shape[0]
+    copies = [
+        pltpu.make_async_copy(x, packed_ref.at[pl.ds(p * rows, rows), :], sem.at[p])
+        for p, x in enumerate(pieces)
+    ]
+    for copy in copies:
+        copy.start()
+    for copy in copies:
+        copy.wait()
+
+
 def token_copies(token_refs, tokens_ref, sems, cut, first):
     copies, row = [], 0
     for p, x in enumerate(token_refs):
@@ -162,9 +175,9 @@
     return copies
 
 
-def update_kernel(mark_ref, turned_ref, weights_ref, master_hbm, m_hbm, v_hbm, *rest, count, tile, layout):
+def update_kernel(turned_ref, master_hbm, m_hbm, v_hbm, *rest, count, tile, layout):
     token_refs = rest[:count]
-    new_hbm, part_refs, last_ref = rest[count], rest[count + 1 : -9], rest[-9]
+    new_hbm, part_refs = rest[count], rest[count + 1 : -8]
     tokens, master, m, v, updated, new, sems, out_sems = rest[-8:]
     depth = master.shape[0]
     tiles = depth // tile
@@ -204,14 +217,6 @@
         outs.append(out)
         updated[cut, :] = master_new.astype(bf16)
     project(tokens, updated, part_refs, layout)
-    late = [p for p, (k, _) in enumerate(layout) if k == 3]
-    rows = tokens.shape[0] // len(layout)
-    project(
-        tokens.at[pl.ds(late[0] * rows, len(late) * rows), :],
-        weights_ref,
-        {3: last_ref},
-        [layout[p] for p in late],
-    )
     for out in outs:
         out.wait()
 
@@ -229,7 +234,7 @@
         p += span
 
 
-def project_kernel(weights_ref, *rest, count, layout):
+def project_kernel(mark_ref, weights_ref, *rest, count, layout):
     token_refs = rest[:count]
     part_refs, (tokens, sems) = rest[count:-2], rest[-2:]
     copies = token_copies(token_refs, tokens, sems, slice(None), 0)
@@ -249,10 +254,7 @@
     return blocks
 
 
-def scatter_sum(parts, *earlier):
-    got1, got3 = swap(parts[1], "dp", 1), swap(parts[3], "dp", 1)
-    if earlier:
-        got1, got3 = after([got1, got3], *earlier)
+def scatter_sum(parts, got1, got3):
     mine = parts[0].astype(f32) + got1.astype(f32)
     other = (parts[2].astype(f32) + got3.astype(f32)).astype(bf16)
     return mine + swap(other, "dp", 2).astype(f32)
@@ -281,14 +283,17 @@
     own = call(
         functools.partial(norm_kernel, tile=tile),
         [like(piece, depth)] * dp,
-        [anywhere, anywhere, smem, vmem, vmem],
+        [smem, vmem, vmem],
         [vmem] * dp,
         8,
         "norm",
-    )(cot2, cot1, where, hidden, norm_gain)
+    )(where, hidden, norm_gain)
     n1, n3 = swap(own[1], "dp", 1), swap(own[3], "dp", 3)
     n2 = swap(own[2], "dp", 2)
-    layout = tuple((k, j) for k in range(dp) for j in (0, 2, 1, 3))
+    layout = tuple(
+        (k, j) for group in ((0,), (1, 2), (3,)) for j in (0, 2, 1, 3) for k in group
+    )
+    across0 = swap(own[0], "tensor", 2)
     *blocks, turned = call(
         functools.partial(arrange_kernel, dp=dp, layout=layout),
         [like(dp * piece, cols)] * tensor + [like(cols, dp * tensor * piece)],
@@ -296,10 +301,9 @@
         [vmem] * (tensor + 1),
         8,
         "arrange",
-    )(own[1], where, cot0, cot1, cot2, cot3)
-    got1 = swap(blocks[1], "tensor", 1)
-    got1, blocks[2], blocks[3] = after([got1, blocks[2], blocks[3]])
-    mine_cot = [blocks[0], got1] + [swap(blocks[j], "tensor", j) for j in (2, 3)]
+    )(across0, where, cot0, cot1, cot2, cot3)
+    mine_cot = [blocks[0]] + [swap(blocks[j], "tensor", j) for j in range(1, tensor)]
+    n1, n2, n3, mine_cot[0] = after([n1, n2, n3, mine_cot[0]], *mine_cot[2:])
     d = call(
         d_kernel,
         like(dp, piece, depth),
@@ -308,11 +312,22 @@
         20,
         "d_normed",
     )(where, *mine_cot, whole_w)
-    n1, n2, n3, d = after([n1, n2, n3, d])
     d = lax.all_to_all(d, "dp", 0, 0, tiled=True)
+
+    def pack(*pieces):
+        return call(
+            pack_kernel,
+            like(len(pieces) * piece, depth),
+            [anywhere] * len(pieces),
+            anywhere,
+            0.25,
+            "pack",
+            scratch=[pltpu.SemaphoreType.DMA((len(pieces),))],
+        )(*pieces)
+
     tokens = []
-    for x in (own[0], n1, n2, n3):
-        across = swap(x, "tensor", 2)
+    for x in (own[0], pack(n1, n2), n3):
+        across = swap(x, "tensor", 2) if tokens else across0
         tokens += [x, across, swap(x, "tensor", 1), swap(across, "tensor", 1)]
     count = len(tokens)
     block = tensor * piece
@@ -321,24 +336,11 @@
     tiles = own_depth // step
     whole = pltpu.VMEM((own_depth, cols), f32)
     all_tokens = pltpu.VMEM((dp * block, depth), bf16)
-    early = count * 3 // 4
-    own_parts = call(
-        functools.partial(project_kernel, count=early, layout=layout[: 3 * tensor]),
-        part_shape[:3],
-        [vmem] + [anywhere] * early,
-        [vmem] * 3,
-        16,
-        "project",
-        scratch=[
-            pltpu.VMEM((3 * block, depth), bf16),
-            pltpu.SemaphoreType.DMA((early,)),
-        ],
-    )(w0, *tokens[:early])
-    master_new, *parts, last = call(
+    master_new, *parts = call(
         functools.partial(update_kernel, count=count, tile=step, layout=layout),
-        [like(own_depth, cols, dtype=f32)] + part_shape + part_shape[:1],
-        [anywhere, vmem, vmem] + [anywhere] * (3 + count),
-        [anywhere] + [vmem] * (dp + 1),
+        [like(own_depth, cols, dtype=f32)] + part_shape,
+        [vmem] + [anywhere] * (3 + count),
+        [anywhere] + [vmem] * dp,
         24,
         "update",
         scratch=[
@@ -351,7 +353,7 @@
             pltpu.SemaphoreType.DMA((tiles * (count + 3),)),
             pltpu.SemaphoreType.DMA((tiles,)),
         ],
-    )(own_parts[0], turned, w0, master_kv[0], moment_m[0], moment_v[0], *tokens)
+    )(turned, master_kv[0], moment_m[0], moment_v[0], *tokens)
 
     def place(x):
         x = x.reshape(tensor, micro, rows, cols)
@@ -359,9 +361,20 @@
             1, micro, tensor * rows, cols
         )
 
-    mine = place(scatter_sum(parts).astype(bf16))
+    got1, got3 = swap(parts[1], "dp", 1), swap(parts[3], "dp", 1)
+    mine = place(scatter_sum(parts, got1, got3).astype(bf16))
     kv_next = from_behind(mine, "segment", -1)
-    kv_own = place(scatter_sum([*own_parts, last]).astype(bf16))
+    own_parts = call(
+        functools.partial(project_kernel, count=count, layout=layout),
+        part_shape,
+        [anywhere, vmem] + [anywhere] * count,
+        [vmem] * dp,
+        16,
+        "project",
+        scratch=[all_tokens, pltpu.SemaphoreType.DMA((count,))],
+    )(got1, w0, *tokens)
+    own_got1, own_got3 = swap(own_parts[1], "dp", 1), swap(own_parts[3], "dp", 1)
+    kv_own = place(scatter_sum(own_parts, own_got1, own_got3).astype(bf16))
     (d,) = after([d], mine, kv_own)
     grad_in = call(
         functools.partial(grad_kernel, tile=tile),

time: 192 us -> 197 us (1.026)
  local copies, waits for them, and re-layouts: 9.31 us -> 20.1 us
  starting transfers between devices: 49.4 us -> 40.4 us
  waiting for transfers between devices: 99.9 us -> 104 us
    unnamed x33 -> x57, local copies, waits for them, and re-layouts: 7.04 us -> 17.8 us
    all_to_all x1, starting transfers between devices: 13.6 us -> 6.32 us  [shards(): d = lax.all_to_all(d, 'dp', 0, 0, tiled=True)]
    ppermute x27 -> x24, waiting for transfers between devices: 99.9 us -> 104 us  [swap(): return lax.ppermute(x, axis, [(i, i ^ bits) for i in range(peers)])]
    pallas_call x1 -> x2, Pallas kernels: 3.63 us -> 5.86 us  [the longest x1 4.83 us: shards(): call(functools.partial(project_kernel, count=count, layout=layout), part_...]
    ppermute x27 -> x24, starting transfers between devices: 29.3 us -> 27.6 us  [swap(): return lax.ppermute(x, axis, [(i, i ^ bits) for i in range(peers)])]
  transfers between devices with their start and end apart: 30 -> 27, of which waited for: 13 -> 15; matrix products, arithmetic and copies ran while one was open for 1% -> 1% of each run, Pallas kernels for 13% -> 12%
where the time goes in v11:
time: 197 us; the launch traced here: 196 us
  waiting for transfers between devices  104 us (53%)
  starting transfers between devices  40.4 us (21%)
  Pallas kernels  26.5 us (13%)
  local copies, waits for them, and re-layouts  20.1 us (10%)
  other arithmetic  4.22 us (2%)
    ppermute x24, waiting for transfers between devices, swap(): return lax.ppermute(x, axis, [(i, i ^ bits) for i in range(peers)])  104 us
    ppermute x24, starting transfers between devices, swap(): return lax.ppermute(x, axis, [(i, i ^ bits) for i in range(peers)])  27.6 us
    unnamed x57, local copies, waits for them, and re-layouts  17.8 us
    pallas_call x1, Pallas kernels, shards(): call(functools.partial(update_kernel, count=count, tile=step, layout=layo...  9.1 us
    all_to_all x1, starting transfers between devices, shards(): d = lax.all_to_all(d, 'dp', 0, 0, tiled=True)  6.32 us
    all_to_all x1, starting transfers between devices, shards(): lax.all_to_all(jnp.broadcast_to(w0, (tensor, own_depth, cols)), 'tensor',...  5.03 us
    pallas_call x1, Pallas kernels, shards(): call(functools.partial(project_kernel, count=count, layout=layout), part_...  4.83 us
    pallas_call x1, Pallas kernels, shards(): call(d_kernel, like(dp, piece, depth), [smem] + [vmem] * 5, vmem, 20, 'd_...  4.56 us
  transfers between devices with their start and end apart: 27, of which 15 were waited for; matrix products, arithmetic and copies ran while one was open for 1% of the time, Pallas kernels for 12%

profile of v11, /device:TPU:0, one launch (start us, length us, event | category | flops | bytes accessed | tf_op | source)
XLA Modules:
  0.0 195.7 jit_solution(13790507431405775989)
XLA Ops:
  0.6 1.7 bitcast_convert_fusion.weights_ref
  2.3 2.3 %broadcast_in_dim.6 = bf16[4,2048,256]{2,1,0:T(8,128)(2,1)} broadcast(bf16[2048,256]{1,0:T(8,128)(2,1)S(1)} %bitcast_convert_fusion.weights_ref), dimensions={1,2} | broadcast | bytes 5242880 | tf_op jit(solution)/shard_map/broadcast_in_dim | solution.py:277
  4.6 5.0 %all-to-all-start = ((bf16[4,2048,256]{2,1,0:T(8,128)(2,1)}), bf16[4,2048,256]{2,1,0:T(8,128)(2,1)}, u32[]{:S(2)}, u32[]{:S(2)}) async-start(bf16[4,2048,256]{2,1,0:T(8,128)(2,1)} %broadcast_in_dim.6), calls=%async_computation | async-start | bytes 8388608 | tf_op jit(solution)/shard_map/all_to_all | solution.py:276
  9.7 4.1 %collective-permute-start.2 = (bf16[2,256,256]{2,1,0:T(8,128)(2,1)S(1)}, bf16[2,256,256]{2,1,0:T(8,128)(2,1)}, u32[]{:S(2)}, u32[]{:S(2)}) collective-permute-start(bf16[2,256,256]{2,1,0:T(8,128)(2,1)S(1)} %bitcast.45), channel_id=1, source_target_pairs={{0,8},{4,12},{8,0},{12,4},{1,9},{5,13},{9,1},{13,5},{2,10},{6,14},... | collective-permute-start | bytes 786440 | tf_op jit(solution)/shard_map/ppermute | solution.py:29
  13.9 2.1 %norm.1 = (bf16[128,2048]{1,0:T(8,128)(2,1)S(1)}, bf16[128,2048]{1,0:T(8,128)(2,1)S(1)}, bf16[128,2048]{1,0:T(8,128)(2,1)S(1)}, bf16[128,2048]{1,0:T(8,128)(2,1)S(1)}) custom-call(s32[2]{0:T(128)S(1)} %pad_add_fusion.where_ref, bf16[128,8192]{1,0:T(8,128)(2,1)S(1)} %bitcast.37, f32[1,8192]{1,0:T(1,128)S(1)} %copy-done.26), custom_call_target="tpu_custom_call" | custom-call | flops 1000 | bytes 1000 | tf_op jit(solution)/shard_map/norm/pallas_call | solution.py:283
  16.0 1.9 collective-permute-start
  18.0 1.6 collective-permute-start.1
  20.0 6.5 %collective-permute-done.2.refs_2_ = bf16[2,256,256]{2,1,0:T(8,128)(2,1)} collective-permute-done((bf16[2,256,256]{2,1,0:T(8,128)(2,1)S(1)}, bf16[2,256,256]{2,1,0:T(8,128)(2,1)}, u32[]{:S(2)}, u32[]{:S(2)}) %collective-permute-start.2) | collective-permute-done | bytes 262176 | tf_op jit(solution)/shard_map/ppermute | solution.py:29
  27.0 3.5 %collective-permute-start.7 = (bf16[128,2048]{1,0:T(8,128)(2,1)S(1)}, bf16[128,2048]{1,0:T(8,128)(2,1)S(1)}, u32[]{:S(2)}, u32[]{:S(2)}) collective-permute-start(bf16[128,2048]{1,0:T(8,128)(2,1)S(1)} %get-tuple-element.29), channel_id=1, source_target_pairs={{0,8},{4,12},{8,0},{12,4},{1,9},{5,13},{9,1},{13,5},{2,10},{6,14},... | collective-permute-start | bytes 1572872 | tf_op jit(solution)/shard_map/ppermute | solution.py:29
  30.6 11.6 %collective-permute-done.1.refs_1_ = bf16[2,256,256]{2,1,0:T(8,128)(2,1)S(1)} collective-permute-done((bf16[2,256,256]{2,1,0:T(8,128)(2,1)S(1)}, bf16[2,256,256]{2,1,0:T(8,128)(2,1)S(1)}, u32[]{:S(2)}, u32[]{:S(2)}) %collective-permute-start.1) | collective-permute-done | bytes 262176 | tf_op jit(solution)/shard_map/ppermute | solution.py:29
  42.1 2.7 %collective-permute-start.8 = (bf16[128,2048]{1,0:T(8,128)(2,1)S(1)}, bf16[128,2048]{1,0:T(8,128)(2,1)S(1)}, u32[]{:S(2)}, u32[]{:S(2)}) collective-permute-start(bf16[128,2048]{1,0:T(8,128)(2,1)S(1)} %get-tuple-element.30), channel_id=1, source_target_pairs={{0,12},{4,8},{8,4},{12,0},{1,13},{5,9},{9,5},{13,1},{2,14},{6,10},... | collective-permute-start | bytes 1572872 | tf_op jit(solution)/shard_map/ppermute | solution.py:29
  44.9 24.7 %collective-permute-done.3.refs_3_ = bf16[2,256,256]{2,1,0:T(8,128)(2,1)S(1)} collective-permute-done((bf16[2,256,256]{2,1,0:T(8,128)(2,1)}, bf16[2,256,256]{2,1,0:T(8,128)(2,1)S(1)}, u32[]{:S(2)}, u32[]{:S(2)}) %collective-permute-start.3) | collective-permute-done | bytes 262176 | tf_op jit(solution)/shard_map/ppermute | solution.py:29
  69.6 1.5 arrange.1
  71.8 8.6 %collective-permute-done.9.refs_4_.c2_ref = bf16[512,256]{1,0:T(8,128)(2,1)S(1)} collective-permute-done((bf16[512,256]{1,0:T(8,128)(2,1)S(1)}, bf16[512,256]{1,0:T(8,128)(2,1)S(1)}, u32[]{:S(2)}, u32[]{:S(2)}) %collective-permute-start.9) | collective-permute-done | bytes 262176 | tf_op jit(solution)/shard_map/ppermute | solution.py:29
  80.4 2.1 %collective-permute-done.10.refs_5_.c3_ref = bf16[512,256]{1,0:T(8,128)(2,1)S(1)} collective-permute-done((bf16[512,256]{1,0:T(8,128)(2,1)S(1)}, bf16[512,256]{1,0:T(8,128)(2,1)S(1)}, u32[]{:S(2)}, u32[]{:S(2)}) %collective-permute-start.10) | collective-permute-done | bytes 262176 | tf_op jit(solution)/shard_map/ppermute | solution.py:29
  90.1 4.6 %d_normed.1 = bf16[4,128,2048]{2,1,0:T(8,128)(2,1)S(1)} custom-call(s32[2]{0:T(128)S(1)} %pad_add_fusion.where_ref, bf16[512,256]{1,0:T(8,128)(2,1)S(1)} %copy-done.18, bf16[512,256]{1,0:T(8,128)(2,1)S(1)} %copy-done.25, bf16[512,256]{1,0:T(8,128)(2,1)S(1)} %collective-permute-done.9.refs_4_.c2_ref, bf16[512,256]{1,0:T(8,128)(2,1)S(1)} %copy-done.16, ...), custom_call_target="tpu_custom_call" | custom-call | flops 1000 | bytes 1000 | tf_op jit(solution)/shard_map/d_normed/pallas_call | solution.py:307
  96.0 6.3 %all-to-all-start.1 = ((bf16[4,128,2048]{2,1,0:T(8,128)(2,1)}), bf16[4,128,2048]{2,1,0:T(8,128)(2,1)S(1)}, u32[]{:S(2)}, u32[]{:S(2)}) async-start(bf16[4,128,2048]{2,1,0:T(8,128)(2,1)} %copy-done.3), calls=%async_computation.1 | async-start | bytes 4194304 | tf_op jit(solution)/shard_map/all_to_all | solution.py:315
  104.0 5.4 %collective-permute-done.11.rest_5_ = bf16[256,2048]{1,0:T(8,128)(2,1)} collective-permute-done((bf16[256,2048]{1,0:T(8,128)(2,1)}, bf16[256,2048]{1,0:T(8,128)(2,1)}, u32[]{:S(2)}, u32[]{:S(2)}) %collective-permute-start.11) | collective-permute-done | bytes 1048608 | tf_op jit(solution)/shard_map/ppermute | solution.py:29
  111.1 9.5 %collective-permute-done.14.rest_9_ = bf16[128,2048]{1,0:T(8,128)(2,1)S(1)} collective-permute-done((bf16[128,2048]{1,0:T(8,128)(2,1)}, bf16[128,2048]{1,0:T(8,128)(2,1)S(1)}, u32[]{:S(2)}, u32[]{:S(2)}) %collective-permute-start.14) | collective-permute-done | bytes 524320 | tf_op jit(solution)/shard_map/ppermute | solution.py:29
  121.2 1.5 collective-permute-done.16.rest_11_
  122.8 1.6 copy-done
  126.4 1.6 copy-done.8
  128.0 1.6 copy-done.9
  131.9 9.1 %update.1 = (f32[2048,256]{1,0:T(8,128)}, bf16[512,256]{1,0:T(8,128)(2,1)S(1)}, bf16[512,256]{1,0:T(8,128)(2,1)S(1)}, bf16[512,256]{1,0:T(8,128)(2,1)S(1)}, bf16[512,256]{1,0:T(8,128)(2,1)S(1)}) custom-call(bf16[256,2048]{1,0:T(8,128)(2,1)S(1)} %copy-done.14, f32[2048,256]{1,0:T(8,128)S(1)} %bitcast.36, f32[2048,256]{1,0:T(8,128)S(1)} %bitcast.39, ...), custom_call_target="tpu_custom_call" | custom-call | flops 1000 | bytes 1000 | tf_op jit(solution)/shard_map/update/pallas_call | solution.py:339
  141.0 3.3 %collective-permute-start.17 = (bf16[512,256]{1,0:T(8,128)(2,1)S(1)}, bf16[512,256]{1,0:T(8,128)(2,1)S(1)}, u32[]{:S(2)}, u32[]{:S(2)}) collective-permute-start(bf16[512,256]{1,0:T(8,128)(2,1)S(1)} %get-tuple-element.37), channel_id=1, source_target_pairs={{0,4},{4,0},{8,12},{12,8},{1,5},{5,1},{9,13},{13,9},{2,6},{6,2},{1... | collective-permute-start | bytes 786440 | tf_op jit(solution)/shard_map/ppermute | solution.py:29
  144.4 12.3 %collective-permute-done.17.mark_ref = bf16[512,256]{1,0:T(8,128)(2,1)S(1)} collective-permute-done((bf16[512,256]{1,0:T(8,128)(2,1)S(1)}, bf16[512,256]{1,0:T(8,128)(2,1)S(1)}, u32[]{:S(2)}, u32[]{:S(2)}) %collective-permute-start.17) | collective-permute-done | bytes 262176 | tf_op jit(solution)/shard_map/ppermute | solution.py:29
  156.7 4.8 %project.1 = (bf16[512,256]{1,0:T(8,128)(2,1)S(1)}, bf16[512,256]{1,0:T(8,128)(2,1)S(1)}, bf16[512,256]{1,0:T(8,128)(2,1)S(1)}, bf16[512,256]{1,0:T(8,128)(2,1)}) custom-call(bf16[512,256]{1,0:T(8,128)(2,1)S(1)} %collective-permute-done.17.mark_ref, bf16[2048,256]{1,0:T(8,128)(2,1)S(1)} %bitcast_convert_fusion.weights_ref, bf16[128,2048]{1,0:T(8,128)(2,1)S(1)} %copy-done.11, ...), custom_call_target="tpu_custom_call" | custom-call | flops 1000 | bytes 1000 | tf_op jit(solution)/shard_map/project/pallas_call | solution.py:367
  165.1 10.4 %collective-permute-done.19 = bf16[512,256]{1,0:T(8,128)(2,1)S(1)} collective-permute-done((bf16[512,256]{1,0:T(8,128)(2,1)}, bf16[512,256]{1,0:T(8,128)(2,1)S(1)}, u32[]{:S(2)}, u32[]{:S(2)}) %collective-permute-start.19) | collective-permute-done | bytes 262176 | tf_op jit(solution)/shard_map/ppermute | solution.py:29
  179.3 1.5 collective-permute-start.24
  180.8 4.4 %collective-permute-done.18 = bf16[512,256]{1,0:T(8,128)(2,1)S(1)} collective-permute-done((bf16[512,256]{1,0:T(8,128)(2,1)}, bf16[512,256]{1,0:T(8,128)(2,1)S(1)}, u32[]{:S(2)}, u32[]{:S(2)}) %collective-permute-start.18) | collective-permute-done | bytes 262176 | tf_op jit(solution)/shard_map/ppermute | solution.py:29
  185.2 4.6 %collective-permute-done.20 = bf16[512,256]{1,0:T(8,128)(2,1)S(1)} collective-permute-done((bf16[512,256]{1,0:T(8,128)(2,1)S(1)}, bf16[512,256]{1,0:T(8,128)(2,1)S(1)}, u32[]{:S(2)}, u32[]{:S(2)}) %collective-permute-start.20) | collective-permute-done | bytes 262176 | tf_op jit(solution)/shard_map/ppermute | solution.py:29
  191.7 3.3 %grad_in.1 = bf16[128,8192]{1,0:T(8,128)(2,1)} custom-call(bf16[128,8192]{1,0:T(8,128)(2,1)S(1)} %bitcast.38, f32[1,8192]{1,0:T(1,128)S(1)} %copy-done.26, bf16[4,128,2048]{2,1,0:T(8,128)(2,1)S(1)} %after.3.d_ref), custom_call_target="tpu_custom_call" | custom-call | flops 1000 | bytes 1000 | tf_op jit(solution)/shard_map/grad_in/pallas_call | solution.py:379
  (99 shorter events, 29.1 us)
Async XLA Ops:
  4.6 82.6 %all-to-all-start = ((bf16[4,2048,256]{2,1,0:T(8,128)(2,1)}), bf16[4,2048,256]{2,1,0:T(8,128)(2,1)}, u32[]{:S(2)}, u32[]{:S(2)}) async-start(bf16[4,2048,256]{2,1,0:T(8,128)(2,1)} %broadcast_in_dim.6), calls=%async_computation | async-start | bytes 8388608 | tf_op jit(solution)/shard_map/all_to_all | solution.py:276
  9.7 16.8 %collective-permute-start.2 = (bf16[2,256,256]{2,1,0:T(8,128)(2,1)S(1)}, bf16[2,256,256]{2,1,0:T(8,128)(2,1)}, u32[]{:S(2)}, u32[]{:S(2)}) collective-permute-start(bf16[2,256,256]{2,1,0:T(8,128)(2,1)S(1)} %bitcast.45), channel_id=1, source_target_pairs={{0,8},{4,12},{8,0},{12,4},{1,9},{5,13},{9,1},{13,5},{2,10},{6,14},... | collective-permute-start | bytes 786440 | tf_op jit(solution)/shard_map/ppermute | solution.py:29
  16.0 28.9 %copy-start.10 = (bf16[128,2048]{1,0:T(8,128)(2,1)}, bf16[128,2048]{1,0:T(8,128)(2,1)S(1)}, u32[]{:S(2)}) copy-start(bf16[128,2048]{1,0:T(8,128)(2,1)S(1)} %get-tuple-element.26.rest_0_) | copy-start | bytes 1572868
  16.0 53.6 %collective-permute-start = (bf16[128,2048]{1,0:T(8,128)(2,1)S(1)}, bf16[128,2048]{1,0:T(8,128)(2,1)S(1)}, u32[]{:S(2)}, u32[]{:S(2)}) collective-permute-start(bf16[128,2048]{1,0:T(8,128)(2,1)S(1)} %get-tuple-element.26.rest_0_), channel_id=1, source_target_pairs={{0,2},{1,3},{2,0},{3,1},{4,6},{5,7},{6,4},{7,5},{8,10},{9,11},{10,... | collective-permute-start | bytes 1572872 | tf_op jit(solution)/shard_map/ppermute | solution.py:29
  18.0 24.2 %collective-permute-start.1 = (bf16[2,256,256]{2,1,0:T(8,128)(2,1)S(1)}, bf16[2,256,256]{2,1,0:T(8,128)(2,1)S(1)}, u32[]{:S(2)}, u32[]{:S(2)}) collective-permute-start(bf16[2,256,256]{2,1,0:T(8,128)(2,1)S(1)} %bitcast.46), channel_id=1, source_target_pairs={{0,4},{4,0},{8,12},{12,8},{1,5},{5,1},{9,13},{13,9},{2,6},{6,2},{1... | collective-permute-start | bytes 786440 | tf_op jit(solution)/shard_map/ppermute | solution.py:29
  19.5 52.2 %collective-permute-start.6 = (bf16[128,2048]{1,0:T(8,128)(2,1)S(1)}, bf16[128,2048]{1,0:T(8,128)(2,1)S(1)}, u32[]{:S(2)}, u32[]{:S(2)}) collective-permute-start(bf16[128,2048]{1,0:T(8,128)(2,1)S(1)} %get-tuple-element.28), channel_id=1, source_target_pairs={{0,4},{4,0},{8,12},{12,8},{1,5},{5,1},{9,13},{13,9},{2,6},{6,2},{1... | collective-permute-start | bytes 1572872 | tf_op jit(solution)/shard_map/ppermute | solution.py:29
  26.5 43.1 %collective-permute-start.3 = (bf16[2,256,256]{2,1,0:T(8,128)(2,1)}, bf16[2,256,256]{2,1,0:T(8,128)(2,1)S(1)}, u32[]{:S(2)}, u32[]{:S(2)}) collective-permute-start(bf16[2,256,256]{2,1,0:T(8,128)(2,1)} %collective-permute-done.2.refs_2_), channel_id=1, source_target_pairs={{0,4},{4,0},{8,12},{12,8},{1,5},{5,1},{9,13},{13,9},{2,6},{6,2},{1... | collective-permute-start | bytes 786440 | tf_op jit(solution)/shard_map/ppermute | solution.py:29
  27.0 44.7 %collective-permute-start.7 = (bf16[128,2048]{1,0:T(8,128)(2,1)S(1)}, bf16[128,2048]{1,0:T(8,128)(2,1)S(1)}, u32[]{:S(2)}, u32[]{:S(2)}) collective-permute-start(bf16[128,2048]{1,0:T(8,128)(2,1)S(1)} %get-tuple-element.29), channel_id=1, source_target_pairs={{0,8},{4,12},{8,0},{12,4},{1,9},{5,13},{9,1},{13,5},{2,10},{6,14},... | collective-permute-start | bytes 1572872 | tf_op jit(solution)/shard_map/ppermute | solution.py:29
  42.1 29.6 %collective-permute-start.8 = (bf16[128,2048]{1,0:T(8,128)(2,1)S(1)}, bf16[128,2048]{1,0:T(8,128)(2,1)S(1)}, u32[]{:S(2)}, u32[]{:S(2)}) collective-permute-start(bf16[128,2048]{1,0:T(8,128)(2,1)S(1)} %get-tuple-element.30), channel_id=1, source_target_pairs={{0,12},{4,8},{8,4},{12,0},{1,13},{5,9},{9,5},{13,1},{2,14},{6,10},... | collective-permute-start | bytes 1572872 | tf_op jit(solution)/shard_map/ppermute | solution.py:29
  69.6 13.9 %copy-start.4 = (bf16[128,2048]{1,0:T(8,128)(2,1)}, bf16[128,2048]{1,0:T(8,128)(2,1)S(1)}, u32[]{:S(2)}) copy-start(bf16[128,2048]{1,0:T(8,128)(2,1)S(1)} %collective-permute-done.mark_ref.rest_1_) | copy-start | bytes 1572868
  71.1 11.4 %copy-start.13 = (bf16[256,2048]{1,0:T(8,128)(2,1)}, bf16[256,2048]{1,0:T(8,128)(2,1)S(1)}, u32[]{:S(2)}) copy-start(bf16[256,2048]{1,0:T(8,128)(2,1)S(1)} %get-tuple-element.27.turned_ref) | copy-start | bytes 3145732
  71.1 9.3 %collective-permute-start.9 = (bf16[512,256]{1,0:T(8,128)(2,1)S(1)}, bf16[512,256]{1,0:T(8,128)(2,1)S(1)}, u32[]{:S(2)}, u32[]{:S(2)}) collective-permute-start(bf16[512,256]{1,0:T(8,128)(2,1)S(1)} %get-tuple-element.32), channel_id=1, source_target_pairs={{0,2},{1,3},{2,0},{3,1},{4,6},{5,7},{6,4},{7,5},{8,10},{9,11},{10,... | collective-permute-start | bytes 786440 | tf_op jit(solution)/shard_map/ppermute | solution.py:29
  71.5 11.0 %collective-permute-start.10 = (bf16[512,256]{1,0:T(8,128)(2,1)S(1)}, bf16[512,256]{1,0:T(8,128)(2,1)S(1)}, u32[]{:S(2)}, u32[]{:S(2)}) collective-permute-start(bf16[512,256]{1,0:T(8,128)(2,1)S(1)} %get-tuple-element.33), channel_id=1, source_target_pairs={{0,3},{1,2},{2,1},{3,0},{4,7},{5,6},{6,5},{7,4},{8,11},{9,10},{10,... | collective-permute-start | bytes 786440 | tf_op jit(solution)/shard_map/ppermute | solution.py:29
  83.5 25.8 %collective-permute-start.11 = (bf16[256,2048]{1,0:T(8,128)(2,1)}, bf16[256,2048]{1,0:T(8,128)(2,1)}, u32[]{:S(2)}, u32[]{:S(2)}) collective-permute-start(bf16[256,2048]{1,0:T(8,128)(2,1)} %pack.1.rest_4_), channel_id=1, source_target_pairs={{0,2},{1,3},{2,0},{3,1},{4,6},{5,7},{6,4},{7,5},{8,10},{9,11},{10,... | collective-permute-start | bytes 3145736 | tf_op jit(solution)/shard_map/ppermute | solution.py:29
  84.9 1.6 collective-permute-start.21
  96.0 94.0 %all-to-all-start.1 = ((bf16[4,128,2048]{2,1,0:T(8,128)(2,1)}), bf16[4,128,2048]{2,1,0:T(8,128)(2,1)S(1)}, u32[]{:S(2)}, u32[]{:S(2)}) async-start(bf16[4,128,2048]{2,1,0:T(8,128)(2,1)} %copy-done.3), calls=%async_computation.1 | async-start | bytes 4194304 | tf_op jit(solution)/shard_map/all_to_all | solution.py:315
  102.3 8.2 %collective-permute-start.4 = (bf16[128,2048]{1,0:T(8,128)(2,1)}, bf16[128,2048]{1,0:T(8,128)(2,1)S(1)}, u32[]{:S(2)}, u32[]{:S(2)}) collective-permute-start(bf16[128,2048]{1,0:T(8,128)(2,1)} %copy-done.10), channel_id=1, source_target_pairs={{0,1},{1,0},{2,3},{3,2},{4,5},{5,4},{6,7},{7,6},{8,9},{9,8},{10,11... | collective-permute-start | bytes 1572872 | tf_op jit(solution)/shard_map/ppermute | solution.py:29
  102.4 18.1 %collective-permute-start.14 = (bf16[128,2048]{1,0:T(8,128)(2,1)}, bf16[128,2048]{1,0:T(8,128)(2,1)S(1)}, u32[]{:S(2)}, u32[]{:S(2)}) collective-permute-start(bf16[128,2048]{1,0:T(8,128)(2,1)} %copy-done.6), channel_id=1, source_target_pairs={{0,2},{1,3},{2,0},{3,1},{4,6},{5,7},{6,4},{7,5},{8,10},{9,11},{10,... | collective-permute-start | bytes 1572872 | tf_op jit(solution)/shard_map/ppermute | solution.py:29
  103.8 19.0 %collective-permute-start.12 = (bf16[256,2048]{1,0:T(8,128)(2,1)}, bf16[256,2048]{1,0:T(8,128)(2,1)S(1)}, u32[]{:S(2)}, u32[]{:S(2)}) collective-permute-start(bf16[256,2048]{1,0:T(8,128)(2,1)} %pack.1.rest_4_), channel_id=1, source_target_pairs={{0,1},{1,0},{2,3},{3,2},{4,5},{5,4},{6,7},{7,6},{8,9},{9,8},{10,11... | collective-permute-start | bytes 3145736 | tf_op jit(solution)/shard_map/ppermute | solution.py:29
  109.4 13.4 %collective-permute-start.13 = (bf16[256,2048]{1,0:T(8,128)(2,1)}, bf16[256,2048]{1,0:T(8,128)(2,1)S(1)}, u32[]{:S(2)}, u32[]{:S(2)}) collective-permute-start(bf16[256,2048]{1,0:T(8,128)(2,1)} %collective-permute-done.11.rest_5_), channel_id=1, source_target_pairs={{0,1},{1,0},{2,3},{3,2},{4,5},{5,4},{6,7},{7,6},{8,9},{9,8},{10,11... | collective-permute-start | bytes 3145736 | tf_op jit(solution)/shard_map/ppermute | solution.py:29
  110.5 10.7 %collective-permute-start.5 = (bf16[128,2048]{1,0:T(8,128)(2,1)}, bf16[128,2048]{1,0:T(8,128)(2,1)S(1)}, u32[]{:S(2)}, u32[]{:S(2)}) collective-permute-start(bf16[128,2048]{1,0:T(8,128)(2,1)} %copy-done.4), channel_id=1, source_target_pairs={{0,1},{1,0},{2,3},{3,2},{4,5},{5,4},{6,7},{7,6},{8,9},{9,8},{10,11... | collective-permute-start | bytes 1572872 | tf_op jit(solution)/shard_map/ppermute | solution.py:29
  110.6 10.7 %collective-permute-start.15 = (bf16[128,2048]{1,0:T(8,128)(2,1)}, bf16[128,2048]{1,0:T(8,128)(2,1)S(1)}, u32[]{:S(2)}, u32[]{:S(2)}) collective-permute-start(bf16[128,2048]{1,0:T(8,128)(2,1)} %copy-done.6), channel_id=1, source_target_pairs={{0,1},{1,0},{2,3},{3,2},{4,5},{5,4},{6,7},{7,6},{8,9},{9,8},{10,11... | collective-permute-start | bytes 1572872 | tf_op jit(solution)/shard_map/ppermute | solution.py:29
  120.5 2.2 %collective-permute-start.16 = (bf16[128,2048]{1,0:T(8,128)(2,1)S(1)}, bf16[128,2048]{1,0:T(8,128)(2,1)S(1)}, u32[]{:S(2)}, u32[]{:S(2)}) collective-permute-start(bf16[128,2048]{1,0:T(8,128)(2,1)S(1)} %collective-permute-done.14.rest_9_), channel_id=1, source_target_pairs={{0,1},{1,0},{2,3},{3,2},{4,5},{5,4},{6,7},{7,6},{8,9},{9,8},{10,11... | collective-permute-start | bytes 1572872 | tf_op jit(solution)/shard_map/ppermute | solution.py:29
  141.0 20.5 %copy-start.23 = (bf16[512,256]{1,0:T(8,128)(2,1)}, bf16[512,256]{1,0:T(8,128)(2,1)S(1)}, u32[]{:S(2)}) copy-start(bf16[512,256]{1,0:T(8,128)(2,1)S(1)} %get-tuple-element.44) | copy-start | bytes 786436
  141.0 15.7 %collective-permute-start.17 = (bf16[512,256]{1,0:T(8,128)(2,1)S(1)}, bf16[512,256]{1,0:T(8,128)(2,1)S(1)}, u32[]{:S(2)}, u32[]{:S(2)}) collective-permute-start(bf16[512,256]{1,0:T(8,128)(2,1)S(1)} %get-tuple-element.37), channel_id=1, source_target_pairs={{0,4},{4,0},{8,12},{12,8},{1,5},{5,1},{9,13},{13,9},{2,6},{6,2},{1... | collective-permute-start | bytes 786440 | tf_op jit(solution)/shard_map/ppermute | solution.py:29
  144.3 17.9 %collective-permute-start.22 = (bf16[512,256]{1,0:T(8,128)(2,1)S(1)}, bf16[512,256]{1,0:T(8,128)(2,1)S(1)}, u32[]{:S(2)}, u32[]{:S(2)}) collective-permute-start(bf16[512,256]{1,0:T(8,128)(2,1)S(1)} %get-tuple-element.46), channel_id=1, source_target_pairs={{0,4},{4,0},{8,12},{12,8},{1,5},{5,1},{9,13},{13,9},{2,6},{6,2},{1... | collective-permute-start | bytes 786440 | tf_op jit(solution)/shard_map/ppermute | solution.py:29
  162.2 13.3 %collective-permute-start.19 = (bf16[512,256]{1,0:T(8,128)(2,1)}, bf16[512,256]{1,0:T(8,128)(2,1)S(1)}, u32[]{:S(2)}, u32[]{:S(2)}) collective-permute-start(bf16[512,256]{1,0:T(8,128)(2,1)} %get-tuple-element.41), channel_id=1, source_target_pairs={{0,4},{4,0},{8,12},{12,8},{1,5},{5,1},{9,13},{13,9},{2,6},{6,2},{1... | collective-permute-start | bytes 786440 | tf_op jit(solution)/shard_map/ppermute | solution.py:29
  163.0 15.0 %collective-permute-start.23 = (bf16[512,256]{1,0:T(8,128)(2,1)S(1)}, bf16[512,256]{1,0:T(8,128)(2,1)}, u32[]{:S(2)}, u32[]{:S(2)}) collective-permute-start(bf16[512,256]{1,0:T(8,128)(2,1)S(1)} %add_convert_fusion.1), channel_id=1, source_target_pairs={{0,8},{4,12},{8,0},{12,4},{1,9},{5,13},{9,1},{13,5},{2,10},{6,14},... | collective-permute-start | bytes 786440 | tf_op jit(solution)/shard_map/ppermute | solution.py:29
  164.4 25.3 %copy-start.22 = (bf16[512,256]{1,0:T(8,128)(2,1)S(1)}, bf16[512,256]{1,0:T(8,128)(2,1)}, u32[]{:S(2)}) copy-start(bf16[512,256]{1,0:T(8,128)(2,1)} %copy-done.21) | copy-start | bytes 786436
  164.4 20.8 %collective-permute-start.18 = (bf16[512,256]{1,0:T(8,128)(2,1)}, bf16[512,256]{1,0:T(8,128)(2,1)S(1)}, u32[]{:S(2)}, u32[]{:S(2)}) collective-permute-start(bf16[512,256]{1,0:T(8,128)(2,1)} %copy-done.27), channel_id=1, source_target_pairs={{0,4},{4,0},{8,12},{12,8},{1,5},{5,1},{9,13},{13,9},{2,6},{6,2},{1... | collective-permute-start | bytes 786440 | tf_op jit(solution)/shard_map/ppermute | solution.py:29
  176.5 13.3 %collective-permute-start.20 = (bf16[512,256]{1,0:T(8,128)(2,1)S(1)}, bf16[512,256]{1,0:T(8,128)(2,1)S(1)}, u32[]{:S(2)}, u32[]{:S(2)}) collective-permute-start(bf16[512,256]{1,0:T(8,128)(2,1)S(1)} %add_convert_fusion.3), channel_id=1, source_target_pairs={{0,8},{4,12},{8,0},{12,4},{1,9},{5,13},{9,1},{13,5},{2,10},{6,14},... | collective-permute-start | bytes 786440 | tf_op jit(solution)/shard_map/ppermute | solution.py:29
  179.3 11.4 %collective-permute-start.24 = (bf16[1,2,256,256]{3,2,1,0:T(8,128)(2,1)S(1)}, bf16[1,2,256,256]{3,2,1,0:T(8,128)(2,1)S(1)}, u32[]{:S(2)}, u32[]{:S(2)}) collective-permute-start(bf16[1,2,256,256]{3,2,1,0:T(8,128)(2,1)S(1)} %bitcast.41), channel_id=1, source_target_pairs={{0,16},{16,0},{1,17},{17,1},{2,18},{18,2},{3,19},{19,3},{4,20},{20... | collective-permute-start | bytes 786440 | tf_op jit(solution)/shard_map/ppermute | solution.py:34
  (23 other events, 48.2 us)

commit v12 on v11

--- a/solution.py
+++ b/solution.py
@@ -42,7 +42,7 @@
     return jax.ShapeDtypeStruct(shape, dtype)
 
 
-def call(body, out_shape, in_specs, out_specs, mib, name, scratch=(), **more):
+def call(body, out_shape, in_specs, out_specs, mib, name, scratch=(), cost=light, **more):
     return pl.pallas_call(
         body,
         out_shape=out_shape,
@@ -50,7 +50,7 @@
         out_specs=out_specs,
         scratch_shapes=list(scratch),
         compiler_params=pltpu.CompilerParams(vmem_limit_bytes=int(mib * 1024 * 1024)),
-        cost_estimate=light,
+        cost_estimate=cost,
         name=name,
         **more,
     )
@@ -175,9 +175,10 @@
     return copies
 
 
-def update_kernel(turned_ref, master_hbm, m_hbm, v_hbm, *rest, count, tile, layout):
+def update_kernel(turned_ref, weights_ref, master_hbm, m_hbm, v_hbm, *rest, count, tile, layout):
     token_refs = rest[:count]
     new_hbm, part_refs = rest[count], rest[count + 1 : -8]
+    part_refs, own_refs = part_refs[:4], part_refs[4:]
     tokens, master, m, v, updated, new, sems, out_sems = rest[-8:]
     depth = master.shape[0]
     tiles = depth // tile
@@ -217,6 +218,7 @@
         outs.append(out)
         updated[cut, :] = master_new.astype(bf16)
     project(tokens, updated, part_refs, layout)
+    project(tokens, weights_ref, own_refs, layout)
     for out in outs:
         out.wait()
 
@@ -234,17 +236,6 @@
         p += span
 
 
-def project_kernel(mark_ref, weights_ref, *rest, count, layout):
-    token_refs = rest[:count]
-    part_refs, (tokens, sems) = rest[count:-2], rest[-2:]
-    copies = token_copies(token_refs, tokens, sems, slice(None), 0)
-    for copy in copies:
-        copy.start()
-    for copy in copies:
-        copy.wait()
-    project(tokens, weights_ref, part_refs, layout)
-
-
 def reorder(blocks, me):
     bit = 1
     while bit < len(blocks):
@@ -279,7 +270,7 @@
     cot0 = kv_cot[0]
     cot2 = swap(cot0, "dp", 2)
     cot1 = swap(cot0, "dp", 1)
-    cot3 = swap(cot2, "dp", 1)
+    cot3 = swap(cot0, "dp", 3)
     own = call(
         functools.partial(norm_kernel, tile=tile),
         [like(piece, depth)] * dp,
@@ -288,6 +279,8 @@
         8,
         "norm",
     )(where, hidden, norm_gain)
+    own = list(own)
+    own[2], own[3] = after([own[2], own[3]], cot1)
     n1, n3 = swap(own[1], "dp", 1), swap(own[3], "dp", 3)
     n2 = swap(own[2], "dp", 2)
     layout = tuple(
@@ -309,7 +302,7 @@
         like(dp, piece, depth),
         [smem] + [vmem] * 5,
         vmem,
-        20,
+        60,
         "d_normed",
     )(where, *mine_cot, whole_w)
     d = lax.all_to_all(d, "dp", 0, 0, tiled=True)
@@ -338,10 +331,10 @@
     all_tokens = pltpu.VMEM((dp * block, depth), bf16)
     master_new, *parts = call(
         functools.partial(update_kernel, count=count, tile=step, layout=layout),
-        [like(own_depth, cols, dtype=f32)] + part_shape,
-        [vmem] + [anywhere] * (3 + count),
-        [anywhere] + [vmem] * dp,
-        24,
+        [like(own_depth, cols, dtype=f32)] + part_shape * 2,
+        [vmem] * 2 + [anywhere] * (3 + count),
+        [anywhere] + [vmem] * (2 * dp),
+        60,
         "update",
         scratch=[
             all_tokens,
@@ -353,7 +346,7 @@
             pltpu.SemaphoreType.DMA((tiles * (count + 3),)),
             pltpu.SemaphoreType.DMA((tiles,)),
         ],
-    )(turned, master_kv[0], moment_m[0], moment_v[0], *tokens)
+    )(turned, w0, master_kv[0], moment_m[0], moment_v[0], *tokens)
 
     def place(x):
         x = x.reshape(tensor, micro, rows, cols)
@@ -364,26 +357,23 @@
     got1, got3 = swap(parts[1], "dp", 1), swap(parts[3], "dp", 1)
     mine = place(scatter_sum(parts, got1, got3).astype(bf16))
     kv_next = from_behind(mine, "segment", -1)
-    own_parts = call(
-        functools.partial(project_kernel, count=count, layout=layout),
-        part_shape,
-        [anywhere, vmem] + [anywhere] * count,
-        [vmem] * dp,
-        16,
-        "project",
-        scratch=[all_tokens, pltpu.SemaphoreType.DMA((count,))],
-    )(got1, w0, *tokens)
+    parts, own_parts = parts[:dp], parts[dp:]
+    own_parts[1], own_parts[3] = after([own_parts[1], own_parts[3]], got1, got3)
     own_got1, own_got3 = swap(own_parts[1], "dp", 1), swap(own_parts[3], "dp", 1)
     kv_own = place(scatter_sum(own_parts, own_got1, own_got3).astype(bf16))
-    (d,) = after([d], mine, kv_own)
+    (d,) = after([d], mine)
     grad_in = call(
         functools.partial(grad_kernel, tile=tile),
         like(piece, width),
         [vmem] * 3,
         vmem,
-        12,
+        60,
         "grad_in",
+        cost=pl.CostEstimate(
+            flops=20 * piece * width, bytes_accessed=6 * piece * width, transcendentals=0
+        ),
     )(hidden, norm_gain, d)
+    (kv_next,) = after([kv_next], grad_in[:16, :128])
     return (kv_own, grad_in.reshape(hidden_in.shape), master_new[None], kv_next)
 
 

time: 197 us -> 201 us (1.020)
  waiting for transfers between devices: 104 us -> 115 us
  local copies, waits for them, and re-layouts: 20.1 us -> 13.2 us
  starting transfers between devices: 40.4 us -> 37.2 us
  Pallas kernels: 26.5 us -> 29.4 us
    ppermute x24, waiting for transfers between devices: 104 us -> 115 us  [swap(): return lax.ppermute(x, axis, [(i, i ^ bits) for i in range(peers)])]
    unnamed x57 -> x55, local copies, waits for them, and re-layouts: 17.8 us -> 9.49 us
    pallas_call x1, Pallas kernels: 9.1 us -> 14.5 us  [shards(): call(functools.partial(update_kernel, count=count, tile=step, layout=layo...]
    ppermute x24, starting transfers between devices: 27.6 us -> 24.3 us  [swap(): return lax.ppermute(x, axis, [(i, i ^ bits) for i in range(peers)])]
    pallas_call x2 -> x1, Pallas kernels: 9.4 us -> 6.22 us  [shards(): call(d_kernel, like(dp, piece, depth), [smem] + [vmem] * 5, vmem, 60, 'd_...]
    pallas_call x1, Pallas kernels: 3.34 us -> 5.58 us  [shards(): call(functools.partial(grad_kernel, tile=tile), like(piece, width), [vmem...]
  transfers between devices with their start and end apart: 27 -> 27, of which waited for: 15 -> 14; matrix products, arithmetic and copies ran while one was open for 1% -> 2% of each run, Pallas kernels for 12% -> 15%
where the time goes in v12:
time: 201 us
  waiting for transfers between devices  115 us (57%)
  starting transfers between devices  37.2 us (19%)
  Pallas kernels  29.4 us (15%)
  local copies, waits for them, and re-layouts  13.2 us (7%)
  other arithmetic  5.13 us (3%)
    ppermute x24, waiting for transfers between devices, swap(): return lax.ppermute(x, axis, [(i, i ^ bits) for i in range(peers)])  115 us
    ppermute x24, starting transfers between devices, swap(): return lax.ppermute(x, axis, [(i, i ^ bits) for i in range(peers)])  24.3 us
    pallas_call x1, Pallas kernels, shards(): call(functools.partial(update_kernel, count=count, tile=step, layout=layo...  14.5 us
    unnamed x55, local copies, waits for them, and re-layouts  9.49 us
    all_to_all x1, starting transfers between devices, shards(): d = lax.all_to_all(d, 'dp', 0, 0, tiled=True)  6.32 us
    pallas_call x1, Pallas kernels, shards(): call(d_kernel, like(dp, piece, depth), [smem] + [vmem] * 5, vmem, 60, 'd_...  6.22 us
    pallas_call x1, Pallas kernels, shards(): call(functools.partial(grad_kernel, tile=tile), like(piece, width), [vmem...  5.58 us
    all_to_all x1, starting transfers between devices, shards(): lax.all_to_all(jnp.broadcast_to(w0, (tensor, own_depth, cols)), 'tensor',...  5.03 us
  transfers between devices with their start and end apart: 27, of which 14 were waited for; matrix products, arithmetic and copies ran while one was open for 2% of the time, Pallas kernels for 15%

profile of v12, /device:TPU:0, one launch (start us, length us, event | category | flops | bytes accessed | tf_op | source)
XLA Modules:
  0.0 200.6 jit_solution(3672719164200013608)
XLA Ops:
  0.6 1.7 bitcast_convert_fusion.weights_ref
  3.3 2.3 %broadcast_in_dim.6 = bf16[4,2048,256]{2,1,0:T(8,128)(2,1)} broadcast(bf16[2048,256]{1,0:T(8,128)(2,1)S(1)} %bitcast_convert_fusion.weights_ref), dimensions={1,2} | broadcast | bytes 5242880 | tf_op jit(solution)/shard_map/broadcast_in_dim | solution.py:268
  5.6 5.0 %all-to-all-start = ((bf16[4,2048,256]{2,1,0:T(8,128)(2,1)}), bf16[4,2048,256]{2,1,0:T(8,128)(2,1)}, u32[]{:S(2)}, u32[]{:S(2)}) async-start(bf16[4,2048,256]{2,1,0:T(8,128)(2,1)} %broadcast_in_dim.6), calls=%async_computation | async-start | bytes 8388608 | tf_op jit(solution)/shard_map/all_to_all | solution.py:267
  10.6 3.1 %collective-permute-start.1 = (bf16[2,256,256]{2,1,0:T(8,128)(2,1)S(1)}, bf16[2,256,256]{2,1,0:T(8,128)(2,1)S(1)}, u32[]{:S(2)}, u32[]{:S(2)}) collective-permute-start(bf16[2,256,256]{2,1,0:T(8,128)(2,1)S(1)} %bitcast.32), channel_id=1, source_target_pairs={{0,4},{4,0},{8,12},{12,8},{1,5},{5,1},{9,13},{13,9},{2,6},{6,2},{1... | collective-permute-start | bytes 786440 | tf_op jit(solution)/shard_map/ppermute | solution.py:29
  13.8 2.1 %norm.1 = (bf16[128,2048]{1,0:T(8,128)(2,1)S(1)}, bf16[128,2048]{1,0:T(8,128)(2,1)S(1)}, bf16[128,2048]{1,0:T(8,128)(2,1)S(1)}, bf16[128,2048]{1,0:T(8,128)(2,1)S(1)}) custom-call(s32[2]{0:T(128)S(1)} %pad_add_fusion.where_ref, bf16[128,8192]{1,0:T(8,128)(2,1)S(1)} %bitcast.29, f32[1,8192]{1,0:T(1,128)S(1)} %copy-done.15), custom_call_target="tpu_custom_call" | custom-call | flops 1000 | bytes 1000 | tf_op jit(solution)/shard_map/norm/pallas_call | solution.py:274
  16.0 1.9 collective-permute-start
  17.9 2.6 %collective-permute-start.2 = (bf16[2,256,256]{2,1,0:T(8,128)(2,1)S(1)}, bf16[2,256,256]{2,1,0:T(8,128)(2,1)S(1)}, u32[]{:S(2)}, u32[]{:S(2)}) collective-permute-start(bf16[2,256,256]{2,1,0:T(8,128)(2,1)S(1)} %bitcast.33), channel_id=1, source_target_pairs={{0,8},{4,12},{8,0},{12,4},{1,9},{5,13},{9,1},{13,5},{2,10},{6,14},... | collective-permute-start | bytes 786440 | tf_op jit(solution)/shard_map/ppermute | solution.py:29
  21.4 3.5 %collective-permute-start.7 = (bf16[128,2048]{1,0:T(8,128)(2,1)S(1)}, bf16[128,2048]{1,0:T(8,128)(2,1)S(1)}, u32[]{:S(2)}, u32[]{:S(2)}) collective-permute-start(bf16[128,2048]{1,0:T(8,128)(2,1)S(1)} %get-tuple-element.35), channel_id=1, source_target_pairs={{0,8},{4,12},{8,0},{12,4},{1,9},{5,13},{9,1},{13,5},{2,10},{6,14},... | collective-permute-start | bytes 1572872 | tf_op jit(solution)/shard_map/ppermute | solution.py:29
  24.9 14.3 %collective-permute-done.2.refs_2_ = bf16[2,256,256]{2,1,0:T(8,128)(2,1)S(1)} collective-permute-done((bf16[2,256,256]{2,1,0:T(8,128)(2,1)S(1)}, bf16[2,256,256]{2,1,0:T(8,128)(2,1)S(1)}, u32[]{:S(2)}, u32[]{:S(2)}) %collective-permute-start.2) | collective-permute-done | bytes 262176 | tf_op jit(solution)/shard_map/ppermute | solution.py:29
  39.3 2.3 %collective-permute-start.8 = (bf16[128,2048]{1,0:T(8,128)(2,1)S(1)}, bf16[128,2048]{1,0:T(8,128)(2,1)S(1)}, u32[]{:S(2)}, u32[]{:S(2)}) collective-permute-start(bf16[128,2048]{1,0:T(8,128)(2,1)S(1)} %get-tuple-element.36), channel_id=1, source_target_pairs={{0,12},{4,8},{8,4},{12,0},{1,13},{5,9},{9,5},{13,1},{2,14},{6,10},... | collective-permute-start | bytes 1572872 | tf_op jit(solution)/shard_map/ppermute | solution.py:29
  41.5 29.0 %collective-permute-done.mark_ref.rest_1_ = bf16[128,2048]{1,0:T(8,128)(2,1)S(1)} collective-permute-done((bf16[128,2048]{1,0:T(8,128)(2,1)S(1)}, bf16[128,2048]{1,0:T(8,128)(2,1)S(1)}, u32[]{:S(2)}, u32[]{:S(2)}) %collective-permute-start) | collective-permute-done | bytes 524320 | tf_op jit(solution)/shard_map/ppermute | solution.py:29
  72.5 7.6 %collective-permute-done.10.refs_5_.c3_ref = bf16[512,256]{1,0:T(8,128)(2,1)S(1)} collective-permute-done((bf16[512,256]{1,0:T(8,128)(2,1)S(1)}, bf16[512,256]{1,0:T(8,128)(2,1)S(1)}, u32[]{:S(2)}, u32[]{:S(2)}) %collective-permute-start.10) | collective-permute-done | bytes 262176 | tf_op jit(solution)/shard_map/ppermute | solution.py:29
  80.1 4.6 %collective-permute-done.9.refs_4_.c2_ref = bf16[512,256]{1,0:T(8,128)(2,1)S(1)} collective-permute-done((bf16[512,256]{1,0:T(8,128)(2,1)S(1)}, bf16[512,256]{1,0:T(8,128)(2,1)S(1)}, u32[]{:S(2)}, u32[]{:S(2)}) %collective-permute-start.9) | collective-permute-done | bytes 262176 | tf_op jit(solution)/shard_map/ppermute | solution.py:29
  86.3 1.5 collective-permute-done.22.c1_ref
  88.5 6.2 %d_normed.1 = bf16[4,128,2048]{2,1,0:T(8,128)(2,1)} custom-call(s32[2]{0:T(128)} %copy-done.16, bf16[512,256]{1,0:T(8,128)(2,1)} %copy-done.8, bf16[512,256]{1,0:T(8,128)(2,1)} %copy-done.26, bf16[512,256]{1,0:T(8,128)(2,1)} %copy-done.7, bf16[512,256]{1,0:T(8,128)(2,1)} %copy-done.6, bf16[4,2048,256]{2,1,0:T(8,128)(2,1)} %all-to-all-done.w_ref), custom_call_target="tpu_custom_call" | custom-call | flops 1000 | bytes 1000 | tf_op jit(solution)/shard_map/d_normed/pallas_call | solution.py:300
  94.7 6.3 %all-to-all-start.1 = ((bf16[4,128,2048]{2,1,0:T(8,128)(2,1)}), bf16[4,128,2048]{2,1,0:T(8,128)(2,1)S(1)}, u32[]{:S(2)}, u32[]{:S(2)}) async-start(bf16[4,128,2048]{2,1,0:T(8,128)(2,1)} %d_normed.1), calls=%async_computation.1 | async-start | bytes 4194304 | tf_op jit(solution)/shard_map/all_to_all | solution.py:308
  101.0 1.3 collective-permute-start.14
  102.6 8.9 %collective-permute-done.11.rest_5_ = bf16[256,2048]{1,0:T(8,128)(2,1)} collective-permute-done((bf16[256,2048]{1,0:T(8,128)(2,1)S(1)}, bf16[256,2048]{1,0:T(8,128)(2,1)}, u32[]{:S(2)}, u32[]{:S(2)}) %collective-permute-start.11) | collective-permute-done | bytes 1048608 | tf_op jit(solution)/shard_map/ppermute | solution.py:29
  112.1 9.9 %collective-permute-done.14.rest_9_ = bf16[128,2048]{1,0:T(8,128)(2,1)S(1)} collective-permute-done((bf16[128,2048]{1,0:T(8,128)(2,1)}, bf16[128,2048]{1,0:T(8,128)(2,1)S(1)}, u32[]{:S(2)}, u32[]{:S(2)}) %collective-permute-start.14) | collective-permute-done | bytes 524320 | tf_op jit(solution)/shard_map/ppermute | solution.py:29
  122.1 1.1 copy-done.18
  124.8 14.5 %update.1 = (f32[2048,256]{1,0:T(8,128)}, bf16[512,256]{1,0:T(8,128)(2,1)}, bf16[512,256]{1,0:T(8,128)(2,1)}, bf16[512,256]{1,0:T(8,128)(2,1)}, bf16[512,256]{1,...) custom-call(bf16[256,2048]{1,0:T(8,128)(2,1)} %copy-done.5, ...), custom_call_target="tpu_custom_call" | custom-call | flops 1000 | bytes 1000 | tf_op jit(solution)/shard_map/update/pallas_call | solution.py:332
  139.3 3.2 %collective-permute-start.18 = (bf16[512,256]{1,0:T(8,128)(2,1)}, bf16[512,256]{1,0:T(8,128)(2,1)S(1)}, u32[]{:S(2)}, u32[]{:S(2)}) collective-permute-start(bf16[512,256]{1,0:T(8,128)(2,1)} %get-tuple-element.47), channel_id=1, source_target_pairs={{0,4},{4,0},{8,12},{12,8},{1,5},{5,1},{9,13},{13,9},{2,6},{6,2},{1... | collective-permute-start | bytes 786440 | tf_op jit(solution)/shard_map/ppermute | solution.py:29
  142.5 12.7 %collective-permute-done.18.refs_3_ = bf16[512,256]{1,0:T(8,128)(2,1)S(1)} collective-permute-done((bf16[512,256]{1,0:T(8,128)(2,1)}, bf16[512,256]{1,0:T(8,128)(2,1)S(1)}, u32[]{:S(2)}, u32[]{:S(2)}) %collective-permute-start.18) | collective-permute-done | bytes 262176 | tf_op jit(solution)/shard_map/ppermute | solution.py:29
  155.2 5.6 %collective-permute-done.17.refs_2_ = bf16[512,256]{1,0:T(8,128)(2,1)S(1)} collective-permute-done((bf16[512,256]{1,0:T(8,128)(2,1)}, bf16[512,256]{1,0:T(8,128)(2,1)S(1)}, u32[]{:S(2)}, u32[]{:S(2)}) %collective-permute-start.17) | collective-permute-done | bytes 262176 | tf_op jit(solution)/shard_map/ppermute | solution.py:29
  165.2 2.0 %collective-permute-start.23 = (bf16[512,256]{1,0:T(8,128)(2,1)S(1)}, bf16[512,256]{1,0:T(8,128)(2,1)}, u32[]{:S(2)}, u32[]{:S(2)}) collective-permute-start(bf16[512,256]{1,0:T(8,128)(2,1)S(1)} %add_convert_fusion.1), channel_id=1, source_target_pairs={{0,8},{4,12},{8,0},{12,4},{1,9},{5,13},{9,1},{13,5},{2,10},{6,14},... | collective-permute-start | bytes 786440 | tf_op jit(solution)/shard_map/ppermute | solution.py:29
  167.3 9.7 %collective-permute-done.20 = bf16[512,256]{1,0:T(8,128)(2,1)S(1)} collective-permute-done((bf16[512,256]{1,0:T(8,128)(2,1)}, bf16[512,256]{1,0:T(8,128)(2,1)S(1)}, u32[]{:S(2)}, u32[]{:S(2)}) %collective-permute-start.20) | collective-permute-done | bytes 262176 | tf_op jit(solution)/shard_map/ppermute | solution.py:29
  178.7 1.6 collective-permute-done.23
  181.4 1.5 collective-permute-start.24
  183.0 4.4 %collective-permute-done.19 = bf16[512,256]{1,0:T(8,128)(2,1)S(1)} collective-permute-done((bf16[512,256]{1,0:T(8,128)(2,1)}, bf16[512,256]{1,0:T(8,128)(2,1)S(1)}, u32[]{:S(2)}, u32[]{:S(2)}) %collective-permute-start.19) | collective-permute-done | bytes 262176 | tf_op jit(solution)/shard_map/ppermute | solution.py:29
  187.4 4.0 %collective-permute-done.21 = bf16[512,256]{1,0:T(8,128)(2,1)S(1)} collective-permute-done((bf16[512,256]{1,0:T(8,128)(2,1)S(1)}, bf16[512,256]{1,0:T(8,128)(2,1)S(1)}, u32[]{:S(2)}, u32[]{:S(2)}) %collective-permute-start.21) | collective-permute-done | bytes 262176 | tf_op jit(solution)/shard_map/ppermute | solution.py:29
  192.3 1.4 copy-done
  193.6 5.6 %grad_in.1 = bf16[128,8192]{1,0:T(8,128)(2,1)} custom-call(bf16[128,8192]{1,0:T(8,128)(2,1)} %bitcast.28, f32[1,8192]{1,0:T(1,128)} %gain_ref.3, bf16[4,128,2048]{2,1,0:T(8,128)(2,1)} %copy-done), custom_call_target="tpu_custom_call" | custom-call | flops 20971520 | bytes 6291456 | tf_op jit(solution)/shard_map/grad_in/pallas_call | solution.py:365
  (101 shorter events, 18.1 us)
Async XLA Ops:
  5.6 82.2 %all-to-all-start = ((bf16[4,2048,256]{2,1,0:T(8,128)(2,1)}), bf16[4,2048,256]{2,1,0:T(8,128)(2,1)}, u32[]{:S(2)}, u32[]{:S(2)}) async-start(bf16[4,2048,256]{2,1,0:T(8,128)(2,1)} %broadcast_in_dim.6), calls=%async_computation | async-start | bytes 8388608 | tf_op jit(solution)/shard_map/all_to_all | solution.py:267
  10.6 10.8 %collective-permute-start.1 = (bf16[2,256,256]{2,1,0:T(8,128)(2,1)S(1)}, bf16[2,256,256]{2,1,0:T(8,128)(2,1)S(1)}, u32[]{:S(2)}, u32[]{:S(2)}) collective-permute-start(bf16[2,256,256]{2,1,0:T(8,128)(2,1)S(1)} %bitcast.32), channel_id=1, source_target_pairs={{0,4},{4,0},{8,12},{12,8},{1,5},{5,1},{9,13},{13,9},{2,6},{6,2},{1... | collective-permute-start | bytes 786440 | tf_op jit(solution)/shard_map/ppermute | solution.py:29
  13.8 57.6 %copy-start.16 = (s32[2]{0:T(128)}, s32[2]{0:T(128)S(1)}, u32[]{:S(2)}) copy-start(s32[2]{0:T(128)S(1)} %pad_add_fusion.where_ref) | copy-start | bytes 28
  16.0 25.6 %copy-start.9 = (bf16[128,2048]{1,0:T(8,128)(2,1)}, bf16[128,2048]{1,0:T(8,128)(2,1)S(1)}, u32[]{:S(2)}) copy-start(bf16[128,2048]{1,0:T(8,128)(2,1)S(1)} %get-tuple-element.30.rest_0_) | copy-start | bytes 1572868
  16.0 54.6 %collective-permute-start = (bf16[128,2048]{1,0:T(8,128)(2,1)S(1)}, bf16[128,2048]{1,0:T(8,128)(2,1)S(1)}, u32[]{:S(2)}, u32[]{:S(2)}) collective-permute-start(bf16[128,2048]{1,0:T(8,128)(2,1)S(1)} %get-tuple-element.30.rest_0_), channel_id=1, source_target_pairs={{0,2},{1,3},{2,0},{3,1},{4,6},{5,7},{6,4},{7,5},{8,10},{9,11},{10,... | collective-permute-start | bytes 1572872 | tf_op jit(solution)/shard_map/ppermute | solution.py:29
  17.9 21.3 %collective-permute-start.2 = (bf16[2,256,256]{2,1,0:T(8,128)(2,1)S(1)}, bf16[2,256,256]{2,1,0:T(8,128)(2,1)S(1)}, u32[]{:S(2)}, u32[]{:S(2)}) collective-permute-start(bf16[2,256,256]{2,1,0:T(8,128)(2,1)S(1)} %bitcast.33), channel_id=1, source_target_pairs={{0,8},{4,12},{8,0},{12,4},{1,9},{5,13},{9,1},{13,5},{2,10},{6,14},... | collective-permute-start | bytes 786440 | tf_op jit(solution)/shard_map/ppermute | solution.py:29
  20.5 21.0 %collective-permute-start.3 = (bf16[2,256,256]{2,1,0:T(8,128)(2,1)S(1)}, bf16[2,256,256]{2,1,0:T(8,128)(2,1)S(1)}, u32[]{:S(2)}, u32[]{:S(2)}) collective-permute-start(bf16[2,256,256]{2,1,0:T(8,128)(2,1)S(1)} %bitcast.34), channel_id=1, source_target_pairs={{0,12},{4,8},{8,4},{12,0},{1,13},{5,9},{9,5},{13,1},{2,14},{6,10},... | collective-permute-start | bytes 786440 | tf_op jit(solution)/shard_map/ppermute | solution.py:29
  20.5 51.9 %collective-permute-start.6 = (bf16[128,2048]{1,0:T(8,128)(2,1)S(1)}, bf16[128,2048]{1,0:T(8,128)(2,1)S(1)}, u32[]{:S(2)}, u32[]{:S(2)}) collective-permute-start(bf16[128,2048]{1,0:T(8,128)(2,1)S(1)} %get-tuple-element.32), channel_id=1, source_target_pairs={{0,4},{4,0},{8,12},{12,8},{1,5},{5,1},{9,13},{13,9},{2,6},{6,2},{1... | collective-permute-start | bytes 1572872 | tf_op jit(solution)/shard_map/ppermute | solution.py:29
  21.4 63.3 %collective-permute-start.7 = (bf16[128,2048]{1,0:T(8,128)(2,1)S(1)}, bf16[128,2048]{1,0:T(8,128)(2,1)S(1)}, u32[]{:S(2)}, u32[]{:S(2)}) collective-permute-start(bf16[128,2048]{1,0:T(8,128)(2,1)S(1)} %get-tuple-element.35), channel_id=1, source_target_pairs={{0,8},{4,12},{8,0},{12,4},{1,9},{5,13},{9,1},{13,5},{2,10},{6,14},... | collective-permute-start | bytes 1572872 | tf_op jit(solution)/shard_map/ppermute | solution.py:29
  39.3 45.5 %collective-permute-start.8 = (bf16[128,2048]{1,0:T(8,128)(2,1)S(1)}, bf16[128,2048]{1,0:T(8,128)(2,1)S(1)}, u32[]{:S(2)}, u32[]{:S(2)}) collective-permute-start(bf16[128,2048]{1,0:T(8,128)(2,1)S(1)} %get-tuple-element.36), channel_id=1, source_target_pairs={{0,12},{4,8},{8,4},{12,0},{1,13},{5,9},{9,5},{13,1},{2,14},{6,10},... | collective-permute-start | bytes 1572872 | tf_op jit(solution)/shard_map/ppermute | solution.py:29
  71.5 8.6 %collective-permute-start.10 = (bf16[512,256]{1,0:T(8,128)(2,1)S(1)}, bf16[512,256]{1,0:T(8,128)(2,1)S(1)}, u32[]{:S(2)}, u32[]{:S(2)}) collective-permute-start(bf16[512,256]{1,0:T(8,128)(2,1)S(1)} %get-tuple-element.39), channel_id=1, source_target_pairs={{0,3},{1,2},{2,1},{3,0},{4,7},{5,6},{6,5},{7,4},{8,11},{9,10},{10,... | collective-permute-start | bytes 786440 | tf_op jit(solution)/shard_map/ppermute | solution.py:29
  71.6 13.2 %collective-permute-start.9 = (bf16[512,256]{1,0:T(8,128)(2,1)S(1)}, bf16[512,256]{1,0:T(8,128)(2,1)S(1)}, u32[]{:S(2)}, u32[]{:S(2)}) collective-permute-start(bf16[512,256]{1,0:T(8,128)(2,1)S(1)} %get-tuple-element.38), channel_id=1, source_target_pairs={{0,2},{1,3},{2,0},{3,1},{4,6},{5,7},{6,4},{7,5},{8,10},{9,11},{10,... | collective-permute-start | bytes 786440 | tf_op jit(solution)/shard_map/ppermute | solution.py:29
  85.4 16.9 %copy-start.2 = (bf16[256,2048]{1,0:T(8,128)(2,1)}, bf16[256,2048]{1,0:T(8,128)(2,1)S(1)}, u32[]{:S(2)}) copy-start(bf16[256,2048]{1,0:T(8,128)(2,1)S(1)} %pack.1.rest_4_) | copy-start | bytes 3145732
  85.4 26.1 %collective-permute-start.11 = (bf16[256,2048]{1,0:T(8,128)(2,1)S(1)}, bf16[256,2048]{1,0:T(8,128)(2,1)}, u32[]{:S(2)}, u32[]{:S(2)}) collective-permute-start(bf16[256,2048]{1,0:T(8,128)(2,1)S(1)} %pack.1.rest_4_), channel_id=1, source_target_pairs={{0,2},{1,3},{2,0},{3,1},{4,6},{5,7},{6,4},{7,5},{8,10},{9,11},{10,... | collective-permute-start | bytes 3145736 | tf_op jit(solution)/shard_map/ppermute | solution.py:29
  86.3 1.5 collective-permute-start.22
  94.7 97.5 %all-to-all-start.1 = ((bf16[4,128,2048]{2,1,0:T(8,128)(2,1)}), bf16[4,128,2048]{2,1,0:T(8,128)(2,1)S(1)}, u32[]{:S(2)}, u32[]{:S(2)}) async-start(bf16[4,128,2048]{2,1,0:T(8,128)(2,1)} %d_normed.1), calls=%async_computation.1 | async-start | bytes 4194304 | tf_op jit(solution)/shard_map/all_to_all | solution.py:308
  101.0 11.0 %collective-permute-start.4 = (bf16[128,2048]{1,0:T(8,128)(2,1)}, bf16[128,2048]{1,0:T(8,128)(2,1)S(1)}, u32[]{:S(2)}, u32[]{:S(2)}) collective-permute-start(bf16[128,2048]{1,0:T(8,128)(2,1)} %copy-done.9), channel_id=1, source_target_pairs={{0,1},{1,0},{2,3},{3,2},{4,5},{5,4},{6,7},{7,6},{8,9},{9,8},{10,11... | collective-permute-start | bytes 1572872 | tf_op jit(solution)/shard_map/ppermute | solution.py:29
  101.0 21.0 %collective-permute-start.14 = (bf16[128,2048]{1,0:T(8,128)(2,1)}, bf16[128,2048]{1,0:T(8,128)(2,1)S(1)}, u32[]{:S(2)}, u32[]{:S(2)}) collective-permute-start(bf16[128,2048]{1,0:T(8,128)(2,1)} %copy-done.4), channel_id=1, source_target_pairs={{0,2},{1,3},{2,0},{3,1},{4,6},{5,7},{6,4},{7,5},{8,10},{9,11},{10,... | collective-permute-start | bytes 1572872 | tf_op jit(solution)/shard_map/ppermute | solution.py:29
  102.4 19.7 %collective-permute-start.12 = (bf16[256,2048]{1,0:T(8,128)(2,1)S(1)}, bf16[256,2048]{1,0:T(8,128)(2,1)S(1)}, u32[]{:S(2)}, u32[]{:S(2)}) collective-permute-start(bf16[256,2048]{1,0:T(8,128)(2,1)S(1)} %pack.1.rest_4_), channel_id=1, source_target_pairs={{0,1},{1,0},{2,3},{3,2},{4,5},{5,4},{6,7},{7,6},{8,9},{9,8},{10,11... | collective-permute-start | bytes 3145736 | tf_op jit(solution)/shard_map/ppermute | solution.py:29
  111.5 12.5 %collective-permute-start.13 = (bf16[256,2048]{1,0:T(8,128)(2,1)}, bf16[256,2048]{1,0:T(8,128)(2,1)}, u32[]{:S(2)}, u32[]{:S(2)}) collective-permute-start(bf16[256,2048]{1,0:T(8,128)(2,1)} %collective-permute-done.11.rest_5_), channel_id=1, source_target_pairs={{0,1},{1,0},{2,3},{3,2},{4,5},{5,4},{6,7},{7,6},{8,9},{9,8},{10,11... | collective-permute-start | bytes 3145736 | tf_op jit(solution)/shard_map/ppermute | solution.py:29
  111.5 10.5 %collective-permute-start.5 = (bf16[128,2048]{1,0:T(8,128)(2,1)}, bf16[128,2048]{1,0:T(8,128)(2,1)S(1)}, u32[]{:S(2)}, u32[]{:S(2)}) collective-permute-start(bf16[128,2048]{1,0:T(8,128)(2,1)} %copy-done.3), channel_id=1, source_target_pairs={{0,1},{1,0},{2,3},{3,2},{4,5},{5,4},{6,7},{7,6},{8,9},{9,8},{10,11... | collective-permute-start | bytes 1572872 | tf_op jit(solution)/shard_map/ppermute | solution.py:29
  112.0 10.0 %collective-permute-start.15 = (bf16[128,2048]{1,0:T(8,128)(2,1)}, bf16[128,2048]{1,0:T(8,128)(2,1)S(1)}, u32[]{:S(2)}, u32[]{:S(2)}) collective-permute-start(bf16[128,2048]{1,0:T(8,128)(2,1)} %copy-done.4), channel_id=1, source_target_pairs={{0,1},{1,0},{2,3},{3,2},{4,5},{5,4},{6,7},{7,6},{8,9},{9,8},{10,11... | collective-permute-start | bytes 1572872 | tf_op jit(solution)/shard_map/ppermute | solution.py:29
  122.0 1.9 collective-permute-start.16
  139.3 16.0 %collective-permute-start.18 = (bf16[512,256]{1,0:T(8,128)(2,1)}, bf16[512,256]{1,0:T(8,128)(2,1)S(1)}, u32[]{:S(2)}, u32[]{:S(2)}) collective-permute-start(bf16[512,256]{1,0:T(8,128)(2,1)} %get-tuple-element.47), channel_id=1, source_target_pairs={{0,4},{4,0},{8,12},{12,8},{1,5},{5,1},{9,13},{13,9},{2,6},{6,2},{1... | collective-permute-start | bytes 786440 | tf_op jit(solution)/shard_map/ppermute | solution.py:29
  142.4 18.3 %collective-permute-start.17 = (bf16[512,256]{1,0:T(8,128)(2,1)}, bf16[512,256]{1,0:T(8,128)(2,1)S(1)}, u32[]{:S(2)}, u32[]{:S(2)}) collective-permute-start(bf16[512,256]{1,0:T(8,128)(2,1)} %get-tuple-element.46), channel_id=1, source_target_pairs={{0,4},{4,0},{8,12},{12,8},{1,5},{5,1},{9,13},{13,9},{2,6},{6,2},{1... | collective-permute-start | bytes 786440 | tf_op jit(solution)/shard_map/ppermute | solution.py:29
  162.7 17.6 %copy-start.25 = (bf16[512,256]{1,0:T(8,128)(2,1)S(1)}, bf16[512,256]{1,0:T(8,128)(2,1)}, u32[]{:S(2)}) copy-start(bf16[512,256]{1,0:T(8,128)(2,1)} %get-tuple-element.53) | copy-start | bytes 786436
  164.1 27.2 %copy-start.24 = (bf16[512,256]{1,0:T(8,128)(2,1)S(1)}, bf16[512,256]{1,0:T(8,128)(2,1)}, u32[]{:S(2)}) copy-start(bf16[512,256]{1,0:T(8,128)(2,1)} %get-tuple-element.43) | copy-start | bytes 786436
  164.1 12.9 %collective-permute-start.20 = (bf16[512,256]{1,0:T(8,128)(2,1)}, bf16[512,256]{1,0:T(8,128)(2,1)S(1)}, u32[]{:S(2)}, u32[]{:S(2)}) collective-permute-start(bf16[512,256]{1,0:T(8,128)(2,1)} %copy-done.14), channel_id=1, source_target_pairs={{0,4},{4,0},{8,12},{12,8},{1,5},{5,1},{9,13},{13,9},{2,6},{6,2},{1... | collective-permute-start | bytes 786440 | tf_op jit(solution)/shard_map/ppermute | solution.py:29
  165.2 15.1 %collective-permute-start.23 = (bf16[512,256]{1,0:T(8,128)(2,1)S(1)}, bf16[512,256]{1,0:T(8,128)(2,1)}, u32[]{:S(2)}, u32[]{:S(2)}) collective-permute-start(bf16[512,256]{1,0:T(8,128)(2,1)S(1)} %add_convert_fusion.1), channel_id=1, source_target_pairs={{0,8},{4,12},{8,0},{12,4},{1,9},{5,13},{9,1},{13,5},{2,10},{6,14},... | collective-permute-start | bytes 786440 | tf_op jit(solution)/shard_map/ppermute | solution.py:29
  167.2 20.1 %collective-permute-start.19 = (bf16[512,256]{1,0:T(8,128)(2,1)}, bf16[512,256]{1,0:T(8,128)(2,1)S(1)}, u32[]{:S(2)}, u32[]{:S(2)}) collective-permute-start(bf16[512,256]{1,0:T(8,128)(2,1)} %copy-done.12), channel_id=1, source_target_pairs={{0,4},{4,0},{8,12},{12,8},{1,5},{5,1},{9,13},{13,9},{2,6},{6,2},{1... | collective-permute-start | bytes 786440 | tf_op jit(solution)/shard_map/ppermute | solution.py:29
  178.0 13.3 %collective-permute-start.21 = (bf16[512,256]{1,0:T(8,128)(2,1)S(1)}, bf16[512,256]{1,0:T(8,128)(2,1)S(1)}, u32[]{:S(2)}, u32[]{:S(2)}) collective-permute-start(bf16[512,256]{1,0:T(8,128)(2,1)S(1)} %add_convert_fusion.3), channel_id=1, source_target_pairs={{0,8},{4,12},{8,0},{12,4},{1,9},{5,13},{9,1},{13,5},{2,10},{6,14},... | collective-permute-start | bytes 786440 | tf_op jit(solution)/shard_map/ppermute | solution.py:29
  181.4 18.5 %collective-permute-start.24 = (bf16[1,2,256,256]{3,2,1,0:T(8,128)(2,1)S(1)}, bf16[1,2,256,256]{3,2,1,0:T(8,128)(2,1)S(1)}, u32[]{:S(2)}, u32[]{:S(2)}) collective-permute-start(bf16[1,2,256,256]{3,2,1,0:T(8,128)(2,1)S(1)} %bitcast.30), channel_id=1, source_target_pairs={{0,16},{16,0},{1,17},{17,1},{2,18},{18,2},{3,19},{19,3},{4,20},{20... | collective-permute-start | bytes 786440 | tf_op jit(solution)/shard_map/ppermute | solution.py:34
  (22 other events, 86.1 us)

commit v13 on v7

--- a/solution.py
+++ b/solution.py
@@ -137,16 +137,16 @@
 
 
 def d_kernel(where_ref, cot_ref, *rest):
-    w_refs, d_ref = rest[:8], rest[8]
+    w_refs, d_ref = rest[:4], rest[4]
     z, t = where_ref[0], where_ref[1]
     dp, rows = d_ref.shape[:2]
     half = w_refs[0].shape[0]
     tile = min(half, 512)
     cot = jnp.concatenate([cot_ref[t ^ j] for j in range(cot_ref.shape[0])], axis=1)
-    for side in range(2):
+    for side in range(1):
         for i in range(half // tile):
             cut = slice(i * tile, (i + 1) * tile)
-            whole = jnp.concatenate([w[cut, :] for w in w_refs[side::2]], axis=1)
+            whole = jnp.concatenate([w[cut, :] for w in w_refs], axis=1)
             part = dot(cot, whole, ((1,), (1,))).astype(bf16)
             for k in range(dp):
                 d_ref[z ^ k, :, side * half + i * tile : side * half + (i + 1) * tile] = part[
@@ -259,10 +259,8 @@
     return blocks
 
 
-def scatter_sum(parts, *earlier):
-    got1, got3 = swap(parts[1], "dp", 1), swap(parts[3], "dp", 1)
-    if earlier:
-        got1, got3 = after([got1, got3], *earlier)
+def scatter_sum(parts, got=None):
+    got1, got3 = got or (swap(parts[1], "dp", 1), swap(parts[3], "dp", 1))
     mine = parts[0].astype(f32) + got1.astype(f32)
     other = (parts[2].astype(f32) + got3.astype(f32)).astype(bf16)
     return mine + swap(other, "dp", 2).astype(f32)
@@ -280,8 +278,7 @@
     depth = width // dp
     tile = min(piece, 16)
 
-    half = own_depth // 2
-    w0 = [master_kv[0, :half].astype(bf16), master_kv[0, half:].astype(bf16)]
+    w0 = [master_kv[0].astype(bf16)]
     w2 = [swap(w, "tensor", 2) for w in w0]
     w1 = [swap(w, "tensor", 1) for w in w0]
     cot0 = kv_cot[0]
@@ -329,7 +326,7 @@
     d = call(
         d_kernel,
         like(dp, piece, depth),
-        [smem] + [vmem] * 9,
+        [smem] + [vmem] * 5,
         vmem,
         20,
         "d_normed",
@@ -370,7 +367,8 @@
             1, micro, tensor * rows, cols
         )
 
-    mine = place(scatter_sum(parts).astype(bf16))
+    got1, got3 = swap(parts[1], "dp", 1), swap(parts[3], "dp", 1)
+    mine = place(scatter_sum(parts, (got1, got3)).astype(bf16))
     kv_next = from_behind(mine, "segment", -1)
     own_parts = call(
         functools.partial(project_kernel, count=count, layout=layout),
@@ -380,7 +378,7 @@
         16,
         "project",
         scratch=[all_tokens, pltpu.SemaphoreType.DMA((count,))],
-    )(parts[1], jnp.concatenate(w0), *tokens)
+    )(got1, w0[0], *tokens)
     kv_own = place(scatter_sum(own_parts).astype(bf16))
     (d,) = after([d], mine, kv_own)
     grad_in = call(

time: 184 us -> 179 us (0.973)
  starting transfers between devices: 35.1 us -> 28.8 us
  local copies, waits for them, and re-layouts: 14.8 us -> 11.9 us
  waiting for transfers between devices: 99.4 us -> 102 us
    ppermute x27 -> x24, starting transfers between devices: 26.3 us -> 19.8 us  [swap(): return lax.ppermute(x, axis, [(i, i ^ bits) for i in range(peers)])]
    ppermute x27 -> x24, waiting for transfers between devices: 90.4 us -> 95.5 us  [swap(): return lax.ppermute(x, axis, [(i, i ^ bits) for i in range(peers)])]
    unnamed x59 -> x37, local copies, waits for them, and re-layouts: 14.7 us -> 11.9 us
    all_to_all x1, waiting for transfers between devices: 9.02 us -> 6.83 us  [shards(): mine_cot = lax.all_to_all(send, 'tensor', 0, 0, tiled=True)]
  transfers between devices with their start and end apart: 30 -> 27, of which waited for: 16 -> 15; matrix products, arithmetic and copies ran while one was open for 2% -> 1% of each run, Pallas kernels for 12% -> 15%
where the time goes in v13:
time: 179 us; the launch traced here: 178 us
  waiting for transfers between devices  102 us (57%)
  Pallas kernels  29.5 us (16%)
  starting transfers between devices  28.8 us (16%)
  local copies, waits for them, and re-layouts  11.9 us (7%)
  other arithmetic  4.37 us (2%)
    ppermute x24, waiting for transfers between devices, swap(): return lax.ppermute(x, axis, [(i, i ^ bits) for i in range(peers)])  95.5 us
    ppermute x24, starting transfers between devices, swap(): return lax.ppermute(x, axis, [(i, i ^ bits) for i in range(peers)])  19.8 us
    unnamed x37, local copies, waits for them, and re-layouts  11.9 us
    pallas_call x1, Pallas kernels, shards(): call(functools.partial(update_kernel, count=count, tile=step, layout=layo...  8.78 us
    all_to_all x1, waiting for transfers between devices, shards(): mine_cot = lax.all_to_all(send, 'tensor', 0, 0, tiled=True)  6.83 us
    pallas_call x1, Pallas kernels, shards(): call(functools.partial(project_kernel, count=count, layout=layout), part_...  4.62 us
    pallas_call x1, Pallas kernels, shards(): call(d_kernel, like(dp, piece, depth), [smem] + [vmem] * 5, vmem, 20, 'd_...  3.91 us
    all_to_all x1, starting transfers between devices, shards(): d = lax.all_to_all(d, 'dp', 0, 0, tiled=True)  3.79 us
  transfers between devices with their start and end apart: 27, of which 15 were waited for; matrix products, arithmetic and copies ran while one was open for 1% of the time, Pallas kernels for 15%

profile of v13, /device:TPU:0, one launch (start us, length us, event | category | flops | bytes accessed | tf_op | source)
XLA Modules:
  0.0 177.9 jit_solution(3370273517768196692)
XLA Ops:
  0.7 1.8 %bitcast_convert_fusion.rest_0_.weights_ref = bf16[2048,256]{1,0:T(8,128)(2,1)S(1)} fusion(f32[1,2048,256]{2,1,0:T(8,128)} %param.9), kind=kLoop, calls=%fused_computation.23 | loop fusion | flops 524288 | bytes 3145728 | tf_op jit(solution)/shard_map/convert_element_type | solution.py:281
  2.5 3.0 %collective-permute-start.13 = (bf16[2048,256]{1,0:T(8,128)(2,1)S(1)}, bf16[2048,256]{1,0:T(8,128)(2,1)}, u32[]{:S(2)}, u32[]{:S(2)}) collective-permute-start(bf16[2048,256]{1,0:T(8,128)(2,1)S(1)} %bitcast_convert_fusion.rest_0_.weights_ref), channel_id=1, source_target_pairs={{0,2},{1,3},{2,0},{3,1},{4,6},{5,7},{6,4},{7,5},{8,10},{9,11},{10,... | collective-permute-start | bytes 3145736 | tf_op jit(solution)/shard_map/ppermute | solution.py:29
  5.5 2.6 %collective-permute-start.1 = (bf16[2,256,256]{2,1,0:T(8,128)(2,1)}, bf16[2,256,256]{2,1,0:T(8,128)(2,1)S(1)}, u32[]{:S(2)}, u32[]{:S(2)}) collective-permute-start(bf16[2,256,256]{2,1,0:T(8,128)(2,1)} %bitcast.2.refs_0_), channel_id=1, source_target_pairs={{0,8},{4,12},{8,0},{12,4},{1,9},{5,13},{9,1},{13,5},{2,10},{6,14},... | collective-permute-start | bytes 786440 | tf_op jit(solution)/shard_map/ppermute | solution.py:29
  8.1 1.6 collective-permute-start
  9.8 10.4 %collective-permute-done.1.refs_2_.mark_ref = bf16[2,256,256]{2,1,0:T(8,128)(2,1)S(1)} collective-permute-done((bf16[2,256,256]{2,1,0:T(8,128)(2,1)}, bf16[2,256,256]{2,1,0:T(8,128)(2,1)S(1)}, u32[]{:S(2)}, u32[]{:S(2)}) %collective-permute-start.1) | collective-permute-done | bytes 262176 | tf_op jit(solution)/shard_map/ppermute | solution.py:29
  20.4 2.9 %norm.1 = (bf16[128,2048]{1,0:T(8,128)(2,1)S(1)}, bf16[128,2048]{1,0:T(8,128)(2,1)}, bf16[128,2048]{1,0:T(8,128)(2,1)S(1)}, bf16[128,2048]{1,0:T(8,128)(2,1)S(1)}) custom-call(bf16[2,256,256]{2,1,0:T(8,128)(2,1)S(1)} %collective-permute-done.1.refs_2_.mark_ref, bf16[2,256,256]{2,1,0:T(8,128)(2,1)} %collective-permute-done.refs_1_.other_ref, ...), custom_call_target="tpu_custom_call" | custom-call | flops 1000 | bytes 1000 | tf_op jit(solution)/shard_map/norm/pallas_call | solution.py:288
  23.8 3.2 %collective-permute-start.8 = (bf16[128,2048]{1,0:T(8,128)(2,1)S(1)}, bf16[128,2048]{1,0:T(8,128)(2,1)}, u32[]{:S(2)}, u32[]{:S(2)}) collective-permute-start(bf16[128,2048]{1,0:T(8,128)(2,1)S(1)} %get-tuple-element.27), channel_id=1, source_target_pairs={{0,12},{4,8},{8,4},{12,0},{1,13},{5,9},{9,5},{13,1},{2,14},{6,10},... | collective-permute-start | bytes 1572872 | tf_op jit(solution)/shard_map/ppermute | solution.py:29
  26.9 2.7 %collective-permute-done.13.rest_2_ = bf16[2048,256]{1,0:T(8,128)(2,1)} collective-permute-done((bf16[2048,256]{1,0:T(8,128)(2,1)S(1)}, bf16[2048,256]{1,0:T(8,128)(2,1)}, u32[]{:S(2)}, u32[]{:S(2)}) %collective-permute-start.13) | collective-permute-done | bytes 1048608 | tf_op jit(solution)/shard_map/ppermute | solution.py:29
  29.6 10.3 %collective-permute-done.3.refs_1_ = bf16[128,2048]{1,0:T(8,128)(2,1)S(1)} collective-permute-done((bf16[128,2048]{1,0:T(8,128)(2,1)S(1)}, bf16[128,2048]{1,0:T(8,128)(2,1)S(1)}, u32[]{:S(2)}, u32[]{:S(2)}) %collective-permute-start.3) | collective-permute-done | bytes 524320 | tf_op jit(solution)/shard_map/ppermute | solution.py:29
  41.0 4.6 %collective-permute-done.2.refs_3_ = bf16[2,256,256]{2,1,0:T(8,128)(2,1)S(1)} collective-permute-done((bf16[2,256,256]{2,1,0:T(8,128)(2,1)S(1)}, bf16[2,256,256]{2,1,0:T(8,128)(2,1)S(1)}, u32[]{:S(2)}, u32[]{:S(2)}) %collective-permute-start.2) | collective-permute-done | bytes 262176 | tf_op jit(solution)/shard_map/ppermute | solution.py:29
  45.6 1.3 collective-permute-start.5
  46.9 2.4 %arrange.1 = (bf16[4,512,256]{2,1,0:T(8,128)(2,1)}, bf16[256,2048]{1,0:T(8,128)(2,1)S(1)}) custom-call(s32[2]{0:T(128)S(1)} %pad_add_fusion.where_ref, bf16[2,256,256]{2,1,0:T(8,128)(2,1)} %bitcast.2.refs_0_, bf16[2,256,256]{2,1,0:T(8,128)(2,1)} %collective-permute-done.refs_1_.other_ref, bf16[2,256,256]{2,1,0:T(8,128)(2,1)S(1)} %collective-permute-done.1.refs_2_.mark_ref, ...), custom_call_target="tpu_custom_call" | custom-call | flops 1000 | bytes 1000 | tf_op jit(solution)/shard_map/arrange/pallas_call | solution.py:299
  51.1 3.5 %all-to-all-start = ((bf16[4,512,256]{2,1,0:T(8,128)(2,1)}), bf16[4,512,256]{2,1,0:T(8,128)(2,1)S(1)}, u32[]{:S(2)}, u32[]{:S(2)}) async-start(bf16[4,512,256]{2,1,0:T(8,128)(2,1)} %after.5), calls=%async_computation | async-start | bytes 2097152 | tf_op jit(solution)/shard_map/all_to_all | solution.py:310
  55.6 5.1 %collective-permute-done.5.refs_0_ = bf16[128,2048]{1,0:T(8,128)(2,1)} collective-permute-done((bf16[128,2048]{1,0:T(8,128)(2,1)}, bf16[128,2048]{1,0:T(8,128)(2,1)}, u32[]{:S(2)}, u32[]{:S(2)}) %collective-permute-start.5) | collective-permute-done | bytes 524320 | tf_op jit(solution)/shard_map/ppermute | solution.py:29
  60.6 1.5 collective-permute-start.9
  62.7 6.8 %all-to-all-done.cot_ref = bf16[4,512,256]{2,1,0:T(8,128)(2,1)S(1)} async-done(((bf16[4,512,256]{2,1,0:T(8,128)(2,1)}), bf16[4,512,256]{2,1,0:T(8,128)(2,1)S(1)}, u32[]{:S(2)}, u32[]{:S(2)}) %all-to-all-start) | async-done | bytes 1048608 | tf_op jit(solution)/shard_map/all_to_all | solution.py:310
  71.7 3.9 %d_normed.1.refs_1_ = bf16[4,128,2048]{2,1,0:T(8,128)(2,1)S(1)} custom-call(s32[2]{0:T(128)S(1)} %pad_add_fusion.where_ref, bf16[4,512,256]{2,1,0:T(8,128)(2,1)S(1)} %copy-done.5, bf16[2048,256]{1,0:T(8,128)(2,1)S(1)} %bitcast_convert_fusion.rest_0_.weights_ref, bf16[2048,256]{1,0:T(8,128)(2,1)S(1)} %collective-permute-done.12.rest_1_, ...), custom_call_target="tpu_custom_call" | custom-call | flops 1000 | bytes 1000 | tf_op jit(solution)/shard_map/d_normed/pallas_call | solution.py:326
  75.6 5.8 %collective-permute-done.11.refs_0_ = bf16[128,2048]{1,0:T(8,128)(2,1)} collective-permute-done((bf16[128,2048]{1,0:T(8,128)(2,1)}, bf16[128,2048]{1,0:T(8,128)(2,1)}, u32[]{:S(2)}, u32[]{:S(2)}) %collective-permute-start.11) | collective-permute-done | bytes 524320 | tf_op jit(solution)/shard_map/ppermute | solution.py:29
  81.4 1.3 copy-done
  82.7 3.8 %all-to-all-start.1 = ((bf16[4,128,2048]{2,1,0:T(8,128)(2,1)}), bf16[4,128,2048]{2,1,0:T(8,128)(2,1)S(1)}, u32[]{:S(2)}, u32[]{:S(2)}) async-start(bf16[4,128,2048]{2,1,0:T(8,128)(2,1)} %copy-done), calls=%async_computation.1 | async-start | bytes 4194304 | tf_op jit(solution)/shard_map/all_to_all | solution.py:335
  86.5 1.4 pack.5.rest_4_
  88.0 3.6 %collective-permute-done.6.refs_1_ = bf16[128,2048]{1,0:T(8,128)(2,1)} collective-permute-done((bf16[128,2048]{1,0:T(8,128)(2,1)}, bf16[128,2048]{1,0:T(8,128)(2,1)}, u32[]{:S(2)}, u32[]{:S(2)}) %collective-permute-start.6) | collective-permute-done | bytes 524320 | tf_op jit(solution)/shard_map/ppermute | solution.py:29
  93.5 14.0 %collective-permute-done.15.rest_7_ = bf16[128,2048]{1,0:T(8,128)(2,1)S(1)} collective-permute-done((bf16[128,2048]{1,0:T(8,128)(2,1)}, bf16[128,2048]{1,0:T(8,128)(2,1)S(1)}, u32[]{:S(2)}, u32[]{:S(2)}) %collective-permute-start.15) | collective-permute-done | bytes 524320 | tf_op jit(solution)/shard_map/ppermute | solution.py:29
  107.5 1.9 %collective-permute-done.17.rest_9_ = bf16[128,2048]{1,0:T(8,128)(2,1)S(1)} collective-permute-done((bf16[128,2048]{1,0:T(8,128)(2,1)S(1)}, bf16[128,2048]{1,0:T(8,128)(2,1)S(1)}, u32[]{:S(2)}, u32[]{:S(2)}) %collective-permute-start.17) | collective-permute-done | bytes 524320 | tf_op jit(solution)/shard_map/ppermute | solution.py:29
  109.4 1.6 copy-done.7
  112.2 8.8 %update.1 = (f32[2048,256]{1,0:T(8,128)}, bf16[512,256]{1,0:T(8,128)(2,1)S(1)}, bf16[512,256]{1,0:T(8,128)(2,1)S(1)}, bf16[512,256]{1,0:T(8,128)(2,1)S(1)}, bf16[512,256]{1,0:T(8,128)(2,1)S(1)}) custom-call(bf16[256,2048]{1,0:T(8,128)(2,1)S(1)} %copy-done.11, f32[2048,256]{1,0:T(8,128)S(1)} %bitcast.36, f32[2048,256]{1,0:T(8,128)S(1)} %bitcast.39, ...), custom_call_target="tpu_custom_call" | custom-call | flops 1000 | bytes 1000 | tf_op jit(solution)/shard_map/update/pallas_call | solution.py:345
  123.1 17.2 %collective-permute-done.18.mark_ref = bf16[512,256]{1,0:T(8,128)(2,1)S(1)} collective-permute-done((bf16[512,256]{1,0:T(8,128)(2,1)S(1)}, bf16[512,256]{1,0:T(8,128)(2,1)S(1)}, u32[]{:S(2)}, u32[]{:S(2)}) %collective-permute-start.18) | collective-permute-done | bytes 262176 | tf_op jit(solution)/shard_map/ppermute | solution.py:29
  140.2 4.6 %project.1 = (bf16[512,256]{1,0:T(8,128)(2,1)S(1)}, bf16[512,256]{1,0:T(8,128)(2,1)S(1)}, bf16[512,256]{1,0:T(8,128)(2,1)S(1)}, bf16[512,256]{1,0:T(8,128)(2,1)}) custom-call(bf16[512,256]{1,0:T(8,128)(2,1)S(1)} %collective-permute-done.18.mark_ref, bf16[2048,256]{1,0:T(8,128)(2,1)S(1)} %bitcast_convert_fusion.rest_0_.weights_ref, ...), custom_call_target="tpu_custom_call" | custom-call | flops 1000 | bytes 1000 | tf_op jit(solution)/shard_map/project/pallas_call | solution.py:373
  148.1 13.7 %collective-permute-done.20 = bf16[512,256]{1,0:T(8,128)(2,1)S(1)} collective-permute-done((bf16[512,256]{1,0:T(8,128)(2,1)}, bf16[512,256]{1,0:T(8,128)(2,1)S(1)}, u32[]{:S(2)}, u32[]{:S(2)}) %collective-permute-start.20) | collective-permute-done | bytes 262176 | tf_op jit(solution)/shard_map/ppermute | solution.py:29
  164.1 1.8 collective-permute-start.24
  166.9 5.1 %collective-permute-done.21 = bf16[512,256]{1,0:T(8,128)(2,1)S(1)} collective-permute-done((bf16[512,256]{1,0:T(8,128)(2,1)S(1)}, bf16[512,256]{1,0:T(8,128)(2,1)S(1)}, u32[]{:S(2)}, u32[]{:S(2)}) %collective-permute-start.21) | collective-permute-done | bytes 262176 | tf_op jit(solution)/shard_map/ppermute | solution.py:29
  173.9 3.3 %grad_in.1 = bf16[128,8192]{1,0:T(8,128)(2,1)} custom-call(bf16[128,8192]{1,0:T(8,128)(2,1)S(1)} %bitcast.38, f32[1,8192]{1,0:T(1,128)S(1)} %copy-done.16, bf16[4,128,2048]{2,1,0:T(8,128)(2,1)S(1)} %after.7.d_ref), custom_call_target="tpu_custom_call" | custom-call | flops 1000 | bytes 1000 | tf_op jit(solution)/shard_map/grad_in/pallas_call | solution.py:384
  (82 shorter events, 21.7 us)
Async XLA Ops:
  0.6 19.8 %copy-start.2 = (bf16[1,2,64,8192]{3,2,1,0:T(8,128)(2,1)S(1)}, bf16[1,2,64,8192]{3,2,1,0:T(8,128)(2,1)}, u32[]{:S(2)}) copy-start(bf16[1,2,64,8192]{3,2,1,0:T(8,128)(2,1)} %param.6) | copy-start | bytes 6291460
  2.5 27.1 %collective-permute-start.13 = (bf16[2048,256]{1,0:T(8,128)(2,1)S(1)}, bf16[2048,256]{1,0:T(8,128)(2,1)}, u32[]{:S(2)}, u32[]{:S(2)}) collective-permute-start(bf16[2048,256]{1,0:T(8,128)(2,1)S(1)} %bitcast_convert_fusion.rest_0_.weights_ref), channel_id=1, source_target_pairs={{0,2},{1,3},{2,0},{3,1},{4,6},{5,7},{6,4},{7,5},{8,10},{9,11},{10,... | collective-permute-start | bytes 3145736 | tf_op jit(solution)/shard_map/ppermute | solution.py:29
  5.5 14.6 %collective-permute-start.1 = (bf16[2,256,256]{2,1,0:T(8,128)(2,1)}, bf16[2,256,256]{2,1,0:T(8,128)(2,1)S(1)}, u32[]{:S(2)}, u32[]{:S(2)}) collective-permute-start(bf16[2,256,256]{2,1,0:T(8,128)(2,1)} %bitcast.2.refs_0_), channel_id=1, source_target_pairs={{0,8},{4,12},{8,0},{12,4},{1,9},{5,13},{9,1},{13,5},{2,10},{6,14},... | collective-permute-start | bytes 786440 | tf_op jit(solution)/shard_map/ppermute | solution.py:29
  8.1 12.3 %collective-permute-start = (bf16[2,256,256]{2,1,0:T(8,128)(2,1)}, bf16[2,256,256]{2,1,0:T(8,128)(2,1)}, u32[]{:S(2)}, u32[]{:S(2)}) collective-permute-start(bf16[2,256,256]{2,1,0:T(8,128)(2,1)} %bitcast.2.refs_0_), channel_id=1, source_target_pairs={{0,4},{4,0},{8,12},{12,8},{1,5},{5,1},{9,13},{13,9},{2,6},{6,2},{1... | collective-permute-start | bytes 786440 | tf_op jit(solution)/shard_map/ppermute | solution.py:29
  23.3 16.6 %collective-permute-start.3 = (bf16[128,2048]{1,0:T(8,128)(2,1)S(1)}, bf16[128,2048]{1,0:T(8,128)(2,1)S(1)}, u32[]{:S(2)}, u32[]{:S(2)}) collective-permute-start(bf16[128,2048]{1,0:T(8,128)(2,1)S(1)} %get-tuple-element.24.refs_0_), channel_id=1, source_target_pairs={{0,2},{1,3},{2,0},{3,1},{4,6},{5,7},{6,4},{7,5},{8,10},{9,11},{10,... | collective-permute-start | bytes 1572872 | tf_op jit(solution)/shard_map/ppermute | solution.py:29
  23.8 38.4 %collective-permute-start.12 = (bf16[2048,256]{1,0:T(8,128)(2,1)S(1)}, bf16[2048,256]{1,0:T(8,128)(2,1)S(1)}, u32[]{:S(2)}, u32[]{:S(2)}) collective-permute-start(bf16[2048,256]{1,0:T(8,128)(2,1)S(1)} %bitcast_convert_fusion.rest_0_.weights_ref), channel_id=1, source_target_pairs={{0,1},{1,0},{2,3},{3,2},{4,5},{5,4},{6,7},{7,6},{8,9},{9,8},{10,11... | collective-permute-start | bytes 3145736 | tf_op jit(solution)/shard_map/ppermute | solution.py:29
  23.8 25.5 %collective-permute-start.8 = (bf16[128,2048]{1,0:T(8,128)(2,1)S(1)}, bf16[128,2048]{1,0:T(8,128)(2,1)}, u32[]{:S(2)}, u32[]{:S(2)}) collective-permute-start(bf16[128,2048]{1,0:T(8,128)(2,1)S(1)} %get-tuple-element.27), channel_id=1, source_target_pairs={{0,12},{4,8},{8,4},{12,0},{1,13},{5,9},{9,5},{13,1},{2,14},{6,10},... | collective-permute-start | bytes 1572872 | tf_op jit(solution)/shard_map/ppermute | solution.py:29
  26.9 18.7 %collective-permute-start.2 = (bf16[2,256,256]{2,1,0:T(8,128)(2,1)S(1)}, bf16[2,256,256]{2,1,0:T(8,128)(2,1)S(1)}, u32[]{:S(2)}, u32[]{:S(2)}) collective-permute-start(bf16[2,256,256]{2,1,0:T(8,128)(2,1)S(1)} %collective-permute-done.1.refs_2_.mark_ref), channel_id=1, source_target_pairs={{0,4},{4,0},{8,12},{12,8},{1,5},{5,1},{9,13},{13,9},{2,6},{6,2},{1... | collective-permute-start | bytes 786440 | tf_op jit(solution)/shard_map/ppermute | solution.py:29
  29.6 40.8 %collective-permute-start.14 = (bf16[2048,256]{1,0:T(8,128)(2,1)}, bf16[2048,256]{1,0:T(8,128)(2,1)}, u32[]{:S(2)}, u32[]{:S(2)}) collective-permute-start(bf16[2048,256]{1,0:T(8,128)(2,1)} %collective-permute-done.13.rest_2_), channel_id=1, source_target_pairs={{0,1},{1,0},{2,3},{3,2},{4,5},{5,4},{6,7},{7,6},{8,9},{9,8},{10,11... | collective-permute-start | bytes 3145736 | tf_op jit(solution)/shard_map/ppermute | solution.py:29
  40.9 40.4 %collective-permute-start.4 = (bf16[256,2048]{1,0:T(8,128)(2,1)}, bf16[256,2048]{1,0:T(8,128)(2,1)}, u32[]{:S(2)}, u32[]{:S(2)}) collective-permute-start(bf16[256,2048]{1,0:T(8,128)(2,1)} %pack.3.rest_0_), channel_id=1, source_target_pairs={{0,1},{1,0},{2,3},{3,2},{4,5},{5,4},{6,7},{7,6},{8,9},{9,8},{10,11... | collective-permute-start | bytes 3145736 | tf_op jit(solution)/shard_map/ppermute | solution.py:29
  45.6 15.0 %collective-permute-start.5 = (bf16[128,2048]{1,0:T(8,128)(2,1)}, bf16[128,2048]{1,0:T(8,128)(2,1)}, u32[]{:S(2)}, u32[]{:S(2)}) collective-permute-start(bf16[128,2048]{1,0:T(8,128)(2,1)} %get-tuple-element.25), channel_id=1, source_target_pairs={{0,4},{4,0},{8,12},{12,8},{1,5},{5,1},{9,13},{13,9},{2,6},{6,2},{1... | collective-permute-start | bytes 1572872 | tf_op jit(solution)/shard_map/ppermute | solution.py:29
  51.1 18.4 %all-to-all-start = ((bf16[4,512,256]{2,1,0:T(8,128)(2,1)}), bf16[4,512,256]{2,1,0:T(8,128)(2,1)S(1)}, u32[]{:S(2)}, u32[]{:S(2)}) async-start(bf16[4,512,256]{2,1,0:T(8,128)(2,1)} %after.5), calls=%async_computation | async-start | bytes 2097152 | tf_op jit(solution)/shard_map/all_to_all | solution.py:310
  54.6 26.8 %collective-permute-start.11 = (bf16[128,2048]{1,0:T(8,128)(2,1)}, bf16[128,2048]{1,0:T(8,128)(2,1)}, u32[]{:S(2)}, u32[]{:S(2)}) collective-permute-start(bf16[128,2048]{1,0:T(8,128)(2,1)} %copy-done.8), channel_id=1, source_target_pairs={{0,8},{4,12},{8,0},{12,4},{1,9},{5,13},{9,1},{13,5},{2,10},{6,14},... | collective-permute-start | bytes 1572872 | tf_op jit(solution)/shard_map/ppermute | solution.py:29
  60.6 25.9 %collective-permute-start.9 = (bf16[128,2048]{1,0:T(8,128)(2,1)}, bf16[128,2048]{1,0:T(8,128)(2,1)}, u32[]{:S(2)}, u32[]{:S(2)}) collective-permute-start(bf16[128,2048]{1,0:T(8,128)(2,1)} %get-tuple-element.28.refs_0_), channel_id=1, source_target_pairs={{0,2},{1,3},{2,0},{3,1},{4,6},{5,7},{6,4},{7,5},{8,10},{9,11},{10,... | collective-permute-start | bytes 1572872 | tf_op jit(solution)/shard_map/ppermute | solution.py:29
  62.1 29.5 %collective-permute-start.6 = (bf16[128,2048]{1,0:T(8,128)(2,1)}, bf16[128,2048]{1,0:T(8,128)(2,1)}, u32[]{:S(2)}, u32[]{:S(2)}) collective-permute-start(bf16[128,2048]{1,0:T(8,128)(2,1)} %collective-permute-done.5.refs_0_), channel_id=1, source_target_pairs={{0,2},{1,3},{2,0},{3,1},{4,6},{5,7},{6,4},{7,5},{8,10},{9,11},{10,... | collective-permute-start | bytes 1572872 | tf_op jit(solution)/shard_map/ppermute | solution.py:29
  82.7 89.5 %all-to-all-start.1 = ((bf16[4,128,2048]{2,1,0:T(8,128)(2,1)}), bf16[4,128,2048]{2,1,0:T(8,128)(2,1)S(1)}, u32[]{:S(2)}, u32[]{:S(2)}) async-start(bf16[4,128,2048]{2,1,0:T(8,128)(2,1)} %copy-done), calls=%async_computation.1 | async-start | bytes 4194304 | tf_op jit(solution)/shard_map/all_to_all | solution.py:335
  86.5 22.9 %copy-start.1 = (f32[1,2048,256]{2,1,0:T(8,128)S(1)}, f32[1,2048,256]{2,1,0:T(8,128)}, u32[]{:S(2)}) copy-start(f32[1,2048,256]{2,1,0:T(8,128)} %param.9) | copy-start | bytes 6291460
  86.5 22.9 %copy-start.6 = (f32[1,2048,256]{2,1,0:T(8,128)S(1)}, f32[1,2048,256]{2,1,0:T(8,128)}, u32[]{:S(2)}) copy-start(f32[1,2048,256]{2,1,0:T(8,128)} %param.10) | copy-start | bytes 6291460
  87.9 19.6 %collective-permute-start.10 = (bf16[256,2048]{1,0:T(8,128)(2,1)S(1)}, bf16[256,2048]{1,0:T(8,128)(2,1)S(1)}, u32[]{:S(2)}, u32[]{:S(2)}) collective-permute-start(bf16[256,2048]{1,0:T(8,128)(2,1)S(1)} %pack.5.rest_4_), channel_id=1, source_target_pairs={{0,1},{1,0},{2,3},{3,2},{4,5},{5,4},{6,7},{7,6},{8,9},{9,8},{10,11... | collective-permute-start | bytes 3145736 | tf_op jit(solution)/shard_map/ppermute | solution.py:29
  92.8 14.6 %collective-permute-start.7 = (bf16[256,2048]{1,0:T(8,128)(2,1)S(1)}, bf16[256,2048]{1,0:T(8,128)(2,1)S(1)}, u32[]{:S(2)}, u32[]{:S(2)}) collective-permute-start(bf16[256,2048]{1,0:T(8,128)(2,1)S(1)} %pack.4.rest_2_), channel_id=1, source_target_pairs={{0,1},{1,0},{2,3},{3,2},{4,5},{5,4},{6,7},{7,6},{8,9},{9,8},{10,11... | collective-permute-start | bytes 3145736 | tf_op jit(solution)/shard_map/ppermute | solution.py:29
  92.9 14.6 %collective-permute-start.15 = (bf16[128,2048]{1,0:T(8,128)(2,1)}, bf16[128,2048]{1,0:T(8,128)(2,1)S(1)}, u32[]{:S(2)}, u32[]{:S(2)}) collective-permute-start(bf16[128,2048]{1,0:T(8,128)(2,1)} %get-tuple-element.31.rest_6_), channel_id=1, source_target_pairs={{0,2},{1,3},{2,0},{3,1},{4,6},{5,7},{6,4},{7,5},{8,10},{9,11},{10,... | collective-permute-start | bytes 1572872 | tf_op jit(solution)/shard_map/ppermute | solution.py:29
  93.3 14.1 %collective-permute-start.16 = (bf16[128,2048]{1,0:T(8,128)(2,1)}, bf16[128,2048]{1,0:T(8,128)(2,1)S(1)}, u32[]{:S(2)}, u32[]{:S(2)}) collective-permute-start(bf16[128,2048]{1,0:T(8,128)(2,1)} %get-tuple-element.31.rest_6_), channel_id=1, source_target_pairs={{0,1},{1,0},{2,3},{3,2},{4,5},{5,4},{6,7},{7,6},{8,9},{9,8},{10,11... | collective-permute-start | bytes 1572872 | tf_op jit(solution)/shard_map/ppermute | solution.py:29
  107.4 1.9 %collective-permute-start.17 = (bf16[128,2048]{1,0:T(8,128)(2,1)S(1)}, bf16[128,2048]{1,0:T(8,128)(2,1)S(1)}, u32[]{:S(2)}, u32[]{:S(2)}) collective-permute-start(bf16[128,2048]{1,0:T(8,128)(2,1)S(1)} %collective-permute-done.15.rest_7_), channel_id=1, source_target_pairs={{0,1},{1,0},{2,3},{3,2},{4,5},{5,4},{6,7},{7,6},{8,9},{9,8},{10,11... | collective-permute-start | bytes 1572872 | tf_op jit(solution)/shard_map/ppermute | solution.py:29
  121.0 23.9 %copy-start.15 = (bf16[512,256]{1,0:T(8,128)(2,1)}, bf16[512,256]{1,0:T(8,128)(2,1)S(1)}, u32[]{:S(2)}) copy-start(bf16[512,256]{1,0:T(8,128)(2,1)S(1)} %get-tuple-element.38) | copy-start | bytes 786436
  121.0 19.2 %collective-permute-start.18 = (bf16[512,256]{1,0:T(8,128)(2,1)S(1)}, bf16[512,256]{1,0:T(8,128)(2,1)S(1)}, u32[]{:S(2)}, u32[]{:S(2)}) collective-permute-start(bf16[512,256]{1,0:T(8,128)(2,1)S(1)} %get-tuple-element.32), channel_id=1, source_target_pairs={{0,4},{4,0},{8,12},{12,8},{1,5},{5,1},{9,13},{13,9},{2,6},{6,2},{1... | collective-permute-start | bytes 786440 | tf_op jit(solution)/shard_map/ppermute | solution.py:29
  121.8 23.8 %collective-permute-start.22 = (bf16[512,256]{1,0:T(8,128)(2,1)S(1)}, bf16[512,256]{1,0:T(8,128)(2,1)S(1)}, u32[]{:S(2)}, u32[]{:S(2)}) collective-permute-start(bf16[512,256]{1,0:T(8,128)(2,1)S(1)} %get-tuple-element.40), channel_id=1, source_target_pairs={{0,4},{4,0},{8,12},{12,8},{1,5},{5,1},{9,13},{13,9},{2,6},{6,2},{1... | collective-permute-start | bytes 786440 | tf_op jit(solution)/shard_map/ppermute | solution.py:29
  145.6 16.2 %collective-permute-start.20 = (bf16[512,256]{1,0:T(8,128)(2,1)}, bf16[512,256]{1,0:T(8,128)(2,1)S(1)}, u32[]{:S(2)}, u32[]{:S(2)}) collective-permute-start(bf16[512,256]{1,0:T(8,128)(2,1)} %get-tuple-element.36), channel_id=1, source_target_pairs={{0,4},{4,0},{8,12},{12,8},{1,5},{5,1},{9,13},{13,9},{2,6},{6,2},{1... | collective-permute-start | bytes 786440 | tf_op jit(solution)/shard_map/ppermute | solution.py:29
  146.4 16.5 %collective-permute-start.23 = (bf16[512,256]{1,0:T(8,128)(2,1)S(1)}, bf16[512,256]{1,0:T(8,128)(2,1)}, u32[]{:S(2)}, u32[]{:S(2)}) collective-permute-start(bf16[512,256]{1,0:T(8,128)(2,1)S(1)} %add_convert_fusion.1), channel_id=1, source_target_pairs={{0,8},{4,12},{8,0},{12,4},{1,9},{5,13},{9,1},{13,5},{2,10},{6,14},... | collective-permute-start | bytes 786440 | tf_op jit(solution)/shard_map/ppermute | solution.py:29
  147.4 24.5 %copy-start.14 = (bf16[512,256]{1,0:T(8,128)(2,1)S(1)}, bf16[512,256]{1,0:T(8,128)(2,1)}, u32[]{:S(2)}) copy-start(bf16[512,256]{1,0:T(8,128)(2,1)} %copy-done.13) | copy-start | bytes 786436
  147.4 19.4 %collective-permute-start.19 = (bf16[512,256]{1,0:T(8,128)(2,1)}, bf16[512,256]{1,0:T(8,128)(2,1)S(1)}, u32[]{:S(2)}, u32[]{:S(2)}) collective-permute-start(bf16[512,256]{1,0:T(8,128)(2,1)} %copy-done.17), channel_id=1, source_target_pairs={{0,4},{4,0},{8,12},{12,8},{1,5},{5,1},{9,13},{13,9},{2,6},{6,2},{1... | collective-permute-start | bytes 786440 | tf_op jit(solution)/shard_map/ppermute | solution.py:29
  162.8 9.2 %collective-permute-start.21 = (bf16[512,256]{1,0:T(8,128)(2,1)S(1)}, bf16[512,256]{1,0:T(8,128)(2,1)S(1)}, u32[]{:S(2)}, u32[]{:S(2)}) collective-permute-start(bf16[512,256]{1,0:T(8,128)(2,1)S(1)} %add_convert_fusion.3), channel_id=1, source_target_pairs={{0,8},{4,12},{8,0},{12,4},{1,9},{5,13},{9,1},{13,5},{2,10},{6,14},... | collective-permute-start | bytes 786440 | tf_op jit(solution)/shard_map/ppermute | solution.py:29
  164.1 8.8 %collective-permute-start.24 = (bf16[1,2,256,256]{3,2,1,0:T(8,128)(2,1)S(1)}, bf16[1,2,256,256]{3,2,1,0:T(8,128)(2,1)S(1)}, u32[]{:S(2)}, u32[]{:S(2)}) collective-permute-start(bf16[1,2,256,256]{3,2,1,0:T(8,128)(2,1)S(1)} %bitcast.41), channel_id=1, source_target_pairs={{0,16},{16,0},{1,17},{17,1},{2,18},{18,2},{3,19},{19,3},{4,20},{20... | collective-permute-start | bytes 786440 | tf_op jit(solution)/shard_map/ppermute | solution.py:34
  (13 other events, 32.5 us)

commit v14 on v13

--- a/solution.py
+++ b/solution.py
@@ -73,7 +73,7 @@
     return pl.ds(pl.multiple_of(index * size, size), size)
 
 
-def norm_kernel(mark_ref, other_ref, where_ref, hidden_ref, gain_ref, *own_refs, tile):
+def norm_kernel(mark_ref, other_ref, third_ref, where_ref, hidden_ref, gain_ref, *own_refs, tile):
     z = where_ref[0]
     rows, width = hidden_ref.shape
     depth = width // len(own_refs)
@@ -259,11 +259,13 @@
     return blocks
 
 
-def scatter_sum(parts, got=None):
-    got1, got3 = got or (swap(parts[1], "dp", 1), swap(parts[3], "dp", 1))
+def scatter_sum(parts, got1, got3, *earlier):
     mine = parts[0].astype(f32) + got1.astype(f32)
     other = (parts[2].astype(f32) + got3.astype(f32)).astype(bf16)
-    return mine + swap(other, "dp", 2).astype(f32)
+    got = swap(other, "dp", 2)
+    if earlier:
+        got = after([got], *earlier)[0]
+    return mine + got.astype(f32), other
 
 
 def shards(hidden_in, norm_gain, kv_cot, master_kv, moment_m, moment_v):
@@ -288,11 +290,11 @@
     own = call(
         functools.partial(norm_kernel, tile=tile),
         [like(piece, depth)] * dp,
-        [anywhere, anywhere, smem, vmem, vmem],
+        [anywhere] * 3 + [smem, vmem, vmem],
         [vmem] * dp,
         8,
         "norm",
-    )(cot2, cot1, where, hidden, norm_gain)
+    )(cot2, cot1, w1[0], where, hidden, norm_gain)
     n1, n3 = swap(own[1], "dp", 1), swap(own[3], "dp", 3)
     w3 = [swap(w, "tensor", 1) for w in w2]
     layout = tuple((k, j) for k in (0, 1, 3, 2) for j in (0, 2, 1, 3))
@@ -368,7 +370,9 @@
         )
 
     got1, got3 = swap(parts[1], "dp", 1), swap(parts[3], "dp", 1)
-    mine = place(scatter_sum(parts, (got1, got3)).astype(bf16))
+    got1, got3 = after([got1, got3])
+    mine, _ = scatter_sum(parts, got1, got3)
+    mine = place(mine.astype(bf16))
     kv_next = from_behind(mine, "segment", -1)
     own_parts = call(
         functools.partial(project_kernel, count=count, layout=layout),
@@ -378,9 +382,8 @@
         16,
         "project",
         scratch=[all_tokens, pltpu.SemaphoreType.DMA((count,))],
-    )(got1, w0[0], *tokens)
-    kv_own = place(scatter_sum(own_parts).astype(bf16))
-    (d,) = after([d], mine, kv_own)
+    )(parts[1], w0[0], *tokens)
+    (d,) = after([d], mine)
     grad_in = call(
         functools.partial(grad_kernel, tile=tile),
         like(piece, width),
@@ -389,6 +392,9 @@
         12,
         "grad_in",
     )(hidden, norm_gain, d)
+    own_got = after([swap(own_parts[1], "dp", 1), swap(own_parts[3], "dp", 1)])
+    kv_own, _ = scatter_sum(own_parts, *own_got, grad_in[:16, :128])
+    kv_own = place(kv_own.astype(bf16))
     return (kv_own, grad_in.reshape(hidden_in.shape), master_new[None], kv_next)
 
 

time: 179 us -> 180 us (level)
  starting transfers between devices: 28.8 us -> 31.7 us
    ppermute x24, waiting for transfers between devices: 95.5 us -> 86.2 us  [swap(): return lax.ppermute(x, axis, [(i, i ^ bits) for i in range(peers)])]
    ppermute x1, waiting for transfers between devices: 0.01 us -> 6.18 us  [from_behind(): return lax.ppermute(x, axis, [(i, (i + by) % peers) for i in range(peers)])]
    ppermute x24, starting transfers between devices: 19.8 us -> 22.9 us  [swap(): return lax.ppermute(x, axis, [(i, i ^ bits) for i in range(peers)])]
    all_to_all x1, waiting for transfers between devices: 6.83 us -> 9.73 us  [shards(): mine_cot = lax.all_to_all(send, 'tensor', 0, 0, tiled=True)]
    unnamed x37 -> x35, local copies, waits for them, and re-layouts: 11.9 us -> 9.8 us
  transfers between devices with their start and end apart: 27 -> 27, of which waited for: 15 -> 17; matrix products, arithmetic and copies ran while one was open for 1% -> 1% of each run, Pallas kernels for 15% -> 17%
where the time goes in v14:
time: 180 us; the launch traced here: 179 us
  waiting for transfers between devices  102 us (57%)
  starting transfers between devices  31.7 us (18%)
  Pallas kernels  29.6 us (16%)
  local copies, waits for them, and re-layouts  11.2 us (6%)
  other arithmetic  3.41 us (2%)
    ppermute x24, waiting for transfers between devices, swap(): return lax.ppermute(x, axis, [(i, i ^ bits) for i in range(peers)])  86.2 us
    ppermute x24, starting transfers between devices, swap(): return lax.ppermute(x, axis, [(i, i ^ bits) for i in range(peers)])  22.9 us
    unnamed x35, local copies, waits for them, and re-layouts  9.8 us
    all_to_all x1, waiting for transfers between devices, shards(): mine_cot = lax.all_to_all(send, 'tensor', 0, 0, tiled=True)  9.73 us
    pallas_call x1, Pallas kernels, shards(): call(functools.partial(update_kernel, count=count, tile=step, layout=layo...  8.78 us
    ppermute x1, waiting for transfers between devices, from_behind(): return lax.ppermute(x, axis, [(i, (i + by) % peers) for i in range(peers)])  6.18 us
    pallas_call x1, Pallas kernels, shards(): call(functools.partial(project_kernel, count=count, layout=layout), part_...  4.63 us
    pallas_call x1, Pallas kernels, shards(): call(d_kernel, like(dp, piece, depth), [smem] + [vmem] * 5, vmem, 20, 'd_...  3.91 us
  transfers between devices with their start and end apart: 27, of which 17 were waited for; matrix products, arithmetic and copies ran while one was open for 1% of the time, Pallas kernels for 17%

profile of v14, /device:TPU:0, one launch (start us, length us, event | category | flops | bytes accessed | tf_op | source)
XLA Modules:
  0.0 179.0 jit_solution(10340562073221954634)
XLA Ops:
  0.7 1.8 %bitcast_convert_fusion.rest_0_.weights_ref = bf16[2048,256]{1,0:T(8,128)(2,1)S(1)} fusion(f32[1,2048,256]{2,1,0:T(8,128)} %param.9), kind=kLoop, calls=%fused_computation.23 | loop fusion | flops 524288 | bytes 3145728 | tf_op jit(solution)/shard_map/convert_element_type | solution.py:283
  3.0 2.6 %collective-permute-start.13 = (bf16[2048,256]{1,0:T(8,128)(2,1)S(1)}, bf16[2048,256]{1,0:T(8,128)(2,1)}, u32[]{:S(2)}, u32[]{:S(2)}) collective-permute-start(bf16[2048,256]{1,0:T(8,128)(2,1)S(1)} %bitcast_convert_fusion.rest_0_.weights_ref), channel_id=1, source_target_pairs={{0,2},{1,3},{2,0},{3,1},{4,6},{5,7},{6,4},{7,5},{8,10},{9,11},{10,... | collective-permute-start | bytes 3145736 | tf_op jit(solution)/shard_map/ppermute | solution.py:29
  5.6 2.6 %collective-permute-start.1 = (bf16[2,256,256]{2,1,0:T(8,128)(2,1)}, bf16[2,256,256]{2,1,0:T(8,128)(2,1)S(1)}, u32[]{:S(2)}, u32[]{:S(2)}) collective-permute-start(bf16[2,256,256]{2,1,0:T(8,128)(2,1)} %bitcast.2.refs_0_), channel_id=1, source_target_pairs={{0,8},{4,12},{8,0},{12,4},{1,9},{5,13},{9,1},{13,5},{2,10},{6,14},... | collective-permute-start | bytes 786440 | tf_op jit(solution)/shard_map/ppermute | solution.py:29
  9.9 11.0 %collective-permute-done.1.refs_2_.mark_ref = bf16[2,256,256]{2,1,0:T(8,128)(2,1)S(1)} collective-permute-done((bf16[2,256,256]{2,1,0:T(8,128)(2,1)}, bf16[2,256,256]{2,1,0:T(8,128)(2,1)S(1)}, u32[]{:S(2)}, u32[]{:S(2)}) %collective-permute-start.1) | collective-permute-done | bytes 262176 | tf_op jit(solution)/shard_map/ppermute | solution.py:29
  21.1 2.9 %norm.1 = (bf16[128,2048]{1,0:T(8,128)(2,1)S(1)}, bf16[128,2048]{1,0:T(8,128)(2,1)}, bf16[128,2048]{1,0:T(8,128)(2,1)S(1)}, bf16[128,2048]{1,0:T(8,128)(2,1)S(1)}) custom-call(bf16[2,256,256]{2,1,0:T(8,128)(2,1)S(1)} %collective-permute-done.1.refs_2_.mark_ref, bf16[2,256,256]{2,1,0:T(8,128)(2,1)} %collective-permute-done.refs_1_.other_ref, ...), custom_call_target="tpu_custom_call" | custom-call | flops 1000 | bytes 1000 | tf_op jit(solution)/shard_map/norm/pallas_call | solution.py:290
  24.5 3.2 %collective-permute-start.9 = (bf16[128,2048]{1,0:T(8,128)(2,1)S(1)}, bf16[128,2048]{1,0:T(8,128)(2,1)}, u32[]{:S(2)}, u32[]{:S(2)}) collective-permute-start(bf16[128,2048]{1,0:T(8,128)(2,1)S(1)} %get-tuple-element.31), channel_id=1, source_target_pairs={{0,12},{4,8},{8,4},{12,0},{1,13},{5,9},{9,5},{13,1},{2,14},{6,10},... | collective-permute-start | bytes 1572872 | tf_op jit(solution)/shard_map/ppermute | solution.py:29
  27.6 2.1 %collective-permute-done.13.rest_2_ = bf16[2048,256]{1,0:T(8,128)(2,1)} collective-permute-done((bf16[2048,256]{1,0:T(8,128)(2,1)S(1)}, bf16[2048,256]{1,0:T(8,128)(2,1)}, u32[]{:S(2)}, u32[]{:S(2)}) %collective-permute-start.13) | collective-permute-done | bytes 1048608 | tf_op jit(solution)/shard_map/ppermute | solution.py:29
  29.7 10.9 %collective-permute-done.4.refs_1_ = bf16[128,2048]{1,0:T(8,128)(2,1)S(1)} collective-permute-done((bf16[128,2048]{1,0:T(8,128)(2,1)S(1)}, bf16[128,2048]{1,0:T(8,128)(2,1)S(1)}, u32[]{:S(2)}, u32[]{:S(2)}) %collective-permute-start.4) | collective-permute-done | bytes 524320 | tf_op jit(solution)/shard_map/ppermute | solution.py:29
  41.7 1.9 %collective-permute-start.6 = (bf16[128,2048]{1,0:T(8,128)(2,1)}, bf16[128,2048]{1,0:T(8,128)(2,1)}, u32[]{:S(2)}, u32[]{:S(2)}) collective-permute-start(bf16[128,2048]{1,0:T(8,128)(2,1)} %get-tuple-element.29), channel_id=1, source_target_pairs={{0,4},{4,0},{8,12},{12,8},{1,5},{5,1},{9,13},{13,9},{2,6},{6,2},{1... | collective-permute-start | bytes 1572872 | tf_op jit(solution)/shard_map/ppermute | solution.py:29
  43.6 1.7 collective-permute-done.2.refs_3_
  45.3 2.4 %arrange.1 = (bf16[4,512,256]{2,1,0:T(8,128)(2,1)}, bf16[256,2048]{1,0:T(8,128)(2,1)S(1)}) custom-call(s32[2]{0:T(128)S(1)} %pad_add_fusion.where_ref, bf16[2,256,256]{2,1,0:T(8,128)(2,1)} %bitcast.2.refs_0_, bf16[2,256,256]{2,1,0:T(8,128)(2,1)} %collective-permute-done.refs_1_.other_ref, bf16[2,256,256]{2,1,0:T(8,128)(2,1)S(1)} %collective-permute-done.1.refs_2_.mark_ref, ...), custom_call_target="tpu_custom_call" | custom-call | flops 1000 | bytes 1000 | tf_op jit(solution)/shard_map/arrange/pallas_call | solution.py:301
  49.4 3.5 %all-to-all-start = ((bf16[4,512,256]{2,1,0:T(8,128)(2,1)}), bf16[4,512,256]{2,1,0:T(8,128)(2,1)S(1)}, u32[]{:S(2)}, u32[]{:S(2)}) async-start(bf16[4,512,256]{2,1,0:T(8,128)(2,1)} %after.8), calls=%async_computation | async-start | bytes 2097152 | tf_op jit(solution)/shard_map/all_to_all | solution.py:312
  54.5 1.9 %collective-permute-start.10 = (bf16[128,2048]{1,0:T(8,128)(2,1)}, bf16[128,2048]{1,0:T(8,128)(2,1)}, u32[]{:S(2)}, u32[]{:S(2)}) collective-permute-start(bf16[128,2048]{1,0:T(8,128)(2,1)} %get-tuple-element.32.refs_0_), channel_id=1, source_target_pairs={{0,2},{1,3},{2,0},{3,1},{4,6},{5,7},{6,4},{7,5},{8,10},{9,11},{10,... | collective-permute-start | bytes 1572872 | tf_op jit(solution)/shard_map/ppermute | solution.py:29
  58.1 9.7 %all-to-all-done.cot_ref = bf16[4,512,256]{2,1,0:T(8,128)(2,1)S(1)} async-done(((bf16[4,512,256]{2,1,0:T(8,128)(2,1)}), bf16[4,512,256]{2,1,0:T(8,128)(2,1)S(1)}, u32[]{:S(2)}, u32[]{:S(2)}) %all-to-all-start) | async-done | bytes 1048608 | tf_op jit(solution)/shard_map/all_to_all | solution.py:312
  70.1 3.9 %d_normed.1.refs_1_ = bf16[4,128,2048]{2,1,0:T(8,128)(2,1)S(1)} custom-call(s32[2]{0:T(128)S(1)} %pad_add_fusion.where_ref, bf16[4,512,256]{2,1,0:T(8,128)(2,1)S(1)} %copy-done.5, bf16[2048,256]{1,0:T(8,128)(2,1)S(1)} %bitcast_convert_fusion.rest_0_.weights_ref, bf16[2048,256]{1,0:T(8,128)(2,1)} %collective-permute-done.3.third_ref.rest_1_, ...), custom_call_target="tpu_custom_call" | custom-call | flops 1000 | bytes 1000 | tf_op jit(solution)/shard_map/d_normed/pallas_call | solution.py:328
  74.0 5.8 %collective-permute-done.12.refs_0_ = bf16[128,2048]{1,0:T(8,128)(2,1)} collective-permute-done((bf16[128,2048]{1,0:T(8,128)(2,1)}, bf16[128,2048]{1,0:T(8,128)(2,1)}, u32[]{:S(2)}, u32[]{:S(2)}) %collective-permute-start.12) | collective-permute-done | bytes 524320 | tf_op jit(solution)/shard_map/ppermute | solution.py:29
  81.1 3.8 %all-to-all-start.1 = ((bf16[4,128,2048]{2,1,0:T(8,128)(2,1)}), bf16[4,128,2048]{2,1,0:T(8,128)(2,1)S(1)}, u32[]{:S(2)}, u32[]{:S(2)}) async-start(bf16[4,128,2048]{2,1,0:T(8,128)(2,1)} %copy-done), calls=%async_computation.1 | async-start | bytes 4194304 | tf_op jit(solution)/shard_map/all_to_all | solution.py:337
  86.3 3.6 %collective-permute-done.7.refs_1_ = bf16[128,2048]{1,0:T(8,128)(2,1)} collective-permute-done((bf16[128,2048]{1,0:T(8,128)(2,1)}, bf16[128,2048]{1,0:T(8,128)(2,1)}, u32[]{:S(2)}, u32[]{:S(2)}) %collective-permute-start.7) | collective-permute-done | bytes 524320 | tf_op jit(solution)/shard_map/ppermute | solution.py:29
  91.9 14.0 %collective-permute-done.15.rest_7_ = bf16[128,2048]{1,0:T(8,128)(2,1)S(1)} collective-permute-done((bf16[128,2048]{1,0:T(8,128)(2,1)}, bf16[128,2048]{1,0:T(8,128)(2,1)S(1)}, u32[]{:S(2)}, u32[]{:S(2)}) %collective-permute-start.15) | collective-permute-done | bytes 524320 | tf_op jit(solution)/shard_map/ppermute | solution.py:29
  105.8 1.9 %collective-permute-done.17.rest_9_ = bf16[128,2048]{1,0:T(8,128)(2,1)S(1)} collective-permute-done((bf16[128,2048]{1,0:T(8,128)(2,1)S(1)}, bf16[128,2048]{1,0:T(8,128)(2,1)S(1)}, u32[]{:S(2)}, u32[]{:S(2)}) %collective-permute-start.17) | collective-permute-done | bytes 524320 | tf_op jit(solution)/shard_map/ppermute | solution.py:29
  110.5 8.8 %update.1 = (f32[2048,256]{1,0:T(8,128)}, bf16[512,256]{1,0:T(8,128)(2,1)S(1)}, bf16[512,256]{1,0:T(8,128)(2,1)S(1)}, bf16[512,256]{1,0:T(8,128)(2,1)S(1)}, bf16[512,256]{1,0:T(8,128)(2,1)S(1)}) custom-call(bf16[256,2048]{1,0:T(8,128)(2,1)S(1)} %copy-done.10, f32[2048,256]{1,0:T(8,128)S(1)} %bitcast.20, f32[2048,256]{1,0:T(8,128)S(1)} %bitcast.23, ...), custom_call_target="tpu_custom_call" | custom-call | flops 1000 | bytes 1000 | tf_op jit(solution)/shard_map/update/pallas_call | solution.py:347
  119.3 1.7 collective-permute-start.22
  121.4 4.6 %project.1 = (bf16[512,256]{1,0:T(8,128)(2,1)S(1)}, bf16[512,256]{1,0:T(8,128)(2,1)}, bf16[512,256]{1,0:T(8,128)(2,1)S(1)}, bf16[512,256]{1,0:T(8,128)(2,1)}) custom-call(bf16[512,256]{1,0:T(8,128)(2,1)S(1)} %get-tuple-element.36.mark_ref, bf16[2048,256]{1,0:T(8,128)(2,1)S(1)} %bitcast_convert_fusion.rest_0_.weights_ref, bf16[256,2048]{1,0:T(8,128)(2,1)} %pack.3.rest_0_, ...), custom_call_target="tpu_custom_call" | custom-call | flops 1000 | bytes 1000 | tf_op jit(solution)/shard_map/project/pallas_call | solution.py:377
  126.1 1.7 collective-permute-start.18
  128.2 10.4 %collective-permute-done.22.refs_1_ = bf16[512,256]{1,0:T(8,128)(2,1)S(1)} collective-permute-done((bf16[512,256]{1,0:T(8,128)(2,1)S(1)}, bf16[512,256]{1,0:T(8,128)(2,1)S(1)}, u32[]{:S(2)}, u32[]{:S(2)}) %collective-permute-start.22) | collective-permute-done | bytes 262176 | tf_op jit(solution)/shard_map/ppermute | solution.py:29
  138.6 5.6 %collective-permute-done.21.refs_0_ = bf16[512,256]{1,0:T(8,128)(2,1)S(1)} collective-permute-done((bf16[512,256]{1,0:T(8,128)(2,1)S(1)}, bf16[512,256]{1,0:T(8,128)(2,1)S(1)}, u32[]{:S(2)}, u32[]{:S(2)}) %collective-permute-start.21) | collective-permute-done | bytes 262176 | tf_op jit(solution)/shard_map/ppermute | solution.py:29
  144.4 5.5 %collective-permute-done.18.refs_0_ = bf16[512,256]{1,0:T(8,128)(2,1)S(1)} collective-permute-done((bf16[512,256]{1,0:T(8,128)(2,1)}, bf16[512,256]{1,0:T(8,128)(2,1)S(1)}, u32[]{:S(2)}, u32[]{:S(2)}) %collective-permute-start.18) | collective-permute-done | bytes 262176 | tf_op jit(solution)/shard_map/ppermute | solution.py:29
  149.9 10.5 %collective-permute-done.19.refs_1_ = bf16[512,256]{1,0:T(8,128)(2,1)S(1)} collective-permute-done((bf16[512,256]{1,0:T(8,128)(2,1)}, bf16[512,256]{1,0:T(8,128)(2,1)S(1)}, u32[]{:S(2)}, u32[]{:S(2)}) %collective-permute-start.19) | collective-permute-done | bytes 262176 | tf_op jit(solution)/shard_map/ppermute | solution.py:29
  163.3 6.2 %collective-permute-done.24 = bf16[1,2,256,256]{3,2,1,0:T(8,128)(2,1)} collective-permute-done((bf16[1,2,256,256]{3,2,1,0:T(8,128)(2,1)S(1)}, bf16[1,2,256,256]{3,2,1,0:T(8,128)(2,1)}, u32[]{:S(2)}, u32[]{:S(2)}) %collective-permute-start.24) | collective-permute-done | bytes 262176 | tf_op jit(solution)/shard_map/ppermute | solution.py:34
  169.5 3.3 %grad_in.1 = bf16[128,8192]{1,0:T(8,128)(2,1)} custom-call(bf16[128,8192]{1,0:T(8,128)(2,1)S(1)} %bitcast.22, f32[1,8192]{1,0:T(1,128)S(1)} %copy-done.16, bf16[4,128,2048]{2,1,0:T(8,128)(2,1)S(1)} %after.12.d_ref), custom_call_target="tpu_custom_call" | custom-call | flops 1000 | bytes 1000 | tf_op jit(solution)/shard_map/grad_in/pallas_call | solution.py:387
  173.5 2.9 %collective-permute-done.20.refs_0_ = bf16[512,256]{1,0:T(8,128)(2,1)S(1)} collective-permute-done((bf16[512,256]{1,0:T(8,128)(2,1)S(1)}, bf16[512,256]{1,0:T(8,128)(2,1)S(1)}, u32[]{:S(2)}, u32[]{:S(2)}) %collective-permute-start.20) | collective-permute-done | bytes 262176 | tf_op jit(solution)/shard_map/ppermute | solution.py:29
  177.3 1.7 copy.35
  (86 shorter events, 24.1 us)
Async XLA Ops:
  0.6 20.5 %copy-start.16 = (f32[1,8192]{1,0:T(1,128)S(1)}, f32[1,8192]{1,0:T(1,128)}, u32[]{:S(2)}) copy-start(f32[1,8192]{1,0:T(1,128)} %gain_ref.3) | copy-start | bytes 98308
  0.6 20.5 %copy-start.2 = (bf16[1,2,64,8192]{3,2,1,0:T(8,128)(2,1)S(1)}, bf16[1,2,64,8192]{3,2,1,0:T(8,128)(2,1)}, u32[]{:S(2)}) copy-start(bf16[1,2,64,8192]{3,2,1,0:T(8,128)(2,1)} %param.6) | copy-start | bytes 6291460
  2.5 18.6 %collective-permute-start.3 = (bf16[2048,256]{1,0:T(8,128)(2,1)S(1)}, bf16[2048,256]{1,0:T(8,128)(2,1)}, u32[]{:S(2)}, u32[]{:S(2)}) collective-permute-start(bf16[2048,256]{1,0:T(8,128)(2,1)S(1)} %bitcast_convert_fusion.rest_0_.weights_ref), channel_id=1, source_target_pairs={{0,1},{1,0},{2,3},{3,2},{4,5},{5,4},{6,7},{7,6},{8,9},{9,8},{10,11... | collective-permute-start | bytes 3145736 | tf_op jit(solution)/shard_map/ppermute | solution.py:29
  3.0 26.7 %collective-permute-start.13 = (bf16[2048,256]{1,0:T(8,128)(2,1)S(1)}, bf16[2048,256]{1,0:T(8,128)(2,1)}, u32[]{:S(2)}, u32[]{:S(2)}) collective-permute-start(bf16[2048,256]{1,0:T(8,128)(2,1)S(1)} %bitcast_convert_fusion.rest_0_.weights_ref), channel_id=1, source_target_pairs={{0,2},{1,3},{2,0},{3,1},{4,6},{5,7},{6,4},{7,5},{8,10},{9,11},{10,... | collective-permute-start | bytes 3145736 | tf_op jit(solution)/shard_map/ppermute | solution.py:29
  5.6 15.2 %collective-permute-start.1 = (bf16[2,256,256]{2,1,0:T(8,128)(2,1)}, bf16[2,256,256]{2,1,0:T(8,128)(2,1)S(1)}, u32[]{:S(2)}, u32[]{:S(2)}) collective-permute-start(bf16[2,256,256]{2,1,0:T(8,128)(2,1)} %bitcast.2.refs_0_), channel_id=1, source_target_pairs={{0,8},{4,12},{8,0},{12,4},{1,9},{5,13},{9,1},{13,5},{2,10},{6,14},... | collective-permute-start | bytes 786440 | tf_op jit(solution)/shard_map/ppermute | solution.py:29
  8.2 12.9 %collective-permute-start = (bf16[2,256,256]{2,1,0:T(8,128)(2,1)}, bf16[2,256,256]{2,1,0:T(8,128)(2,1)}, u32[]{:S(2)}, u32[]{:S(2)}) collective-permute-start(bf16[2,256,256]{2,1,0:T(8,128)(2,1)} %bitcast.2.refs_0_), channel_id=1, source_target_pairs={{0,4},{4,0},{8,12},{12,8},{1,5},{5,1},{9,13},{13,9},{2,6},{6,2},{1... | collective-permute-start | bytes 786440 | tf_op jit(solution)/shard_map/ppermute | solution.py:29
  24.0 16.6 %collective-permute-start.4 = (bf16[128,2048]{1,0:T(8,128)(2,1)S(1)}, bf16[128,2048]{1,0:T(8,128)(2,1)S(1)}, u32[]{:S(2)}, u32[]{:S(2)}) collective-permute-start(bf16[128,2048]{1,0:T(8,128)(2,1)S(1)} %get-tuple-element.28.refs_0_), channel_id=1, source_target_pairs={{0,2},{1,3},{2,0},{3,1},{4,6},{5,7},{6,4},{7,5},{8,10},{9,11},{10,... | collective-permute-start | bytes 1572872 | tf_op jit(solution)/shard_map/ppermute | solution.py:29
  24.5 23.2 %collective-permute-start.9 = (bf16[128,2048]{1,0:T(8,128)(2,1)S(1)}, bf16[128,2048]{1,0:T(8,128)(2,1)}, u32[]{:S(2)}, u32[]{:S(2)}) collective-permute-start(bf16[128,2048]{1,0:T(8,128)(2,1)S(1)} %get-tuple-element.31), channel_id=1, source_target_pairs={{0,12},{4,8},{8,4},{12,0},{1,13},{5,9},{9,5},{13,1},{2,14},{6,10},... | collective-permute-start | bytes 1572872 | tf_op jit(solution)/shard_map/ppermute | solution.py:29
  27.6 17.7 %collective-permute-start.2 = (bf16[2,256,256]{2,1,0:T(8,128)(2,1)S(1)}, bf16[2,256,256]{2,1,0:T(8,128)(2,1)S(1)}, u32[]{:S(2)}, u32[]{:S(2)}) collective-permute-start(bf16[2,256,256]{2,1,0:T(8,128)(2,1)S(1)} %collective-permute-done.1.refs_2_.mark_ref), channel_id=1, source_target_pairs={{0,4},{4,0},{8,12},{12,8},{1,5},{5,1},{9,13},{13,9},{2,6},{6,2},{1... | collective-permute-start | bytes 786440 | tf_op jit(solution)/shard_map/ppermute | solution.py:29
  29.7 28.4 %collective-permute-start.14 = (bf16[2048,256]{1,0:T(8,128)(2,1)}, bf16[2048,256]{1,0:T(8,128)(2,1)S(1)}, u32[]{:S(2)}, u32[]{:S(2)}) collective-permute-start(bf16[2048,256]{1,0:T(8,128)(2,1)} %collective-permute-done.13.rest_2_), channel_id=1, source_target_pairs={{0,1},{1,0},{2,3},{3,2},{4,5},{5,4},{6,7},{7,6},{8,9},{9,8},{10,11... | collective-permute-start | bytes 3145736 | tf_op jit(solution)/shard_map/ppermute | solution.py:29
  41.6 38.1 %collective-permute-start.5 = (bf16[256,2048]{1,0:T(8,128)(2,1)}, bf16[256,2048]{1,0:T(8,128)(2,1)}, u32[]{:S(2)}, u32[]{:S(2)}) collective-permute-start(bf16[256,2048]{1,0:T(8,128)(2,1)} %pack.3.rest_0_), channel_id=1, source_target_pairs={{0,1},{1,0},{2,3},{3,2},{4,5},{5,4},{6,7},{7,6},{8,9},{9,8},{10,11... | collective-permute-start | bytes 3145736 | tf_op jit(solution)/shard_map/ppermute | solution.py:29
  41.7 14.8 %collective-permute-start.6 = (bf16[128,2048]{1,0:T(8,128)(2,1)}, bf16[128,2048]{1,0:T(8,128)(2,1)}, u32[]{:S(2)}, u32[]{:S(2)}) collective-permute-start(bf16[128,2048]{1,0:T(8,128)(2,1)} %get-tuple-element.29), channel_id=1, source_target_pairs={{0,4},{4,0},{8,12},{12,8},{1,5},{5,1},{9,13},{13,9},{2,6},{6,2},{1... | collective-permute-start | bytes 1572872 | tf_op jit(solution)/shard_map/ppermute | solution.py:29
  49.4 18.4 %all-to-all-start = ((bf16[4,512,256]{2,1,0:T(8,128)(2,1)}), bf16[4,512,256]{2,1,0:T(8,128)(2,1)S(1)}, u32[]{:S(2)}, u32[]{:S(2)}) async-start(bf16[4,512,256]{2,1,0:T(8,128)(2,1)} %after.8), calls=%async_computation | async-start | bytes 2097152 | tf_op jit(solution)/shard_map/all_to_all | solution.py:312
  53.0 26.8 %collective-permute-start.12 = (bf16[128,2048]{1,0:T(8,128)(2,1)}, bf16[128,2048]{1,0:T(8,128)(2,1)}, u32[]{:S(2)}, u32[]{:S(2)}) collective-permute-start(bf16[128,2048]{1,0:T(8,128)(2,1)} %copy-done.8), channel_id=1, source_target_pairs={{0,8},{4,12},{8,0},{12,4},{1,9},{5,13},{9,1},{13,5},{2,10},{6,14},... | collective-permute-start | bytes 1572872 | tf_op jit(solution)/shard_map/ppermute | solution.py:29
  54.5 30.4 %collective-permute-start.10 = (bf16[128,2048]{1,0:T(8,128)(2,1)}, bf16[128,2048]{1,0:T(8,128)(2,1)}, u32[]{:S(2)}, u32[]{:S(2)}) collective-permute-start(bf16[128,2048]{1,0:T(8,128)(2,1)} %get-tuple-element.32.refs_0_), channel_id=1, source_target_pairs={{0,2},{1,3},{2,0},{3,1},{4,6},{5,7},{6,4},{7,5},{8,10},{9,11},{10,... | collective-permute-start | bytes 1572872 | tf_op jit(solution)/shard_map/ppermute | solution.py:29
  56.5 33.4 %collective-permute-start.7 = (bf16[128,2048]{1,0:T(8,128)(2,1)}, bf16[128,2048]{1,0:T(8,128)(2,1)}, u32[]{:S(2)}, u32[]{:S(2)}) collective-permute-start(bf16[128,2048]{1,0:T(8,128)(2,1)} %collective-permute-done.6.refs_0_), channel_id=1, source_target_pairs={{0,2},{1,3},{2,0},{3,1},{4,6},{5,7},{6,4},{7,5},{8,10},{9,11},{10,... | collective-permute-start | bytes 1572872 | tf_op jit(solution)/shard_map/ppermute | solution.py:29
  81.1 82.2 %all-to-all-start.1 = ((bf16[4,128,2048]{2,1,0:T(8,128)(2,1)}), bf16[4,128,2048]{2,1,0:T(8,128)(2,1)S(1)}, u32[]{:S(2)}, u32[]{:S(2)}) async-start(bf16[4,128,2048]{2,1,0:T(8,128)(2,1)} %copy-done), calls=%async_computation.1 | async-start | bytes 4194304 | tf_op jit(solution)/shard_map/all_to_all | solution.py:337
  84.8 22.9 %copy-start.1 = (f32[1,2048,256]{2,1,0:T(8,128)S(1)}, f32[1,2048,256]{2,1,0:T(8,128)}, u32[]{:S(2)}) copy-start(f32[1,2048,256]{2,1,0:T(8,128)} %param.9) | copy-start | bytes 6291460
  84.9 22.9 %copy-start.6 = (f32[1,2048,256]{2,1,0:T(8,128)S(1)}, f32[1,2048,256]{2,1,0:T(8,128)}, u32[]{:S(2)}) copy-start(f32[1,2048,256]{2,1,0:T(8,128)} %param.10) | copy-start | bytes 6291460
  86.3 19.6 %collective-permute-start.11 = (bf16[256,2048]{1,0:T(8,128)(2,1)S(1)}, bf16[256,2048]{1,0:T(8,128)(2,1)S(1)}, u32[]{:S(2)}, u32[]{:S(2)}) collective-permute-start(bf16[256,2048]{1,0:T(8,128)(2,1)S(1)} %pack.5.rest_4_), channel_id=1, source_target_pairs={{0,1},{1,0},{2,3},{3,2},{4,5},{5,4},{6,7},{7,6},{8,9},{9,8},{10,11... | collective-permute-start | bytes 3145736 | tf_op jit(solution)/shard_map/ppermute | solution.py:29
  91.2 14.6 %collective-permute-start.8 = (bf16[256,2048]{1,0:T(8,128)(2,1)S(1)}, bf16[256,2048]{1,0:T(8,128)(2,1)S(1)}, u32[]{:S(2)}, u32[]{:S(2)}) collective-permute-start(bf16[256,2048]{1,0:T(8,128)(2,1)S(1)} %pack.4.rest_2_), channel_id=1, source_target_pairs={{0,1},{1,0},{2,3},{3,2},{4,5},{5,4},{6,7},{7,6},{8,9},{9,8},{10,11... | collective-permute-start | bytes 3145736 | tf_op jit(solution)/shard_map/ppermute | solution.py:29
  91.3 14.6 %collective-permute-start.15 = (bf16[128,2048]{1,0:T(8,128)(2,1)}, bf16[128,2048]{1,0:T(8,128)(2,1)S(1)}, u32[]{:S(2)}, u32[]{:S(2)}) collective-permute-start(bf16[128,2048]{1,0:T(8,128)(2,1)} %get-tuple-element.35.rest_6_), channel_id=1, source_target_pairs={{0,2},{1,3},{2,0},{3,1},{4,6},{5,7},{6,4},{7,5},{8,10},{9,11},{10,... | collective-permute-start | bytes 1572872 | tf_op jit(solution)/shard_map/ppermute | solution.py:29
  91.7 14.1 %collective-permute-start.16 = (bf16[128,2048]{1,0:T(8,128)(2,1)}, bf16[128,2048]{1,0:T(8,128)(2,1)S(1)}, u32[]{:S(2)}, u32[]{:S(2)}) collective-permute-start(bf16[128,2048]{1,0:T(8,128)(2,1)} %get-tuple-element.35.rest_6_), channel_id=1, source_target_pairs={{0,1},{1,0},{2,3},{3,2},{4,5},{5,4},{6,7},{7,6},{8,9},{9,8},{10,11... | collective-permute-start | bytes 1572872 | tf_op jit(solution)/shard_map/ppermute | solution.py:29
  105.8 1.9 %collective-permute-start.17 = (bf16[128,2048]{1,0:T(8,128)(2,1)S(1)}, bf16[128,2048]{1,0:T(8,128)(2,1)S(1)}, u32[]{:S(2)}, u32[]{:S(2)}) collective-permute-start(bf16[128,2048]{1,0:T(8,128)(2,1)S(1)} %collective-permute-done.15.rest_7_), channel_id=1, source_target_pairs={{0,1},{1,0},{2,3},{3,2},{4,5},{5,4},{6,7},{7,6},{8,9},{9,8},{10,11... | collective-permute-start | bytes 1572872 | tf_op jit(solution)/shard_map/ppermute | solution.py:29
  119.3 19.3 %collective-permute-start.22 = (bf16[512,256]{1,0:T(8,128)(2,1)S(1)}, bf16[512,256]{1,0:T(8,128)(2,1)S(1)}, u32[]{:S(2)}, u32[]{:S(2)}) collective-permute-start(bf16[512,256]{1,0:T(8,128)(2,1)S(1)} %get-tuple-element.45), channel_id=1, source_target_pairs={{0,4},{4,0},{8,12},{12,8},{1,5},{5,1},{9,13},{13,9},{2,6},{6,2},{1... | collective-permute-start | bytes 786440 | tf_op jit(solution)/shard_map/ppermute | solution.py:29
  121.0 23.2 %collective-permute-start.21 = (bf16[512,256]{1,0:T(8,128)(2,1)S(1)}, bf16[512,256]{1,0:T(8,128)(2,1)S(1)}, u32[]{:S(2)}, u32[]{:S(2)}) collective-permute-start(bf16[512,256]{1,0:T(8,128)(2,1)S(1)} %get-tuple-element.36.mark_ref), channel_id=1, source_target_pairs={{0,4},{4,0},{8,12},{12,8},{1,5},{5,1},{9,13},{13,9},{2,6},{6,2},{1... | collective-permute-start | bytes 786440 | tf_op jit(solution)/shard_map/ppermute | solution.py:29
  126.1 23.8 %collective-permute-start.18 = (bf16[512,256]{1,0:T(8,128)(2,1)}, bf16[512,256]{1,0:T(8,128)(2,1)S(1)}, u32[]{:S(2)}, u32[]{:S(2)}) collective-permute-start(bf16[512,256]{1,0:T(8,128)(2,1)} %get-tuple-element.38), channel_id=1, source_target_pairs={{0,4},{4,0},{8,12},{12,8},{1,5},{5,1},{9,13},{13,9},{2,6},{6,2},{1... | collective-permute-start | bytes 786440 | tf_op jit(solution)/shard_map/ppermute | solution.py:29
  127.8 32.6 %collective-permute-start.19 = (bf16[512,256]{1,0:T(8,128)(2,1)}, bf16[512,256]{1,0:T(8,128)(2,1)S(1)}, u32[]{:S(2)}, u32[]{:S(2)}) collective-permute-start(bf16[512,256]{1,0:T(8,128)(2,1)} %get-tuple-element.39), channel_id=1, source_target_pairs={{0,4},{4,0},{8,12},{12,8},{1,5},{5,1},{9,13},{13,9},{2,6},{6,2},{1... | collective-permute-start | bytes 786440 | tf_op jit(solution)/shard_map/ppermute | solution.py:29
  144.3 16.1 %collective-permute-start.23 = (bf16[512,256]{1,0:T(8,128)(2,1)S(1)}, bf16[512,256]{1,0:T(8,128)(2,1)}, u32[]{:S(2)}, u32[]{:S(2)}) collective-permute-start(bf16[512,256]{1,0:T(8,128)(2,1)S(1)} %add_convert_fusion.2), channel_id=1, source_target_pairs={{0,8},{4,12},{8,0},{12,4},{1,9},{5,13},{9,1},{13,5},{2,10},{6,14},... | collective-permute-start | bytes 786440 | tf_op jit(solution)/shard_map/ppermute | solution.py:29
  144.4 18.7 %copy-start.12 = (bf16[512,256]{1,0:T(8,128)(2,1)S(1)}, bf16[512,256]{1,0:T(8,128)(2,1)}, u32[]{:S(2)}) copy-start(bf16[512,256]{1,0:T(8,128)(2,1)} %copy-done.11) | copy-start | bytes 786436
  161.7 7.8 %collective-permute-start.24 = (bf16[1,2,256,256]{3,2,1,0:T(8,128)(2,1)S(1)}, bf16[1,2,256,256]{3,2,1,0:T(8,128)(2,1)}, u32[]{:S(2)}, u32[]{:S(2)}) collective-permute-start(bf16[1,2,256,256]{3,2,1,0:T(8,128)(2,1)S(1)} %bitcast.25), channel_id=1, source_target_pairs={{0,16},{16,0},{1,17},{17,1},{2,18},{18,2},{3,19},{19,3},{4,20},{20... | collective-permute-start | bytes 786440 | tf_op jit(solution)/shard_map/ppermute | solution.py:34
  163.2 13.2 %collective-permute-start.20 = (bf16[512,256]{1,0:T(8,128)(2,1)S(1)}, bf16[512,256]{1,0:T(8,128)(2,1)S(1)}, u32[]{:S(2)}, u32[]{:S(2)}) collective-permute-start(bf16[512,256]{1,0:T(8,128)(2,1)S(1)} %add_convert_fusion.3), channel_id=1, source_target_pairs={{0,8},{4,12},{8,0},{12,4},{1,9},{5,13},{9,1},{13,5},{2,10},{6,14},... | collective-permute-start | bytes 786440 | tf_op jit(solution)/shard_map/ppermute | solution.py:29
  (12 other events, 70.6 us)

commit v15 on v14

--- a/solution.py
+++ b/solution.py
@@ -265,7 +265,7 @@
     got = swap(other, "dp", 2)
     if earlier:
         got = after([got], *earlier)[0]
-    return mine + got.astype(f32), other
+    return mine + got.astype(f32)
 
 
 def shards(hidden_in, norm_gain, kv_cot, master_kv, moment_m, moment_v):
@@ -370,9 +370,7 @@
         )
 
     got1, got3 = swap(parts[1], "dp", 1), swap(parts[3], "dp", 1)
-    got1, got3 = after([got1, got3])
-    mine, _ = scatter_sum(parts, got1, got3)
-    mine = place(mine.astype(bf16))
+    mine = place(scatter_sum(parts, got1, got3).astype(bf16))
     kv_next = from_behind(mine, "segment", -1)
     own_parts = call(
         functools.partial(project_kernel, count=count, layout=layout),
@@ -382,7 +380,7 @@
         16,
         "project",
         scratch=[all_tokens, pltpu.SemaphoreType.DMA((count,))],
-    )(parts[1], w0[0], *tokens)
+    )(got1, w0[0], *tokens)
     (d,) = after([d], mine)
     grad_in = call(
         functools.partial(grad_kernel, tile=tile),
@@ -393,8 +391,7 @@
         "grad_in",
     )(hidden, norm_gain, d)
     own_got = after([swap(own_parts[1], "dp", 1), swap(own_parts[3], "dp", 1)])
-    kv_own, _ = scatter_sum(own_parts, *own_got, grad_in[:16, :128])
-    kv_own = place(kv_own.astype(bf16))
+    kv_own = place(scatter_sum(own_parts, *own_got, grad_in[:16, :128]).astype(bf16))
     return (kv_own, grad_in.reshape(hidden_in.shape), master_new[None], kv_next)
 
 

time: 180 us -> 188 us (1.044)
  local copies, waits for them, and re-layouts: 11.2 us -> 21 us
  waiting for transfers between devices: 102 us -> 99.2 us
    unnamed x35 -> x61, local copies, waits for them, and re-layouts: 9.8 us -> 19.6 us
    ppermute x1, waiting for transfers between devices: 6.18 us -> 0.01 us  [from_behind(): return lax.ppermute(x, axis, [(i, (i + by) % peers) for i in range(peers)])]
    ppermute x24, waiting for transfers between devices: 86.2 us -> 89.5 us  [swap(): return lax.ppermute(x, axis, [(i, i ^ bits) for i in range(peers)])]
  transfers between devices with their start and end apart: 27 -> 27, of which waited for: 17 -> 16; matrix products, arithmetic and copies ran while one was open for 1% -> 1% of each run, Pallas kernels for 17% -> 16%
where the time goes in v15:
time: 188 us; the launch traced here: 187 us
  waiting for transfers between devices  99.2 us (53%)
  starting transfers between devices  31.9 us (17%)
  Pallas kernels  29.8 us (16%)
  local copies, waits for them, and re-layouts  21 us (11%)
  other arithmetic  4.03 us (2%)
    ppermute x24, waiting for transfers between devices, swap(): return lax.ppermute(x, axis, [(i, i ^ bits) for i in range(peers)])  89.5 us
    ppermute x24, starting transfers between devices, swap(): return lax.ppermute(x, axis, [(i, i ^ bits) for i in range(peers)])  23.2 us
    unnamed x61, local copies, waits for them, and re-layouts  19.6 us
    all_to_all x1, waiting for transfers between devices, shards(): mine_cot = lax.all_to_all(send, 'tensor', 0, 0, tiled=True)  9.73 us
    pallas_call x1, Pallas kernels, shards(): call(functools.partial(update_kernel, count=count, tile=step, layout=layo...  9.48 us
    pallas_call x1, Pallas kernels, shards(): call(functools.partial(project_kernel, count=count, layout=layout), part_...  4.19 us
    pallas_call x1, Pallas kernels, shards(): call(d_kernel, like(dp, piece, depth), [smem] + [vmem] * 5, vmem, 20, 'd_...  3.91 us
    all_to_all x1, starting transfers between devices, shards(): d = lax.all_to_all(d, 'dp', 0, 0, tiled=True)  3.79 us
  transfers between devices with their start and end apart: 27, of which 16 were waited for; matrix products, arithmetic and copies ran while one was open for 1% of the time, Pallas kernels for 16%

profile of v15, /device:TPU:0, one launch (start us, length us, event | category | flops | bytes accessed | tf_op | source)
XLA Modules:
  0.0 187.1 jit_solution(9028799932207883920)
XLA Ops:
  0.7 1.8 bitcast_convert_fusion.rest_0_.weights_ref
  3.0 2.6 %collective-permute-start.13 = (bf16[2048,256]{1,0:T(8,128)(2,1)S(1)}, bf16[2048,256]{1,0:T(8,128)(2,1)}, u32[]{:S(2)}, u32[]{:S(2)}) collective-permute-start(bf16[2048,256]{1,0:T(8,128)(2,1)S(1)} %bitcast_convert_fusion.rest_0_.weights_ref), channel_id=1, source_target_pairs={{0,2},{1,3},{2,0},{3,1},{4,6},{5,7},{6,4},{7,5},{8,10},{9,11},{10,... | collective-permute-start | bytes 3145736 | tf_op jit(solution)/shard_map/ppermute | solution.py:29
  5.6 2.6 %collective-permute-start.1 = (bf16[2,256,256]{2,1,0:T(8,128)(2,1)}, bf16[2,256,256]{2,1,0:T(8,128)(2,1)S(1)}, u32[]{:S(2)}, u32[]{:S(2)}) collective-permute-start(bf16[2,256,256]{2,1,0:T(8,128)(2,1)} %bitcast.2.refs_0_), channel_id=1, source_target_pairs={{0,8},{4,12},{8,0},{12,4},{1,9},{5,13},{9,1},{13,5},{2,10},{6,14},... | collective-permute-start | bytes 786440 | tf_op jit(solution)/shard_map/ppermute | solution.py:29
  9.9 11.0 %collective-permute-done.1.refs_2_.mark_ref = bf16[2,256,256]{2,1,0:T(8,128)(2,1)S(1)} collective-permute-done((bf16[2,256,256]{2,1,0:T(8,128)(2,1)}, bf16[2,256,256]{2,1,0:T(8,128)(2,1)S(1)}, u32[]{:S(2)}, u32[]{:S(2)}) %collective-permute-start.1) | collective-permute-done | bytes 262176 | tf_op jit(solution)/shard_map/ppermute | solution.py:29
  21.1 2.9 %norm.1 = (bf16[128,2048]{1,0:T(8,128)(2,1)S(1)}, bf16[128,2048]{1,0:T(8,128)(2,1)}, bf16[128,2048]{1,0:T(8,128)(2,1)S(1)}, bf16[128,2048]{1,0:T(8,128)(2,1)S(1)}) custom-call(bf16[2,256,256]{2,1,0:T(8,128)(2,1)S(1)} %collective-permute-done.1.refs_2_.mark_ref, bf16[2,256,256]{2,1,0:T(8,128)(2,1)} %collective-permute-done.refs_1_.other_ref, ...), custom_call_target="tpu_custom_call" | custom-call | flops 1000 | bytes 1000 | tf_op jit(solution)/shard_map/norm/pallas_call | solution.py:290
  24.5 3.2 %collective-permute-start.9 = (bf16[128,2048]{1,0:T(8,128)(2,1)S(1)}, bf16[128,2048]{1,0:T(8,128)(2,1)}, u32[]{:S(2)}, u32[]{:S(2)}) collective-permute-start(bf16[128,2048]{1,0:T(8,128)(2,1)S(1)} %get-tuple-element.29), channel_id=1, source_target_pairs={{0,12},{4,8},{8,4},{12,0},{1,13},{5,9},{9,5},{13,1},{2,14},{6,10},... | collective-permute-start | bytes 1572872 | tf_op jit(solution)/shard_map/ppermute | solution.py:29
  27.6 2.1 %collective-permute-done.13.rest_2_ = bf16[2048,256]{1,0:T(8,128)(2,1)} collective-permute-done((bf16[2048,256]{1,0:T(8,128)(2,1)S(1)}, bf16[2048,256]{1,0:T(8,128)(2,1)}, u32[]{:S(2)}, u32[]{:S(2)}) %collective-permute-start.13) | collective-permute-done | bytes 1048608 | tf_op jit(solution)/shard_map/ppermute | solution.py:29
  29.7 10.9 %collective-permute-done.4.refs_1_ = bf16[128,2048]{1,0:T(8,128)(2,1)S(1)} collective-permute-done((bf16[128,2048]{1,0:T(8,128)(2,1)S(1)}, bf16[128,2048]{1,0:T(8,128)(2,1)S(1)}, u32[]{:S(2)}, u32[]{:S(2)}) %collective-permute-start.4) | collective-permute-done | bytes 524320 | tf_op jit(solution)/shard_map/ppermute | solution.py:29
  41.7 1.9 %collective-permute-start.6 = (bf16[128,2048]{1,0:T(8,128)(2,1)}, bf16[128,2048]{1,0:T(8,128)(2,1)}, u32[]{:S(2)}, u32[]{:S(2)}) collective-permute-start(bf16[128,2048]{1,0:T(8,128)(2,1)} %get-tuple-element.27), channel_id=1, source_target_pairs={{0,4},{4,0},{8,12},{12,8},{1,5},{5,1},{9,13},{13,9},{2,6},{6,2},{1... | collective-permute-start | bytes 1572872 | tf_op jit(solution)/shard_map/ppermute | solution.py:29
  43.6 1.7 collective-permute-done.2.refs_3_
  45.3 2.4 %arrange.1 = (bf16[4,512,256]{2,1,0:T(8,128)(2,1)}, bf16[256,2048]{1,0:T(8,128)(2,1)S(1)}) custom-call(s32[2]{0:T(128)S(1)} %pad_add_fusion.where_ref, bf16[2,256,256]{2,1,0:T(8,128)(2,1)} %bitcast.2.refs_0_, bf16[2,256,256]{2,1,0:T(8,128)(2,1)} %collective-permute-done.refs_1_.other_ref, bf16[2,256,256]{2,1,0:T(8,128)(2,1)S(1)} %collective-permute-done.1.refs_2_.mark_ref, ...), custom_call_target="tpu_custom_call" | custom-call | flops 1000 | bytes 1000 | tf_op jit(solution)/shard_map/arrange/pallas_call | solution.py:301
  49.4 3.5 %all-to-all-start = ((bf16[4,512,256]{2,1,0:T(8,128)(2,1)}), bf16[4,512,256]{2,1,0:T(8,128)(2,1)S(1)}, u32[]{:S(2)}, u32[]{:S(2)}) async-start(bf16[4,512,256]{2,1,0:T(8,128)(2,1)} %after.7), calls=%async_computation | async-start | bytes 2097152 | tf_op jit(solution)/shard_map/all_to_all | solution.py:312
  54.5 1.9 %collective-permute-start.10 = (bf16[128,2048]{1,0:T(8,128)(2,1)}, bf16[128,2048]{1,0:T(8,128)(2,1)}, u32[]{:S(2)}, u32[]{:S(2)}) collective-permute-start(bf16[128,2048]{1,0:T(8,128)(2,1)} %get-tuple-element.30.refs_0_), channel_id=1, source_target_pairs={{0,2},{1,3},{2,0},{3,1},{4,6},{5,7},{6,4},{7,5},{8,10},{9,11},{10,... | collective-permute-start | bytes 1572872 | tf_op jit(solution)/shard_map/ppermute | solution.py:29
  58.1 9.7 %all-to-all-done.cot_ref = bf16[4,512,256]{2,1,0:T(8,128)(2,1)S(1)} async-done(((bf16[4,512,256]{2,1,0:T(8,128)(2,1)}), bf16[4,512,256]{2,1,0:T(8,128)(2,1)S(1)}, u32[]{:S(2)}, u32[]{:S(2)}) %all-to-all-start) | async-done | bytes 1048608 | tf_op jit(solution)/shard_map/all_to_all | solution.py:312
  70.1 3.9 %d_normed.1.refs_1_ = bf16[4,128,2048]{2,1,0:T(8,128)(2,1)S(1)} custom-call(s32[2]{0:T(128)S(1)} %pad_add_fusion.where_ref, bf16[4,512,256]{2,1,0:T(8,128)(2,1)S(1)} %copy-done.9, bf16[2048,256]{1,0:T(8,128)(2,1)S(1)} %bitcast_convert_fusion.rest_0_.weights_ref, bf16[2048,256]{1,0:T(8,128)(2,1)} %collective-permute-done.3.third_ref.rest_1_, ...), custom_call_target="tpu_custom_call" | custom-call | flops 1000 | bytes 1000 | tf_op jit(solution)/shard_map/d_normed/pallas_call | solution.py:328
  74.0 5.8 %collective-permute-done.12.refs_0_ = bf16[128,2048]{1,0:T(8,128)(2,1)} collective-permute-done((bf16[128,2048]{1,0:T(8,128)(2,1)}, bf16[128,2048]{1,0:T(8,128)(2,1)}, u32[]{:S(2)}, u32[]{:S(2)}) %collective-permute-start.12) | collective-permute-done | bytes 524320 | tf_op jit(solution)/shard_map/ppermute | solution.py:29
  81.1 3.8 %all-to-all-start.1 = ((bf16[4,128,2048]{2,1,0:T(8,128)(2,1)}), bf16[4,128,2048]{2,1,0:T(8,128)(2,1)S(1)}, u32[]{:S(2)}, u32[]{:S(2)}) async-start(bf16[4,128,2048]{2,1,0:T(8,128)(2,1)} %copy-done), calls=%async_computation.1 | async-start | bytes 4194304 | tf_op jit(solution)/shard_map/all_to_all | solution.py:337
  86.4 3.6 %collective-permute-done.7.refs_1_ = bf16[128,2048]{1,0:T(8,128)(2,1)} collective-permute-done((bf16[128,2048]{1,0:T(8,128)(2,1)}, bf16[128,2048]{1,0:T(8,128)(2,1)}, u32[]{:S(2)}, u32[]{:S(2)}) %collective-permute-start.7) | collective-permute-done | bytes 524320 | tf_op jit(solution)/shard_map/ppermute | solution.py:29
  91.9 14.0 %collective-permute-done.15.rest_7_ = bf16[128,2048]{1,0:T(8,128)(2,1)S(1)} collective-permute-done((bf16[128,2048]{1,0:T(8,128)(2,1)}, bf16[128,2048]{1,0:T(8,128)(2,1)S(1)}, u32[]{:S(2)}, u32[]{:S(2)}) %collective-permute-start.15) | collective-permute-done | bytes 524320 | tf_op jit(solution)/shard_map/ppermute | solution.py:29
  105.9 1.9 collective-permute-done.17.rest_9_
  107.8 1.8 copy-done.15
  110.8 9.5 %update.1 = (f32[2048,256]{1,0:T(8,128)}, bf16[512,256]{1,0:T(8,128)(2,1)S(1)}, bf16[512,256]{1,0:T(8,128)(2,1)}, bf16[512,256]{1,0:T(8,128)(2,1)S(1)}, bf16[512,256]{1,0:T(8,128)(2,1)S(1)}) custom-call(bf16[256,2048]{1,0:T(8,128)(2,1)S(1)} %copy-done.24, f32[2048,256]{1,0:T(8,128)S(1)} %bitcast.20, f32[2048,256]{1,0:T(8,128)S(1)} %bitcast.23, ...), custom_call_target="tpu_custom_call" | custom-call | flops 1000 | bytes 1000 | tf_op jit(solution)/shard_map/update/pallas_call | solution.py:347
  120.3 1.7 collective-permute-start.22
  122.4 16.2 %collective-permute-done.22 = bf16[512,256]{1,0:T(8,128)(2,1)S(1)} collective-permute-done((bf16[512,256]{1,0:T(8,128)(2,1)S(1)}, bf16[512,256]{1,0:T(8,128)(2,1)S(1)}, u32[]{:S(2)}, u32[]{:S(2)}) %collective-permute-start.22) | collective-permute-done | bytes 262176 | tf_op jit(solution)/shard_map/ppermute | solution.py:29
  139.4 4.9 %collective-permute-done.18.mark_ref = bf16[512,256]{1,0:T(8,128)(2,1)S(1)} collective-permute-done((bf16[512,256]{1,0:T(8,128)(2,1)}, bf16[512,256]{1,0:T(8,128)(2,1)S(1)}, u32[]{:S(2)}, u32[]{:S(2)}) %collective-permute-start.18) | collective-permute-done | bytes 262176 | tf_op jit(solution)/shard_map/ppermute | solution.py:29
  152.3 4.2 %project.1 = (bf16[512,256]{1,0:T(8,128)(2,1)S(1)}, bf16[512,256]{1,0:T(8,128)(2,1)S(1)}, bf16[512,256]{1,0:T(8,128)(2,1)S(1)}, bf16[512,256]{1,0:T(8,128)(2,1)S(1)}) custom-call(bf16[512,256]{1,0:T(8,128)(2,1)S(1)} %collective-permute-done.18.mark_ref, bf16[2048,256]{1,0:T(8,128)(2,1)S(1)} %bitcast_convert_fusion.rest_0_.weights_ref, ...), custom_call_target="tpu_custom_call" | custom-call | flops 1000 | bytes 1000 | tf_op jit(solution)/shard_map/project/pallas_call | solution.py:375
  156.6 2.0 %collective-permute-start.20 = (bf16[512,256]{1,0:T(8,128)(2,1)S(1)}, bf16[512,256]{1,0:T(8,128)(2,1)S(1)}, u32[]{:S(2)}, u32[]{:S(2)}) collective-permute-start(bf16[512,256]{1,0:T(8,128)(2,1)S(1)} %get-tuple-element.37), channel_id=1, source_target_pairs={{0,4},{4,0},{8,12},{12,8},{1,5},{5,1},{9,13},{13,9},{2,6},{6,2},{1... | collective-permute-start | bytes 786440 | tf_op jit(solution)/shard_map/ppermute | solution.py:29
  161.2 4.5 %collective-permute-done.19.refs_0_ = bf16[512,256]{1,0:T(8,128)(2,1)S(1)} collective-permute-done((bf16[512,256]{1,0:T(8,128)(2,1)S(1)}, bf16[512,256]{1,0:T(8,128)(2,1)S(1)}, u32[]{:S(2)}, u32[]{:S(2)}) %collective-permute-start.19) | collective-permute-done | bytes 262176 | tf_op jit(solution)/shard_map/ppermute | solution.py:29
  165.7 4.7 %collective-permute-done.20.refs_1_ = bf16[512,256]{1,0:T(8,128)(2,1)S(1)} collective-permute-done((bf16[512,256]{1,0:T(8,128)(2,1)S(1)}, bf16[512,256]{1,0:T(8,128)(2,1)S(1)}, u32[]{:S(2)}, u32[]{:S(2)}) %collective-permute-start.20) | collective-permute-done | bytes 262176 | tf_op jit(solution)/shard_map/ppermute | solution.py:29
  172.5 3.3 %grad_in.1 = bf16[128,8192]{1,0:T(8,128)(2,1)} custom-call(bf16[128,8192]{1,0:T(8,128)(2,1)S(1)} %bitcast.22, f32[1,8192]{1,0:T(1,128)S(1)} %copy-done.29, bf16[4,128,2048]{2,1,0:T(8,128)(2,1)S(1)} %after.10.d_ref), custom_call_target="tpu_custom_call" | custom-call | flops 1000 | bytes 1000 | tf_op jit(solution)/shard_map/grad_in/pallas_call | solution.py:385
  176.5 8.0 %collective-permute-done.21.refs_0_ = bf16[512,256]{1,0:T(8,128)(2,1)S(1)} collective-permute-done((bf16[512,256]{1,0:T(8,128)(2,1)S(1)}, bf16[512,256]{1,0:T(8,128)(2,1)S(1)}, u32[]{:S(2)}, u32[]{:S(2)}) %collective-permute-start.21) | collective-permute-done | bytes 262176 | tf_op jit(solution)/shard_map/ppermute | solution.py:29
  185.4 1.7 copy.31
  (111 shorter events, 32.7 us)
Async XLA Ops:
  0.6 20.5 %copy-start.29 = (f32[1,8192]{1,0:T(1,128)S(1)}, f32[1,8192]{1,0:T(1,128)}, u32[]{:S(2)}) copy-start(f32[1,8192]{1,0:T(1,128)} %gain_ref.3) | copy-start | bytes 98308
  2.5 18.6 %collective-permute-start.3 = (bf16[2048,256]{1,0:T(8,128)(2,1)S(1)}, bf16[2048,256]{1,0:T(8,128)(2,1)}, u32[]{:S(2)}, u32[]{:S(2)}) collective-permute-start(bf16[2048,256]{1,0:T(8,128)(2,1)S(1)} %bitcast_convert_fusion.rest_0_.weights_ref), channel_id=1, source_target_pairs={{0,1},{1,0},{2,3},{3,2},{4,5},{5,4},{6,7},{7,6},{8,9},{9,8},{10,11... | collective-permute-start | bytes 3145736 | tf_op jit(solution)/shard_map/ppermute | solution.py:29
  3.0 26.7 %collective-permute-start.13 = (bf16[2048,256]{1,0:T(8,128)(2,1)S(1)}, bf16[2048,256]{1,0:T(8,128)(2,1)}, u32[]{:S(2)}, u32[]{:S(2)}) collective-permute-start(bf16[2048,256]{1,0:T(8,128)(2,1)S(1)} %bitcast_convert_fusion.rest_0_.weights_ref), channel_id=1, source_target_pairs={{0,2},{1,3},{2,0},{3,1},{4,6},{5,7},{6,4},{7,5},{8,10},{9,11},{10,... | collective-permute-start | bytes 3145736 | tf_op jit(solution)/shard_map/ppermute | solution.py:29
  5.6 15.2 %collective-permute-start.1 = (bf16[2,256,256]{2,1,0:T(8,128)(2,1)}, bf16[2,256,256]{2,1,0:T(8,128)(2,1)S(1)}, u32[]{:S(2)}, u32[]{:S(2)}) collective-permute-start(bf16[2,256,256]{2,1,0:T(8,128)(2,1)} %bitcast.2.refs_0_), channel_id=1, source_target_pairs={{0,8},{4,12},{8,0},{12,4},{1,9},{5,13},{9,1},{13,5},{2,10},{6,14},... | collective-permute-start | bytes 786440 | tf_op jit(solution)/shard_map/ppermute | solution.py:29
  8.2 12.9 %collective-permute-start = (bf16[2,256,256]{2,1,0:T(8,128)(2,1)}, bf16[2,256,256]{2,1,0:T(8,128)(2,1)}, u32[]{:S(2)}, u32[]{:S(2)}) collective-permute-start(bf16[2,256,256]{2,1,0:T(8,128)(2,1)} %bitcast.2.refs_0_), channel_id=1, source_target_pairs={{0,4},{4,0},{8,12},{12,8},{1,5},{5,1},{9,13},{13,9},{2,6},{6,2},{1... | collective-permute-start | bytes 786440 | tf_op jit(solution)/shard_map/ppermute | solution.py:29
  24.0 16.6 %collective-permute-start.4 = (bf16[128,2048]{1,0:T(8,128)(2,1)S(1)}, bf16[128,2048]{1,0:T(8,128)(2,1)S(1)}, u32[]{:S(2)}, u32[]{:S(2)}) collective-permute-start(bf16[128,2048]{1,0:T(8,128)(2,1)S(1)} %get-tuple-element.26.refs_0_), channel_id=1, source_target_pairs={{0,2},{1,3},{2,0},{3,1},{4,6},{5,7},{6,4},{7,5},{8,10},{9,11},{10,... | collective-permute-start | bytes 1572872 | tf_op jit(solution)/shard_map/ppermute | solution.py:29
  24.5 23.2 %collective-permute-start.9 = (bf16[128,2048]{1,0:T(8,128)(2,1)S(1)}, bf16[128,2048]{1,0:T(8,128)(2,1)}, u32[]{:S(2)}, u32[]{:S(2)}) collective-permute-start(bf16[128,2048]{1,0:T(8,128)(2,1)S(1)} %get-tuple-element.29), channel_id=1, source_target_pairs={{0,12},{4,8},{8,4},{12,0},{1,13},{5,9},{9,5},{13,1},{2,14},{6,10},... | collective-permute-start | bytes 1572872 | tf_op jit(solution)/shard_map/ppermute | solution.py:29
  27.6 17.7 %collective-permute-start.2 = (bf16[2,256,256]{2,1,0:T(8,128)(2,1)S(1)}, bf16[2,256,256]{2,1,0:T(8,128)(2,1)S(1)}, u32[]{:S(2)}, u32[]{:S(2)}) collective-permute-start(bf16[2,256,256]{2,1,0:T(8,128)(2,1)S(1)} %collective-permute-done.1.refs_2_.mark_ref), channel_id=1, source_target_pairs={{0,4},{4,0},{8,12},{12,8},{1,5},{5,1},{9,13},{13,9},{2,6},{6,2},{1... | collective-permute-start | bytes 786440 | tf_op jit(solution)/shard_map/ppermute | solution.py:29
  29.7 28.4 %collective-permute-start.14 = (bf16[2048,256]{1,0:T(8,128)(2,1)}, bf16[2048,256]{1,0:T(8,128)(2,1)S(1)}, u32[]{:S(2)}, u32[]{:S(2)}) collective-permute-start(bf16[2048,256]{1,0:T(8,128)(2,1)} %collective-permute-done.13.rest_2_), channel_id=1, source_target_pairs={{0,1},{1,0},{2,3},{3,2},{4,5},{5,4},{6,7},{7,6},{8,9},{9,8},{10,11... | collective-permute-start | bytes 3145736 | tf_op jit(solution)/shard_map/ppermute | solution.py:29
  41.6 38.1 %collective-permute-start.5 = (bf16[256,2048]{1,0:T(8,128)(2,1)}, bf16[256,2048]{1,0:T(8,128)(2,1)}, u32[]{:S(2)}, u32[]{:S(2)}) collective-permute-start(bf16[256,2048]{1,0:T(8,128)(2,1)} %pack.3.rest_0_), channel_id=1, source_target_pairs={{0,1},{1,0},{2,3},{3,2},{4,5},{5,4},{6,7},{7,6},{8,9},{9,8},{10,11... | collective-permute-start | bytes 3145736 | tf_op jit(solution)/shard_map/ppermute | solution.py:29
  41.7 14.8 %collective-permute-start.6 = (bf16[128,2048]{1,0:T(8,128)(2,1)}, bf16[128,2048]{1,0:T(8,128)(2,1)}, u32[]{:S(2)}, u32[]{:S(2)}) collective-permute-start(bf16[128,2048]{1,0:T(8,128)(2,1)} %get-tuple-element.27), channel_id=1, source_target_pairs={{0,4},{4,0},{8,12},{12,8},{1,5},{5,1},{9,13},{13,9},{2,6},{6,2},{1... | collective-permute-start | bytes 1572872 | tf_op jit(solution)/shard_map/ppermute | solution.py:29
  49.4 18.4 %all-to-all-start = ((bf16[4,512,256]{2,1,0:T(8,128)(2,1)}), bf16[4,512,256]{2,1,0:T(8,128)(2,1)S(1)}, u32[]{:S(2)}, u32[]{:S(2)}) async-start(bf16[4,512,256]{2,1,0:T(8,128)(2,1)} %after.7), calls=%async_computation | async-start | bytes 2097152 | tf_op jit(solution)/shard_map/all_to_all | solution.py:312
  53.0 26.8 %collective-permute-start.12 = (bf16[128,2048]{1,0:T(8,128)(2,1)}, bf16[128,2048]{1,0:T(8,128)(2,1)}, u32[]{:S(2)}, u32[]{:S(2)}) collective-permute-start(bf16[128,2048]{1,0:T(8,128)(2,1)} %copy-done.22), channel_id=1, source_target_pairs={{0,8},{4,12},{8,0},{12,4},{1,9},{5,13},{9,1},{13,5},{2,10},{6,14},... | collective-permute-start | bytes 1572872 | tf_op jit(solution)/shard_map/ppermute | solution.py:29
  54.5 30.4 %collective-permute-start.10 = (bf16[128,2048]{1,0:T(8,128)(2,1)}, bf16[128,2048]{1,0:T(8,128)(2,1)}, u32[]{:S(2)}, u32[]{:S(2)}) collective-permute-start(bf16[128,2048]{1,0:T(8,128)(2,1)} %get-tuple-element.30.refs_0_), channel_id=1, source_target_pairs={{0,2},{1,3},{2,0},{3,1},{4,6},{5,7},{6,4},{7,5},{8,10},{9,11},{10,... | collective-permute-start | bytes 1572872 | tf_op jit(solution)/shard_map/ppermute | solution.py:29
  56.5 33.4 %collective-permute-start.7 = (bf16[128,2048]{1,0:T(8,128)(2,1)}, bf16[128,2048]{1,0:T(8,128)(2,1)}, u32[]{:S(2)}, u32[]{:S(2)}) collective-permute-start(bf16[128,2048]{1,0:T(8,128)(2,1)} %collective-permute-done.6.refs_0_), channel_id=1, source_target_pairs={{0,2},{1,3},{2,0},{3,1},{4,6},{5,7},{6,4},{7,5},{8,10},{9,11},{10,... | collective-permute-start | bytes 1572872 | tf_op jit(solution)/shard_map/ppermute | solution.py:29
  81.1 89.8 %all-to-all-start.1 = ((bf16[4,128,2048]{2,1,0:T(8,128)(2,1)}), bf16[4,128,2048]{2,1,0:T(8,128)(2,1)S(1)}, u32[]{:S(2)}, u32[]{:S(2)}) async-start(bf16[4,128,2048]{2,1,0:T(8,128)(2,1)} %copy-done), calls=%async_computation.1 | async-start | bytes 4194304 | tf_op jit(solution)/shard_map/all_to_all | solution.py:337
  84.9 22.9 %copy-start.5 = (f32[1,2048,256]{2,1,0:T(8,128)S(1)}, f32[1,2048,256]{2,1,0:T(8,128)}, u32[]{:S(2)}) copy-start(f32[1,2048,256]{2,1,0:T(8,128)} %param.9) | copy-start | bytes 6291460
  84.9 22.9 %copy-start.14 = (f32[1,2048,256]{2,1,0:T(8,128)S(1)}, f32[1,2048,256]{2,1,0:T(8,128)}, u32[]{:S(2)}) copy-start(f32[1,2048,256]{2,1,0:T(8,128)} %param.10) | copy-start | bytes 6291460
  86.3 34.0 %copy-start.1 = (bf16[256,2048]{1,0:T(8,128)(2,1)}, bf16[256,2048]{1,0:T(8,128)(2,1)S(1)}, u32[]{:S(2)}) copy-start(bf16[256,2048]{1,0:T(8,128)(2,1)S(1)} %pack.5.rest_4_) | copy-start | bytes 3145732
  86.3 19.6 %collective-permute-start.11 = (bf16[256,2048]{1,0:T(8,128)(2,1)S(1)}, bf16[256,2048]{1,0:T(8,128)(2,1)S(1)}, u32[]{:S(2)}, u32[]{:S(2)}) collective-permute-start(bf16[256,2048]{1,0:T(8,128)(2,1)S(1)} %pack.5.rest_4_), channel_id=1, source_target_pairs={{0,1},{1,0},{2,3},{3,2},{4,5},{5,4},{6,7},{7,6},{8,9},{9,8},{10,11... | collective-permute-start | bytes 3145736 | tf_op jit(solution)/shard_map/ppermute | solution.py:29
  91.2 29.1 %copy-start.3 = (bf16[256,2048]{1,0:T(8,128)(2,1)}, bf16[256,2048]{1,0:T(8,128)(2,1)S(1)}, u32[]{:S(2)}) copy-start(bf16[256,2048]{1,0:T(8,128)(2,1)S(1)} %pack.4.rest_2_) | copy-start | bytes 3145732
  91.2 14.7 %collective-permute-start.8 = (bf16[256,2048]{1,0:T(8,128)(2,1)S(1)}, bf16[256,2048]{1,0:T(8,128)(2,1)S(1)}, u32[]{:S(2)}, u32[]{:S(2)}) collective-permute-start(bf16[256,2048]{1,0:T(8,128)(2,1)S(1)} %pack.4.rest_2_), channel_id=1, source_target_pairs={{0,1},{1,0},{2,3},{3,2},{4,5},{5,4},{6,7},{7,6},{8,9},{9,8},{10,11... | collective-permute-start | bytes 3145736 | tf_op jit(solution)/shard_map/ppermute | solution.py:29
  91.3 14.6 %collective-permute-start.15 = (bf16[128,2048]{1,0:T(8,128)(2,1)}, bf16[128,2048]{1,0:T(8,128)(2,1)S(1)}, u32[]{:S(2)}, u32[]{:S(2)}) collective-permute-start(bf16[128,2048]{1,0:T(8,128)(2,1)} %get-tuple-element.33.rest_6_), channel_id=1, source_target_pairs={{0,2},{1,3},{2,0},{3,1},{4,6},{5,7},{6,4},{7,5},{8,10},{9,11},{10,... | collective-permute-start | bytes 1572872 | tf_op jit(solution)/shard_map/ppermute | solution.py:29
  91.7 14.2 %collective-permute-start.16 = (bf16[128,2048]{1,0:T(8,128)(2,1)}, bf16[128,2048]{1,0:T(8,128)(2,1)S(1)}, u32[]{:S(2)}, u32[]{:S(2)}) collective-permute-start(bf16[128,2048]{1,0:T(8,128)(2,1)} %get-tuple-element.33.rest_6_), channel_id=1, source_target_pairs={{0,1},{1,0},{2,3},{3,2},{4,5},{5,4},{6,7},{7,6},{8,9},{9,8},{10,11... | collective-permute-start | bytes 1572872 | tf_op jit(solution)/shard_map/ppermute | solution.py:29
  105.8 1.9 %collective-permute-start.17 = (bf16[128,2048]{1,0:T(8,128)(2,1)S(1)}, bf16[128,2048]{1,0:T(8,128)(2,1)S(1)}, u32[]{:S(2)}, u32[]{:S(2)}) collective-permute-start(bf16[128,2048]{1,0:T(8,128)(2,1)S(1)} %collective-permute-done.15.rest_7_), channel_id=1, source_target_pairs={{0,1},{1,0},{2,3},{3,2},{4,5},{5,4},{6,7},{7,6},{8,9},{9,8},{10,11... | collective-permute-start | bytes 1572872 | tf_op jit(solution)/shard_map/ppermute | solution.py:29
  120.3 18.3 %collective-permute-start.22 = (bf16[512,256]{1,0:T(8,128)(2,1)S(1)}, bf16[512,256]{1,0:T(8,128)(2,1)S(1)}, u32[]{:S(2)}, u32[]{:S(2)}) collective-permute-start(bf16[512,256]{1,0:T(8,128)(2,1)S(1)} %get-tuple-element.44), channel_id=1, source_target_pairs={{0,4},{4,0},{8,12},{12,8},{1,5},{5,1},{9,13},{13,9},{2,6},{6,2},{1... | collective-permute-start | bytes 786440 | tf_op jit(solution)/shard_map/ppermute | solution.py:29
  122.0 22.3 %collective-permute-start.18 = (bf16[512,256]{1,0:T(8,128)(2,1)}, bf16[512,256]{1,0:T(8,128)(2,1)S(1)}, u32[]{:S(2)}, u32[]{:S(2)}) collective-permute-start(bf16[512,256]{1,0:T(8,128)(2,1)} %get-tuple-element.34), channel_id=1, source_target_pairs={{0,4},{4,0},{8,12},{12,8},{1,5},{5,1},{9,13},{13,9},{2,6},{6,2},{1... | collective-permute-start | bytes 786440 | tf_op jit(solution)/shard_map/ppermute | solution.py:29
  139.4 19.2 %collective-permute-start.23 = (bf16[512,256]{1,0:T(8,128)(2,1)}, bf16[512,256]{1,0:T(8,128)(2,1)}, u32[]{:S(2)}, u32[]{:S(2)}) collective-permute-start(bf16[512,256]{1,0:T(8,128)(2,1)} %add_convert_fusion.2), channel_id=1, source_target_pairs={{0,8},{4,12},{8,0},{12,4},{1,9},{5,13},{9,1},{13,5},{2,10},{6,14},... | collective-permute-start | bytes 786440 | tf_op jit(solution)/shard_map/ppermute | solution.py:29
  156.5 9.2 %collective-permute-start.19 = (bf16[512,256]{1,0:T(8,128)(2,1)S(1)}, bf16[512,256]{1,0:T(8,128)(2,1)S(1)}, u32[]{:S(2)}, u32[]{:S(2)}) collective-permute-start(bf16[512,256]{1,0:T(8,128)(2,1)S(1)} %get-tuple-element.36), channel_id=1, source_target_pairs={{0,4},{4,0},{8,12},{12,8},{1,5},{5,1},{9,13},{13,9},{2,6},{6,2},{1... | collective-permute-start | bytes 786440 | tf_op jit(solution)/shard_map/ppermute | solution.py:29
  156.6 13.8 %collective-permute-start.20 = (bf16[512,256]{1,0:T(8,128)(2,1)S(1)}, bf16[512,256]{1,0:T(8,128)(2,1)S(1)}, u32[]{:S(2)}, u32[]{:S(2)}) collective-permute-start(bf16[512,256]{1,0:T(8,128)(2,1)S(1)} %get-tuple-element.37), channel_id=1, source_target_pairs={{0,4},{4,0},{8,12},{12,8},{1,5},{5,1},{9,13},{13,9},{2,6},{6,2},{1... | collective-permute-start | bytes 786440 | tf_op jit(solution)/shard_map/ppermute | solution.py:29
  159.8 11.1 %collective-permute-start.24 = (bf16[1,2,256,256]{3,2,1,0:T(8,128)(2,1)S(1)}, bf16[1,2,256,256]{3,2,1,0:T(8,128)(2,1)}, u32[]{:S(2)}, u32[]{:S(2)}) collective-permute-start(bf16[1,2,256,256]{3,2,1,0:T(8,128)(2,1)S(1)} %bitcast.25), channel_id=1, source_target_pairs={{0,16},{16,0},{1,17},{17,1},{2,18},{18,2},{3,19},{19,3},{4,20},{20... | collective-permute-start | bytes 786440 | tf_op jit(solution)/shard_map/ppermute | solution.py:34
  170.5 14.0 %collective-permute-start.21 = (bf16[512,256]{1,0:T(8,128)(2,1)S(1)}, bf16[512,256]{1,0:T(8,128)(2,1)S(1)}, u32[]{:S(2)}, u32[]{:S(2)}) collective-permute-start(bf16[512,256]{1,0:T(8,128)(2,1)S(1)} %add_convert_fusion.3), channel_id=1, source_target_pairs={{0,8},{4,12},{8,0},{12,4},{1,9},{5,13},{9,1},{13,5},{2,10},{6,14},... | collective-permute-start | bytes 786440 | tf_op jit(solution)/shard_map/ppermute | solution.py:29
  (25 other events, 161.7 us)
